TPU v7x, 32 devices: a whole 2x2x4 slice. The times are simulated.
32 devices in a mesh: dp: 16 (over z, y, core), tensor: 2 (over x).
Axes of the slice: x: 2, y: 2, z: 4, core: 2. Of those that a mesh axis runs over, the one named last changes fastest.
Arguments:
- cot_student: bfloat16 [16384, 2432], P(('dp', 'tensor')), may hold values from -32 to 32
- cot_fake: bfloat16 [16384, 2432], P(('dp', 'tensor')), may hold values from -32 to 32
- act_student: bfloat16 [1216, 16384], P('tensor', 'dp'), may hold values from -5 to 5
- act_fake: bfloat16 [1216, 16384], P('tensor', 'dp'), may hold values from -5 to 5
- weight_student: bfloat16 [1216, 2432], P('tensor'), may hold values from -0.125 to 0.125
- weight_fake: bfloat16 [1216, 2432], P('tensor'), may hold values from -0.125 to 0.125
- master_student: float32 [1216, 2432], P('tensor', 'dp'), may hold values from -0.15625 to 0.15625
- first_student: float32 [1216, 2432], P('tensor', 'dp'), may hold values from -6 to 6
- second_student: float32 [1216, 2432], P('tensor', 'dp'), may hold values from 0.25 to 4
- master_fake: float32 [1216, 2432], P('tensor', 'dp'), may hold values from -0.15625 to 0.15625
- first_fake: float32 [1216, 2432], P('tensor', 'dp'), may hold values from -6 to 6
- second_fake: float32 [1216, 2432], P('tensor', 'dp'), may hold values from 0.25 to 4
- timesteps: int32 [16, 2, 1], P('dp'), may hold values from 0 to 999
Outputs:
- back_student: bfloat16 [1216, 16384], P('tensor', 'dp')
- back_fake: bfloat16 [1216, 16384], P('tensor', 'dp')
- new_master_student: float32 [1216, 2432], P('tensor', 'dp')
- new_first_student: float32 [1216, 2432], P('tensor', 'dp')
- new_second_student: float32 [1216, 2432], P('tensor', 'dp')
- new_master_fake: float32 [1216, 2432], P('tensor', 'dp')
- new_first_fake: float32 [1216, 2432], P('tensor', 'dp')
- new_second_fake: float32 [1216, 2432], P('tensor', 'dp')
- params_student: bfloat16 [1216, 2432], P('tensor')
- params_fake: bfloat16 [1216, 2432], P('tensor')
All inputs are finite; a program needn't handle non-finite values.
Results may differ from a plain program's by a relative error of at most 0.0011.
Values may be sent and summed in bfloat16 or wider, within the bound.
No kernel may reach another device: no remote copies, remote signals or barrier semaphores. Data moves between devices by JAX's collectives and lax.ppermute only.
A program may use at most 128 MiB of HBM per device.

v0:
```python
import jax
import jax.numpy as jnp
from jax import lax
from jax.sharding import PartitionSpec as P

D = 2432
F = 1216
ROWS = 1024


FIRST_CORRECTION = 0.9999734386011124
SECOND_CORRECTION = 0.0952078529183


def sample_scale(steps, count):
    weights = 1.0 / (0.1 + steps.astype(jnp.float32) / 1000.0)
    which = jnp.arange(count) // ROWS
    onehot = which[:, None] == jnp.arange(steps.shape[0])[None, :]
    return jnp.sum(jnp.where(onehot, weights[None, :], 0.0), axis=1)


def column_term(full_cot, scaled):
    return lax.dot_general(
        full_cot, scaled, (((0,), (1,)), ((), ())), preferred_element_type=jnp.float32
    )


def backward_cols(full_cot, weight, scale):
    product = lax.dot_general(
        weight, full_cot, (((1,), (1,)), ((), ())), preferred_element_type=jnp.float32
    )
    return (product * scale[None, :]).astype(jnp.bfloat16)


def adam_update(grad, squares, master, first, second):
    clip = jnp.minimum(1.0, jnp.sqrt(jnp.float32(D * F)) / jnp.sqrt(squares + 1e-06))
    clipped = grad * clip
    new_first = 0.9 * first + 0.1 * clipped
    new_second = 0.999 * second + 0.001 * clipped * clipped
    step_dir = new_first / FIRST_CORRECTION / (jnp.sqrt(new_second / SECOND_CORRECTION) + 1e-08)
    new_master = master * (1.0 - 0.01 * 0.01) - 0.01 * step_dir
    return (new_master, new_first, new_second)


def per_device(
    cot_student,
    cot_fake,
    act_student,
    act_fake,
    weight_student,
    weight_fake,
    master_student,
    first_student,
    second_student,
    master_fake,
    first_fake,
    second_fake,
    timesteps,
):
    count = act_student.shape[1]
    local_f = act_student.shape[0]
    scale_student = sample_scale(timesteps[0, 0], count)
    scale_fake = sample_scale(timesteps[0, 1], count)
    scaled_student = (act_student.astype(jnp.float32) * scale_student[None, :]).astype(jnp.bfloat16)
    scaled_fake = (act_fake.astype(jnp.float32) * scale_fake[None, :]).astype(jnp.bfloat16)
    full_student, full_fake = (
        lax.all_gather(cot_student, "tensor", axis=0, tiled=True),
        lax.all_gather(cot_fake, "tensor", axis=0, tiled=True),
    )
    summed = lax.psum_scatter(
        jnp.concatenate(
            [column_term(full_student, scaled_student), column_term(full_fake, scaled_fake)], axis=1
        ),
        "dp",
        scatter_dimension=0,
        tiled=True,
    )
    grad_student = summed[:, :local_f].T
    grad_fake = summed[:, local_f:].T
    back_student = backward_cols(full_student, weight_student, scale_student)
    back_fake = backward_cols(full_fake, weight_fake, scale_fake)
    squares_student, squares_fake = lax.psum(
        (jnp.sum(grad_student * grad_student), jnp.sum(grad_fake * grad_fake)), ("dp", "tensor")
    )
    master_s, first_s, second_s = adam_update(
        grad_student, squares_student, master_student, first_student, second_student
    )
    master_f, first_f, second_f = adam_update(
        grad_fake, squares_fake, master_fake, first_fake, second_fake
    )
    params_student, params_fake = (
        lax.all_gather(master_s.astype(jnp.bfloat16), "dp", axis=1, tiled=True),
        lax.all_gather(master_f.astype(jnp.bfloat16), "dp", axis=1, tiled=True),
    )
    return (
        back_student,
        back_fake,
        master_s,
        first_s,
        second_s,
        master_f,
        first_f,
        second_f,
        params_student,
        params_fake,
    )


def solution(mesh):
    placed = (
        P(("dp", "tensor"), None),
        P(("dp", "tensor"), None),
        P("tensor", "dp"),
        P("tensor", "dp"),
        P("tensor", None),
        P("tensor", None),
        P("tensor", "dp"),
        P("tensor", "dp"),
        P("tensor", "dp"),
        P("tensor", "dp"),
        P("tensor", "dp"),
        P("tensor", "dp"),
        P("dp", None, None),
    )
    return jax.shard_map(
        per_device,
        mesh=mesh,
        in_specs=placed,
        out_specs=(
            P("tensor", "dp"),
            P("tensor", "dp"),
            P("tensor", "dp"),
            P("tensor", "dp"),
            P("tensor", "dp"),
            P("tensor", "dp"),
            P("tensor", "dp"),
            P("tensor", "dp"),
            P("tensor", None),
            P("tensor", None),
        ),
        check_vma=False,
    )
```

profile of v0, /device:TPU:0, one launch (start us, length us, event | category | flops | bytes accessed | tf_op | source)
XLA Modules:
  0.0 462.0 jit_solution(12865829918058561908)
XLA Ops:
  7.2 0.0 copy-start
  7.2 0.0 copy-start.2
  7.2 0.0 all-gather.5.cloned.1.call-start
  7.2 0.7 all-gather.5.cloned.1.call-update
  7.9 0.0 all-gather.7.cloned.1.call-start
  8.0 0.7 all-gather.7.cloned.1.call-update
  8.7 0.0 reduce-scatter.4.cloned.1.call-start
  8.7 0.6 fusion.16
  10.7 67.2 %all-gather.5.cloned.1.call-done = bf16[1024,2432]{1,0:T(8,128)(2,1)} async-done(((bf16[512,2432]{1,0:T(8,128)(2,1)}), bf16[1024,2432]{1,0:T(8,128)(2,1)}) %all-gather.5.cloned.1.call-update) | async-done | bytes 4980752 | tf_op jit(solution)/shard_map/all_gather | solution.py:67
  77.9 9.0 %convolution_bitcast_fusion.1 = f32[2432,608]{0,1:T(8,128)} fusion(bf16[1024,2432]{1,0:T(8,128)(2,1)} %all-gather.5.cloned.1.call-done, bf16[608,1024]{1,0:T(8,128)(2,1)} %param.15, f32[1024]{0:T(1024)S(1)} %broadcast_select_fusion.1), kind=kOutput, calls=%fused_computation.2 | convolution fusion | flops 3030155264 | bytes 12144640 | tf_op jit(solution)/shard_map/dot_general | solution.py:23
  86.9 58.2 %all-gather.7.cloned.1.call-done = bf16[1024,2432]{1,0:T(8,128)(2,1)} async-done(((bf16[512,2432]{1,0:T(8,128)(2,1)}), bf16[1024,2432]{1,0:T(8,128)(2,1)}) %all-gather.7.cloned.1.call-update) | async-done | bytes 4980752 | tf_op jit(solution)/shard_map/all_gather | solution.py:68
  145.1 8.7 %convolution_bitcast_fusion = f32[2432,608]{0,1:T(8,128)} fusion(bf16[1024,2432]{1,0:T(8,128)(2,1)} %all-gather.7.cloned.1.call-done, bf16[608,1024]{1,0:T(8,128)(2,1)} %param.16, f32[1024]{0:T(1024)S(1)} %broadcast_select_fusion), kind=kOutput, calls=%fused_computation.1 | convolution fusion | flops 3030155264 | bytes 12144640 | tf_op jit(solution)/shard_map/dot_general | solution.py:23
  153.8 9.5 %pad_maximum_fusion = f32[2432,1216]{0,1:T(8,128)} fusion(f32[2432,608]{0,1:T(8,128)} %convolution_bitcast_fusion, f32[2432,608]{0,1:T(8,128)} %convolution_bitcast_fusion.1), kind=kLoop, calls=%fused_computation | loop fusion | flops 2957312 | bytes 23658496 | tf_op jit(solution)/shard_map/concatenate | solution.py:71
  163.3 13.7 %copy.55 = f32[2432,1216]{1,0:T(8,128)} copy(f32[2432,1216]{0,1:T(8,128)} %pad_maximum_fusion) | data formatting | bytes 23658496
  177.0 0.0 reduce-scatter.4.cloned.1.call-update
  177.0 0.0 all-gather.11.cloned.1.call-start
  177.1 134.2 %reduce-scatter.4.cloned.1.call-done = f32[152,1216]{1,0:T(8,128)} async-done(((f32[2432,1216]{1,0:T(8,128)}), f32[152,1216]{1,0:T(8,128)}) %reduce-scatter.4.cloned.1.call-update) | async-done | bytes 739344 | tf_op jit(solution)/shard_map/reduce_scatter | solution.py:70
  311.3 1.9 multiply_reduce_fusion
  313.2 39.6 %all-reduce = (f32[]{:T(128)}, f32[]{:T(128)}) all-reduce(f32[]{:T(128)} %get-tuple-element.41, f32[]{:T(128)} %get-tuple-element.40), channel_id=1, replica_groups=mesh['dp'=16,'tensor'=2] {'dp','tensor'}, use_global_device_ids=true, to_apply=%region_2.3 | all-reduce | flops 2 | bytes 16 | tf_op jit(solution)/shard_map/psum | solution.py:82
  354.2 0.0 copy-done.1
  354.2 3.6 fusion.10
  357.8 0.0 all-gather.11.cloned.1.call-update
  357.8 0.0 all-gather.9.cloned.1.call-start
  357.9 0.5 all-gather.9.cloned.1.call-update
  358.4 0.0 copy-start.3
  358.5 7.0 %multiply_convert_fusion.3 = bf16[608,1024]{1,0:T(8,128)(2,1)} fusion(bf16[608,2432]{1,0:T(8,128)(2,1)S(1)} %copy-done, bf16[1024,2432]{1,0:T(8,128)(2,1)} %all-gather.5.cloned.1.call-done, f32[1024]{0:T(1024)S(1)} %broadcast_select_fusion.1), kind=kOutput, calls=%fused_computation.6 | convolution fusion | flops 3029532672 | bytes 9187328 | tf_op jit(solution)/shard_map/dot_general | solution.py:29
  365.5 0.0 copy-done.3
  365.5 6.9 %multiply_convert_fusion.2 = bf16[608,1024]{1,0:T(8,128)(2,1)} fusion(bf16[608,2432]{1,0:T(8,128)(2,1)S(1)} %copy-done.3, bf16[1024,2432]{1,0:T(8,128)(2,1)} %all-gather.7.cloned.1.call-done, f32[1024]{0:T(1024)S(1)} %broadcast_select_fusion), kind=kOutput, calls=%fused_computation.5 | convolution fusion | flops 3029532672 | bytes 9187328 | tf_op jit(solution)/shard_map/dot_general | solution.py:29
  372.4 30.9 %all-gather.11.cloned.1.call-done = bf16[608,2432]{0,1:T(8,128)(2,1)} async-done(((bf16[608,152]{0,1:T(8,128)(2,1)}), bf16[608,2432]{0,1:T(8,128)(2,1)}) %all-gather.11.cloned.1.call-update) | async-done | bytes 2957328 | tf_op jit(solution)/shard_map/all_gather | solution.py:93
  403.3 5.5 %copy.54 = bf16[608,2432]{1,0:T(8,128)(2,1)} copy(bf16[608,2432]{0,1:T(8,128)(2,1)} %all-gather.11.cloned.1.call-done) | data formatting | bytes 5914624
  408.8 41.2 %all-gather.9.cloned.1.call-done = bf16[608,2432]{0,1:T(8,128)(2,1)} async-done(((bf16[608,152]{0,1:T(8,128)(2,1)}), bf16[608,2432]{0,1:T(8,128)(2,1)}) %all-gather.9.cloned.1.call-update) | async-done | bytes 2957328 | tf_op jit(solution)/shard_map/all_gather | solution.py:92
  450.0 5.5 %copy.53 = bf16[608,2432]{1,0:T(8,128)(2,1)} copy(bf16[608,2432]{0,1:T(8,128)(2,1)} %all-gather.9.cloned.1.call-done) | data formatting | bytes 5914624
  (5 shorter events, 0.0 us)
Async XLA Ops:
  7.2 351.3 %copy-start = (bf16[608,2432]{1,0:T(8,128)(2,1)S(1)}, bf16[608,2432]{1,0:T(8,128)(2,1)}, u32[]{:S(2)}) copy-start(bf16[608,2432]{1,0:T(8,128)(2,1)} %param.17) | copy-start | bytes 8871940
  7.2 1.5 copy-start.2
  7.2 70.7 %all-gather.5.cloned.1.call-start = ((), (), s32[]{:S(2)}) async-start(), calls=%async_computation.1 | async-start | bytes 7471104 | tf_op jit(solution)/shard_map/all_gather | solution.py:67
  7.9 137.2 %all-gather.7.cloned.1.call-start = ((), (), s32[]{:S(2)}) async-start(), calls=%async_computation.2 | async-start | bytes 7471104 | tf_op jit(solution)/shard_map/all_gather | solution.py:68
  8.7 302.6 %reduce-scatter.4.cloned.1.call-start = ((), (), s32[]{:S(2)}) async-start(), calls=%async_computation.5 | async-start | bytes 13230080 | tf_op jit(solution)/shard_map/reduce_scatter | solution.py:70
  177.0 177.2 %copy-start.1 = (f32[608,152]{0,1:T(8,128)S(1)}, f32[608,152]{0,1:T(8,128)}, u32[]{:S(2)}) copy-start(f32[608,152]{0,1:T(8,128)} %param.22) | copy-start | bytes 1108996
  177.0 226.3 %all-gather.11.cloned.1.call-start = ((), (), s32[]{:S(2)}) async-start(), calls=%async_computation.4 | async-start | bytes 3307520 | tf_op jit(solution)/shard_map/all_gather | solution.py:93
  357.8 92.2 %all-gather.9.cloned.1.call-start = ((), (), s32[]{:S(2)}) async-start(), calls=%async_computation.3 | async-start | bytes 3307520 | tf_op jit(solution)/shard_map/all_gather | solution.py:92
  358.4 7.0 %copy-start.3 = (bf16[608,2432]{1,0:T(8,128)(2,1)S(1)}, bf16[608,2432]{1,0:T(8,128)(2,1)}, u32[]{:S(2)}) copy-start(bf16[608,2432]{1,0:T(8,128)(2,1)} %param.18) | copy-start | bytes 8871940
Sparse Core Ops, SparseCore 0:
  9.6 68.2 all-gather.4
  79.5 65.5 all-gather.6
  177.2 134.0 reduce-scatter.3
  358.0 45.3 all-gather.10
  406.1 43.8 all-gather.8
where the time goes:
time: 463 us; the launch traced here: 462 us
  waiting for transfers between devices  334 us (72%)
  blocking collectives  39.6 us (9%)
  matrix products  31.6 us (7%)
  local copies, waits for them, and re-layouts  25.3 us (5%)
  between operations  16.6 us (4%)
  other arithmetic  15 us (3%)
    reduce_scatter x1, waiting for transfers between devices, per_device(): lax.psum_scatter(jnp.concatenate([column_term(full_student, scaled_studen...  134 us
    all_gather x1, waiting for transfers between devices, per_device(): lax.all_gather(cot_student, 'tensor', axis=0, tiled=True)  67.2 us
    all_gather x1, waiting for transfers between devices, per_device(): lax.all_gather(cot_fake, 'tensor', axis=0, tiled=True)  58.2 us
    all_gather x1, waiting for transfers between devices, per_device(): lax.all_gather(master_s.astype(jnp.bfloat16), 'dp', axis=1, tiled=True)  41.2 us
    psum x1, blocking collectives, per_device(): lax.psum((jnp.sum(grad_student * grad_student), jnp.sum(grad_fake * grad_...  39.6 us
    all_gather x1, waiting for transfers between devices, per_device(): lax.all_gather(master_f.astype(jnp.bfloat16), 'dp', axis=1, tiled=True)  30.9 us
    unnamed x11, local copies, waits for them, and re-layouts  24.7 us
    dot_general x2, matrix products, column_term(): lax.dot_general(full_cot, scaled, (((0,), (1,)), ((), ())), preferred_ele...  17.7 us
  transfers between devices with their start and end apart: 5, of which 5 were waited for; matrix products, arithmetic and copies ran while one was open for 6% of the time, Pallas kernels for 0%

commit v1 on v0

v1 whole, which is shorter than its diff:
```python
import jax
import jax.numpy as jnp
from jax import lax
from jax.sharding import PartitionSpec as P

D = 2432
F = 1216
ROWS = 1024


FIRST_CORRECTION = 0.9999734386011124
SECOND_CORRECTION = 0.0952078529183

OUTER = 4


def sample_scale(steps, count):
    weights = 1.0 / (0.1 + steps.astype(jnp.float32) / 1000.0)
    which = jnp.arange(count) // ROWS
    onehot = which[:, None] == jnp.arange(steps.shape[0])[None, :]
    return jnp.sum(jnp.where(onehot, weights[None, :], 0.0), axis=1)


def adam_update(grad, squares, master, first, second):
    clip = jnp.minimum(1.0, jnp.sqrt(jnp.float32(D * F)) / jnp.sqrt(squares + 1e-06))
    clipped = grad * clip
    new_first = 0.9 * first + 0.1 * clipped
    new_second = 0.999 * second + 0.001 * clipped * clipped
    step_dir = new_first / FIRST_CORRECTION / (jnp.sqrt(new_second / SECOND_CORRECTION) + 1e-08)
    new_master = master * (1.0 - 0.01 * 0.01) - 0.01 * step_dir
    return (new_master, new_first, new_second)


def after(value, *others):
    return lax.optimization_barrier((value, *others))[0]


def solution(mesh):
    n_dp, n_tensor = mesh.shape["dp"], mesh.shape["tensor"]
    inner = n_dp // (2 * OUTER)

    def split(p):
        return (p >> inner.bit_length()) & (OUTER - 1), (p >> 1) & (inner - 1), p & 1

    def join(z, m, c):
        return (z * inner + m) * 2 + c

    def move_dp(value, where):
        perm = [(p, join(*where(*split(p)))) for p in range(n_dp)]
        return lax.ppermute(value, "dp", perm)

    def to_plane(value, k):
        return move_dp(value, lambda z, m, c: ((z + k) & (OUTER - 1), m, c))

    def to_middle(value, k):
        return move_dp(value, lambda z, m, c: (z, (m + k) & (inner - 1), c))

    def to_core(value):
        return move_dp(value, lambda z, m, c: (z, m, 1 - c))

    def from_tensor(value, k):
        perm = [(s, (s - k) & (n_tensor - 1)) for s in range(n_tensor)]
        return lax.ppermute(value, "tensor", perm)

    def all_sum(value):
        step = 1
        while step < n_dp:
            value = value + lax.ppermute(value, "dp", [(p, p ^ step) for p in range(n_dp)])
            step *= 2
        step = 1
        while step < n_tensor:
            value = value + lax.ppermute(value, "tensor", [(p, p ^ step) for p in range(n_tensor)])
            step *= 2
        return value

    def per_device(
        cot_student, cot_fake, act_student, act_fake, weight_student, weight_fake,
        master_student, first_student, second_student, master_fake, first_fake, second_fake,
        timesteps,
    ):
        t = lax.axis_index("tensor")
        z, m, c = split(lax.axis_index("dp"))
        f, count = act_student.shape
        r = cot_student.shape[0]
        width = D // n_dp
        plane = D // OUTER

        def pick(value, index):
            return lax.dynamic_index_in_dim(value, index, 0, keepdims=False)

        def rows_of(value, k):
            start = ((t + k) & (n_tensor - 1)) * r
            return lax.dynamic_slice(value, (0, start), (value.shape[0], r))

        nets = (
            (cot_student, act_student, timesteps[0, 0]),
            (cot_fake, act_fake, timesteps[0, 1]),
        )
        prepared = []
        for cot, act, steps in nets:
            scale = sample_scale(steps, count)
            scaled = (act.astype(jnp.float32) * scale[None, :]).astype(jnp.bfloat16)
            prepared.append((cot.T, scaled, scale))

        order = [(n, k) for n in range(2) for k in reversed(range(OUTER))]
        pieces, arrived = {}, []
        for place, (n, k) in enumerate(order):
            own = lax.dynamic_slice(
                prepared[n][0], (plane * ((z + k) & (OUTER - 1)), 0), (plane, r)
            )
            if place >= 2:
                own = after(own, arrived[place - 2])
            others = [from_tensor(own, i) for i in range(1, n_tensor)]
            arrived.append(others[-1])
            pieces[n, k] = [own, *others]

        totals = [None, None]
        for n, k in order:
            grad = None
            for i, piece in enumerate(pieces[n, k]):
                term = lax.dot_general(
                    piece, rows_of(prepared[n][1], i), (((1,), (1,)), ((), ())),
                    preferred_element_type=jnp.float32,
                )
                grad = term if grad is None else grad + term
            grad = grad.reshape(inner, 2, width, f).swapaxes(0, 1)
            grad = pick(grad, c) + to_core(pick(grad, 1 - c))
            mine = pick(grad, m)
            for i in range(1, inner):
                mine = mine + to_middle(pick(grad, (m + i) & (inner - 1)), i)
            if k:
                mine = to_plane(mine, k)
            totals[n] = mine if totals[n] is None else totals[n] + mine

        states = (
            (master_student, first_student, second_student),
            (master_fake, first_fake, second_fake),
        )
        updated, params = [], []
        for n in range(2):
            squares = all_sum(jnp.sum(totals[n] * totals[n]))
            new = adam_update(totals[n], squares, *(state.T for state in states[n]))
            updated.append([value.T for value in new])
            own = new[0].astype(jnp.bfloat16)
            planes = []
            for k in range(OUTER):
                got = to_plane(own, -k) if k else own
                planes.append([got] + [to_middle(got, -i) for i in range(1, inner)])
            stack = jnp.stack([jnp.stack(row) for row in planes])
            stack = jnp.concatenate([stack, stack], axis=0)
            stack = lax.dynamic_slice_in_dim(stack, (OUTER - z) & (OUTER - 1), OUTER, 0)
            stack = jnp.concatenate([stack, stack], axis=1)
            stack = lax.dynamic_slice_in_dim(stack, (inner - m) & (inner - 1), inner, 1)
            other = to_core(stack)
            both = jnp.stack(
                [jnp.where(c == 0, stack, other), jnp.where(c == 0, other, stack)], axis=2
            )
            params.append(both.reshape(D, f).T)

        backs = []
        for n, weight in enumerate((weight_student, weight_fake)):
            scale = prepared[n][2]
            cols = []
            for i in range(n_tensor):
                whole = jnp.concatenate([pieces[n, k][i] for k in range(OUTER)], axis=0)
                whole = jnp.concatenate([whole, whole], axis=0)
                whole = lax.dynamic_slice_in_dim(whole, plane * ((OUTER - z) & (OUTER - 1)), D, 0)
                cols.append(
                    lax.dot_general(
                        weight, whole, (((1,), (0,)), ((), ())),
                        preferred_element_type=jnp.float32,
                    )
                )
            product = jnp.concatenate(cols + cols, axis=1)
            product = lax.dynamic_slice_in_dim(
                product, r * ((n_tensor - t) & (n_tensor - 1)), count, 1
            )
            backs.append((product * scale[None, :]).astype(jnp.bfloat16))

        return (
            backs[0], backs[1], *updated[0], *updated[1], params[0], params[1],
        )

    placed = (
        P(("dp", "tensor"), None),
        P(("dp", "tensor"), None),
        P("tensor", "dp"),
        P("tensor", "dp"),
        P("tensor", None),
        P("tensor", None),
        P("tensor", "dp"),
        P("tensor", "dp"),
        P("tensor", "dp"),
        P("tensor", "dp"),
        P("tensor", "dp"),
        P("tensor", "dp"),
        P("dp", None, None),
    )
    return jax.shard_map(
        per_device,
        mesh=mesh,
        in_specs=placed,
        out_specs=(
            P("tensor", "dp"),
            P("tensor", "dp"),
            P("tensor", "dp"),
            P("tensor", "dp"),
            P("tensor", "dp"),
            P("tensor", "dp"),
            P("tensor", "dp"),
            P("tensor", "dp"),
            P("tensor", None),
            P("tensor", None),
        ),
        check_vma=False,
    )
```

time: 463 us -> 330 us (0.71)
  waiting for transfers between devices: 334 us -> 129 us
  starting transfers between devices: 0.2 us -> 84.6 us
  blocking collectives: 39.6 us -> 0 us
  local copies, waits for them, and re-layouts: 25.3 us -> 56.7 us
  matrix products: 31.6 us -> 21.4 us
  other arithmetic: 15 us -> 24.8 us
  between operations: 16.6 us -> 10.8 us
    all_gather x4 -> x0, waiting for transfers between devices: 198 us -> none  [the longest x1 67.2 us: per_device(): lax.all_gather(cot_student, 'tensor', axis=0, tiled=True)]
    reduce_scatter x1 -> x0, waiting for transfers between devices: 134 us -> none  [per_device(): lax.psum_scatter(jnp.concatenate([column_term(full_student, scaled_studen...]
    ppermute x0 -> x56, waiting for transfers between devices: none -> 129 us  [the longest x38 75 us: move_dp(): return lax.ppermute(value, 'dp', perm)]
    ppermute x0 -> x56, starting transfers between devices: none -> 84.6 us  [the longest x38 42.7 us: move_dp(): return lax.ppermute(value, 'dp', perm)]
    psum x1 -> x0, blocking collectives: 39.6 us -> none  [per_device(): lax.psum((jnp.sum(grad_student * grad_student), jnp.sum(grad_fake * grad_...]
    unnamed x11 -> x88, local copies, waits for them, and re-layouts: 24.7 us -> 38.4 us
    another operation x0 -> x3, local copies, waits for them, and re-layouts: none -> 12.1 us
    dot_general x4 -> x20, matrix products: 31.6 us -> 21.4 us  [the longest x16 14.3 us: per_device(): lax.dot_general(piece, rows_of(prepared[n][1], i), (((1,), (1,)), ((), ()...]
  transfers between devices with their start and end apart: 5 -> 56, of which waited for: 5 -> 33; matrix products, arithmetic and copies ran while one was open for 6% -> 21% of each run, Pallas kernels for 0% -> 0%
where the time goes in v1:
time: 330 us; the launch traced here: 327 us
  waiting for transfers between devices  129 us (39%)
  starting transfers between devices  84.6 us (26%)
  local copies, waits for them, and re-layouts  56.7 us (17%)
  other arithmetic  24.8 us (8%)
  matrix products  21.4 us (6%)
  between operations  10.8 us (3%)
    ppermute x38, waiting for transfers between devices, move_dp(): return lax.ppermute(value, 'dp', perm)  75 us
    ppermute x8, waiting for transfers between devices, from_tensor(): return lax.ppermute(value, 'tensor', perm)  46.5 us
    ppermute x38, starting transfers between devices, move_dp(): return lax.ppermute(value, 'dp', perm)  42.7 us
    unnamed x88, local copies, waits for them, and re-layouts  38.4 us
    ppermute x8, starting transfers between devices, all_sum(): lax.ppermute(value, 'dp', [(p, p ^ step) for p in range(n_dp)])  24.9 us
    dot_general x16, matrix products, per_device(): lax.dot_general(piece, rows_of(prepared[n][1], i), (((1,), (1,)), ((), ()...  14.3 us
    ppermute x8, starting transfers between devices, from_tensor(): return lax.ppermute(value, 'tensor', perm)  11.3 us
    another operation x1, local copies, waits for them, and re-layouts  8.34 us
  transfers between devices with their start and end apart: 56, of which 33 were waited for; matrix products, arithmetic and copies ran while one was open for 21% of the time, Pallas kernels for 0%

profile of v1, /device:TPU:0, one launch (start us, length us, event | category | flops | bytes accessed | tf_op | source)
XLA Modules:
  0.0 326.9 jit_solution(14406798284242887161)
XLA Ops:
  0.7 8.3 %constant_dynamic-slice_fusion.2 = (bf16[512,608]{1,0:T(8,128)(2,1)}, bf16[512,608]{1,0:T(8,128)(2,1)}, bf16[512,608]{1,0:T(8,128)(2,1)}, bf16[512,608]{1,0:T(8,...) fusion(bf16[512,2432]{1,0:T(8,128)(2,1)} %param.14, ...), kind=kLoop, calls=%fused_computation.200 | loop fusion | bytes 9961488 | tf_op jit(solution)/shard_map/dynamic-slice.7
  11.2 2.9 collective-permute-start
  34.5 8.2 %collective-permute-done.1 = bf16[608,512]{1,0:T(8,128)(2,1)} collective-permute-done((bf16[608,512]{1,0:T(8,128)(2,1)}, bf16[608,512]{1,0:T(8,128)(2,1)}, u32[]{:S(2)}, u32[]{:S(2)}) %collective-permute-start.1) | collective-permute-done | bytes 622624 | tf_op jit(solution)/shard_map/ppermute | solution.py:63
  49.0 6.8 %collective-permute-done.2 = bf16[608,512]{1,0:T(8,128)(2,1)S(1)} collective-permute-done((bf16[608,512]{1,0:T(8,128)(2,1)}, bf16[608,512]{1,0:T(8,128)(2,1)S(1)}, u32[]{:S(2)}, u32[]{:S(2)}) %collective-permute-start.2) | collective-permute-done | bytes 622624 | tf_op jit(solution)/shard_map/ppermute | solution.py:63
  55.9 12.5 %collective-permute-done.3 = bf16[608,512]{1,0:T(8,128)(2,1)S(1)} collective-permute-done((bf16[608,512]{1,0:T(8,128)(2,1)}, bf16[608,512]{1,0:T(8,128)(2,1)S(1)}, u32[]{:S(2)}, u32[]{:S(2)}) %collective-permute-start.3) | collective-permute-done | bytes 622624 | tf_op jit(solution)/shard_map/ppermute | solution.py:63
  88.6 7.4 %collective-permute-done.5 = bf16[608,512]{1,0:T(8,128)(2,1)S(1)} collective-permute-done((bf16[608,512]{1,0:T(8,128)(2,1)S(1)}, bf16[608,512]{1,0:T(8,128)(2,1)S(1)}, u32[]{:S(2)}, u32[]{:S(2)}) %collective-permute-start.5) | collective-permute-done | bytes 622624 | tf_op jit(solution)/shard_map/ppermute | solution.py:63
  96.0 11.6 %collective-permute-done.4 = bf16[608,512]{1,0:T(8,128)(2,1)S(1)} collective-permute-done((bf16[608,512]{1,0:T(8,128)(2,1)S(1)}, bf16[608,512]{1,0:T(8,128)(2,1)S(1)}, u32[]{:S(2)}, u32[]{:S(2)}) %collective-permute-start.4) | collective-permute-done | bytes 622624 | tf_op jit(solution)/shard_map/ppermute | solution.py:63
  117.7 8.0 %collective-permute-done.12 = f32[152,608]{1,0:T(8,128)S(1)} collective-permute-done((f32[152,608]{1,0:T(8,128)S(1)}, f32[152,608]{1,0:T(8,128)S(1)}, u32[]{:S(2)}, u32[]{:S(2)}) %collective-permute-start.12) | collective-permute-done | bytes 369696 | tf_op jit(solution)/shard_map/ppermute | solution.py:50
  127.2 6.8 %collective-permute-done.9 = f32[152,608]{1,0:T(8,128)S(1)} collective-permute-done((f32[152,608]{1,0:T(8,128)S(1)}, f32[152,608]{1,0:T(8,128)S(1)}, u32[]{:S(2)}, u32[]{:S(2)}) %collective-permute-start.9) | collective-permute-done | bytes 369696 | tf_op jit(solution)/shard_map/ppermute | solution.py:50
  136.6 5.8 %collective-permute-done.15 = f32[152,608]{1,0:T(8,128)S(1)} collective-permute-done((f32[152,608]{1,0:T(8,128)S(1)}, f32[152,608]{1,0:T(8,128)S(1)}, u32[]{:S(2)}, u32[]{:S(2)}) %collective-permute-start.15) | collective-permute-done | bytes 369696 | tf_op jit(solution)/shard_map/ppermute | solution.py:50
  142.4 3.5 %collective-permute-start.10 = (f32[152,608]{1,0:T(8,128)S(1)}, f32[152,608]{1,0:T(8,128)S(1)}, u32[]{:S(2)}, u32[]{:S(2)}) collective-permute-start(f32[152,608]{1,0:T(8,128)S(1)} %bitcast_add_fusion.16), channel_id=1, source_target_pairs={{0,24},{2,26},{4,28},{6,30},{8,0},{10,2},{12,4},{14,6},{16,8},{18,... | collective-permute-start | bytes 1109000 | tf_op jit(solution)/shard_map/ppermute | solution.py:50
  164.7 2.8 collective-permute-start.20
  168.9 5.8 %collective-permute-start.21 = (f32[]{:T(128)}, f32[]{:T(128)}, u32[]{:S(2)}, u32[]{:S(2)}) collective-permute-start(f32[]{:T(128)} %add.326), channel_id=1, source_target_pairs={{0,8},{2,10},{4,12},{6,14},{8,0},{10,2},{12,4},{14,6},{16,24},{18,... | collective-permute-start | bytes 20 | tf_op jit(solution)/shard_map/ppermute | solution.py:68
  175.6 4.7 %collective-permute-start.22 = (f32[]{:T(128)}, f32[]{:T(128)}, u32[]{:S(2)}, u32[]{:S(2)}) collective-permute-start(f32[]{:T(128)} %add.327), channel_id=1, source_target_pairs={{0,16},{2,18},{4,20},{6,22},{8,24},{10,26},{12,28},{14,30},{16,0},... | collective-permute-start | bytes 20 | tf_op jit(solution)/shard_map/ppermute | solution.py:68
  181.1 2.8 collective-permute-start.23
  185.3 2.7 fusion.105
  196.7 6.9 %collective-permute-start.45 = (bf16[152,608]{1,0:T(8,128)(2,1)S(1)}, bf16[152,608]{1,0:T(8,128)(2,1)S(1)}, u32[]{:S(2)}, u32[]{:S(2)}) collective-permute-start(bf16[152,608]{1,0:T(8,128)(2,1)S(1)} %get-tuple-element.44), channel_id=1, source_target_pairs={{0,8},{2,10},{4,12},{6,14},{8,16},{10,18},{12,20},{14,22},{16,24},... | collective-permute-start | bytes 554504 | tf_op jit(solution)/shard_map/ppermute | solution.py:50
  207.9 4.4 %collective-permute-done.44 = bf16[152,608]{1,0:T(8,128)(2,1)S(1)} collective-permute-done((bf16[152,608]{1,0:T(8,128)(2,1)S(1)}, bf16[152,608]{1,0:T(8,128)(2,1)S(1)}, u32[]{:S(2)}, u32[]{:S(2)}) %collective-permute-start.44) | collective-permute-done | bytes 184864 | tf_op jit(solution)/shard_map/ppermute | solution.py:50
  221.6 6.9 %collective-permute-done.28 = f32[152,608]{1,0:T(8,128)S(1)} collective-permute-done((f32[152,608]{1,0:T(8,128)S(1)}, f32[152,608]{1,0:T(8,128)S(1)}, u32[]{:S(2)}, u32[]{:S(2)}) %collective-permute-start.28) | collective-permute-done | bytes 369696 | tf_op jit(solution)/shard_map/ppermute | solution.py:50
  228.6 8.2 %collective-permute-done.25 = f32[152,608]{1,0:T(8,128)S(1)} collective-permute-done((f32[152,608]{1,0:T(8,128)S(1)}, f32[152,608]{1,0:T(8,128)S(1)}, u32[]{:S(2)}, u32[]{:S(2)}) %collective-permute-start.25) | collective-permute-done | bytes 369696 | tf_op jit(solution)/shard_map/ppermute | solution.py:50
  237.0 7.9 %collective-permute-done.31 = f32[152,608]{1,0:T(8,128)S(1)} collective-permute-done((f32[152,608]{1,0:T(8,128)S(1)}, f32[152,608]{1,0:T(8,128)S(1)}, u32[]{:S(2)}, u32[]{:S(2)}) %collective-permute-start.31) | collective-permute-done | bytes 369696 | tf_op jit(solution)/shard_map/ppermute | solution.py:50
  245.3 3.8 %collective-permute-done.34 = f32[152,608]{1,0:T(8,128)S(1)} collective-permute-done((f32[152,608]{1,0:T(8,128)S(1)}, f32[152,608]{1,0:T(8,128)S(1)}, u32[]{:S(2)}, u32[]{:S(2)}) %collective-permute-start.34) | collective-permute-done | bytes 369696 | tf_op jit(solution)/shard_map/ppermute | solution.py:50
  250.3 4.3 %collective-permute-done.32 = f32[152,608]{1,0:T(8,128)S(1)} collective-permute-done((f32[152,608]{1,0:T(8,128)S(1)}, f32[152,608]{1,0:T(8,128)S(1)}, u32[]{:S(2)}, u32[]{:S(2)}) %collective-permute-start.32) | collective-permute-done | bytes 369696 | tf_op jit(solution)/shard_map/ppermute | solution.py:50
  258.1 2.7 collective-permute-start.36
  262.4 3.9 %collective-permute-start.37 = (f32[]{:T(128)}, f32[]{:T(128)}, u32[]{:S(2)}, u32[]{:S(2)}) collective-permute-start(f32[]{:T(128)} %add.350), channel_id=1, source_target_pairs={{0,8},{2,10},{4,12},{6,14},{8,0},{10,2},{12,4},{14,6},{16,24},{18,... | collective-permute-start | bytes 20 | tf_op jit(solution)/shard_map/ppermute | solution.py:68
  267.3 5.0 %collective-permute-start.38 = (f32[]{:T(128)}, f32[]{:T(128)}, u32[]{:S(2)}, u32[]{:S(2)}) collective-permute-start(f32[]{:T(128)} %add.351), channel_id=1, source_target_pairs={{0,16},{2,18},{4,20},{6,22},{8,24},{10,26},{12,28},{14,30},{16,0},... | collective-permute-start | bytes 20 | tf_op jit(solution)/shard_map/ppermute | solution.py:68
  273.3 2.8 collective-permute-start.39
  278.9 3.5 %collective-permute-start.49 = (bf16[152,608]{1,0:T(8,128)(2,1)S(1)}, bf16[152,608]{1,0:T(8,128)(2,1)S(1)}, u32[]{:S(2)}, u32[]{:S(2)}) collective-permute-start(bf16[152,608]{1,0:T(8,128)(2,1)S(1)} %get-tuple-element.42), channel_id=1, source_target_pairs={{0,24},{2,26},{4,28},{6,30},{8,0},{10,2},{12,4},{14,6},{16,8},{18,... | collective-permute-start | bytes 554504 | tf_op jit(solution)/shard_map/ppermute | solution.py:50
  290.5 5.0 %collective-permute-done.51 = bf16[152,608]{1,0:T(8,128)(2,1)S(1)} collective-permute-done((bf16[152,608]{1,0:T(8,128)(2,1)S(1)}, bf16[152,608]{1,0:T(8,128)(2,1)S(1)}, u32[]{:S(2)}, u32[]{:S(2)}) %collective-permute-start.51) | collective-permute-done | bytes 184864 | tf_op jit(solution)/shard_map/ppermute | solution.py:50
  297.7 4.3 %collective-permute-done.52 = bf16[152,608]{1,0:T(8,128)(2,1)S(1)} collective-permute-done((bf16[152,608]{1,0:T(8,128)(2,1)S(1)}, bf16[152,608]{1,0:T(8,128)(2,1)S(1)}, u32[]{:S(2)}, u32[]{:S(2)}) %collective-permute-start.52) | collective-permute-done | bytes 184864 | tf_op jit(solution)/shard_map/ppermute | solution.py:50
  311.1 5.5 %copy.39 = bf16[608,2432]{1,0:T(8,128)(2,1)} copy(bf16[608,2432]{0,1:T(8,128)(2,1)} %bitcast.242) | data formatting | bytes 5914624
  321.2 5.6 %copy.40 = bf16[608,2432]{1,0:T(8,128)(2,1)} copy(bf16[608,2432]{0,1:T(8,128)(2,1)} %bitcast.243) | data formatting | bytes 5914624
  (258 shorter events, 134.6 us)
Async XLA Ops:
  11.2 20.0 %collective-permute-start = (bf16[608,512]{1,0:T(8,128)(2,1)}, bf16[608,512]{1,0:T(8,128)(2,1)}, u32[]{:S(2)}, u32[]{:S(2)}) collective-permute-start(bf16[608,512]{1,0:T(8,128)(2,1)} %bitcast.284), channel_id=1, source_target_pairs={{0,1},{1,0},{2,3},{3,2},{4,5},{5,4},{6,7},{7,6},{8,9},{9,8},{10,11... | collective-permute-start | bytes 1867784 | tf_op jit(solution)/shard_map/ppermute | solution.py:63
  16.3 26.4 %collective-permute-start.1 = (bf16[608,512]{1,0:T(8,128)(2,1)}, bf16[608,512]{1,0:T(8,128)(2,1)}, u32[]{:S(2)}, u32[]{:S(2)}) collective-permute-start(bf16[608,512]{1,0:T(8,128)(2,1)} %bitcast.285), channel_id=1, source_target_pairs={{0,1},{1,0},{2,3},{3,2},{4,5},{5,4},{6,7},{7,6},{8,9},{9,8},{10,11... | collective-permute-start | bytes 1867784 | tf_op jit(solution)/shard_map/ppermute | solution.py:63
  31.2 24.7 %collective-permute-start.2 = (bf16[608,512]{1,0:T(8,128)(2,1)}, bf16[608,512]{1,0:T(8,128)(2,1)S(1)}, u32[]{:S(2)}, u32[]{:S(2)}) collective-permute-start(bf16[608,512]{1,0:T(8,128)(2,1)} %bitcast.260), channel_id=1, source_target_pairs={{0,1},{1,0},{2,3},{3,2},{4,5},{5,4},{6,7},{7,6},{8,9},{9,8},{10,11... | collective-permute-start | bytes 1867784 | tf_op jit(solution)/shard_map/ppermute | solution.py:63
  42.6 25.7 %collective-permute-start.3 = (bf16[608,512]{1,0:T(8,128)(2,1)}, bf16[608,512]{1,0:T(8,128)(2,1)S(1)}, u32[]{:S(2)}, u32[]{:S(2)}) collective-permute-start(bf16[608,512]{1,0:T(8,128)(2,1)} %bitcast.264), channel_id=1, source_target_pairs={{0,1},{1,0},{2,3},{3,2},{4,5},{5,4},{6,7},{7,6},{8,9},{9,8},{10,11... | collective-permute-start | bytes 1867784 | tf_op jit(solution)/shard_map/ppermute | solution.py:63
  79.0 17.0 %collective-permute-start.5 = (bf16[608,512]{1,0:T(8,128)(2,1)S(1)}, bf16[608,512]{1,0:T(8,128)(2,1)S(1)}, u32[]{:S(2)}, u32[]{:S(2)}) collective-permute-start(bf16[608,512]{1,0:T(8,128)(2,1)S(1)} %bitcast.252), channel_id=1, source_target_pairs={{0,1},{1,0},{2,3},{3,2},{4,5},{5,4},{6,7},{7,6},{8,9},{9,8},{10,11... | collective-permute-start | bytes 1867784 | tf_op jit(solution)/shard_map/ppermute | solution.py:63
  80.8 26.8 %collective-permute-start.4 = (bf16[608,512]{1,0:T(8,128)(2,1)S(1)}, bf16[608,512]{1,0:T(8,128)(2,1)S(1)}, u32[]{:S(2)}, u32[]{:S(2)}) collective-permute-start(bf16[608,512]{1,0:T(8,128)(2,1)S(1)} %bitcast.256), channel_id=1, source_target_pairs={{0,1},{1,0},{2,3},{3,2},{4,5},{5,4},{6,7},{7,6},{8,9},{9,8},{10,11... | collective-permute-start | bytes 1867784 | tf_op jit(solution)/shard_map/ppermute | solution.py:63
  82.9 29.9 %collective-permute-start.11 = (f32[2,152,608]{2,1,0:T(8,128)S(1)}, f32[2,152,608]{2,1,0:T(8,128)S(1)}, u32[]{:S(2)}, u32[]{:S(2)}) collective-permute-start(f32[2,152,608]{2,1,0:T(8,128)S(1)} %dynamic-slice_bitcast_fusion.6), channel_id=1, source_target_pairs={{0,2},{2,0},{4,6},{6,4},{8,10},{10,8},{12,14},{14,12},{16,18},{18,... | collective-permute-start | bytes 2217992 | tf_op jit(solution)/shard_map/ppermute | solution.py:50
  84.8 28.8 %collective-permute-start.8 = (f32[2,152,608]{2,1,0:T(8,128)S(1)}, f32[2,152,608]{2,1,0:T(8,128)S(1)}, u32[]{:S(2)}, u32[]{:S(2)}) collective-permute-start(f32[2,152,608]{2,1,0:T(8,128)S(1)} %dynamic-slice_bitcast_fusion.7), channel_id=1, source_target_pairs={{0,2},{2,0},{4,6},{6,4},{8,10},{10,8},{12,14},{14,12},{16,18},{18,... | collective-permute-start | bytes 2217992 | tf_op jit(solution)/shard_map/ppermute | solution.py:50
  87.0 28.3 %collective-permute-start.14 = (f32[2,152,608]{2,1,0:T(8,128)S(1)}, f32[2,152,608]{2,1,0:T(8,128)S(1)}, u32[]{:S(2)}, u32[]{:S(2)}) collective-permute-start(f32[2,152,608]{2,1,0:T(8,128)S(1)} %dynamic-slice_bitcast_fusion.5), channel_id=1, source_target_pairs={{0,2},{2,0},{4,6},{6,4},{8,10},{10,8},{12,14},{14,12},{16,18},{18,... | collective-permute-start | bytes 2217992 | tf_op jit(solution)/shard_map/ppermute | solution.py:50
  96.0 20.1 %collective-permute-start.17 = (f32[2,152,608]{2,1,0:T(8,128)S(1)}, f32[2,152,608]{2,1,0:T(8,128)S(1)}, u32[]{:S(2)}, u32[]{:S(2)}) collective-permute-start(f32[2,152,608]{2,1,0:T(8,128)S(1)} %dynamic-slice_bitcast_fusion.4), channel_id=1, source_target_pairs={{0,2},{2,0},{4,6},{6,4},{8,10},{10,8},{12,14},{14,12},{16,18},{18,... | collective-permute-start | bytes 2217992 | tf_op jit(solution)/shard_map/ppermute | solution.py:50
  107.7 38.4 %collective-permute-start.7 = (bf16[608,512]{1,0:T(8,128)(2,1)S(1)}, bf16[608,512]{1,0:T(8,128)(2,1)S(1)}, u32[]{:S(2)}, u32[]{:S(2)}) collective-permute-start(bf16[608,512]{1,0:T(8,128)(2,1)S(1)} %bitcast.248), channel_id=1, source_target_pairs={{0,1},{1,0},{2,3},{3,2},{4,5},{5,4},{6,7},{7,6},{8,9},{9,8},{10,11... | collective-permute-start | bytes 1867784 | tf_op jit(solution)/shard_map/ppermute | solution.py:63
  112.8 33.1 %collective-permute-start.6 = (bf16[608,512]{1,0:T(8,128)(2,1)S(1)}, bf16[608,512]{1,0:T(8,128)(2,1)S(1)}, u32[]{:S(2)}, u32[]{:S(2)}) collective-permute-start(bf16[608,512]{1,0:T(8,128)(2,1)S(1)} %bitcast.246), channel_id=1, source_target_pairs={{0,1},{1,0},{2,3},{3,2},{4,5},{5,4},{6,7},{7,6},{8,9},{9,8},{10,11... | collective-permute-start | bytes 1867784 | tf_op jit(solution)/shard_map/ppermute | solution.py:63
  115.3 18.7 %collective-permute-start.9 = (f32[152,608]{1,0:T(8,128)S(1)}, f32[152,608]{1,0:T(8,128)S(1)}, u32[]{:S(2)}, u32[]{:S(2)}) collective-permute-start(f32[152,608]{1,0:T(8,128)S(1)} %dynamic-slice_bitcast_fusion.15), channel_id=1, source_target_pairs={{0,4},{2,6},{4,0},{6,2},{8,12},{10,14},{12,8},{14,10},{16,20},{18,... | collective-permute-start | bytes 1109000 | tf_op jit(solution)/shard_map/ppermute | solution.py:50
  116.1 26.3 %collective-permute-start.15 = (f32[152,608]{1,0:T(8,128)S(1)}, f32[152,608]{1,0:T(8,128)S(1)}, u32[]{:S(2)}, u32[]{:S(2)}) collective-permute-start(f32[152,608]{1,0:T(8,128)S(1)} %dynamic-slice_bitcast_fusion.13), channel_id=1, source_target_pairs={{0,4},{2,6},{4,0},{6,2},{8,12},{10,14},{12,8},{14,10},{16,20},{18,... | collective-permute-start | bytes 1109000 | tf_op jit(solution)/shard_map/ppermute | solution.py:50
  125.7 33.2 %collective-permute-start.18 = (f32[152,608]{1,0:T(8,128)S(1)}, f32[152,608]{1,0:T(8,128)S(1)}, u32[]{:S(2)}, u32[]{:S(2)}) collective-permute-start(f32[152,608]{1,0:T(8,128)S(1)} %dynamic-slice_bitcast_fusion.12), channel_id=1, source_target_pairs={{0,4},{2,6},{4,0},{6,2},{8,12},{10,14},{12,8},{14,10},{16,20},{18,... | collective-permute-start | bytes 1109000 | tf_op jit(solution)/shard_map/ppermute | solution.py:50
  134.0 25.1 %collective-permute-start.13 = (f32[152,608]{1,0:T(8,128)S(1)}, f32[152,608]{1,0:T(8,128)S(1)}, u32[]{:S(2)}, u32[]{:S(2)}) collective-permute-start(f32[152,608]{1,0:T(8,128)S(1)} %bitcast_add_fusion.15), channel_id=1, source_target_pairs={{0,16},{2,18},{4,20},{6,22},{8,24},{10,26},{12,28},{14,30},{16,0},... | collective-permute-start | bytes 1109000 | tf_op jit(solution)/shard_map/ppermute | solution.py:50
  142.4 18.3 %collective-permute-start.10 = (f32[152,608]{1,0:T(8,128)S(1)}, f32[152,608]{1,0:T(8,128)S(1)}, u32[]{:S(2)}, u32[]{:S(2)}) collective-permute-start(f32[152,608]{1,0:T(8,128)S(1)} %bitcast_add_fusion.16), channel_id=1, source_target_pairs={{0,24},{2,26},{4,28},{6,30},{8,0},{10,2},{12,4},{14,6},{16,8},{18,... | collective-permute-start | bytes 1109000 | tf_op jit(solution)/shard_map/ppermute | solution.py:50
  146.0 14.7 %collective-permute-start.16 = (f32[152,608]{1,0:T(8,128)S(1)}, f32[152,608]{1,0:T(8,128)S(1)}, u32[]{:S(2)}, u32[]{:S(2)}) collective-permute-start(f32[152,608]{1,0:T(8,128)S(1)} %bitcast_add_fusion.14), channel_id=1, source_target_pairs={{0,8},{2,10},{4,12},{6,14},{8,16},{10,18},{12,20},{14,22},{16,24},... | collective-permute-start | bytes 1109000 | tf_op jit(solution)/shard_map/ppermute | solution.py:50
  153.0 61.5 %collective-permute-start.27 = (f32[2,152,608]{2,1,0:T(8,128)}, f32[2,152,608]{2,1,0:T(8,128)}, u32[]{:S(2)}, u32[]{:S(2)}) collective-permute-start(f32[2,152,608]{2,1,0:T(8,128)} %dynamic-slice_bitcast_fusion.2), channel_id=1, source_target_pairs={{0,2},{2,0},{4,6},{6,4},{8,10},{10,8},{12,14},{14,12},{16,18},{18,... | collective-permute-start | bytes 2217992 | tf_op jit(solution)/shard_map/ppermute | solution.py:50
  158.9 56.9 %collective-permute-start.24 = (f32[2,152,608]{2,1,0:T(8,128)}, f32[2,152,608]{2,1,0:T(8,128)}, u32[]{:S(2)}, u32[]{:S(2)}) collective-permute-start(f32[2,152,608]{2,1,0:T(8,128)} %dynamic-slice_bitcast_fusion.3), channel_id=1, source_target_pairs={{0,2},{2,0},{4,6},{6,4},{8,10},{10,8},{12,14},{14,12},{16,18},{18,... | collective-permute-start | bytes 2217992 | tf_op jit(solution)/shard_map/ppermute | solution.py:50
  192.6 13.2 %collective-permute-start.43 = (bf16[152,608]{1,0:T(8,128)(2,1)S(1)}, bf16[152,608]{1,0:T(8,128)(2,1)S(1)}, u32[]{:S(2)}, u32[]{:S(2)}) collective-permute-start(bf16[152,608]{1,0:T(8,128)(2,1)S(1)} %get-tuple-element.44), channel_id=1, source_target_pairs={{0,16},{2,18},{4,20},{6,22},{8,24},{10,26},{12,28},{14,30},{16,0},... | collective-permute-start | bytes 554504 | tf_op jit(solution)/shard_map/ppermute | solution.py:50
  194.4 12.8 %collective-permute-start.42 = (bf16[152,608]{1,0:T(8,128)(2,1)S(1)}, bf16[152,608]{1,0:T(8,128)(2,1)S(1)}, u32[]{:S(2)}, u32[]{:S(2)}) collective-permute-start(bf16[152,608]{1,0:T(8,128)(2,1)S(1)} %collective-permute-done.41), channel_id=1, source_target_pairs={{0,4},{2,6},{4,0},{6,2},{8,12},{10,14},{12,8},{14,10},{16,20},{18,... | collective-permute-start | bytes 554504 | tf_op jit(solution)/shard_map/ppermute | solution.py:50
  212.3 32.7 %collective-permute-start.46 = (bf16[152,608]{1,0:T(8,128)(2,1)S(1)}, bf16[152,608]{1,0:T(8,128)(2,1)S(1)}, u32[]{:S(2)}, u32[]{:S(2)}) collective-permute-start(bf16[152,608]{1,0:T(8,128)(2,1)S(1)} %collective-permute-done.45), channel_id=1, source_target_pairs={{0,4},{2,6},{4,0},{6,2},{8,12},{10,14},{12,8},{14,10},{16,20},{18,... | collective-permute-start | bytes 554504 | tf_op jit(solution)/shard_map/ppermute | solution.py:50
  215.7 12.8 %collective-permute-start.28 = (f32[152,608]{1,0:T(8,128)S(1)}, f32[152,608]{1,0:T(8,128)S(1)}, u32[]{:S(2)}, u32[]{:S(2)}) collective-permute-start(f32[152,608]{1,0:T(8,128)S(1)} %dynamic-slice_bitcast_fusion.10), channel_id=1, source_target_pairs={{0,4},{2,6},{4,0},{6,2},{8,12},{10,14},{12,8},{14,10},{16,20},{18,... | collective-permute-start | bytes 1109000 | tf_op jit(solution)/shard_map/ppermute | solution.py:50
  217.1 19.8 %collective-permute-start.25 = (f32[152,608]{1,0:T(8,128)S(1)}, f32[152,608]{1,0:T(8,128)S(1)}, u32[]{:S(2)}, u32[]{:S(2)}) collective-permute-start(f32[152,608]{1,0:T(8,128)S(1)} %dynamic-slice_bitcast_fusion.11), channel_id=1, source_target_pairs={{0,4},{2,6},{4,0},{6,2},{8,12},{10,14},{12,8},{14,10},{16,20},{18,... | collective-permute-start | bytes 1109000 | tf_op jit(solution)/shard_map/ppermute | solution.py:50
  219.3 25.6 %collective-permute-start.31 = (f32[152,608]{1,0:T(8,128)S(1)}, f32[152,608]{1,0:T(8,128)S(1)}, u32[]{:S(2)}, u32[]{:S(2)}) collective-permute-start(f32[152,608]{1,0:T(8,128)S(1)} %dynamic-slice_bitcast_fusion.9), channel_id=1, source_target_pairs={{0,4},{2,6},{4,0},{6,2},{8,12},{10,14},{12,8},{14,10},{16,20},{18,... | collective-permute-start | bytes 1109000 | tf_op jit(solution)/shard_map/ppermute | solution.py:50
  219.5 29.5 %collective-permute-start.34 = (f32[152,608]{1,0:T(8,128)S(1)}, f32[152,608]{1,0:T(8,128)S(1)}, u32[]{:S(2)}, u32[]{:S(2)}) collective-permute-start(f32[152,608]{1,0:T(8,128)S(1)} %dynamic-slice_bitcast_fusion.8), channel_id=1, source_target_pairs={{0,4},{2,6},{4,0},{6,2},{8,12},{10,14},{12,8},{14,10},{16,20},{18,... | collective-permute-start | bytes 1109000 | tf_op jit(solution)/shard_map/ppermute | solution.py:50
  228.6 20.5 %collective-permute-start.29 = (f32[152,608]{1,0:T(8,128)S(1)}, f32[152,608]{1,0:T(8,128)S(1)}, u32[]{:S(2)}, u32[]{:S(2)}) collective-permute-start(f32[152,608]{1,0:T(8,128)S(1)} %bitcast_add_fusion.10), channel_id=1, source_target_pairs={{0,16},{2,18},{4,20},{6,22},{8,24},{10,26},{12,28},{14,30},{16,0},... | collective-permute-start | bytes 1109000 | tf_op jit(solution)/shard_map/ppermute | solution.py:50
  236.9 13.4 %collective-permute-start.26 = (f32[152,608]{1,0:T(8,128)S(1)}, f32[152,608]{1,0:T(8,128)S(1)}, u32[]{:S(2)}, u32[]{:S(2)}) collective-permute-start(f32[152,608]{1,0:T(8,128)S(1)} %bitcast_add_fusion.11), channel_id=1, source_target_pairs={{0,24},{2,26},{4,28},{6,30},{8,0},{10,2},{12,4},{14,6},{16,8},{18,... | collective-permute-start | bytes 1109000 | tf_op jit(solution)/shard_map/ppermute | solution.py:50
  283.2 14.4 %collective-permute-start.48 = (bf16[152,608]{1,0:T(8,128)(2,1)S(1)}, bf16[152,608]{1,0:T(8,128)(2,1)S(1)}, u32[]{:S(2)}, u32[]{:S(2)}) collective-permute-start(bf16[152,608]{1,0:T(8,128)(2,1)S(1)} %get-tuple-element.42), channel_id=1, source_target_pairs={{0,4},{2,6},{4,0},{6,2},{8,12},{10,14},{12,8},{14,10},{16,20},{18,... | collective-permute-start | bytes 554504 | tf_op jit(solution)/shard_map/ppermute | solution.py:50
  284.1 12.4 %collective-permute-start.53 = (bf16[152,608]{1,0:T(8,128)(2,1)S(1)}, bf16[152,608]{1,0:T(8,128)(2,1)S(1)}, u32[]{:S(2)}, u32[]{:S(2)}) collective-permute-start(bf16[152,608]{1,0:T(8,128)(2,1)S(1)} %get-tuple-element.42), channel_id=1, source_target_pairs={{0,8},{2,10},{4,12},{6,14},{8,16},{10,18},{12,20},{14,22},{16,24},... | collective-permute-start | bytes 554504 | tf_op jit(solution)/shard_map/ppermute | solution.py:50
  290.5 16.0 %collective-permute-start.47 = (bf16[4,2,152,608]{3,2,1,0:T(8,128)(2,1)}, bf16[4,2,152,608]{3,2,1,0:T(8,128)(2,1)}, u32[]{:S(2)}, u32[]{:S(2)}) collective-permute-start(bf16[4,2,152,608]{3,2,1,0:T(8,128)(2,1)} %fusion.19), channel_id=1, source_target_pairs={{0,2},{2,0},{4,6},{6,4},{8,10},{10,8},{12,14},{14,12},{16,18},{18,... | collective-permute-start | bytes 4435976 | tf_op jit(solution)/shard_map/ppermute | solution.py:50
  (49 other events, 497.6 us)

commit v2 on v1

v2 whole, which is shorter than its diff:
```python
import functools

import jax
import jax.numpy as jnp
from jax import lax
from jax.experimental import pallas as pl
from jax.experimental.pallas import tpu as pltpu
from jax.sharding import PartitionSpec as P

D = 2432
F = 1216
ROWS = 1024


FIRST_CORRECTION = 0.9999734386011124
SECOND_CORRECTION = 0.0952078529183

OUTER = 4
HALF_LIMIT = 60000.0
TILE = 256
VMEM_LIMIT = 48 * 1024 * 1024

NT = (((1,), (1,)), ((), ()))
NN = (((1,), (0,)), ((), ()))


def sample_scale(steps, count):
    weights = 1.0 / (0.1 + steps.astype(jnp.float32) / 1000.0)
    which = jnp.arange(count) // ROWS
    onehot = which[:, None] == jnp.arange(steps.shape[0])[None, :]
    return jnp.sum(jnp.where(onehot, weights[None, :], 0.0), axis=1)


def adam_update(grad, squares, master, first, second):
    clip = jnp.minimum(1.0, jnp.sqrt(jnp.float32(D * F)) / jnp.sqrt(squares + 1e-06))
    clipped = grad * clip
    new_first = 0.9 * first + 0.1 * clipped
    new_second = 0.999 * second + 0.001 * clipped * clipped
    step_dir = new_first / FIRST_CORRECTION / (jnp.sqrt(new_second / SECOND_CORRECTION) + 1e-08)
    new_master = master * (1.0 - 0.01 * 0.01) - 0.01 * step_dir
    return (new_master, new_first, new_second)


def dot(a, b, dims):
    return lax.dot_general(a, b, dims, preferred_element_type=jnp.float32)


def identity(size):
    rows = lax.broadcasted_iota(jnp.int32, (size, size), 0)
    cols = lax.broadcasted_iota(jnp.int32, (size, size), 1)
    return jnp.where(rows == cols, 1.0, 0.0).astype(jnp.bfloat16)


def after(value, *others):
    return lax.optimization_barrier((value, *others))[0]


def cost(flops, nbytes):
    return pl.CostEstimate(flops=flops, bytes_accessed=nbytes, transcendentals=0)


def params_of(**kwargs):
    return pltpu.CompilerParams(vmem_limit_bytes=VMEM_LIMIT, **kwargs)


def solution(mesh):
    n_dp, n_tensor = mesh.shape["dp"], mesh.shape["tensor"]
    inner = n_dp // (2 * OUTER)
    width = D // n_dp

    def split(p):
        return (p >> inner.bit_length()) & (OUTER - 1), (p >> 1) & (inner - 1), p & 1

    def join(z, m, c):
        return (z * inner + m) * 2 + c

    def move_dp(value, where):
        perm = [(p, join(*where(*split(p)))) for p in range(n_dp)]
        return lax.ppermute(value, "dp", perm)

    def to_plane(value, k):
        return move_dp(value, lambda z, m, c: ((z + k) & (OUTER - 1), m, c))

    def to_middle(value, k):
        return move_dp(value, lambda z, m, c: (z, (m + k) & (inner - 1), c))

    def to_core(value):
        return move_dp(value, lambda z, m, c: (z, m, 1 - c))

    def from_tensor(value, k):
        perm = [(s, (s - k) & (n_tensor - 1)) for s in range(n_tensor)]
        return lax.ppermute(value, "tensor", perm)

    def butterfly(value, combine):
        for axis, size in (("dp", n_dp), ("tensor", n_tensor)):
            step = 1
            while step < size:
                perm = [(p, p ^ step) for p in range(size)]
                value = combine(value, lax.ppermute(value, axis, perm))
                step *= 2
        return value

    def relative(place_ref, p):
        z, m, c = split(p)
        return (
            (z - place_ref[0]) & (OUTER - 1),
            (m - place_ref[1]) & (inner - 1),
            c ^ place_ref[2],
        )

    def turn(cot, place, planes_first):
        r = cot.shape[0]
        step = min(r, TILE)

        def kernel(place_ref, cot_ref, out_ref, wide_ref):
            eye = identity(TILE)
            for start in range(0, D, TILE):
                size = min(TILE, D - start)
                wide_ref[start : start + size, :] = dot(
                    eye[:size, :size], cot_ref[:, start : start + size], NT
                )
            for p in range(n_dp):
                k, i, other = relative(place_ref, p)
                block = wide_ref[p * width : (p + 1) * width, :].astype(jnp.bfloat16)
                if planes_first:
                    out_ref[k, other, i] = block
                else:
                    out_ref[other, i, k] = block

        lead = (OUTER, 2, inner) if planes_first else (2, inner, OUTER)
        return pl.pallas_call(
            kernel,
            out_shape=jax.ShapeDtypeStruct((*lead, width, r), jnp.bfloat16),
            grid=(r // step,),
            in_specs=[
                pl.BlockSpec(memory_space=pltpu.SMEM),
                pl.BlockSpec((step, D), lambda s: (s, 0)),
            ],
            out_specs=pl.BlockSpec((*lead, width, step), lambda s: (0, 0, 0, 0, s)),
            scratch_shapes=[pltpu.VMEM((D, step), jnp.float32)],
            compiler_params=params_of(),
            cost_estimate=cost(2 * TILE * D * r, 4 * D * r),
        )(place, cot)

    def back_other(weight, pieces, scale, place):
        f = weight.shape[0]
        r = pieces[0].shape[-1]

        def kernel(place_ref, weight_ref, *refs):
            piece_refs, (scale_ref, out_ref, wide_ref) = refs[:OUTER], refs[OUTER:]
            z, m, c = (place_ref[n] for n in range(3))
            for k in range(OUTER):
                for other in range(2):
                    for i in range(inner):
                        p = join((z + k) & (OUTER - 1), (m + i) & (inner - 1), c ^ other)
                        wide_ref[p] = piece_refs[k][other, i].astype(jnp.float32)
            turned = wide_ref[...].reshape(D, r).astype(jnp.bfloat16)
            out_ref[...] = (dot(weight_ref[...], turned, NN) * scale_ref[...]).astype(jnp.bfloat16)

        whole = pl.BlockSpec(memory_space=pltpu.VMEM)
        return pl.pallas_call(
            kernel,
            out_shape=jax.ShapeDtypeStruct((f, r), jnp.bfloat16),
            in_specs=[pl.BlockSpec(memory_space=pltpu.SMEM)] + [whole] * (OUTER + 2),
            out_specs=whole,
            scratch_shapes=[pltpu.VMEM((n_dp, width, r), jnp.float32)],
            compiler_params=params_of(),
            cost_estimate=cost(2 * f * D * r, 2 * (f * D + D * r + f * r)),
        )(place, weight, *pieces, scale)

    def spread(blocks, net, place):
        f = blocks[0].shape[-1]

        def kernel(place_ref, *refs):
            block_refs, (out_ref, wide_ref) = refs[:-2], refs[-2:]
            z, m, c = (place_ref[n] for n in range(3))
            at = 0
            for other in range(2):
                for k in range(OUTER):
                    for i in range(inner):
                        p = join((z + k) & (OUTER - 1), (m + i) & (inner - 1), c ^ other)
                        wide_ref[p] = block_refs[at][...].reshape(width, f).astype(jnp.float32)
                        at += 1
            flat = wide_ref[...].reshape(D, f).astype(jnp.bfloat16)
            eye = identity(TILE)
            for start in range(0, f, TILE):
                size = min(TILE, f - start)
                out_ref[start : start + size, :] = dot(
                    eye[:size, :size], flat[:, start : start + size], NT
                ).astype(jnp.bfloat16)

        specs, operands = [], []
        for array, lead in blocks_index(blocks):
            zeros = (0,) * (array.ndim - 2 - len(lead) - 1)
            index = (*lead, net, *zeros, 0, 0)
            specs.append(
                pl.BlockSpec((1,) * (array.ndim - 2) + (width, f), functools.partial(lambda index, s: index, index))
            )
            operands.append(array)
        return pl.pallas_call(
            kernel,
            out_shape=jax.ShapeDtypeStruct((f, D), jnp.bfloat16),
            grid=(1,),
            in_specs=[pl.BlockSpec(memory_space=pltpu.SMEM)] + specs,
            out_specs=pl.BlockSpec((f, D), lambda s: (0, 0)),
            scratch_shapes=[pltpu.VMEM((n_dp, width, f), jnp.float32)],
            compiler_params=params_of(),
            cost_estimate=cost(2 * TILE * D * f, 4 * D * f),
        )(place, *operands)

    def blocks_index(blocks):
        for block in blocks:
            if block.ndim == 3:
                yield block, ()
            else:
                for at in range(block.shape[0]):
                    yield block, (at,)

    def per_device(
        cot_student, cot_fake, act_student, act_fake, weight_student, weight_fake,
        master_student, first_student, second_student, master_fake, first_fake, second_fake,
        timesteps,
    ):
        t = lax.axis_index("tensor")
        z, m, c = split(lax.axis_index("dp"))
        place = jnp.stack([z, m, c]).astype(jnp.int32)
        f, count = act_student.shape
        r = cot_student.shape[0]

        def rows_of(value, k):
            start = ((t + k) & (n_tensor - 1)) * r
            return lax.dynamic_slice_in_dim(value, start, r, value.ndim - 1)

        def scaled_by(act, scale):
            return (act.astype(jnp.float32) * scale[None, :]).astype(jnp.bfloat16)

        scale_student = sample_scale(timesteps[0, 0], count)
        scale_fake = sample_scale(timesteps[0, 1], count)

        acts = [
            from_tensor(rows_of(act_fake, j), -j) for j in range(1, n_tensor)
        ]
        acts = [rows_of(act_fake, 0), *acts]
        own_scale = rows_of(scale_fake, 0)
        scaled_fake = [scaled_by(act, own_scale) for act in acts]
        scaled_student = scaled_by(act_student, scale_student)

        turned_student = turn(cot_student, place, True)
        turned_fake = turn(cot_fake, place, False).reshape(2, -1, r)

        def bound(cot, act, scale):
            return (
                jnp.max(jnp.abs(cot)).astype(jnp.float32)
                * jnp.max(jnp.abs(act)).astype(jnp.float32)
                * jnp.max(scale)
            )

        bounds = butterfly(
            jnp.stack(
                [
                    bound(cot_student, act_student, scale_student),
                    bound(cot_fake, act_fake, scale_fake),
                ]
            ),
            jnp.maximum,
        )
        bounds = jnp.maximum(bounds, 1e-30) * (1.01 * count * n_dp / HALF_LIMIT)

        def shrink(value, net):
            return (value * (1.0 / bounds[net])).astype(jnp.float16)

        def widen(value, net):
            return value.astype(jnp.float32) * bounds[net]

        def over_middle(blocks, net):
            mine = blocks[0]
            for i in range(1, inner):
                mine = mine + widen(to_middle(shrink(blocks[i], net), i), net)
            return mine

        parts_fake = []
        for scaled in scaled_fake:
            keep = dot(turned_fake[0], scaled, NT)
            send = dot(turned_fake[1], scaled, NT)
            both = (keep + to_core(send)).reshape(inner, OUTER, width, f)
            mine = over_middle(both, 1)
            total = mine[0]
            for k in range(1, OUTER):
                total = total + widen(to_plane(shrink(mine[k], 1), k), 1)
            parts_fake.append(total)

        order = (3, 1, 2, 0)
        pieces, arrived = {}, [scaled_fake[-1]]
        total_student = None
        for at, k in enumerate(order):
            own = turned_student[k]
            if at >= 2:
                own = after(own, arrived[at - 2])
            others = [from_tensor(own, j) for j in range(1, n_tensor)]
            arrived.append(others[-1])
            pieces[k] = others
            halves = [own, *others]
            sums = []
            for other in range(2):
                grad = None
                for j, piece in enumerate(halves):
                    term = dot(piece[other].reshape(-1, r), rows_of(scaled_student, j), NT)
                    grad = term if grad is None else grad + term
                sums.append(grad)
            both = (sums[0] + to_core(sums[1])).reshape(inner, width, f)
            mine = over_middle(both, 0)
            if k:
                mine = widen(to_plane(shrink(mine, 0), k), 0)
            total_student = mine if total_student is None else total_student + mine

        total_fake = parts_fake[0]
        last = None
        for j in range(1, n_tensor):
            last = shrink(parts_fake[j], 1)
            total_fake = total_fake + widen(from_tensor(last, j), 1)

        raw = after(cot_fake, last, arrived[-2])
        cots_fake = [cot_fake] + [from_tensor(raw, j) for j in range(1, n_tensor)]

        totals = (total_student, total_fake)
        squares = butterfly(jnp.stack([jnp.sum(total * total) for total in totals]), jnp.add)
        states = (
            (master_student, first_student, second_student),
            (master_fake, first_fake, second_fake),
        )
        updated = [
            adam_update(totals[n], squares[n], *(state.T for state in states[n])) for n in range(2)
        ]
        own = jnp.stack([new[0].astype(jnp.bfloat16) for new in updated])
        mine = []
        for k in range(OUTER):
            got = to_plane(own, -k) if k else own
            mine.append(got)
            for i in range(1, inner):
                mine.append(to_middle(got, -i))
        half = len(mine) // 2
        theirs = [to_core(jnp.stack(mine[:half])), to_core(jnp.stack(mine[half:]))]
        params = [spread([*mine, *theirs], n, place) for n in range(2)]

        def assemble(parts):
            whole = jnp.concatenate(parts + parts, axis=1)
            return lax.dynamic_slice_in_dim(
                whole, r * ((n_tensor - t) & (n_tensor - 1)), count, 1
            )

        def back_rows(weight, cot, scale):
            return (dot(weight, cot, NT) * scale[None, :]).astype(jnp.bfloat16)

        back_student = [back_rows(weight_student, cot_student, rows_of(scale_student, 0))]
        back_student += [
            back_other(
                weight_student,
                [pieces[k][j - 1] for k in range(OUTER)],
                rows_of(scale_student, j)[None, :],
                place,
            )
            for j in range(1, n_tensor)
        ]
        back_fake = [
            back_rows(weight_fake, cots_fake[j], rows_of(scale_fake, j)) for j in range(n_tensor)
        ]

        new_states = [value.T for new in updated for value in new]
        return (assemble(back_student), assemble(back_fake), *new_states, *params)

    placed = (
        P(("dp", "tensor"), None),
        P(("dp", "tensor"), None),
        P("tensor", "dp"),
        P("tensor", "dp"),
        P("tensor", None),
        P("tensor", None),
        P("tensor", "dp"),
        P("tensor", "dp"),
        P("tensor", "dp"),
        P("tensor", "dp"),
        P("tensor", "dp"),
        P("tensor", "dp"),
        P("dp", None, None),
    )
    return jax.shard_map(
        per_device,
        mesh=mesh,
        in_specs=placed,
        out_specs=(
            P("tensor", "dp"),
            P("tensor", "dp"),
            P("tensor", "dp"),
            P("tensor", "dp"),
            P("tensor", "dp"),
            P("tensor", "dp"),
            P("tensor", "dp"),
            P("tensor", "dp"),
            P("tensor", None),
            P("tensor", None),
        ),
        check_vma=False,
    )
```

time: 330 us -> 308 us (0.933)
  local copies, waits for them, and re-layouts: 56.7 us -> 15.4 us
  starting transfers between devices: 84.6 us -> 54.5 us
  waiting for transfers between devices: 129 us -> 147 us
  Pallas kernels: 0 us -> 17 us
  matrix products: 21.4 us -> 29.6 us
  other arithmetic: 24.8 us -> 30.8 us
    unnamed x88 -> x90, local copies, waits for them, and re-layouts: 38.4 us -> 5.81 us
    ppermute x8 -> x7, waiting for transfers between devices: 46.5 us -> 20.4 us  [from_tensor(): return lax.ppermute(value, 'tensor', perm)]
    ppermute x38 -> x30, waiting for transfers between devices: 75 us -> 100 us  [move_dp(): return lax.ppermute(value, 'dp', perm)]
    ppermute x10, starting transfers between devices: 30.6 us -> 8.43 us  [butterfly(): value = combine(value, lax.ppermute(value, axis, perm))]
    ppermute x10, waiting for transfers between devices: 7.04 us -> 26 us  [butterfly(): value = combine(value, lax.ppermute(value, axis, perm))]
    pallas_call x0 -> x5, Pallas kernels: none -> 17 us  [the longest x2 9.12 us: spread(): pl.pallas_call(kernel, out_shape=jax.ShapeDtypeStruct((f, D), jnp.bfloat1...]
    another operation x3 -> x0, local copies, waits for them, and re-layouts: 12.1 us -> none
    dot_general x20 -> x23, matrix products: 21.4 us -> 29.6 us  [dot(): return lax.dot_general(a, b, dims, preferred_element_type=jnp.float32)]
  transfers between devices with their start and end apart: 56 -> 47, of which waited for: 33 -> 23; matrix products, arithmetic and copies ran while one was open for 21% -> 16% of each run, Pallas kernels for 0% -> 6%
where the time goes in v2:
time: 308 us; the launch traced here: 304 us
  waiting for transfers between devices  147 us (48%)
  starting transfers between devices  54.5 us (18%)
  other arithmetic  30.8 us (10%)
  matrix products  29.6 us (10%)
  Pallas kernels  17 us (6%)
  local copies, waits for them, and re-layouts  15.4 us (5%)
  between operations  9.54 us (3%)
    ppermute x30, waiting for transfers between devices, move_dp(): return lax.ppermute(value, 'dp', perm)  100 us
    ppermute x30, starting transfers between devices, move_dp(): return lax.ppermute(value, 'dp', perm)  36.4 us
    dot_general x23, matrix products, dot(): return lax.dot_general(a, b, dims, preferred_element_type=jnp.float32)  29.6 us
    ppermute x10, waiting for transfers between devices, butterfly(): value = combine(value, lax.ppermute(value, axis, perm))  26 us
    ppermute x7, waiting for transfers between devices, from_tensor(): return lax.ppermute(value, 'tensor', perm)  20.4 us
    ppermute x7, starting transfers between devices, from_tensor(): return lax.ppermute(value, 'tensor', perm)  9.74 us
    pallas_call x2, Pallas kernels, spread(): pl.pallas_call(kernel, out_shape=jax.ShapeDtypeStruct((f, D), jnp.bfloat1...  9.12 us
    ppermute x10, starting transfers between devices, butterfly(): value = combine(value, lax.ppermute(value, axis, perm))  8.43 us
  transfers between devices with their start and end apart: 47, of which 23 were waited for; matrix products, arithmetic and copies ran while one was open for 16% of the time, Pallas kernels for 6%

profile of v2, /device:TPU:0, one launch (start us, length us, event | category | flops | bytes accessed | tf_op | source)
XLA Modules:
  0.0 303.7 jit_solution(18274145088938306770)
XLA Ops:
  2.9 2.8 abs_reduce_fusion
  27.2 2.6 shard_map.206
  31.6 4.4 %fusion.16 = f32[1216,608]{1,0:T(8,128)} fusion(bf16[1216,512]{1,0:T(8,128)(2,1)} %bitcast.177, bf16[608,1024]{1,0:T(8,128)(2,1)} %param.16, s32[]{:T(128)S(6)} %select_n.95, f32[512]{0:T(512)S(1)} %bitcast.203), kind=kOutput, calls=%fused_computation.56 | convolution fusion | flops 758005760 | bytes 4827140 | tf_op jit(solution)/shard_map/dot_general | solution.py:45
  50.2 2.6 collective-permute-start.9
  54.9 6.1 %collective-permute-done.10 = f32[2]{0:T(128)S(1)} collective-permute-done((f32[2]{0:T(128)S(1)}, f32[2]{0:T(128)S(1)}, u32[]{:S(2)}, u32[]{:S(2)}) %collective-permute-start.10) | collective-permute-done | bytes 40 | tf_op jit(solution)/shard_map/ppermute | solution.py:99
  73.4 20.4 %collective-permute-done.1.refs_0_ = bf16[2,2,152,512]{3,2,1,0:T(8,128)(2,1)S(1)} collective-permute-done((bf16[2,2,152,512]{3,2,1,0:T(8,128)(2,1)S(1)}, bf16[2,2,152,512]{3,2,1,0:T(8,128)(2,1)S(1)}, u32[]{:S(2)}, u32[]{:S(2)}) %collective-permute-start.1) | collective-permute-done | bytes 622624 | tf_op jit(solution)/shard_map/ppermute | solution.py:92
  98.7 4.9 %collective-permute-done.17 = f16[152,608]{1,0:T(8,128)(2,1)S(1)} collective-permute-done((f16[152,608]{1,0:T(8,128)(2,1)S(1)}, f16[152,608]{1,0:T(8,128)(2,1)S(1)}, u32[]{:S(2)}, u32[]{:S(2)}) %collective-permute-start.17) | collective-permute-done | bytes 184864 | tf_op jit(solution)/shard_map/ppermute | solution.py:79
  105.9 3.9 %collective-permute-done.20 = f16[152,608]{1,0:T(8,128)(2,1)S(1)} collective-permute-done((f16[152,608]{1,0:T(8,128)(2,1)S(1)}, f16[152,608]{1,0:T(8,128)(2,1)S(1)}, u32[]{:S(2)}, u32[]{:S(2)}) %collective-permute-start.20) | collective-permute-done | bytes 184864 | tf_op jit(solution)/shard_map/ppermute | solution.py:79
  109.7 3.7 %collective-permute-start.18 = (f16[152,608]{1,0:T(8,128)(2,1)S(1)}, f16[152,608]{1,0:T(8,128)(2,1)S(1)}, u32[]{:S(2)}, u32[]{:S(2)}) collective-permute-start(f16[152,608]{1,0:T(8,128)(2,1)S(1)} %fusion.36), channel_id=1, source_target_pairs={{0,24},{2,26},{4,28},{6,30},{8,0},{10,2},{12,4},{14,6},{16,8},{18,... | collective-permute-start | bytes 554504 | tf_op jit(solution)/shard_map/ppermute | solution.py:79
  118.0 3.1 %convolution_add_fusion = f32[1216,608]{1,0:T(8,128)S(1)} fusion(f32[1216,608]{1,0:T(8,128)} %collective-permute-done.27, bf16[1216,512]{1,0:T(8,128)(2,1)S(1)} %bitcast.179, bf16[608,1024]{1,0:T(8,128)(2,1)S(1)} %copy-done.29, s32[]{:T(128)S(6)} %select_n.95, f32[512]{0:T(512)S(1)} %bitcast.205), kind=kOutput, calls=%fused_computation | convolution fusion | flops 758745088 | bytes 7784452 | tf_op jit(solution)/shard_map/dot_general | solution.py:45
  125.6 16.0 %collective-permute-done.28 = f16[4,152,608]{2,1,0:T(8,128)(2,1)S(1)} collective-permute-done((f16[4,152,608]{2,1,0:T(8,128)(2,1)S(1)}, f16[4,152,608]{2,1,0:T(8,128)(2,1)S(1)}, u32[]{:S(2)}, u32[]{:S(2)}) %collective-permute-start.28) | collective-permute-done | bytes 739360 | tf_op jit(solution)/shard_map/ppermute | solution.py:79
  142.5 12.8 %collective-permute-done.11 = f16[4,152,608]{2,1,0:T(8,128)(2,1)S(1)} collective-permute-done((f16[4,152,608]{2,1,0:T(8,128)(2,1)S(1)}, f16[4,152,608]{2,1,0:T(8,128)(2,1)S(1)}, u32[]{:S(2)}, u32[]{:S(2)}) %collective-permute-start.11) | collective-permute-done | bytes 739360 | tf_op jit(solution)/shard_map/ppermute | solution.py:79
  156.2 3.8 %collective-permute-start.14 = (f16[152,608]{1,0:T(8,128)(2,1)S(1)}, f16[152,608]{1,0:T(8,128)(2,1)S(1)}, u32[]{:S(2)}, u32[]{:S(2)}) collective-permute-start(f16[152,608]{1,0:T(8,128)(2,1)S(1)} %get-tuple-element.42), channel_id=1, source_target_pairs={{0,24},{2,26},{4,28},{6,30},{8,0},{10,2},{12,4},{14,6},{16,8},{18,... | collective-permute-start | bytes 554504 | tf_op jit(solution)/shard_map/ppermute | solution.py:79
  160.4 5.5 %collective-permute-done.12 = f16[152,608]{1,0:T(8,128)(2,1)S(1)} collective-permute-done((f16[152,608]{1,0:T(8,128)(2,1)S(1)}, f16[152,608]{1,0:T(8,128)(2,1)S(1)}, u32[]{:S(2)}, u32[]{:S(2)}) %collective-permute-start.12) | collective-permute-done | bytes 184864 | tf_op jit(solution)/shard_map/ppermute | solution.py:79
  166.4 8.9 %collective-permute-start.24 = (f16[152,608]{1,0:T(8,128)(2,1)S(1)}, f16[152,608]{1,0:T(8,128)(2,1)S(1)}, u32[]{:S(2)}, u32[]{:S(2)}) collective-permute-start(f16[152,608]{1,0:T(8,128)(2,1)S(1)} %fusion.30), channel_id=1, source_target_pairs={{0,16},{2,18},{4,20},{6,22},{8,24},{10,26},{12,28},{14,30},{16,0},... | collective-permute-start | bytes 554504 | tf_op jit(solution)/shard_map/ppermute | solution.py:79
  175.3 3.2 %collective-permute-done.13 = f16[152,608]{1,0:T(8,128)(2,1)S(1)} collective-permute-done((f16[152,608]{1,0:T(8,128)(2,1)S(1)}, f16[152,608]{1,0:T(8,128)(2,1)S(1)}, u32[]{:S(2)}, u32[]{:S(2)}) %collective-permute-start.13) | collective-permute-done | bytes 184864 | tf_op jit(solution)/shard_map/ppermute | solution.py:79
  179.3 3.9 %collective-permute-start.31 = (f16[152,608]{1,0:T(8,128)(2,1)S(1)}, f16[152,608]{1,0:T(8,128)(2,1)S(1)}, u32[]{:S(2)}, u32[]{:S(2)}) collective-permute-start(f16[152,608]{1,0:T(8,128)(2,1)S(1)} %get-tuple-element.39), channel_id=1, source_target_pairs={{0,24},{2,26},{4,28},{6,30},{8,0},{10,2},{12,4},{14,6},{16,8},{18,... | collective-permute-start | bytes 554504 | tf_op jit(solution)/shard_map/ppermute | solution.py:79
  184.9 6.1 %collective-permute-done.24 = f16[152,608]{1,0:T(8,128)(2,1)S(1)} collective-permute-done((f16[152,608]{1,0:T(8,128)(2,1)S(1)}, f16[152,608]{1,0:T(8,128)(2,1)S(1)}, u32[]{:S(2)}, u32[]{:S(2)}) %collective-permute-start.24) | collective-permute-done | bytes 184864 | tf_op jit(solution)/shard_map/ppermute | solution.py:79
  192.4 6.9 %collective-permute-done.30 = f16[152,608]{1,0:T(8,128)(2,1)S(1)} collective-permute-done((f16[152,608]{1,0:T(8,128)(2,1)S(1)}, f16[152,608]{1,0:T(8,128)(2,1)S(1)}, u32[]{:S(2)}, u32[]{:S(2)}) %collective-permute-start.30) | collective-permute-done | bytes 184864 | tf_op jit(solution)/shard_map/ppermute | solution.py:79
  205.2 3.0 collective-permute-done.34
  209.6 3.5 %collective-permute-done.35 = f32[2]{0:T(128)S(1)} collective-permute-done((f32[2]{0:T(128)S(1)}, f32[2]{0:T(128)S(1)}, u32[]{:S(2)}, u32[]{:S(2)}) %collective-permute-start.35) | collective-permute-done | bytes 40 | tf_op jit(solution)/shard_map/ppermute | solution.py:99
  213.2 4.4 %collective-permute-done.36 = f32[2]{0:T(128)S(1)} collective-permute-done((f32[2]{0:T(128)S(1)}, f32[2]{0:T(128)S(1)}, u32[]{:S(2)}, u32[]{:S(2)}) %collective-permute-start.36) | collective-permute-done | bytes 40 | tf_op jit(solution)/shard_map/ppermute | solution.py:99
  231.0 8.5 %collective-permute-done.43.refs_6_ = bf16[2,152,608]{2,1,0:T(8,128)(2,1)S(1)} collective-permute-done((bf16[2,152,608]{2,1,0:T(8,128)(2,1)S(1)}, bf16[2,152,608]{2,1,0:T(8,128)(2,1)S(1)}, u32[]{:S(2)}, u32[]{:S(2)}) %collective-permute-start.43) | collective-permute-done | bytes 369696 | tf_op jit(solution)/shard_map/ppermute | solution.py:79
  240.0 10.9 %collective-permute-done.41.refs_4_ = bf16[2,152,608]{2,1,0:T(8,128)(2,1)S(1)} collective-permute-done((bf16[2,152,608]{2,1,0:T(8,128)(2,1)S(1)}, bf16[2,152,608]{2,1,0:T(8,128)(2,1)S(1)}, u32[]{:S(2)}, u32[]{:S(2)}) %collective-permute-start.41) | collective-permute-done | bytes 369696 | tf_op jit(solution)/shard_map/ppermute | solution.py:79
  253.5 9.4 %collective-permute-done.42.refs_5_ = bf16[2,152,608]{2,1,0:T(8,128)(2,1)S(1)} collective-permute-done((bf16[2,152,608]{2,1,0:T(8,128)(2,1)S(1)}, bf16[2,152,608]{2,1,0:T(8,128)(2,1)S(1)}, u32[]{:S(2)}, u32[]{:S(2)}) %collective-permute-start.42) | collective-permute-done | bytes 369696 | tf_op jit(solution)/shard_map/ppermute | solution.py:79
  264.5 6.8 %collective-permute-done.38.refs_1_ = bf16[2,152,608]{2,1,0:T(8,128)(2,1)S(1)} collective-permute-done((bf16[2,152,608]{2,1,0:T(8,128)(2,1)S(1)}, bf16[2,152,608]{2,1,0:T(8,128)(2,1)S(1)}, u32[]{:S(2)}, u32[]{:S(2)}) %collective-permute-start.38) | collective-permute-done | bytes 369696 | tf_op jit(solution)/shard_map/ppermute | solution.py:79
  271.3 5.5 %collective-permute-done.40.refs_3_ = bf16[2,152,608]{2,1,0:T(8,128)(2,1)S(1)} collective-permute-done((bf16[2,152,608]{2,1,0:T(8,128)(2,1)S(1)}, bf16[2,152,608]{2,1,0:T(8,128)(2,1)S(1)}, u32[]{:S(2)}, u32[]{:S(2)}) %collective-permute-start.40) | collective-permute-done | bytes 369696 | tf_op jit(solution)/shard_map/ppermute | solution.py:79
  278.2 3.7 %fusion.3 = bf16[608,512]{1,0:T(8,128)(2,1)S(1)} fusion(bf16[608,2432]{1,0:T(8,128)(2,1)S(1)} %copy-done, bf16[512,2432]{1,0:T(8,128)(2,1)} %cot_ref.3, f32[512]{0:T(512)S(1)} %bitcast.206), kind=kOutput, calls=%fused_computation.25 | convolution fusion | flops 1514766336 | bytes 6072320 | tf_op jit(solution)/shard_map/dot_general | solution.py:45
  283.8 3.4 %shard_map.205 = bf16[608,512]{1,0:T(8,128)(2,1)S(1)} custom-call(s32[3]{0:T(128)S(1)} %pad_add_fusion.place_ref, bf16[608,2432]{1,0:T(8,128)(2,1)S(1)} %copy-done.20, bf16[2,2,152,512]{3,2,1,0:T(8,128)(2,1)S(1)} %copy-done.24, bf16[2,2,152,512]{3,2,1,0:T(8,128)(2,1)} %collective-permute-done.2.refs_1_, bf16[2,2,152,512]{3,2,1,0:T(8,128)(2,1)S(1)} %copy-done.22, ...), custom_call_target="tpu_custom_call" | custom-call | flops 1514143744 | bytes 6070272 | tf_op jit(solution)/shard_map/pallas_call | solution.py:161
  289.2 4.6 %shard_map.208 = bf16[608,2432]{1,0:T(8,128)(2,1)} custom-call(s32[3]{0:T(128)S(1)} %pad_add_fusion.place_ref, bf16[2,152,608]{2,1,0:T(8,128)(2,1)S(1)} %copy-done.19, bf16[2,152,608]{2,1,0:T(8,128)(2,1)S(1)} %copy-done.15, bf16[2,152,608]{2,1,0:T(8,128)(2,1)S(1)} %copy-done.9, bf16[2,152,608]{2,1,0:T(8,128)(2,1)S(1)} %copy-done.17, ...), custom_call_target="tpu_custom_call" | custom-call | flops 757071872 | bytes 5914624 | tf_op jit(solution)/shard_map/pallas_call | solution.py:200
  293.8 4.6 %shard_map.207 = bf16[608,2432]{1,0:T(8,128)(2,1)} custom-call(s32[3]{0:T(128)S(1)} %pad_add_fusion.place_ref, bf16[2,152,608]{2,1,0:T(8,128)(2,1)S(1)} %copy-done.19, bf16[2,152,608]{2,1,0:T(8,128)(2,1)S(1)} %copy-done.15, bf16[2,152,608]{2,1,0:T(8,128)(2,1)S(1)} %copy-done.9, bf16[2,152,608]{2,1,0:T(8,128)(2,1)S(1)} %copy-done.17, ...), custom_call_target="tpu_custom_call" | custom-call | flops 757071872 | bytes 5914624 | tf_op jit(solution)/shard_map/pallas_call | solution.py:200
  298.3 3.5 %fusion.9 = bf16[608,512]{1,0:T(8,128)(2,1)S(1)} fusion(bf16[512,2432]{1,0:T(8,128)(2,1)} %collective-permute-done.15, bf16[608,2432]{1,0:T(8,128)(2,1)S(1)} %copy-done, f32[512]{0:T(512)S(1)} %bitcast.207), kind=kOutput, calls=%fused_computation.39 | convolution fusion | flops 1514766336 | bytes 6072320 | tf_op jit(solution)/shard_map/dot_general | solution.py:45
  (240 shorter events, 101.0 us)
Async XLA Ops:
  14.3 28.6 %collective-permute-start.6 = (f32[2]{0:T(128)S(1)}, f32[2]{0:T(128)S(1)}, u32[]{:S(2)}, u32[]{:S(2)}) collective-permute-start(f32[2]{0:T(128)S(1)} %pad_maximum_fusion.3), channel_id=1, source_target_pairs={{0,2},{2,0},{4,6},{6,4},{8,10},{10,8},{12,14},{14,12},{16,18},{18,... | collective-permute-start | bytes 32 | tf_op jit(solution)/shard_map/ppermute | solution.py:99
  16.8 46.2 %collective-permute-start.3 = (bf16[608,512]{1,0:T(8,128)(2,1)}, bf16[608,512]{1,0:T(8,128)(2,1)}, u32[]{:S(2)}, u32[]{:S(2)}) collective-permute-start(bf16[608,512]{1,0:T(8,128)(2,1)} %constant_dynamic-slice_fusion.3), channel_id=1, source_target_pairs={{0,1},{1,0},{2,3},{3,2},{4,5},{5,4},{6,7},{7,6},{8,9},{9,8},{10,11... | collective-permute-start | bytes 1867784 | tf_op jit(solution)/shard_map/ppermute | solution.py:92
  25.2 44.8 %collective-permute-start.2 = (bf16[2,2,152,512]{3,2,1,0:T(8,128)(2,1)}, bf16[2,2,152,512]{3,2,1,0:T(8,128)(2,1)}, u32[]{:S(2)}, u32[]{:S(2)}) collective-permute-start(bf16[2,2,152,512]{3,2,1,0:T(8,128)(2,1)} %get-tuple-element.35), channel_id=1, source_target_pairs={{0,1},{1,0},{2,3},{3,2},{4,5},{5,4},{6,7},{7,6},{8,9},{9,8},{10,11... | collective-permute-start | bytes 1867784 | tf_op jit(solution)/shard_map/ppermute | solution.py:92
  25.2 40.9 %collective-permute-start = (bf16[2,2,152,512]{3,2,1,0:T(8,128)(2,1)}, bf16[2,2,152,512]{3,2,1,0:T(8,128)(2,1)}, u32[]{:S(2)}, u32[]{:S(2)}) collective-permute-start(bf16[2,2,152,512]{3,2,1,0:T(8,128)(2,1)} %get-tuple-element.36), channel_id=1, source_target_pairs={{0,1},{1,0},{2,3},{3,2},{4,5},{5,4},{6,7},{7,6},{8,9},{9,8},{10,11... | collective-permute-start | bytes 1867784 | tf_op jit(solution)/shard_map/ppermute | solution.py:92
  36.0 80.8 %collective-permute-start.27 = (f32[1216,608]{1,0:T(8,128)}, f32[1216,608]{1,0:T(8,128)}, u32[]{:S(2)}, u32[]{:S(2)}) collective-permute-start(f32[1216,608]{1,0:T(8,128)} %fusion.16), channel_id=1, source_target_pairs={{0,2},{2,0},{4,6},{6,4},{8,10},{10,8},{12,14},{14,12},{16,18},{18,... | collective-permute-start | bytes 8871944 | tf_op jit(solution)/shard_map/ppermute | solution.py:79
  64.3 30.3 %collective-permute-start.4 = (bf16[2,2,152,512]{3,2,1,0:T(8,128)(2,1)}, bf16[2,2,152,512]{3,2,1,0:T(8,128)(2,1)S(1)}, u32[]{:S(2)}, u32[]{:S(2)}) collective-permute-start(bf16[2,2,152,512]{3,2,1,0:T(8,128)(2,1)} %get-tuple-element.14), channel_id=1, source_target_pairs={{0,1},{1,0},{2,3},{3,2},{4,5},{5,4},{6,7},{7,6},{8,9},{9,8},{10,11... | collective-permute-start | bytes 1867784 | tf_op jit(solution)/shard_map/ppermute | solution.py:92
  66.2 27.5 %collective-permute-start.1 = (bf16[2,2,152,512]{3,2,1,0:T(8,128)(2,1)S(1)}, bf16[2,2,152,512]{3,2,1,0:T(8,128)(2,1)S(1)}, u32[]{:S(2)}, u32[]{:S(2)}) collective-permute-start(bf16[2,2,152,512]{3,2,1,0:T(8,128)(2,1)S(1)} %copy-done.37), channel_id=1, source_target_pairs={{0,1},{1,0},{2,3},{3,2},{4,5},{5,4},{6,7},{7,6},{8,9},{9,8},{10,11... | collective-permute-start | bytes 1867784 | tf_op jit(solution)/shard_map/ppermute | solution.py:92
  69.0 26.3 %collective-permute-start.16 = (f32[304,608]{1,0:T(8,128)S(1)}, f32[304,608]{1,0:T(8,128)S(1)}, u32[]{:S(2)}, u32[]{:S(2)}) collective-permute-start(f32[304,608]{1,0:T(8,128)S(1)} %convolution_add_fusion.8), channel_id=1, source_target_pairs={{0,2},{2,0},{4,6},{6,4},{8,10},{10,8},{12,14},{14,12},{16,18},{18,... | collective-permute-start | bytes 2217992 | tf_op jit(solution)/shard_map/ppermute | solution.py:79
  72.8 23.7 %collective-permute-start.19 = (f32[304,608]{1,0:T(8,128)S(1)}, f32[304,608]{1,0:T(8,128)S(1)}, u32[]{:S(2)}, u32[]{:S(2)}) collective-permute-start(f32[304,608]{1,0:T(8,128)S(1)} %convolution_add_fusion.6), channel_id=1, source_target_pairs={{0,2},{2,0},{4,6},{6,4},{8,10},{10,8},{12,14},{14,12},{16,18},{18,... | collective-permute-start | bytes 2217992 | tf_op jit(solution)/shard_map/ppermute | solution.py:79
  93.7 28.1 %collective-permute-start.5 = (f32[1216,608]{1,0:T(8,128)S(1)}, f32[1216,608]{1,0:T(8,128)S(1)}, u32[]{:S(2)}, u32[]{:S(2)}) collective-permute-start(f32[1216,608]{1,0:T(8,128)S(1)} %fusion.117), channel_id=1, source_target_pairs={{0,2},{2,0},{4,6},{6,4},{8,10},{10,8},{12,14},{14,12},{16,18},{18,... | collective-permute-start | bytes 8871944 | tf_op jit(solution)/shard_map/ppermute | solution.py:79
  94.6 20.2 %collective-permute-start.25 = (f32[304,608]{1,0:T(8,128)S(1)}, f32[304,608]{1,0:T(8,128)S(1)}, u32[]{:S(2)}, u32[]{:S(2)}) collective-permute-start(f32[304,608]{1,0:T(8,128)S(1)} %convolution_add_fusion.2), channel_id=1, source_target_pairs={{0,2},{2,0},{4,6},{6,4},{8,10},{10,8},{12,14},{14,12},{16,18},{18,... | collective-permute-start | bytes 2217992 | tf_op jit(solution)/shard_map/ppermute | solution.py:79
  95.4 18.8 %collective-permute-start.22 = (f32[304,608]{1,0:T(8,128)S(1)}, f32[304,608]{1,0:T(8,128)S(1)}, u32[]{:S(2)}, u32[]{:S(2)}) collective-permute-start(f32[304,608]{1,0:T(8,128)S(1)} %convolution_add_fusion.4), channel_id=1, source_target_pairs={{0,2},{2,0},{4,6},{6,4},{8,10},{10,8},{12,14},{14,12},{16,18},{18,... | collective-permute-start | bytes 2217992 | tf_op jit(solution)/shard_map/ppermute | solution.py:79
  109.7 69.6 %collective-permute-start.18 = (f16[152,608]{1,0:T(8,128)(2,1)S(1)}, f16[152,608]{1,0:T(8,128)(2,1)S(1)}, u32[]{:S(2)}, u32[]{:S(2)}) collective-permute-start(f16[152,608]{1,0:T(8,128)(2,1)S(1)} %fusion.36), channel_id=1, source_target_pairs={{0,24},{2,26},{4,28},{6,30},{8,0},{10,2},{12,4},{14,6},{16,8},{18,... | collective-permute-start | bytes 554504 | tf_op jit(solution)/shard_map/ppermute | solution.py:79
  114.1 69.1 %collective-permute-start.21 = (f16[152,608]{1,0:T(8,128)(2,1)S(1)}, f16[152,608]{1,0:T(8,128)(2,1)S(1)}, u32[]{:S(2)}, u32[]{:S(2)}) collective-permute-start(f16[152,608]{1,0:T(8,128)(2,1)S(1)} %fusion.33), channel_id=1, source_target_pairs={{0,8},{2,10},{4,12},{6,14},{8,16},{10,18},{12,20},{14,22},{16,24},... | collective-permute-start | bytes 554504 | tf_op jit(solution)/shard_map/ppermute | solution.py:79
  121.3 20.4 %collective-permute-start.28 = (f16[4,152,608]{2,1,0:T(8,128)(2,1)S(1)}, f16[4,152,608]{2,1,0:T(8,128)(2,1)S(1)}, u32[]{:S(2)}, u32[]{:S(2)}) collective-permute-start(f16[4,152,608]{2,1,0:T(8,128)(2,1)S(1)} %bitcast.199), channel_id=1, source_target_pairs={{0,4},{2,6},{4,0},{6,2},{8,12},{10,14},{12,8},{14,10},{16,20},{18,... | collective-permute-start | bytes 2217992 | tf_op jit(solution)/shard_map/ppermute | solution.py:79
  123.3 32.0 %collective-permute-start.11 = (f16[4,152,608]{2,1,0:T(8,128)(2,1)S(1)}, f16[4,152,608]{2,1,0:T(8,128)(2,1)S(1)}, u32[]{:S(2)}, u32[]{:S(2)}) collective-permute-start(f16[4,152,608]{2,1,0:T(8,128)(2,1)S(1)} %bitcast.200), channel_id=1, source_target_pairs={{0,4},{2,6},{4,0},{6,2},{8,12},{10,14},{12,8},{14,10},{16,20},{18,... | collective-permute-start | bytes 2217992 | tf_op jit(solution)/shard_map/ppermute | solution.py:79
  160.0 18.5 %collective-permute-start.13 = (f16[152,608]{1,0:T(8,128)(2,1)S(1)}, f16[152,608]{1,0:T(8,128)(2,1)S(1)}, u32[]{:S(2)}, u32[]{:S(2)}) collective-permute-start(f16[152,608]{1,0:T(8,128)(2,1)S(1)} %get-tuple-element.43), channel_id=1, source_target_pairs={{0,16},{2,18},{4,20},{6,22},{8,24},{10,26},{12,28},{14,30},{16,0},... | collective-permute-start | bytes 554504 | tf_op jit(solution)/shard_map/ppermute | solution.py:79
  165.9 17.4 %collective-permute-start.26 = (f16[152,608]{1,0:T(8,128)(2,1)S(1)}, f16[152,608]{1,0:T(8,128)(2,1)S(1)}, u32[]{:S(2)}, u32[]{:S(2)}) collective-permute-start(f16[152,608]{1,0:T(8,128)(2,1)S(1)} %fusion.26), channel_id=1, source_target_pairs={{0,4},{2,6},{4,0},{6,2},{8,12},{10,14},{12,8},{14,10},{16,20},{18,... | collective-permute-start | bytes 554504 | tf_op jit(solution)/shard_map/ppermute | solution.py:79
  166.4 24.6 %collective-permute-start.24 = (f16[152,608]{1,0:T(8,128)(2,1)S(1)}, f16[152,608]{1,0:T(8,128)(2,1)S(1)}, u32[]{:S(2)}, u32[]{:S(2)}) collective-permute-start(f16[152,608]{1,0:T(8,128)(2,1)S(1)} %fusion.30), channel_id=1, source_target_pairs={{0,16},{2,18},{4,20},{6,22},{8,24},{10,26},{12,28},{14,30},{16,0},... | collective-permute-start | bytes 554504 | tf_op jit(solution)/shard_map/ppermute | solution.py:79
  178.5 13.9 %collective-permute-start.29 = (f16[152,608]{1,0:T(8,128)(2,1)S(1)}, f16[152,608]{1,0:T(8,128)(2,1)S(1)}, u32[]{:S(2)}, u32[]{:S(2)}) collective-permute-start(f16[152,608]{1,0:T(8,128)(2,1)S(1)} %get-tuple-element.38), channel_id=1, source_target_pairs={{0,8},{2,10},{4,12},{6,14},{8,16},{10,18},{12,20},{14,22},{16,24},... | collective-permute-start | bytes 554504 | tf_op jit(solution)/shard_map/ppermute | solution.py:79
  179.3 13.1 %collective-permute-start.31 = (f16[152,608]{1,0:T(8,128)(2,1)S(1)}, f16[152,608]{1,0:T(8,128)(2,1)S(1)}, u32[]{:S(2)}, u32[]{:S(2)}) collective-permute-start(f16[152,608]{1,0:T(8,128)(2,1)S(1)} %get-tuple-element.39), channel_id=1, source_target_pairs={{0,24},{2,26},{4,28},{6,30},{8,0},{10,2},{12,4},{14,6},{16,8},{18,... | collective-permute-start | bytes 554504 | tf_op jit(solution)/shard_map/ppermute | solution.py:79
  183.2 16.0 %collective-permute-start.30 = (f16[152,608]{1,0:T(8,128)(2,1)S(1)}, f16[152,608]{1,0:T(8,128)(2,1)S(1)}, u32[]{:S(2)}, u32[]{:S(2)}) collective-permute-start(f16[152,608]{1,0:T(8,128)(2,1)S(1)} %get-tuple-element.40), channel_id=1, source_target_pairs={{0,16},{2,18},{4,20},{6,22},{8,24},{10,26},{12,28},{14,30},{16,0},... | collective-permute-start | bytes 554504 | tf_op jit(solution)/shard_map/ppermute | solution.py:79
  183.3 15.9 %collective-permute-start.32 = (f16[152,608]{1,0:T(8,128)(2,1)S(1)}, f16[152,608]{1,0:T(8,128)(2,1)S(1)}, u32[]{:S(2)}, u32[]{:S(2)}) collective-permute-start(f16[152,608]{1,0:T(8,128)(2,1)S(1)} %fusion.44), channel_id=1, source_target_pairs={{0,1},{1,0},{2,3},{3,2},{4,5},{5,4},{6,7},{7,6},{8,9},{9,8},{10,11... | collective-permute-start | bytes 554504 | tf_op jit(solution)/shard_map/ppermute | solution.py:92
  225.6 13.9 %collective-permute-start.43 = (bf16[2,152,608]{2,1,0:T(8,128)(2,1)S(1)}, bf16[2,152,608]{2,1,0:T(8,128)(2,1)S(1)}, u32[]{:S(2)}, u32[]{:S(2)}) collective-permute-start(bf16[2,152,608]{2,1,0:T(8,128)(2,1)S(1)} %get-tuple-element.61.refs_0_), channel_id=1, source_target_pairs={{0,8},{2,10},{4,12},{6,14},{8,16},{10,18},{12,20},{14,22},{16,24},... | collective-permute-start | bytes 1109000 | tf_op jit(solution)/shard_map/ppermute | solution.py:79
  225.7 25.3 %collective-permute-start.41 = (bf16[2,152,608]{2,1,0:T(8,128)(2,1)S(1)}, bf16[2,152,608]{2,1,0:T(8,128)(2,1)S(1)}, u32[]{:S(2)}, u32[]{:S(2)}) collective-permute-start(bf16[2,152,608]{2,1,0:T(8,128)(2,1)S(1)} %get-tuple-element.61.refs_0_), channel_id=1, source_target_pairs={{0,16},{2,18},{4,20},{6,22},{8,24},{10,26},{12,28},{14,30},{16,0},... | collective-permute-start | bytes 1109000 | tf_op jit(solution)/shard_map/ppermute | solution.py:79
  227.8 25.2 %collective-permute-start.39 = (bf16[2,152,608]{2,1,0:T(8,128)(2,1)S(1)}, bf16[2,152,608]{2,1,0:T(8,128)(2,1)S(1)}, u32[]{:S(2)}, u32[]{:S(2)}) collective-permute-start(bf16[2,152,608]{2,1,0:T(8,128)(2,1)S(1)} %get-tuple-element.61.refs_0_), channel_id=1, source_target_pairs={{0,24},{2,26},{4,28},{6,30},{8,0},{10,2},{12,4},{14,6},{16,8},{18,... | collective-permute-start | bytes 1109000 | tf_op jit(solution)/shard_map/ppermute | solution.py:79
  229.5 68.8 %collective-permute-start.15 = (bf16[512,2432]{1,0:T(8,128)(2,1)}, bf16[512,2432]{1,0:T(8,128)(2,1)}, u32[]{:S(2)}, u32[]{:S(2)}) collective-permute-start(bf16[512,2432]{1,0:T(8,128)(2,1)} %cot_ref.3), channel_id=1, source_target_pairs={{0,1},{1,0},{2,3},{3,2},{4,5},{5,4},{6,7},{7,6},{8,9},{9,8},{10,11... | collective-permute-start | bytes 7471112 | tf_op jit(solution)/shard_map/ppermute | solution.py:92
  239.5 14.0 %collective-permute-start.44 = (bf16[2,152,608]{2,1,0:T(8,128)(2,1)S(1)}, bf16[2,152,608]{2,1,0:T(8,128)(2,1)S(1)}, u32[]{:S(2)}, u32[]{:S(2)}) collective-permute-start(bf16[2,152,608]{2,1,0:T(8,128)(2,1)S(1)} %collective-permute-done.43.refs_6_), channel_id=1, source_target_pairs={{0,4},{2,6},{4,0},{6,2},{8,12},{10,14},{12,8},{14,10},{16,20},{18,... | collective-permute-start | bytes 1109000 | tf_op jit(solution)/shard_map/ppermute | solution.py:79
  250.9 12.0 %collective-permute-start.42 = (bf16[2,152,608]{2,1,0:T(8,128)(2,1)S(1)}, bf16[2,152,608]{2,1,0:T(8,128)(2,1)S(1)}, u32[]{:S(2)}, u32[]{:S(2)}) collective-permute-start(bf16[2,152,608]{2,1,0:T(8,128)(2,1)S(1)} %collective-permute-done.41.refs_4_), channel_id=1, source_target_pairs={{0,4},{2,6},{4,0},{6,2},{8,12},{10,14},{12,8},{14,10},{16,20},{18,... | collective-permute-start | bytes 1109000 | tf_op jit(solution)/shard_map/ppermute | solution.py:79
  251.5 19.8 %collective-permute-start.38 = (bf16[2,152,608]{2,1,0:T(8,128)(2,1)S(1)}, bf16[2,152,608]{2,1,0:T(8,128)(2,1)S(1)}, u32[]{:S(2)}, u32[]{:S(2)}) collective-permute-start(bf16[2,152,608]{2,1,0:T(8,128)(2,1)S(1)} %get-tuple-element.61.refs_0_), channel_id=1, source_target_pairs={{0,4},{2,6},{4,0},{6,2},{8,12},{10,14},{12,8},{14,10},{16,20},{18,... | collective-permute-start | bytes 1109000 | tf_op jit(solution)/shard_map/ppermute | solution.py:79
  253.0 23.7 %collective-permute-start.40 = (bf16[2,152,608]{2,1,0:T(8,128)(2,1)S(1)}, bf16[2,152,608]{2,1,0:T(8,128)(2,1)S(1)}, u32[]{:S(2)}, u32[]{:S(2)}) collective-permute-start(bf16[2,152,608]{2,1,0:T(8,128)(2,1)S(1)} %collective-permute-done.39.refs_2_), channel_id=1, source_target_pairs={{0,4},{2,6},{4,0},{6,2},{8,12},{10,14},{12,8},{14,10},{16,20},{18,... | collective-permute-start | bytes 1109000 | tf_op jit(solution)/shard_map/ppermute | solution.py:79
  264.4 24.8 %collective-permute-start.46 = (bf16[4,2,152,608]{3,2,1,0:T(8,128)(2,1)}, bf16[4,2,152,608]{3,2,1,0:T(8,128)(2,1)}, u32[]{:S(2)}, u32[]{:S(2)}) collective-permute-start(bf16[4,2,152,608]{3,2,1,0:T(8,128)(2,1)} %pad_maximum_fusion.1), channel_id=1, source_target_pairs={{0,2},{2,0},{4,6},{6,4},{8,10},{10,8},{12,14},{14,12},{16,18},{18,... | collective-permute-start | bytes 4435976 | tf_op jit(solution)/shard_map/ppermute | solution.py:79
  (60 other events, 722.2 us)

commit v3 on v2

--- a/solution.py
+++ b/solution.py
@@ -51,10 +51,6 @@
     return jnp.where(rows == cols, 1.0, 0.0).astype(jnp.bfloat16)
 
 
-def after(value, *others):
-    return lax.optimization_barrier((value, *others))[0]
-
-
 def cost(flops, nbytes):
     return pl.CostEstimate(flops=flops, bytes_accessed=nbytes, transcendentals=0)
 
@@ -90,15 +86,6 @@
     def from_tensor(value, k):
         perm = [(s, (s - k) & (n_tensor - 1)) for s in range(n_tensor)]
         return lax.ppermute(value, "tensor", perm)
-
-    def butterfly(value, combine):
-        for axis, size in (("dp", n_dp), ("tensor", n_tensor)):
-            step = 1
-            while step < size:
-                perm = [(p, p ^ step) for p in range(size)]
-                value = combine(value, lax.ppermute(value, axis, perm))
-                step *= 2
-        return value
 
     def relative(place_ref, p):
         z, m, c = split(p)
@@ -108,39 +95,57 @@
             c ^ place_ref[2],
         )
 
-    def turn(cot, place, planes_first):
+    def turn(cot, place, by_planes):
         r = cot.shape[0]
         step = min(r, TILE)
-
-        def kernel(place_ref, cot_ref, out_ref, wide_ref):
+        count = OUTER if by_planes else 2
+        lead = (2, inner) if by_planes else (inner, OUTER)
+
+        def kernel(place_ref, cot_ref, *refs):
+            out_refs, (top_ref, wide_ref) = refs[:count], refs[count:]
             eye = identity(TILE)
             for start in range(0, D, TILE):
                 size = min(TILE, D - start)
                 wide_ref[start : start + size, :] = dot(
                     eye[:size, :size], cot_ref[:, start : start + size], NT
                 )
+            top = jnp.max(jnp.abs(wide_ref[...]).reshape(D // 8, 8, step), axis=0)
+            top = jnp.broadcast_to(jnp.max(top), (8, 128))
+
+            @pl.when(pl.program_id(0) == 0)
+            def _():
+                top_ref[...] = top
+
+            @pl.when(pl.program_id(0) > 0)
+            def _():
+                top_ref[...] = jnp.maximum(top_ref[...], top)
+
             for p in range(n_dp):
                 k, i, other = relative(place_ref, p)
                 block = wide_ref[p * width : (p + 1) * width, :].astype(jnp.bfloat16)
-                if planes_first:
-                    out_ref[k, other, i] = block
-                else:
-                    out_ref[other, i, k] = block
-
-        lead = (OUTER, 2, inner) if planes_first else (2, inner, OUTER)
-        return pl.pallas_call(
+                which, at = (k, (other, i)) if by_planes else (other, (i, k))
+                for n in range(count):
+
+                    @pl.when(which == n)
+                    def _(n=n, at=at, block=block):
+                        out_refs[n][at] = block
+
+        *outs, top = pl.pallas_call(
             kernel,
-            out_shape=jax.ShapeDtypeStruct((*lead, width, r), jnp.bfloat16),
+            out_shape=[jax.ShapeDtypeStruct((*lead, width, r), jnp.bfloat16)] * count
+            + [jax.ShapeDtypeStruct((8, 128), jnp.float32)],
             grid=(r // step,),
             in_specs=[
                 pl.BlockSpec(memory_space=pltpu.SMEM),
                 pl.BlockSpec((step, D), lambda s: (s, 0)),
             ],
-            out_specs=pl.BlockSpec((*lead, width, step), lambda s: (0, 0, 0, 0, s)),
+            out_specs=[pl.BlockSpec((*lead, width, step), lambda s: (0, 0, 0, s))] * count
+            + [pl.BlockSpec((8, 128), lambda s: (0, 0))],
             scratch_shapes=[pltpu.VMEM((D, step), jnp.float32)],
             compiler_params=params_of(),
             cost_estimate=cost(2 * TILE * D * r, 4 * D * r),
         )(place, cot)
+        return outs, top
 
     def back_other(weight, pieces, scale, place):
         f = weight.shape[0]
@@ -237,110 +242,272 @@
         scale_student = sample_scale(timesteps[0, 0], count)
         scale_fake = sample_scale(timesteps[0, 1], count)
 
-        acts = [
-            from_tensor(rows_of(act_fake, j), -j) for j in range(1, n_tensor)
+        token = []
+
+        def step(work, *inputs):
+            if token:
+                *inputs, _ = lax.optimization_barrier((*inputs, token[0]))
+            out = work(*inputs)
+            token[:] = jax.tree.leaves(out)[:1]
+            return out
+
+        row = lax.broadcasted_iota(jnp.int32, (8, 128), 0)
+
+        def pair(student, fake):
+            return jnp.where(row == 0, student, fake)
+
+        def gather_planes(value, combine):
+            got = [to_plane(value, k) for k in range(1, OUTER)]
+            return lambda: step(lambda *all_of: functools.reduce(combine, all_of), value, *got)
+
+        def gather_chips(value, combine):
+            got = [
+                move_dp(value, lambda z, m, c, i=i, o=o: (z, (m + i) & (inner - 1), c ^ o))
+                for i in range(inner)
+                for o in range(2)
+                if i or o
+            ]
+            return lambda: step(lambda *all_of: functools.reduce(combine, all_of), value, *got)
+
+        own_scale = rows_of(scale_fake, 0)
+        act_sent = step(lambda act: [rows_of(act, j) for j in range(1, n_tensor)], act_fake)
+        acts = [from_tensor(act, -j) for j, act in enumerate(act_sent, 1)]
+        planes, top_student = step(lambda cot: turn(cot, place, True), cot_student)
+        order = (3, 1, 2, 0)
+        others = {k: [from_tensor(planes[k], j) for j in range(1, n_tensor)] for k in order}
+        cores, top_fake = step(lambda cot: turn(cot, place, False), cot_fake)
+        cores = [core.reshape(-1, r) for core in cores]
+
+        def bound(top_s, top_f, act_s, act_f):
+            tops = [
+                top[0, 0] * jnp.max(jnp.abs(act)).astype(jnp.float32) * jnp.max(scale)
+                for top, act, scale in (
+                    (top_s, act_s, scale_student),
+                    (top_f, act_f, scale_fake),
+                )
+            ]
+            return pair(*tops)
+
+        bounds = step(bound, top_student, top_fake, act_student, act_fake)
+        finish = gather_planes(bounds, jnp.maximum)
+        scaled = step(lambda act: scaled_by(rows_of(act, 0), own_scale), act_fake)
+        sends, keeps = [], []
+        sends.append(to_core(step(lambda a, b: dot(a, b, NT), cores[1], scaled)))
+        bounds = finish()
+        finish = gather_chips(bounds, jnp.maximum)
+        keeps.append(step(lambda a, b: dot(a, b, NT), cores[0], scaled))
+        scaled_student = [
+            step(lambda act, j=j: scaled_by(rows_of(act, j), rows_of(scale_student, j)), act_student)
+            for j in range(n_tensor)
         ]
-        acts = [rows_of(act_fake, 0), *acts]
-        own_scale = rows_of(scale_fake, 0)
-        scaled_fake = [scaled_by(act, own_scale) for act in acts]
-        scaled_student = scaled_by(act_student, scale_student)
-
-        turned_student = turn(cot_student, place, True)
-        turned_fake = turn(cot_fake, place, False).reshape(2, -1, r)
-
-        def bound(cot, act, scale):
-            return (
-                jnp.max(jnp.abs(cot)).astype(jnp.float32)
-                * jnp.max(jnp.abs(act)).astype(jnp.float32)
-                * jnp.max(scale)
-            )
-
-        bounds = butterfly(
-            jnp.stack(
-                [
-                    bound(cot_student, act_student, scale_student),
-                    bound(cot_fake, act_fake, scale_fake),
-                ]
-            ),
-            jnp.maximum,
-        )
-        bounds = jnp.maximum(bounds, 1e-30) * (1.01 * count * n_dp / HALF_LIMIT)
+        bounds = finish()
+
+        def factors(bounds):
+            bounds = jnp.maximum(bounds, 1e-30) * (1.01 * count * n_dp / HALF_LIMIT)
+            return bounds[:2, 0], 1.0 / bounds[:2, 0]
+
+        grow, fit = step(factors, bounds)
 
         def shrink(value, net):
-            return (value * (1.0 / bounds[net])).astype(jnp.float16)
+            return (value * fit[net]).astype(jnp.float16)
 
         def widen(value, net):
-            return value.astype(jnp.float32) * bounds[net]
-
-        def over_middle(blocks, net):
-            mine = blocks[0]
-            for i in range(1, inner):
-                mine = mine + widen(to_middle(shrink(blocks[i], net), i), net)
-            return mine
-
-        parts_fake = []
-        for scaled in scaled_fake:
-            keep = dot(turned_fake[0], scaled, NT)
-            send = dot(turned_fake[1], scaled, NT)
-            both = (keep + to_core(send)).reshape(inner, OUTER, width, f)
-            mine = over_middle(both, 1)
-            total = mine[0]
-            for k in range(1, OUTER):
-                total = total + widen(to_plane(shrink(mine[k], 1), k), 1)
-            parts_fake.append(total)
-
-        order = (3, 1, 2, 0)
-        pieces, arrived = {}, [scaled_fake[-1]]
-        total_student = None
-        for at, k in enumerate(order):
-            own = turned_student[k]
-            if at >= 2:
-                own = after(own, arrived[at - 2])
-            others = [from_tensor(own, j) for j in range(1, n_tensor)]
-            arrived.append(others[-1])
-            pieces[k] = others
-            halves = [own, *others]
-            sums = []
-            for other in range(2):
-                grad = None
-                for j, piece in enumerate(halves):
-                    term = dot(piece[other].reshape(-1, r), rows_of(scaled_student, j), NT)
-                    grad = term if grad is None else grad + term
-                sums.append(grad)
-            both = (sums[0] + to_core(sums[1])).reshape(inner, width, f)
-            mine = over_middle(both, 0)
-            if k:
-                mine = widen(to_plane(shrink(mine, 0), k), 0)
-            total_student = mine if total_student is None else total_student + mine
-
-        total_fake = parts_fake[0]
-        last = None
+            return value.astype(jnp.float32) * grow[net]
+
+        halves = ((2, 3), (0, 1))
+
+        def fake_middle(keep, send):
+            both = (keep + send).reshape(inner, OUTER, width, f)
+            sent = [
+                [shrink(both[i, lo : hi + 1], 1) for i in range(1, inner)] for lo, hi in halves
+            ]
+            return sent, [both[0, lo : hi + 1] for lo, hi in halves]
+
+        def start_middle(keep, send):
+            sent, mine = step(fake_middle, keep, send)
+            return [
+                (own, [to_middle(value, i) for i, value in enumerate(values, 1)])
+                for own, values in zip(mine, sent)
+            ]
+
+        middles = [start_middle(keeps[0], sends[0])]
+        for act in acts:
+            scaled = step(lambda act: scaled_by(act, own_scale), act)
+            sends.append(to_core(step(lambda a, b: dot(a, b, NT), cores[1], scaled)))
+            keeps.append(step(lambda a, b: dot(a, b, NT), cores[0], scaled))
+        for keep, send in zip(keeps[1:], sends[1:]):
+            middles.append(start_middle(keep, send))
+
+        def own_term(piece, scaled):
+            return [dot(piece[other].reshape(-1, r), scaled, NT) for other in range(2)]
+
+        own_terms = {k: step(own_term, planes[k], scaled_student[0]) for k in order}
+        kept = {}
+
+        def multiply(k):
+            def half(other, *operands):
+                term, *operands = operands
+                pieces, scales = operands[: n_tensor - 1], operands[n_tensor - 1 :]
+                for piece, scaled in zip(pieces, scales):
+                    term = term + dot(piece[other].reshape(-1, r), scaled, NT)
+                return term
+
+            operands = [*others[k], *scaled_student[1:]]
+            send = to_core(step(functools.partial(half, 1), own_terms[k][1], *operands))
+            kept[k] = step(functools.partial(half, 0), own_terms[k][0], *operands), send
+
+        crossing = {}
+
+        def cross_middle(k):
+            def work(keep, send):
+                both = (keep + send).reshape(inner, width, f)
+                return [shrink(both[i], 0) for i in range(1, inner)], both[0]
+
+            sent, own = step(work, *kept[k])
+            crossing[k] = own, [to_middle(value, i) for i, value in enumerate(sent, 1)]
+
+        to_sum = []
+
+        def cross_planes(k):
+            def work(own, *got):
+                for value in got:
+                    own = own + widen(value, 0)
+                return shrink(own, 0) if k else own
+
+            own, got = crossing[k]
+            value = step(work, own, *got)
+            to_sum.append(to_plane(value, k) if k else value)
+
+        fake_sums = [[] for _ in range(n_tensor)]
+
+        def fake_planes(j, part):
+            lo, hi = halves[part]
+
+            def work(own, *got):
+                for value in got:
+                    own = own + widen(value, 1)
+                return [shrink(own[k - lo], 1) if k else own[0] for k in range(hi, lo - 1, -1)]
+
+            own, got = middles[j][part]
+            values = step(work, own, *got)
+            for k, value in zip(range(hi, lo - 1, -1), values):
+                fake_sums[j].append(to_plane(value, k) if k else value)
+
+        def fake_total(j):
+            def work(*values):
+                total = values[-1]
+                for value in values[:-1]:
+                    total = total + widen(value, 1)
+                return total
+
+            return step(work, *fake_sums[j])
+
+        fake_planes(0, 0)
+        multiply(3)
+        cross_middle(3)
+        fake_planes(0, 1)
+        multiply(1)
+        cross_middle(1)
         for j in range(1, n_tensor):
-            last = shrink(parts_fake[j], 1)
-            total_fake = total_fake + widen(from_tensor(last, j), 1)
-
-        raw = after(cot_fake, last, arrived[-2])
-        cots_fake = [cot_fake] + [from_tensor(raw, j) for j in range(1, n_tensor)]
+            fake_planes(j, 0)
+        multiply(2)
+        cross_middle(2)
+        for j in range(1, n_tensor):
+            fake_planes(j, 1)
+        cross_planes(3)
+        fake_mine = fake_total(0)
+        fake_others = [fake_total(j) for j in range(1, n_tensor)]
+        fake_got = [from_tensor(value, j) for j, value in enumerate(fake_others, 1)]
+
+        quarter = r // 4
+        cuts = ((0, quarter), (quarter, 3 * quarter), (3 * quarter, r))
+        raw_first = step(lambda cot: cot[: cuts[0][1]], cot_fake)
+        raw = [[from_tensor(raw_first, j) for j in range(1, n_tensor)]]
+        cross_planes(1)
+        multiply(0)
+        cross_planes(2)
+        cross_middle(0)
+
+        def student_partial(*values):
+            total = widen(values[0], 0)
+            for value in values[1:]:
+                total = total + widen(value, 0)
+            return total
+
+        total_student = step(student_partial, *to_sum)
+        to_sum.clear()
+
+        def fake_all(mine, *got):
+            for value in got:
+                mine = mine + value
+            return mine, jnp.sum(mine * mine)
+
+        total_fake, square_fake = step(fake_all, fake_mine, *fake_got)
+        cross_planes(0)
+
+        def student_all(total, value, square_fake):
+            total = total + value
+            return pair(jnp.sum(total * total), square_fake), total
+
+        squares, total_student = step(student_all, total_student, to_sum[0], square_fake)
+        squares = gather_planes(squares, jnp.add)()
+        squares = gather_chips(squares, jnp.add)()
+        got = [from_tensor(squares, j) for j in range(1, n_tensor)]
+        for lo, hi in cuts[1:]:
+            rows = step(lambda cot: cot[lo:hi], cot_fake)
+            raw.append([from_tensor(rows, j) for j in range(1, n_tensor)])
+        squares = step(lambda *values: functools.reduce(jnp.add, values), squares, *got)
 
         totals = (total_student, total_fake)
-        squares = butterfly(jnp.stack([jnp.sum(total * total) for total in totals]), jnp.add)
         states = (
             (master_student, first_student, second_student),
             (master_fake, first_fake, second_fake),
         )
-        updated = [
-            adam_update(totals[n], squares[n], *(state.T for state in states[n])) for n in range(2)
+
+        def update(squares, *totals):
+            updated = [
+                adam_update(totals[n], squares[n, 0], *(state.T for state in states[n]))
+                for n in range(2)
+            ]
+            return jnp.stack([new[0].astype(jnp.bfloat16) for new in updated]), updated
+
+        own, updated = step(update, squares, *totals)
+
+        def back_rows(weight, cot, scale):
+            return (dot(weight, cot, NT) * scale[None, :]).astype(jnp.bfloat16)
+
+        mine = {}
+
+        def spread_middle(k, value):
+            mine[k] = [value] + [to_middle(value, -i) for i in range(1, inner)]
+
+        planes_got = {k: to_plane(own, -k) for k in (1, 3, 2)}
+        spread_middle(0, own)
+        back_student = [
+            step(lambda w, cot: back_rows(w, cot, rows_of(scale_student, 0)), weight_student, cot_student)
         ]
-        own = jnp.stack([new[0].astype(jnp.bfloat16) for new in updated])
-        mine = []
-        for k in range(OUTER):
-            got = to_plane(own, -k) if k else own
-            mine.append(got)
-            for i in range(1, inner):
-                mine.append(to_middle(got, -i))
-        half = len(mine) // 2
-        theirs = [to_core(jnp.stack(mine[:half])), to_core(jnp.stack(mine[half:]))]
-        params = [spread([*mine, *theirs], n, place) for n in range(2)]
+        spread_middle(1, step(lambda value: value, planes_got[1]))
+        for j in range(1, n_tensor):
+            back_student.append(
+                step(
+                    lambda w, *pieces: back_other(
+                        w, pieces, rows_of(scale_student, j)[None, :], place
+                    ),
+                    weight_student,
+                    *[others[k][j - 1] for k in range(OUTER)],
+                )
+            )
+        spread_middle(3, step(lambda value: value, planes_got[3]))
+        back_fake_own = step(
+            lambda w, cot: back_rows(w, cot, rows_of(scale_fake, 0)), weight_fake, cot_fake
+        )
+        first_half = step(lambda *values: jnp.stack(values), *mine[0], *mine[1])
+        theirs = [to_core(first_half)]
+        spread_middle(2, step(lambda value: value, planes_got[2]))
+        second_half = step(lambda *values: jnp.stack(values), *mine[2], *mine[3])
+        theirs.append(to_core(second_half))
+        blocks = [first_half, second_half, *theirs]
+        params = [spread(blocks, n, place) for n in range(2)]
 
         def assemble(parts):
             whole = jnp.concatenate(parts + parts, axis=1)
@@ -348,22 +515,14 @@
                 whole, r * ((n_tensor - t) & (n_tensor - 1)), count, 1
             )
 
-        def back_rows(weight, cot, scale):
-            return (dot(weight, cot, NT) * scale[None, :]).astype(jnp.bfloat16)
-
-        back_student = [back_rows(weight_student, cot_student, rows_of(scale_student, 0))]
-        back_student += [
-            back_other(
-                weight_student,
-                [pieces[k][j - 1] for k in range(OUTER)],
-                rows_of(scale_student, j)[None, :],
-                place,
-            )
-            for j in range(1, n_tensor)
-        ]
-        back_fake = [
-            back_rows(weight_fake, cots_fake[j], rows_of(scale_fake, j)) for j in range(n_tensor)
-        ]
+        back_fake = [back_fake_own]
+        for j in range(1, n_tensor):
+            scale = rows_of(scale_fake, j)
+            parts = [
+                back_rows(weight_fake, raw[n][j - 1], scale[lo:hi])
+                for n, (lo, hi) in enumerate(cuts)
+            ]
+            back_fake.append(jnp.concatenate(parts, axis=1))
 
         new_states = [value.T for new in updated for value in new]
         return (assemble(back_student), assemble(back_fake), *new_states, *params)

time: 308 us -> 260 us (0.84); the launches traced: 304 us -> 259 us
  waiting for transfers between devices: 147 us -> 99.6 us
  matrix products: 29.6 us -> 23.8 us
  local copies, waits for them, and re-layouts: 15.4 us -> 20.2 us
    ppermute x10 -> x0, waiting for transfers between devices: 26 us -> none  [butterfly(): value = combine(value, lax.ppermute(value, axis, perm))]
    ppermute x30 -> x44, waiting for transfers between devices: 100 us -> 89.7 us  [move_dp(): return lax.ppermute(value, 'dp', perm)]
    ppermute x7 -> x10, waiting for transfers between devices: 20.4 us -> 9.88 us  [from_tensor(): return lax.ppermute(value, 'tensor', perm)]
    ppermute x10 -> x0, starting transfers between devices: 8.43 us -> none  [butterfly(): value = combine(value, lax.ppermute(value, axis, perm))]
    ppermute x30 -> x44, starting transfers between devices: 36.4 us -> 44.5 us  [move_dp(): return lax.ppermute(value, 'dp', perm)]
    dot_general x23 -> x25, matrix products: 29.6 us -> 23.8 us  [dot(): return lax.dot_general(a, b, dims, preferred_element_type=jnp.float32)]
    unnamed x90 -> x73, local copies, waits for them, and re-layouts: 5.81 us -> 9.61 us
    reduce_max x2 -> x0, other arithmetic: 3.7 us -> none  [bound(): jnp.max(jnp.abs(cot)).astype(jnp.float32)]
  transfers between devices with their start and end apart: 47 -> 54, of which waited for: 23 -> 26; matrix products, arithmetic and copies ran while one was open for 16% -> 20% of each run, Pallas kernels for 6% -> 1%
where the time goes in v3:
time: 260 us; the launch traced here: 259 us
  waiting for transfers between devices  99.6 us (38%)
  starting transfers between devices  56.9 us (22%)
  other arithmetic  33 us (13%)
  matrix products  23.8 us (9%)
  local copies, waits for them, and re-layouts  20.2 us (8%)
  Pallas kernels  17.4 us (7%)
  between operations  8.32 us (3%)
    ppermute x44, waiting for transfers between devices, move_dp(): return lax.ppermute(value, 'dp', perm)  89.7 us
    ppermute x44, starting transfers between devices, move_dp(): return lax.ppermute(value, 'dp', perm)  44.5 us
    dot_general x25, matrix products, dot(): return lax.dot_general(a, b, dims, preferred_element_type=jnp.float32)  23.8 us
    ppermute x10, starting transfers between devices, from_tensor(): return lax.ppermute(value, 'tensor', perm)  12.4 us
    ppermute x10, waiting for transfers between devices, from_tensor(): return lax.ppermute(value, 'tensor', perm)  9.88 us
    unnamed x73, local copies, waits for them, and re-layouts  9.61 us
    pallas_call x2, Pallas kernels, spread(): pl.pallas_call(kernel, out_shape=jax.ShapeDtypeStruct((f, D), jnp.bfloat1...  8.62 us
    convert_element_type x7, other arithmetic, shrink(): return (value * fit[net]).astype(jnp.float16)  7.2 us
  transfers between devices with their start and end apart: 54, of which 26 were waited for; matrix products, arithmetic and copies ran while one was open for 20% of the time, Pallas kernels for 1%

profile of v3, /device:TPU:0, one launch (start us, length us, event | category | flops | bytes accessed | tf_op | source)
XLA Modules:
  0.0 259.2 jit_solution(15183182203141895438)
XLA Ops:
  4.1 1.9 constant_dynamic-slice_fusion.7
  8.0 3.2 %shard_map.204 = (bf16[2,2,152,512]{3,2,1,0:T(8,128)(2,1)S(1)}, bf16[2,2,152,512]{3,2,1,0:T(8,128)(2,1)S(1)}, bf16[2,2,152,512]{3,2,1,0:T(8,128)(2,1)S(1)}, bf16...) custom-call(s32[3]{0:T(128)S(1)} %pad_add_fusion.place_ref, bf16[512,2432]{1,0:T(8,128)(2,1)S(1)} %copy-done.11), custom_call_target="tpu_custom_call" | custom-call | flops 637534208 | bytes 4980736 | tf_op jit(solution)/shard_map/pallas_call | solution.py:133
  14.5 2.9 %shard_map.205 = (bf16[2,4,152,512]{3,2,1,0:T(8,128)(2,1)S(1)}, bf16[2,4,152,512]{3,2,1,0:T(8,128)(2,1)S(1)}, f32[8,128]{1,0:T(8,128)S(1)}) custom-call(s32[3]{0:T(128)S(1)} %pad_add_fusion.place_ref, bf16[512,2432]{1,0:T(8,128)(2,1)S(1)} %copy-done.6), custom_call_target="tpu_custom_call" | custom-call | flops 637534208 | bytes 4980736 | tf_op jit(solution)/shard_map/pallas_call | solution.py:133
  26.8 2.6 %fusion.58 = f32[1216,608]{1,0:T(8,128)S(1)} fusion(bf16[1216,512]{1,0:T(8,128)(2,1)} %bitcast.192, bf16[608,512]{1,0:T(8,128)(2,1)S(1)} %multiply_convert_fusion.3), kind=kOutput, calls=%fused_computation.155 | convolution fusion | flops 757071872 | bytes 4825088 | tf_op jit(solution)/shard_map/dot_general | solution.py:45
  29.9 2.6 %collective-permute-start = (f32[8,128]{0,1:T(8,128)S(1)}, f32[8,128]{0,1:T(8,128)S(1)}, u32[]{:S(2)}, u32[]{:S(2)}) collective-permute-start(f32[8,128]{0,1:T(8,128)S(1)} %iota.24), channel_id=1, source_target_pairs={{0,8},{2,10},{4,12},{6,14},{8,16},{10,18},{12,20},{14,22},{16,24},... | collective-permute-start | bytes 12296 | tf_op jit(solution)/shard_map/ppermute | solution.py:75
  32.5 2.6 collective-permute-start.1
  38.0 2.2 collective-permute-done.1
  48.1 3.9 %collective-permute-done.3 = bf16[608,512]{1,0:T(8,128)(2,1)S(1)} collective-permute-done((bf16[608,512]{1,0:T(8,128)(2,1)S(1)}, bf16[608,512]{1,0:T(8,128)(2,1)S(1)}, u32[]{:S(2)}, u32[]{:S(2)}) %collective-permute-start.3) | collective-permute-done | bytes 622624 | tf_op jit(solution)/shard_map/ppermute | solution.py:88
  63.0 3.7 %collective-permute-done.10 = f16[2,152,608]{2,1,0:T(8,128)(2,1)S(1)} collective-permute-done((f16[2,152,608]{2,1,0:T(8,128)(2,1)S(1)}, f16[2,152,608]{2,1,0:T(8,128)(2,1)S(1)}, u32[]{:S(2)}, u32[]{:S(2)}) %collective-permute-start.10) | collective-permute-done | bytes 369696 | tf_op jit(solution)/shard_map/ppermute | solution.py:75
  75.4 7.8 %collective-permute-done.17 = f16[2,152,608]{2,1,0:T(8,128)(2,1)S(1)} collective-permute-done((f16[2,152,608]{2,1,0:T(8,128)(2,1)S(1)}, f16[2,152,608]{2,1,0:T(8,128)(2,1)S(1)}, u32[]{:S(2)}, u32[]{:S(2)}) %collective-permute-start.17) | collective-permute-done | bytes 369696 | tf_op jit(solution)/shard_map/ppermute | solution.py:75
  84.6 2.3 collective-permute-done.16.refs_1_
  92.5 7.8 %collective-permute-done.15 = f16[2,152,608]{2,1,0:T(8,128)(2,1)S(1)} collective-permute-done((f16[2,152,608]{2,1,0:T(8,128)(2,1)S(1)}, f16[2,152,608]{2,1,0:T(8,128)(2,1)S(1)}, u32[]{:S(2)}, u32[]{:S(2)}) %collective-permute-start.15) | collective-permute-done | bytes 369696 | tf_op jit(solution)/shard_map/ppermute | solution.py:75
  101.7 2.3 collective-permute-done.14.refs_2_
  112.3 6.3 %collective-permute-done.13 = f16[2,152,608]{2,1,0:T(8,128)(2,1)S(1)} collective-permute-done((f16[2,152,608]{2,1,0:T(8,128)(2,1)S(1)}, f16[2,152,608]{2,1,0:T(8,128)(2,1)S(1)}, u32[]{:S(2)}, u32[]{:S(2)}) %collective-permute-start.13) | collective-permute-done | bytes 369696 | tf_op jit(solution)/shard_map/ppermute | solution.py:75
  124.7 2.3 collective-permute-start.22
  129.1 3.2 %collective-permute-done.22 = f16[152,608]{1,0:T(8,128)(2,1)S(1)} collective-permute-done((f16[152,608]{1,0:T(8,128)(2,1)S(1)}, f16[152,608]{1,0:T(8,128)(2,1)S(1)}, u32[]{:S(2)}, u32[]{:S(2)}) %collective-permute-start.22) | collective-permute-done | bytes 184864 | tf_op jit(solution)/shard_map/ppermute | solution.py:75
  132.3 11.3 %collective-permute-done.23 = f16[152,608]{1,0:T(8,128)(2,1)S(1)} collective-permute-done((f16[152,608]{1,0:T(8,128)(2,1)S(1)}, f16[152,608]{1,0:T(8,128)(2,1)S(1)}, u32[]{:S(2)}, u32[]{:S(2)}) %collective-permute-start.23) | collective-permute-done | bytes 184864 | tf_op jit(solution)/shard_map/ppermute | solution.py:75
  151.1 3.5 %collective-permute-done.29 = f16[152,608]{1,0:T(8,128)(2,1)S(1)} collective-permute-done((f16[152,608]{1,0:T(8,128)(2,1)S(1)}, f16[152,608]{1,0:T(8,128)(2,1)S(1)}, u32[]{:S(2)}, u32[]{:S(2)}) %collective-permute-start.29) | collective-permute-done | bytes 184864 | tf_op jit(solution)/shard_map/ppermute | solution.py:75
  159.6 8.3 %collective-permute-done.31 = f16[152,608]{1,0:T(8,128)(2,1)S(1)} collective-permute-done((f16[152,608]{1,0:T(8,128)(2,1)S(1)}, f16[152,608]{1,0:T(8,128)(2,1)S(1)}, u32[]{:S(2)}, u32[]{:S(2)}) %collective-permute-start.31) | collective-permute-done | bytes 184864 | tf_op jit(solution)/shard_map/ppermute | solution.py:75
  172.2 2.3 collective-permute-start.36
  191.0 3.3 %collective-permute-start.42 = (bf16[2,152,608]{2,1,0:T(8,128)(2,1)S(1)}, bf16[2,152,608]{2,1,0:T(8,128)(2,1)S(1)}, u32[]{:S(2)}, u32[]{:S(2)}) collective-permute-start(bf16[2,152,608]{2,1,0:T(8,128)(2,1)S(1)} %pad_maximum_fusion.2), channel_id=1, source_target_pairs={{0,24},{2,26},{4,28},{6,30},{8,0},{10,2},{12,4},{14,6},{16,8},{18,... | collective-permute-start | bytes 1109000 | tf_op jit(solution)/shard_map/ppermute | solution.py:75
  195.7 2.6 %fusion = bf16[608,512]{1,0:T(8,128)(2,1)} fusion(bf16[608,2432]{1,0:T(8,128)(2,1)S(1)} %copy-done.8, bf16[512,2432]{1,0:T(8,128)(2,1)S(1)} %copy-done.12, f32[512]{0:T(512)S(1)} %bitcast.225), kind=kOutput, calls=%fused_computation.8 | convolution fusion | flops 1514766336 | bytes 6072320 | tf_op jit(solution)/shard_map/dot_general | solution.py:45
  198.3 5.5 %collective-permute-done.42 = bf16[2,152,608]{2,1,0:T(8,128)(2,1)S(1)} collective-permute-done((bf16[2,152,608]{2,1,0:T(8,128)(2,1)S(1)}, bf16[2,152,608]{2,1,0:T(8,128)(2,1)S(1)}, u32[]{:S(2)}, u32[]{:S(2)}) %collective-permute-start.42) | collective-permute-done | bytes 369696 | tf_op jit(solution)/shard_map/ppermute | solution.py:75
  204.8 2.7 %shard_map.206 = bf16[608,512]{1,0:T(8,128)(2,1)S(1)} custom-call(s32[3]{0:T(128)S(1)} %pad_add_fusion.place_ref, bf16[608,2432]{1,0:T(8,128)(2,1)S(1)} %copy-done.8, bf16[2,2,152,512]{3,2,1,0:T(8,128)(2,1)S(1)} %collective-permute-done.30.refs_0_, bf16[2,2,152,512]{3,2,1,0:T(8,128)(2,1)S(1)} %collective-permute-done.16.refs_1_, ...), custom_call_target="tpu_custom_call" | custom-call | flops 1514143744 | bytes 6070272 | tf_op jit(solution)/shard_map/pallas_call | solution.py:166
  207.5 5.2 %collective-permute-done.43 = bf16[2,152,608]{2,1,0:T(8,128)(2,1)S(1)} collective-permute-done((bf16[2,152,608]{2,1,0:T(8,128)(2,1)S(1)}, bf16[2,152,608]{2,1,0:T(8,128)(2,1)S(1)}, u32[]{:S(2)}, u32[]{:S(2)}) %collective-permute-start.43) | collective-permute-done | bytes 369696 | tf_op jit(solution)/shard_map/ppermute | solution.py:75
  214.0 2.8 %constant_dynamic-update-slice_fusion.7 = (bf16[608,2048]{1,0:T(8,128)(2,1)}, bf16[608,512]{1,0:T(8,128)(2,1)}) fusion(f32[512]{0:T(512)S(1)} %bitcast.223, bf16[608,2432]{1,0:T(8,128)(2,1)S(1)} %copy-done, bf16[512,2432]{1,0:T(8,128)(2,1)S(1)} %copy-done.7), kind=kOutput, calls=%fused_computation.110 | convolution fusion | flops 1514766336 | bytes 6694912 | tf_op jit(solution)/shard_map/dot_general | solution.py:45
  217.6 7.1 %collective-permute-done.48 = bf16[2,152,608]{2,1,0:T(8,128)(2,1)S(1)} collective-permute-done((bf16[2,152,608]{2,1,0:T(8,128)(2,1)S(1)}, bf16[2,152,608]{2,1,0:T(8,128)(2,1)S(1)}, u32[]{:S(2)}, u32[]{:S(2)}) %collective-permute-start.48) | collective-permute-done | bytes 369696 | tf_op jit(solution)/shard_map/ppermute | solution.py:75
  230.7 8.2 %collective-permute-done.50 = bf16[2,152,608]{2,1,0:T(8,128)(2,1)} collective-permute-done((bf16[2,152,608]{2,1,0:T(8,128)(2,1)}, bf16[2,152,608]{2,1,0:T(8,128)(2,1)}, u32[]{:S(2)}, u32[]{:S(2)}) %collective-permute-start.50) | collective-permute-done | bytes 369696 | tf_op jit(solution)/shard_map/ppermute | solution.py:75
  240.6 2.1 constant_dynamic-update-slice_fusion.6
  244.7 2.3 constant_dynamic-update-slice_fusion.5
  250.6 4.3 %shard_map.207 = bf16[608,2432]{1,0:T(8,128)(2,1)} custom-call(s32[3]{0:T(128)S(1)} %pad_add_fusion.place_ref, bf16[4,2,152,608]{3,2,1,0:T(8,128)(2,1)S(1)} %copy-done.1, bf16[4,2,152,608]{3,2,1,0:T(8,128)(2,1)S(1)} %copy-done.1, bf16[4,2,152,608]{3,2,1,0:T(8,128)(2,1)S(1)} %copy-done.1, bf16[4,2,152,608]{3,2,1,0:T(8,128)(2,1)S(1)} %copy-done.1, ...), custom_call_target="tpu_custom_call" | custom-call | flops 757071872 | bytes 5914624 | tf_op jit(solution)/shard_map/pallas_call | solution.py:205
  254.9 4.3 %shard_map.208 = bf16[608,2432]{1,0:T(8,128)(2,1)} custom-call(s32[3]{0:T(128)S(1)} %pad_add_fusion.place_ref, bf16[4,2,152,608]{3,2,1,0:T(8,128)(2,1)S(1)} %copy-done.1, bf16[4,2,152,608]{3,2,1,0:T(8,128)(2,1)S(1)} %copy-done.1, bf16[4,2,152,608]{3,2,1,0:T(8,128)(2,1)S(1)} %copy-done.1, bf16[4,2,152,608]{3,2,1,0:T(8,128)(2,1)S(1)} %copy-done.1, ...), custom_call_target="tpu_custom_call" | custom-call | flops 757071872 | bytes 5914624 | tf_op jit(solution)/shard_map/pallas_call | solution.py:205
  (269 shorter events, 117.3 us)
Async XLA Ops:
  29.4 17.4 %collective-permute-start.4 = (f32[1216,608]{1,0:T(8,128)S(1)}, f32[1216,608]{1,0:T(8,128)S(1)}, u32[]{:S(2)}, u32[]{:S(2)}) collective-permute-start(f32[1216,608]{1,0:T(8,128)S(1)} %fusion.58), channel_id=1, source_target_pairs={{0,2},{2,0},{4,6},{6,4},{8,10},{10,8},{12,14},{14,12},{16,18},{18,... | collective-permute-start | bytes 8871944 | tf_op jit(solution)/shard_map/ppermute | solution.py:75
  36.5 15.5 %collective-permute-start.3 = (bf16[608,512]{1,0:T(8,128)(2,1)S(1)}, bf16[608,512]{1,0:T(8,128)(2,1)S(1)}, u32[]{:S(2)}, u32[]{:S(2)}) collective-permute-start(bf16[608,512]{1,0:T(8,128)(2,1)S(1)} %copy-done.25), channel_id=1, source_target_pairs={{0,1},{1,0},{2,3},{3,2},{4,5},{5,4},{6,7},{7,6},{8,9},{9,8},{10,11... | collective-permute-start | bytes 1867784 | tf_op jit(solution)/shard_map/ppermute | solution.py:88
  53.4 16.4 %collective-permute-start.9 = (bf16[2,2,152,512]{3,2,1,0:T(8,128)(2,1)S(1)}, bf16[2,2,152,512]{3,2,1,0:T(8,128)(2,1)S(1)}, u32[]{:S(2)}, u32[]{:S(2)}) collective-permute-start(bf16[2,2,152,512]{3,2,1,0:T(8,128)(2,1)S(1)} %copy-done.20), channel_id=1, source_target_pairs={{0,1},{1,0},{2,3},{3,2},{4,5},{5,4},{6,7},{7,6},{8,9},{9,8},{10,11... | collective-permute-start | bytes 1867784 | tf_op jit(solution)/shard_map/ppermute | solution.py:88
  55.6 11.1 %collective-permute-start.10 = (f16[2,152,608]{2,1,0:T(8,128)(2,1)S(1)}, f16[2,152,608]{2,1,0:T(8,128)(2,1)S(1)}, u32[]{:S(2)}, u32[]{:S(2)}) collective-permute-start(f16[2,152,608]{2,1,0:T(8,128)(2,1)S(1)} %get-tuple-element.313), channel_id=1, source_target_pairs={{0,4},{2,6},{4,0},{6,2},{8,12},{10,14},{12,8},{14,10},{16,20},{18,... | collective-permute-start | bytes 1109000 | tf_op jit(solution)/shard_map/ppermute | solution.py:75
  70.5 16.4 %collective-permute-start.16 = (bf16[2,2,152,512]{3,2,1,0:T(8,128)(2,1)S(1)}, bf16[2,2,152,512]{3,2,1,0:T(8,128)(2,1)S(1)}, u32[]{:S(2)}, u32[]{:S(2)}) collective-permute-start(bf16[2,2,152,512]{3,2,1,0:T(8,128)(2,1)S(1)} %copy-done.18), channel_id=1, source_target_pairs={{0,1},{1,0},{2,3},{3,2},{4,5},{5,4},{6,7},{7,6},{8,9},{9,8},{10,11... | collective-permute-start | bytes 1867784 | tf_op jit(solution)/shard_map/ppermute | solution.py:88
  72.1 11.1 %collective-permute-start.17 = (f16[2,152,608]{2,1,0:T(8,128)(2,1)S(1)}, f16[2,152,608]{2,1,0:T(8,128)(2,1)S(1)}, u32[]{:S(2)}, u32[]{:S(2)}) collective-permute-start(f16[2,152,608]{2,1,0:T(8,128)(2,1)S(1)} %get-tuple-element.310), channel_id=1, source_target_pairs={{0,4},{2,6},{4,0},{6,2},{8,12},{10,14},{12,8},{14,10},{16,20},{18,... | collective-permute-start | bytes 1109000 | tf_op jit(solution)/shard_map/ppermute | solution.py:75
  87.6 16.4 %collective-permute-start.14 = (bf16[2,2,152,512]{3,2,1,0:T(8,128)(2,1)S(1)}, bf16[2,2,152,512]{3,2,1,0:T(8,128)(2,1)S(1)}, u32[]{:S(2)}, u32[]{:S(2)}) collective-permute-start(bf16[2,2,152,512]{3,2,1,0:T(8,128)(2,1)S(1)} %copy-done.16), channel_id=1, source_target_pairs={{0,1},{1,0},{2,3},{3,2},{4,5},{5,4},{6,7},{7,6},{8,9},{9,8},{10,11... | collective-permute-start | bytes 1867784 | tf_op jit(solution)/shard_map/ppermute | solution.py:88
  89.2 11.1 %collective-permute-start.15 = (f16[2,152,608]{2,1,0:T(8,128)(2,1)S(1)}, f16[2,152,608]{2,1,0:T(8,128)(2,1)S(1)}, u32[]{:S(2)}, u32[]{:S(2)}) collective-permute-start(f16[2,152,608]{2,1,0:T(8,128)(2,1)S(1)} %get-tuple-element.317), channel_id=1, source_target_pairs={{0,4},{2,6},{4,0},{6,2},{8,12},{10,14},{12,8},{14,10},{16,20},{18,... | collective-permute-start | bytes 1109000 | tf_op jit(solution)/shard_map/ppermute | solution.py:75
  104.7 42.1 %collective-permute-start.30 = (bf16[2,2,152,512]{3,2,1,0:T(8,128)(2,1)S(1)}, bf16[2,2,152,512]{3,2,1,0:T(8,128)(2,1)S(1)}, u32[]{:S(2)}, u32[]{:S(2)}) collective-permute-start(bf16[2,2,152,512]{3,2,1,0:T(8,128)(2,1)S(1)} %copy-done.14), channel_id=1, source_target_pairs={{0,1},{1,0},{2,3},{3,2},{4,5},{5,4},{6,7},{7,6},{8,9},{9,8},{10,11... | collective-permute-start | bytes 1867784 | tf_op jit(solution)/shard_map/ppermute | solution.py:88
  106.2 18.5 %collective-permute-start.25 = (f16[152,608]{1,0:T(8,128)(2,1)S(1)}, f16[152,608]{1,0:T(8,128)(2,1)S(1)}, u32[]{:S(2)}, u32[]{:S(2)}) collective-permute-start(f16[152,608]{1,0:T(8,128)(2,1)S(1)} %get-tuple-element.329), channel_id=1, source_target_pairs={{0,24},{2,26},{4,28},{6,30},{8,0},{10,2},{12,4},{14,6},{16,8},{18,... | collective-permute-start | bytes 554504 | tf_op jit(solution)/shard_map/ppermute | solution.py:75
  106.7 11.9 %collective-permute-start.13 = (f16[2,152,608]{2,1,0:T(8,128)(2,1)S(1)}, f16[2,152,608]{2,1,0:T(8,128)(2,1)S(1)}, u32[]{:S(2)}, u32[]{:S(2)}) collective-permute-start(f16[2,152,608]{2,1,0:T(8,128)(2,1)S(1)} %get-tuple-element.315), channel_id=1, source_target_pairs={{0,4},{2,6},{4,0},{6,2},{8,12},{10,14},{12,8},{14,10},{16,20},{18,... | collective-permute-start | bytes 1109000 | tf_op jit(solution)/shard_map/ppermute | solution.py:75
  108.2 18.8 %collective-permute-start.26 = (f16[152,608]{1,0:T(8,128)(2,1)S(1)}, f16[152,608]{1,0:T(8,128)(2,1)S(1)}, u32[]{:S(2)}, u32[]{:S(2)}) collective-permute-start(f16[152,608]{1,0:T(8,128)(2,1)S(1)} %get-tuple-element.328), channel_id=1, source_target_pairs={{0,16},{2,18},{4,20},{6,22},{8,24},{10,26},{12,28},{14,30},{16,0},... | collective-permute-start | bytes 554504 | tf_op jit(solution)/shard_map/ppermute | solution.py:75
  110.9 10.9 %collective-permute-start.12 = (f16[152,608]{1,0:T(8,128)(2,1)S(1)}, f16[152,608]{1,0:T(8,128)(2,1)S(1)}, u32[]{:S(2)}, u32[]{:S(2)}) collective-permute-start(f16[152,608]{1,0:T(8,128)(2,1)S(1)} %get-tuple-element.336), channel_id=1, source_target_pairs={{0,4},{2,6},{4,0},{6,2},{8,12},{10,14},{12,8},{14,10},{16,20},{18,... | collective-permute-start | bytes 554504 | tf_op jit(solution)/shard_map/ppermute | solution.py:75
  121.8 23.6 %collective-permute-start.21 = (f16[152,608]{1,0:T(8,128)(2,1)S(1)}, f16[152,608]{1,0:T(8,128)(2,1)S(1)}, u32[]{:S(2)}, u32[]{:S(2)}) collective-permute-start(f16[152,608]{1,0:T(8,128)(2,1)S(1)} %get-tuple-element.335), channel_id=1, source_target_pairs={{0,4},{2,6},{4,0},{6,2},{8,12},{10,14},{12,8},{14,10},{16,20},{18,... | collective-permute-start | bytes 554504 | tf_op jit(solution)/shard_map/ppermute | solution.py:75
  127.0 16.6 %collective-permute-start.23 = (f16[152,608]{1,0:T(8,128)(2,1)S(1)}, f16[152,608]{1,0:T(8,128)(2,1)S(1)}, u32[]{:S(2)}, u32[]{:S(2)}) collective-permute-start(f16[152,608]{1,0:T(8,128)(2,1)S(1)} %get-tuple-element.332), channel_id=1, source_target_pairs={{0,16},{2,18},{4,20},{6,22},{8,24},{10,26},{12,28},{14,30},{16,0},... | collective-permute-start | bytes 554504 | tf_op jit(solution)/shard_map/ppermute | solution.py:75
  127.7 16.0 %collective-permute-start.24 = (f16[152,608]{1,0:T(8,128)(2,1)S(1)}, f16[152,608]{1,0:T(8,128)(2,1)S(1)}, u32[]{:S(2)}, u32[]{:S(2)}) collective-permute-start(f16[152,608]{1,0:T(8,128)(2,1)S(1)} %get-tuple-element.331), channel_id=1, source_target_pairs={{0,8},{2,10},{4,12},{6,14},{8,16},{10,18},{12,20},{14,22},{16,24},... | collective-permute-start | bytes 554504 | tf_op jit(solution)/shard_map/ppermute | solution.py:75
  147.4 11.4 %collective-permute-start.20 = (f16[152,608]{1,0:T(8,128)(2,1)S(1)}, f16[152,608]{1,0:T(8,128)(2,1)S(1)}, u32[]{:S(2)}, u32[]{:S(2)}) collective-permute-start(f16[152,608]{1,0:T(8,128)(2,1)S(1)} %multiply_convert_fusion.6), channel_id=1, source_target_pairs={{0,24},{2,26},{4,28},{6,30},{8,0},{10,2},{12,4},{14,6},{16,8},{18,... | collective-permute-start | bytes 554504 | tf_op jit(solution)/shard_map/ppermute | solution.py:75
  148.1 11.5 %collective-permute-start.28 = (f16[152,608]{1,0:T(8,128)(2,1)S(1)}, f16[152,608]{1,0:T(8,128)(2,1)S(1)}, u32[]{:S(2)}, u32[]{:S(2)}) collective-permute-start(f16[152,608]{1,0:T(8,128)(2,1)S(1)} %multiply_convert_fusion.5), channel_id=1, source_target_pairs={{0,8},{2,10},{4,12},{6,14},{8,16},{10,18},{12,20},{14,22},{16,24},... | collective-permute-start | bytes 554504 | tf_op jit(solution)/shard_map/ppermute | solution.py:75
  150.0 18.6 %collective-permute-start.34 = (f32[152,608]{1,0:T(8,128)S(1)}, f32[152,608]{1,0:T(8,128)S(1)}, u32[]{:S(2)}, u32[]{:S(2)}) collective-permute-start(f32[152,608]{1,0:T(8,128)S(1)} %multiply_add_fusion.5), channel_id=1, source_target_pairs={{0,1},{1,0},{2,3},{3,2},{4,5},{5,4},{6,7},{7,6},{8,9},{9,8},{10,11... | collective-permute-start | bytes 1109000 | tf_op jit(solution)/shard_map/ppermute | solution.py:88
  156.0 11.9 %collective-permute-start.31 = (f16[152,608]{1,0:T(8,128)(2,1)S(1)}, f16[152,608]{1,0:T(8,128)(2,1)S(1)}, u32[]{:S(2)}, u32[]{:S(2)}) collective-permute-start(f16[152,608]{1,0:T(8,128)(2,1)S(1)} %multiply_convert_fusion.4), channel_id=1, source_target_pairs={{0,16},{2,18},{4,20},{6,22},{8,24},{10,26},{12,28},{14,30},{16,0},... | collective-permute-start | bytes 554504 | tf_op jit(solution)/shard_map/ppermute | solution.py:75
  158.2 11.2 %collective-permute-start.33 = (f16[152,608]{1,0:T(8,128)(2,1)S(1)}, f16[152,608]{1,0:T(8,128)(2,1)S(1)}, u32[]{:S(2)}, u32[]{:S(2)}) collective-permute-start(f16[152,608]{1,0:T(8,128)(2,1)S(1)} %get-tuple-element.323), channel_id=1, source_target_pairs={{0,4},{2,6},{4,0},{6,2},{8,12},{10,14},{12,8},{14,10},{16,20},{18,... | collective-permute-start | bytes 554504 | tf_op jit(solution)/shard_map/ppermute | solution.py:75
  182.5 58.1 %collective-permute-start.44 = (bf16[128,2432]{1,0:T(8,128)(2,1)}, bf16[128,2432]{1,0:T(8,128)(2,1)}, u32[]{:S(2)}, u32[]{:S(2)}) collective-permute-start(bf16[128,2432]{1,0:T(8,128)(2,1)} %slice.260), channel_id=1, source_target_pairs={{0,1},{1,0},{2,3},{3,2},{4,5},{5,4},{6,7},{7,6},{8,9},{9,8},{10,11... | collective-permute-start | bytes 1867784 | tf_op jit(solution)/shard_map/ppermute | solution.py:88
  185.1 59.5 %collective-permute-start.45 = (bf16[256,2432]{1,0:T(8,128)(2,1)}, bf16[256,2432]{1,0:T(8,128)(2,1)}, u32[]{:S(2)}, u32[]{:S(2)}) collective-permute-start(bf16[256,2432]{1,0:T(8,128)(2,1)} %slice.267), channel_id=1, source_target_pairs={{0,1},{1,0},{2,3},{3,2},{4,5},{5,4},{6,7},{7,6},{8,9},{9,8},{10,11... | collective-permute-start | bytes 3735560 | tf_op jit(solution)/shard_map/ppermute | solution.py:88
  191.0 12.8 %collective-permute-start.42 = (bf16[2,152,608]{2,1,0:T(8,128)(2,1)S(1)}, bf16[2,152,608]{2,1,0:T(8,128)(2,1)S(1)}, u32[]{:S(2)}, u32[]{:S(2)}) collective-permute-start(bf16[2,152,608]{2,1,0:T(8,128)(2,1)S(1)} %pad_maximum_fusion.2), channel_id=1, source_target_pairs={{0,24},{2,26},{4,28},{6,30},{8,0},{10,2},{12,4},{14,6},{16,8},{18,... | collective-permute-start | bytes 1109000 | tf_op jit(solution)/shard_map/ppermute | solution.py:75
  194.3 18.4 %collective-permute-start.43 = (bf16[2,152,608]{2,1,0:T(8,128)(2,1)S(1)}, bf16[2,152,608]{2,1,0:T(8,128)(2,1)S(1)}, u32[]{:S(2)}, u32[]{:S(2)}) collective-permute-start(bf16[2,152,608]{2,1,0:T(8,128)(2,1)S(1)} %pad_maximum_fusion.2), channel_id=1, source_target_pairs={{0,8},{2,10},{4,12},{6,14},{8,16},{10,18},{12,20},{14,22},{16,24},... | collective-permute-start | bytes 1109000 | tf_op jit(solution)/shard_map/ppermute | solution.py:75
  194.3 22.6 %collective-permute-start.47 = (bf16[2,152,608]{2,1,0:T(8,128)(2,1)S(1)}, bf16[2,152,608]{2,1,0:T(8,128)(2,1)S(1)}, u32[]{:S(2)}, u32[]{:S(2)}) collective-permute-start(bf16[2,152,608]{2,1,0:T(8,128)(2,1)S(1)} %pad_maximum_fusion.2), channel_id=1, source_target_pairs={{0,4},{2,6},{4,0},{6,2},{8,12},{10,14},{12,8},{14,10},{16,20},{18,... | collective-permute-start | bytes 1109000 | tf_op jit(solution)/shard_map/ppermute | solution.py:75
  203.8 24.0 %collective-permute-start.49 = (bf16[2,152,608]{2,1,0:T(8,128)(2,1)S(1)}, bf16[2,152,608]{2,1,0:T(8,128)(2,1)}, u32[]{:S(2)}, u32[]{:S(2)}) collective-permute-start(bf16[2,152,608]{2,1,0:T(8,128)(2,1)S(1)} %pad_maximum_fusion.2), channel_id=1, source_target_pairs={{0,16},{2,18},{4,20},{6,22},{8,24},{10,26},{12,28},{14,30},{16,0},... | collective-permute-start | bytes 1109000 | tf_op jit(solution)/shard_map/ppermute | solution.py:75
  212.7 12.0 %collective-permute-start.48 = (bf16[2,152,608]{2,1,0:T(8,128)(2,1)S(1)}, bf16[2,152,608]{2,1,0:T(8,128)(2,1)S(1)}, u32[]{:S(2)}, u32[]{:S(2)}) collective-permute-start(bf16[2,152,608]{2,1,0:T(8,128)(2,1)S(1)} %collective-permute-done.42), channel_id=1, source_target_pairs={{0,4},{2,6},{4,0},{6,2},{8,12},{10,14},{12,8},{14,10},{16,20},{18,... | collective-permute-start | bytes 1109000 | tf_op jit(solution)/shard_map/ppermute | solution.py:75
  216.9 13.8 %collective-permute-start.51 = (bf16[2,152,608]{2,1,0:T(8,128)(2,1)S(1)}, bf16[2,152,608]{2,1,0:T(8,128)(2,1)}, u32[]{:S(2)}, u32[]{:S(2)}) collective-permute-start(bf16[2,152,608]{2,1,0:T(8,128)(2,1)S(1)} %collective-permute-done.43), channel_id=1, source_target_pairs={{0,4},{2,6},{4,0},{6,2},{8,12},{10,14},{12,8},{14,10},{16,20},{18,... | collective-permute-start | bytes 1109000 | tf_op jit(solution)/shard_map/ppermute | solution.py:75
  227.8 11.2 %collective-permute-start.50 = (bf16[2,152,608]{2,1,0:T(8,128)(2,1)}, bf16[2,152,608]{2,1,0:T(8,128)(2,1)}, u32[]{:S(2)}, u32[]{:S(2)}) collective-permute-start(bf16[2,152,608]{2,1,0:T(8,128)(2,1)} %collective-permute-done.49), channel_id=1, source_target_pairs={{0,4},{2,6},{4,0},{6,2},{8,12},{10,14},{12,8},{14,10},{16,20},{18,... | collective-permute-start | bytes 1109000 | tf_op jit(solution)/shard_map/ppermute | solution.py:75
  229.3 17.7 %collective-permute-start.46 = (bf16[128,2432]{1,0:T(8,128)(2,1)}, bf16[128,2432]{1,0:T(8,128)(2,1)S(1)}, u32[]{:S(2)}, u32[]{:S(2)}) collective-permute-start(bf16[128,2432]{1,0:T(8,128)(2,1)} %slice.268), channel_id=1, source_target_pairs={{0,1},{1,0},{2,3},{3,2},{4,5},{5,4},{6,7},{7,6},{8,9},{9,8},{10,11... | collective-permute-start | bytes 1867784 | tf_op jit(solution)/shard_map/ppermute | solution.py:88
  230.7 18.7 %collective-permute-start.52 = (bf16[4,2,152,608]{3,2,1,0:T(8,128)(2,1)}, bf16[4,2,152,608]{3,2,1,0:T(8,128)(2,1)S(1)}, u32[]{:S(2)}, u32[]{:S(2)}) collective-permute-start(bf16[4,2,152,608]{3,2,1,0:T(8,128)(2,1)} %pad_maximum_fusion.refs_0_.refs_1_.refs_2_.refs_3_), channel_id=1, source_target_pairs={{0,2},{2,0},{4,6},{6,4},{8,10},{10,8},{12,14},{14,12},{16,18},{18,... | collective-permute-start | bytes 4435976 | tf_op jit(solution)/shard_map/ppermute | solution.py:75
  (57 other events, 550.6 us)

commit v4 on v3

v4 whole, which is shorter than its diff:
```python
import functools

import jax
import jax.numpy as jnp
from jax import lax
from jax.experimental import pallas as pl
from jax.experimental.pallas import tpu as pltpu
from jax.sharding import PartitionSpec as P

D = 2432
F = 1216
ROWS = 1024


FIRST_CORRECTION = 0.9999734386011124
SECOND_CORRECTION = 0.0952078529183

OUTER = 4
HALF_LIMIT = 60000.0
TILE = 256
LANES = 128

NT = (((1,), (1,)), ((), ()))
NN = (((1,), (0,)), ((), ()))

SMEM = pl.BlockSpec(memory_space=pltpu.SMEM)
VMEM = pl.BlockSpec(memory_space=pltpu.VMEM)
ANY = pl.BlockSpec(memory_space=pl.ANY)


def adam_update(grad, squares, master, first, second):
    clip = jnp.minimum(1.0, jnp.sqrt(jnp.float32(D * F)) / jnp.sqrt(squares + 1e-06))
    clipped = grad * clip
    new_first = 0.9 * first + 0.1 * clipped
    new_second = 0.999 * second + 0.001 * clipped * clipped
    step_dir = new_first / FIRST_CORRECTION / (jnp.sqrt(new_second / SECOND_CORRECTION) + 1e-08)
    new_master = master * (1.0 - 0.01 * 0.01) - 0.01 * step_dir
    return (new_master, new_first, new_second)


def dot(a, b, dims):
    return lax.dot_general(a, b, dims, preferred_element_type=jnp.float32)


def identity(size):
    rows = lax.broadcasted_iota(jnp.int32, (size, size), 0)
    cols = lax.broadcasted_iota(jnp.int32, (size, size), 1)
    return jnp.where(rows == cols, 1.0, 0.0).astype(jnp.bfloat16)


def array(shape, dtype):
    return jax.ShapeDtypeStruct(shape, dtype)


def call(kernel, out_shape, *operands, mib=12, **kwargs):
    return pl.pallas_call(
        kernel,
        out_shape=out_shape,
        compiler_params=pltpu.CompilerParams(vmem_limit_bytes=mib * 1024 * 1024),
        cost_estimate=pl.CostEstimate(flops=0, bytes_accessed=0, transcendentals=0),
        **kwargs,
    )(*operands)


def solution(mesh):
    n_dp, n_tensor = mesh.shape["dp"], mesh.shape["tensor"]
    inner = n_dp // (2 * OUTER)
    width = D // n_dp

    def split(p):
        return (p >> inner.bit_length()) & (OUTER - 1), (p >> 1) & (inner - 1), p & 1

    def join(z, m, c):
        return (z * inner + m) * 2 + c

    def move_dp(value, where):
        perm = [(p, join(*where(*split(p)))) for p in range(n_dp)]
        return lax.ppermute(value, "dp", perm)

    def to_plane(value, k):
        return move_dp(value, lambda z, m, c: ((z + k) & (OUTER - 1), m, c))

    def to_middle(value, k):
        return move_dp(value, lambda z, m, c: (z, (m + k) & (inner - 1), c))

    def to_core(value):
        return move_dp(value, lambda z, m, c: (z, m, 1 - c))

    def from_tensor(value, k):
        perm = [(s, (s - k) & (n_tensor - 1)) for s in range(n_tensor)]
        return lax.ppermute(value, "tensor", perm)

    def my_place():
        return split(lax.axis_index("dp"))

    def relative(p):
        z, m, c = split(p)
        my_z, my_m, my_c = my_place()
        return (z - my_z) & (OUTER - 1), (m - my_m) & (inner - 1), c ^ my_c

    def owner(k, i, other):
        z, m, c = my_place()
        return join((z + k) & (OUTER - 1), (m + i) & (inner - 1), c ^ other)

    def first_row(j, r):
        start = ((lax.axis_index("tensor") + j) & (n_tensor - 1)) * r
        return pl.multiple_of(start, LANES)

    def cut_acts(act, r):
        count = n_tensor - 1

        def kernel(act_ref, *refs):
            out_refs, sem = refs[:-1], refs[-1]
            copies = [
                pltpu.make_async_copy(
                    act_ref.at[:, pl.ds(first_row(j + 1, r), r)], out_refs[j], sem.at[j]
                )
                for j in range(count)
            ]
            for copy in copies:
                copy.start()
            for copy in copies:
                copy.wait()

        return call(
            kernel,
            [array((act.shape[0], r), act.dtype)] * count,
            act,
            in_specs=[ANY],
            out_specs=[VMEM] * count,
            scratch_shapes=[pltpu.SemaphoreType.DMA((count,))],
        )

    def turn(cot, by_planes):
        r = cot.shape[0]
        step = min(r, TILE)
        count = OUTER if by_planes else 2
        lead = (2, inner) if by_planes else (inner, OUTER)

        def kernel(cot_ref, *refs):
            out_refs, (top_ref, wide_ref) = refs[:count], refs[count:]
            eye = identity(TILE)
            for start in range(0, D, TILE):
                size = min(TILE, D - start)
                wide_ref[start : start + size, :] = dot(
                    eye[:size, :size], cot_ref[:, start : start + size], NT
                )
            top = jnp.max(jnp.abs(wide_ref[...]).reshape(D // 8, 8, step), axis=0)
            top = jnp.broadcast_to(jnp.max(top), (8, LANES))

            @pl.when(pl.program_id(0) == 0)
            def _():
                top_ref[...] = top

            @pl.when(pl.program_id(0) > 0)
            def _():
                top_ref[...] = jnp.maximum(top_ref[...], top)

            for p in range(n_dp):
                k, i, other = relative(p)
                block = wide_ref[p * width : (p + 1) * width, :].astype(jnp.bfloat16)
                which, at = (k, (other, i)) if by_planes else (other, (i, k))
                for n in range(count):

                    @pl.when(which == n)
                    def _(n=n, at=at, block=block):
                        out_refs[n][at] = block

        *outs, top = call(
            kernel,
            [array((*lead, width, r), jnp.bfloat16)] * count + [array((8, LANES), jnp.float32)],
            cot,
            grid=(r // step,),
            in_specs=[pl.BlockSpec((step, D), lambda s: (s, 0))],
            out_specs=[pl.BlockSpec((*lead, width, step), lambda s: (0, 0, 0, s))] * count
            + [pl.BlockSpec((8, LANES), lambda s: (0, 0))],
            scratch_shapes=[pltpu.VMEM((D, step), jnp.float32)],
        )
        return outs, top

    def prepare(act_s, act_f, top_s, top_f, scales, r):
        f = act_s.shape[0]

        def kernel(scale_ref, act_s_ref, act_f_ref, top_s_ref, top_f_ref, *refs):
            bound_ref, fake_ref, *student_refs = refs
            bounds = []
            for net, act_ref, top_ref in ((0, act_s_ref, top_s_ref), (1, act_f_ref, top_f_ref)):
                top = jnp.max(jnp.abs(act_ref[...].astype(jnp.float32)))
                bounds.append(top_ref[...] * (top * scale_ref[net]))
            rows = lax.broadcasted_iota(jnp.int32, (8, LANES), 0)
            bound_ref[...] = jnp.where(rows == 0, *bounds)
            own = act_f_ref[:, pl.ds(first_row(0, r), r)].astype(jnp.float32)
            fake_ref[...] = (own * scale_ref[1]).astype(jnp.bfloat16)
            for j, out_ref in enumerate(student_refs):
                part = act_s_ref[:, pl.ds(first_row(j, r), r)].astype(jnp.float32)
                out_ref[...] = (part * scale_ref[0]).astype(jnp.bfloat16)

        return call(
            kernel,
            [array((8, LANES), jnp.float32)] + [array((f, r), jnp.bfloat16)] * (1 + n_tensor),
            scales, act_s, act_f, top_s, top_f,
            in_specs=[SMEM] + [VMEM] * 4,
            out_specs=[VMEM] * (2 + n_tensor),
            mib=16,
        )

    def multiply_rows(pieces, scaled):
        rows, r = pieces[0].shape
        f = scaled[0].shape[0]
        step = D // (2 * OUTER)
        count = len(pieces)

        def kernel(*refs):
            piece_refs, scaled_refs, out_ref = refs[:count], refs[count:-1], refs[-1]
            total = dot(piece_refs[0][...], scaled_refs[0][...], NT)
            for piece_ref, scaled_ref in zip(piece_refs[1:], scaled_refs[1:]):
                total = total + dot(piece_ref[...], scaled_ref[...], NT)
            out_ref[...] = total

        return call(
            kernel,
            array((rows, f), jnp.float32),
            *pieces, *scaled,
            grid=(rows // step,),
            in_specs=[pl.BlockSpec((step, r), lambda s: (s, 0))] * count
            + [pl.BlockSpec((f, r), lambda s: (0, 0))] * count,
            out_specs=pl.BlockSpec((step, f), lambda s: (s, 0)),
        )

    def multiply_half(other, pieces, scaled):
        _, _, _, r = pieces[0].shape
        f = scaled[0].shape[0]
        count = len(pieces)

        def kernel(*refs):
            piece_refs, scaled_refs, out_ref = refs[:count], refs[count:-1], refs[-1]
            for i in range(inner):
                total = dot(piece_refs[0][0, i], scaled_refs[0][...], NT)
                for piece_ref, scaled_ref in zip(piece_refs[1:], scaled_refs[1:]):
                    total = total + dot(piece_ref[0, i], scaled_ref[...], NT)
                out_ref[i] = total

        return call(
            kernel,
            array((inner, width, f), jnp.float32),
            *pieces, *scaled,
            grid=(1,),
            in_specs=[pl.BlockSpec((1, inner, width, r), lambda s: (other, 0, 0, 0))] * count
            + [pl.BlockSpec((f, r), lambda s: (0, 0))] * count,
            out_specs=pl.BlockSpec((inner, width, f), lambda s: (0, 0, 0)),
        )

    def scale_rows(act, scales):
        def kernel(scale_ref, act_ref, out_ref):
            out_ref[...] = (act_ref[...].astype(jnp.float32) * scale_ref[1]).astype(jnp.bfloat16)

        return call(
            kernel, array(act.shape, jnp.bfloat16), scales, act,
            in_specs=[SMEM, VMEM], out_specs=VMEM,
        )

    def norms(total_s, total_f):
        def kernel(s_ref, f_ref, out_ref):
            sums = [jnp.sum(ref[...] * ref[...]) for ref in (s_ref, f_ref)]
            rows = lax.broadcasted_iota(jnp.int32, (8, LANES), 0)
            out_ref[...] = jnp.where(rows == 0, *sums)

        return call(
            kernel, array((8, LANES), jnp.float32), total_s, total_f,
            in_specs=[VMEM] * 2, out_specs=VMEM,
        )

    def update(squares, totals, states):
        shape = totals[0].shape

        def kernel(squares_ref, *refs):
            total_refs, state_refs, (own_ref, *out_refs) = refs[:2], refs[2:8], refs[8:]
            for net in range(2):
                new = adam_update(
                    total_refs[net][...],
                    squares_ref[net : net + 1, :1],
                    *(ref[...] for ref in state_refs[3 * net : 3 * net + 3]),
                )
                own_ref[net] = new[0].astype(jnp.bfloat16)
                for ref, value in zip(out_refs[3 * net :], new):
                    ref[...] = value

        own, *new = call(
            kernel,
            [array((2, *shape), jnp.bfloat16)] + [array(shape, jnp.float32)] * 6,
            squares, *totals, *states,
            in_specs=[VMEM] * 9,
            out_specs=[VMEM] * 7,
        )
        return own, new

    def back_part(whole, weight, pieces, scales, net, j, low, size, r, count):
        f = weight.shape[0]
        turned = len(pieces) > 1

        def kernel(scale_ref, weight_ref, *refs):
            piece_refs = refs[: len(pieces)]
            if turned:
                out_ref, done_ref, sem, wide_ref = refs[-4:]
                for k in range(OUTER):
                    for other in range(2):
                        for i in range(inner):
                            block = piece_refs[k][other, i].astype(jnp.float32)
                            wide_ref[owner(k, i, other)] = block
                flat = wide_ref[...].reshape(D, size).astype(jnp.bfloat16)
                product = dot(weight_ref[...], flat, NN)
            else:
                out_ref, done_ref, sem = refs[-3:]
                product = dot(weight_ref[...], piece_refs[0][...], NT)
            done_ref[...] = (product * scale_ref[net]).astype(jnp.bfloat16)
            start = pl.multiple_of(first_row(j, r) + low, LANES)
            copy = pltpu.make_async_copy(done_ref, out_ref.at[:, pl.ds(start, size)], sem)
            copy.start()
            copy.wait()

        scratch = [pltpu.VMEM((f, size), jnp.bfloat16), pltpu.SemaphoreType.DMA]
        if turned:
            scratch.append(pltpu.VMEM((n_dp, width, size), jnp.float32))
        operands = [scales, weight, *pieces]
        in_specs = [SMEM] + [VMEM] * (len(operands) - 1)
        aliases = {}
        if whole is not None:
            aliases = {len(operands): 0}
            operands.append(whole)
            in_specs.append(ANY)
        return call(
            kernel, array((f, count), jnp.bfloat16), *operands,
            in_specs=in_specs, out_specs=ANY, scratch_shapes=scratch,
            input_output_aliases=aliases, mib=20,
        )

    def spread(stacks, net):
        count, _, _, f = stacks[0].shape

        def kernel(*refs):
            stack_refs, (out_ref, wide_ref) = refs[:4], refs[4:]
            lanes = lax.broadcasted_iota(jnp.int32, (width, LANES), 1)
            inside = lanes + pl.program_id(0) * LANES < f
            for n, ref in enumerate(stack_refs):
                for at in range(count):
                    k, i = divmod((n & 1) * count + at, inner)
                    block = jnp.where(inside, ref[at, 0].astype(jnp.float32), 0.0)
                    wide_ref[owner(k, i, n >> 1)] = block
            flat = wide_ref[...].reshape(D, LANES).astype(jnp.bfloat16)
            out_ref[...] = dot(identity(LANES), flat, NT).astype(jnp.bfloat16)

        return call(
            kernel, array((f, D), jnp.bfloat16), *stacks,
            grid=(pl.cdiv(f, LANES),),
            in_specs=[pl.BlockSpec((count, 1, width, LANES), lambda s: (0, net, 0, s))] * 4,
            out_specs=pl.BlockSpec((LANES, D), lambda s: (s, 0)),
            scratch_shapes=[pltpu.VMEM((n_dp, width, LANES), jnp.float32)],
        )

    def per_device(
        cot_student, cot_fake, act_student, act_fake, weight_student, weight_fake,
        master_student, first_student, second_student, master_fake, first_fake, second_fake,
        timesteps,
    ):
        f, count = act_student.shape
        r = cot_student.shape[0]
        assert timesteps.shape[2] == 1 and count == ROWS

        token = []

        def step(work, *inputs):
            if token:
                *inputs, _ = lax.optimization_barrier((*inputs, token[0]))
            out = work(*inputs)
            token[:] = jax.tree.leaves(out)[:1]
            return out

        def reduced(combine, value, got):
            return step(lambda *values: functools.reduce(combine, values), value, *got)

        def gather_planes(value):
            return [to_plane(value, k) for k in range(1, OUTER)]

        def gather_chips(value):
            return [
                move_dp(value, lambda z, m, c, i=i, o=o: (z, (m + i) & (inner - 1), c ^ o))
                for i in range(inner)
                for o in range(2)
                if i or o
            ]

        acts = [from_tensor(act, -j) for j, act in enumerate(step(lambda act: cut_acts(act, r), act_fake), 1)]
        planes, top_student = step(lambda cot: turn(cot, True), cot_student)
        order = (3, 1, 2, 0)
        others = {k: [from_tensor(planes[k], j) for j in range(1, n_tensor)] for k in order}
        cores, top_fake = step(lambda cot: turn(cot, False), cot_fake)
        cores = [core.reshape(-1, r) for core in cores]

        scales = step(
            lambda steps: 1.0 / (0.1 + steps.astype(jnp.float32) / 1000.0), timesteps[0, :, 0]
        )
        bounds, scaled, *scaled_student = step(
            lambda *values: prepare(*values, r),
            act_student, act_fake, top_student, top_fake, scales,
        )
        got = gather_planes(bounds)
        sends, keeps = [], []
        for j in range(n_tensor):
            if j:
                scaled = step(scale_rows, acts[j - 1], scales)
            sends.append(to_core(step(lambda a, b: multiply_rows([a], [b]), cores[1], scaled)))
            keeps.append(step(lambda a, b: multiply_rows([a], [b]), cores[0], scaled))
        bounds = reduced(jnp.maximum, bounds, got)
        bounds = reduced(jnp.maximum, bounds, gather_chips(bounds))

        def factors(bounds):
            bounds = jnp.maximum(bounds, 1e-30) * (1.01 * count * n_dp / HALF_LIMIT)
            return bounds[:2, 0], 1.0 / bounds[:2, 0]

        grow, fit = step(factors, bounds)

        def shrink(value, net):
            return (value * fit[net]).astype(jnp.float16)

        def widen(value, net):
            return value.astype(jnp.float32) * grow[net]

        halves = ((2, 3), (0, 1))

        def fake_middle(keep, send):
            both = (keep + send).reshape(inner, OUTER, width, f)
            sent = [
                [shrink(both[i, lo : hi + 1], 1) for i in range(1, inner)] for lo, hi in halves
            ]
            return sent, [both[0, lo : hi + 1] for lo, hi in halves]

        def start_middle(keep, send):
            sent, mine = step(fake_middle, keep, send)
            return [
                (own, [to_middle(value, i) for i, value in enumerate(values, 1)])
                for own, values in zip(mine, sent)
            ]

        kept, crossing, to_sum = {}, {}, []

        def multiply(k):
            def half(other, *operands):
                pieces, scaled = operands[:n_tensor], operands[n_tensor:]
                return multiply_half(other, pieces, scaled)

            operands = [planes[k], *others[k], *scaled_student]
            send = to_core(step(functools.partial(half, 1), *operands))
            kept[k] = step(functools.partial(half, 0), *operands), send

        def cross_middle(k):
            def work(keep, send):
                both = keep + send
                return [shrink(both[i], 0) for i in range(1, inner)], both[0]

            sent, own = step(work, *kept[k])
            crossing[k] = own, [to_middle(value, i) for i, value in enumerate(sent, 1)]

        def cross_planes(k):
            def work(own, *got):
                for value in got:
                    own = own + widen(value, 0)
                return shrink(own, 0) if k else own

            own, got = crossing[k]
            value = step(work, own, *got)
            to_sum.append(to_plane(value, k) if k else value)

        fake_sums = [[] for _ in range(n_tensor)]

        def fake_planes(j, part):
            lo, hi = halves[part]

            def work(own, *got):
                for value in got:
                    own = own + widen(value, 1)
                return [shrink(own[k - lo], 1) if k else own[0] for k in range(hi, lo - 1, -1)]

            own, got = middles[j][part]
            values = step(work, own, *got)
            for k, value in zip(range(hi, lo - 1, -1), values):
                fake_sums[j].append(to_plane(value, k) if k else value)

        def fake_total(j):
            def work(*values):
                total = values[-1]
                for value in values[:-1]:
                    total = total + widen(value, 1)
                return total

            return step(work, *fake_sums[j])

        def back(whole, net, pieces, j, low, size):
            weight = (weight_student, weight_fake)[net]
            has = [] if whole is None else [whole]

            def work(weight, *values):
                return back_part(
                    values[-1] if has else None, weight, values[: len(pieces)], scales,
                    net, j, low, size, r, count,
                )

            return step(work, weight, *pieces, *has)

        multiply(3)
        middles = [start_middle(keep, send) for keep, send in zip(keeps, sends)]
        fake_planes(0, 0)
        fake_planes(0, 1)
        back_student = back(None, 0, [cot_student], 0, 0, r)
        multiply(1)
        cross_middle(3)
        for j in range(1, n_tensor):
            fake_planes(j, 0)
        back_fake = back(None, 1, [cot_fake], 0, 0, r)
        for j in range(1, n_tensor):
            fake_planes(j, 1)
        multiply(2)
        cross_middle(1)
        cross_planes(3)
        fake_others = [fake_total(j) for j in range(1, n_tensor)]
        fake_got = [from_tensor(value, j) for j, value in enumerate(fake_others, 1)]

        part = r // 4
        cuts = ((0, part), (part, 3 * part), (3 * part, r)) if part % LANES == 0 else ((0, r),)
        raw = []

        def send_raw(lo, hi):
            rows = step(lambda cot: cot[lo:hi], cot_fake)
            raw.append([from_tensor(rows, j) for j in range(1, n_tensor)])

        send_raw(*cuts[0])
        cross_middle(2)
        cross_planes(1)
        fake_mine = fake_total(0)
        cross_planes(2)
        multiply(0)
        cross_middle(0)

        def student_partial(*values):
            total = widen(values[0], 0)
            for value in values[1:]:
                total = total + widen(value, 0)
            return total

        total_student = step(student_partial, *to_sum)
        to_sum.clear()
        total_fake = reduced(jnp.add, fake_mine, fake_got)
        cross_planes(0)
        total_student = reduced(jnp.add, total_student, to_sum)
        squares = step(norms, total_student, total_fake)
        squares = reduced(jnp.add, squares, gather_planes(squares))
        squares = reduced(jnp.add, squares, gather_chips(squares))
        got = [from_tensor(squares, j) for j in range(1, n_tensor)]
        for lo, hi in cuts[1:]:
            send_raw(lo, hi)

        def back_raw(n):
            nonlocal back_fake
            lo, hi = cuts[n]
            for j in range(1, n_tensor):
                back_fake = back(back_fake, 1, [raw[n][j - 1]], j, lo, hi - lo)

        back_raw(0)
        squares = reduced(jnp.add, squares, got)

        states = (
            master_student, first_student, second_student, master_fake, first_fake, second_fake,
        )
        own, updated = step(
            lambda squares, *values: update(squares, values[:2], values[2:]),
            squares, total_student, total_fake, *(state.T for state in states),
        )

        mine = {}

        def spread_middle(k, value):
            mine[k] = [value] + [to_middle(value, -i) for i in range(1, inner)]

        planes_got = {k: to_plane(own, -k) for k in (1, 3, 2)}
        spread_middle(0, own)
        for j in range(1, n_tensor):
            pieces = [others[k][j - 1] for k in range(OUTER)]
            back_student = back(back_student, 0, pieces, j, 0, r)
        spread_middle(1, step(lambda value: value, planes_got[1]))
        spread_middle(3, step(lambda value: value, planes_got[3]))

        first_half = step(lambda *values: jnp.stack(values), *mine[0], *mine[1])
        theirs = [to_core(first_half)]
        spread_middle(2, step(lambda value: value, planes_got[2]))
        second_half = step(lambda *values: jnp.stack(values), *mine[2], *mine[3])
        theirs.append(to_core(second_half))
        for n in range(1, len(cuts)):
            back_raw(n)
        stacks = [first_half, second_half, *theirs]
        params = [step(lambda *values: spread(values, n), *stacks) for n in range(2)]

        new_states = [value.T for value in updated]
        return (back_student, back_fake, *new_states, *params)

    placed = (
        P(("dp", "tensor"), None),
        P(("dp", "tensor"), None),
        P("tensor", "dp"),
        P("tensor", "dp"),
        P("tensor", None),
        P("tensor", None),
        P("tensor", "dp"),
        P("tensor", "dp"),
        P("tensor", "dp"),
        P("tensor", "dp"),
        P("tensor", "dp"),
        P("tensor", "dp"),
        P("dp", None, None),
    )
    return jax.shard_map(
        per_device,
        mesh=mesh,
        in_specs=placed,
        out_specs=(
            P("tensor", "dp"),
            P("tensor", "dp"),
            P("tensor", "dp"),
            P("tensor", "dp"),
            P("tensor", "dp"),
            P("tensor", "dp"),
            P("tensor", "dp"),
            P("tensor", "dp"),
            P("tensor", None),
            P("tensor", None),
        ),
        check_vma=False,
    )
```

time: 260 us -> 272 us (1.046)
  waiting for transfers between devices: 99.6 us -> 141 us
  Pallas kernels: 17.4 us -> 48.7 us
  matrix products: 23.8 us -> 0 us
  local copies, waits for them, and re-layouts: 20.2 us -> 4.92 us
  other arithmetic: 33 us -> 19.6 us
  between operations: 8.32 us -> 1.42 us
    ppermute x10, waiting for transfers between devices: 9.88 us -> 50.5 us  [from_tensor(): return lax.ppermute(value, 'tensor', perm)]
    pallas_call x5 -> x27, Pallas kernels: 17.4 us -> 48.7 us  [call(): pl.pallas_call(kernel, out_shape=out_shape, compiler_params=pltpu.Compile...]
    dot_general x25 -> x0, matrix products: 23.8 us -> none  [dot(): return lax.dot_general(a, b, dims, preferred_element_type=jnp.float32)]
    unnamed x73 -> x30, local copies, waits for them, and re-layouts: 9.61 us -> 3.52 us
    slice x20 -> x4, local copies, waits for them, and re-layouts: 6.17 us -> 0.3 us  [the longest x3 0.18 us: send_raw(): rows = step(lambda cot: cot[lo:hi], cot_fake)]
    dynamic_slice x4 -> x0, local copies, waits for them, and re-layouts: 3.13 us -> none  [the longest x3 1.96 us: rows_of(): return lax.dynamic_slice_in_dim(value, start, r, value.ndim - 1)]
  transfers between devices with their start and end apart: 54 -> 54, of which waited for: 26 -> 25; matrix products, arithmetic and copies ran while one was open for 20% -> 8% of each run, Pallas kernels for 1% -> 14%
where the time goes in v4:
time: 272 us
  waiting for transfers between devices  141 us (52%)
  starting transfers between devices  56.3 us (21%)
  Pallas kernels  48.7 us (18%)
  other arithmetic  19.6 us (7%)
  local copies, waits for them, and re-layouts  4.92 us (2%)
    ppermute x44, waiting for transfers between devices, move_dp(): return lax.ppermute(value, 'dp', perm)  90.3 us
    ppermute x10, waiting for transfers between devices, from_tensor(): return lax.ppermute(value, 'tensor', perm)  50.5 us
    pallas_call x27, Pallas kernels, call(): pl.pallas_call(kernel, out_shape=out_shape, compiler_params=pltpu.Compile...  48.7 us
    ppermute x44, starting transfers between devices, move_dp(): return lax.ppermute(value, 'dp', perm)  43.4 us
    ppermute x10, starting transfers between devices, from_tensor(): return lax.ppermute(value, 'tensor', perm)  12.8 us
    convert_element_type x7, other arithmetic, shrink(): return (value * fit[net]).astype(jnp.float16)  7.11 us
  transfers between devices with their start and end apart: 54, of which 25 were waited for; matrix products, arithmetic and copies ran while one was open for 8% of the time, Pallas kernels for 14%

profile of v4, /device:TPU:0, one launch (start us, length us, event | category | flops | bytes accessed | tf_op | source)
XLA Modules:
  0.0 271.7 jit_solution(5449700332922098623)
XLA Ops:
  2.0 3.0 %collective-permute-start.8 = (bf16[608,512]{1,0:T(8,128)(2,1)S(1)}, bf16[608,512]{1,0:T(8,128)(2,1)S(1)}, u32[]{:S(2)}, u32[]{:S(2)}) collective-permute-start(bf16[608,512]{1,0:T(8,128)(2,1)S(1)} %shard_map.204), channel_id=1, source_target_pairs={{0,1},{1,0},{2,3},{3,2},{4,5},{5,4},{6,7},{7,6},{8,9},{9,8},{10,11... | collective-permute-start | bytes 1867784 | tf_op jit(solution)/shard_map/ppermute | solution.py:91
  6.8 2.5 shard_map.205
  9.3 2.2 shard_map.206
  16.7 2.4 collective-permute-done.8.act_ref
  23.5 2.6 collective-permute-start.6
  37.6 8.6 %collective-permute-done.3.refs_1_.refs_3_ = bf16[2,2,152,512]{3,2,1,0:T(8,128)(2,1)S(1)} collective-permute-done((bf16[2,2,152,512]{3,2,1,0:T(8,128)(2,1)S(1)}, bf16[2,2,152,512]{3,2,1,0:T(8,128)(2,1)S(1)}, u32[]{:S(2)}, u32[]{:S(2)}) %collective-permute-start.3) | collective-permute-done | bytes 622624 | tf_op jit(solution)/shard_map/ppermute | solution.py:91
  54.7 6.0 %collective-permute-done.13 = f16[2,152,608]{2,1,0:T(8,128)(2,1)S(1)} collective-permute-done((f16[2,152,608]{2,1,0:T(8,128)(2,1)S(1)}, f16[2,152,608]{2,1,0:T(8,128)(2,1)S(1)}, u32[]{:S(2)}, u32[]{:S(2)}) %collective-permute-start.13) | collective-permute-done | bytes 369696 | tf_op jit(solution)/shard_map/ppermute | solution.py:78
  63.8 6.7 %collective-permute-done.12 = f16[2,152,608]{2,1,0:T(8,128)(2,1)S(1)} collective-permute-done((f16[2,152,608]{2,1,0:T(8,128)(2,1)S(1)}, f16[2,152,608]{2,1,0:T(8,128)(2,1)S(1)}, u32[]{:S(2)}, u32[]{:S(2)}) %collective-permute-start.12) | collective-permute-done | bytes 369696 | tf_op jit(solution)/shard_map/ppermute | solution.py:78
  73.8 3.2 %shard_map.215.refs_4_ = bf16[608,1024]{1,0:T(8,128)(2,1)} custom-call(f32[2]{0:T(128)S(1)} %add_divide_fusion.scale_ref, bf16[608,2432]{1,0:T(8,128)(2,1)S(1)} %copy-done.2, bf16[512,2432]{1,0:T(8,128)(2,1)S(1)} %copy-done.4), custom_call_target="tpu_custom_call" | custom-call | tf_op jit(solution)/shard_map/pallas_call | solution.py:56
  83.8 3.2 %shard_map.218.refs_1_ = bf16[608,1024]{1,0:T(8,128)(2,1)} custom-call(f32[2]{0:T(128)S(1)} %add_divide_fusion.scale_ref, bf16[608,2432]{1,0:T(8,128)(2,1)S(1)} %copy-done, bf16[512,2432]{1,0:T(8,128)(2,1)S(1)} %copy-done.1), custom_call_target="tpu_custom_call" | custom-call | tf_op jit(solution)/shard_map/pallas_call | solution.py:56
  87.0 3.9 %collective-permute-done.18 = f16[2,152,608]{2,1,0:T(8,128)(2,1)S(1)} collective-permute-done((f16[2,152,608]{2,1,0:T(8,128)(2,1)S(1)}, f16[2,152,608]{2,1,0:T(8,128)(2,1)S(1)}, u32[]{:S(2)}, u32[]{:S(2)}) %collective-permute-start.18) | collective-permute-done | bytes 369696 | tf_op jit(solution)/shard_map/ppermute | solution.py:78
  102.5 2.3 collective-permute-start.28
  104.8 10.0 %collective-permute-done.24 = f16[152,608]{1,0:T(8,128)(2,1)S(1)} collective-permute-done((f16[152,608]{1,0:T(8,128)(2,1)S(1)}, f16[152,608]{1,0:T(8,128)(2,1)S(1)}, u32[]{:S(2)}, u32[]{:S(2)}) %collective-permute-start.24) | collective-permute-done | bytes 184864 | tf_op jit(solution)/shard_map/ppermute | solution.py:78
  117.0 4.7 %collective-permute-done.21 = f16[152,608]{1,0:T(8,128)(2,1)S(1)} collective-permute-done((f16[152,608]{1,0:T(8,128)(2,1)S(1)}, f16[152,608]{1,0:T(8,128)(2,1)S(1)}, u32[]{:S(2)}, u32[]{:S(2)}) %collective-permute-start.21) | collective-permute-done | bytes 184864 | tf_op jit(solution)/shard_map/ppermute | solution.py:78
  123.7 2.7 %collective-permute-done.29 = f16[152,608]{1,0:T(8,128)(2,1)S(1)} collective-permute-done((f16[152,608]{1,0:T(8,128)(2,1)S(1)}, f16[152,608]{1,0:T(8,128)(2,1)S(1)}, u32[]{:S(2)}, u32[]{:S(2)}) %collective-permute-start.29) | collective-permute-done | bytes 184864 | tf_op jit(solution)/shard_map/ppermute | solution.py:78
  129.8 3.0 %collective-permute-start.20 = (f16[152,608]{1,0:T(8,128)(2,1)S(1)}, f16[152,608]{1,0:T(8,128)(2,1)S(1)}, u32[]{:S(2)}, u32[]{:S(2)}) collective-permute-start(f16[152,608]{1,0:T(8,128)(2,1)S(1)} %multiply_convert_fusion.2), channel_id=1, source_target_pairs={{0,24},{2,26},{4,28},{6,30},{8,0},{10,2},{12,4},{14,6},{16,8},{18,... | collective-permute-start | bytes 554504 | tf_op jit(solution)/shard_map/ppermute | solution.py:78
  139.1 5.5 %collective-permute-done.26 = f16[152,608]{1,0:T(8,128)(2,1)S(1)} collective-permute-done((f16[152,608]{1,0:T(8,128)(2,1)S(1)}, f16[152,608]{1,0:T(8,128)(2,1)S(1)}, u32[]{:S(2)}, u32[]{:S(2)}) %collective-permute-start.26) | collective-permute-done | bytes 184864 | tf_op jit(solution)/shard_map/ppermute | solution.py:78
  144.6 7.7 %collective-permute-done.31 = f16[152,608]{1,0:T(8,128)(2,1)S(1)} collective-permute-done((f16[152,608]{1,0:T(8,128)(2,1)S(1)}, f16[152,608]{1,0:T(8,128)(2,1)S(1)}, u32[]{:S(2)}, u32[]{:S(2)}) %collective-permute-start.31) | collective-permute-done | bytes 184864 | tf_op jit(solution)/shard_map/ppermute | solution.py:78
  165.2 2.1 shard_map.224.refs_1_
  168.2 2.1 shard_map.225
  170.3 3.3 %collective-permute-start.47 = (bf16[2,152,608]{2,1,0:T(8,128)(2,1)S(1)}, bf16[2,152,608]{2,1,0:T(8,128)(2,1)S(1)}, u32[]{:S(2)}, u32[]{:S(2)}) collective-permute-start(bf16[2,152,608]{2,1,0:T(8,128)(2,1)S(1)} %get-tuple-element.345), channel_id=1, source_target_pairs={{0,24},{2,26},{4,28},{6,30},{8,0},{10,2},{12,4},{14,6},{16,8},{18,... | collective-permute-start | bytes 1109000 | tf_op jit(solution)/shard_map/ppermute | solution.py:78
  174.9 3.5 %shard_map.226 = bf16[608,1024]{1,0:T(8,128)(2,1)} custom-call(f32[2]{0:T(128)S(1)} %add_divide_fusion.scale_ref, bf16[608,2432]{1,0:T(8,128)(2,1)S(1)} %copy-done.2, bf16[2,2,152,512]{3,2,1,0:T(8,128)(2,1)S(1)} %collective-permute-done.refs_1_.refs_0_, bf16[2,2,152,512]{3,2,1,0:T(8,128)(2,1)S(1)} %collective-permute-done.1.refs_1_, ...), custom_call_target="tpu_custom_call", output_to_operand_aliasing={{}: (6, {})} | custom-call | tf_op jit(solution)/shard_map/pallas_call | solution.py:56
  178.4 4.5 %collective-permute-done.47 = bf16[2,152,608]{2,1,0:T(8,128)(2,1)S(1)} collective-permute-done((bf16[2,152,608]{2,1,0:T(8,128)(2,1)S(1)}, bf16[2,152,608]{2,1,0:T(8,128)(2,1)S(1)}, u32[]{:S(2)}, u32[]{:S(2)}) %collective-permute-start.47) | collective-permute-done | bytes 369696 | tf_op jit(solution)/shard_map/ppermute | solution.py:78
  185.5 6.5 %collective-permute-done.49 = bf16[2,152,608]{2,1,0:T(8,128)(2,1)S(1)} collective-permute-done((bf16[2,152,608]{2,1,0:T(8,128)(2,1)S(1)}, bf16[2,152,608]{2,1,0:T(8,128)(2,1)S(1)}, u32[]{:S(2)}, u32[]{:S(2)}) %collective-permute-start.49) | collective-permute-done | bytes 369696 | tf_op jit(solution)/shard_map/ppermute | solution.py:78
  193.8 13.0 %collective-permute-done.45 = bf16[2,152,608]{2,1,0:T(8,128)(2,1)S(1)} collective-permute-done((bf16[2,152,608]{2,1,0:T(8,128)(2,1)S(1)}, bf16[2,152,608]{2,1,0:T(8,128)(2,1)S(1)}, u32[]{:S(2)}, u32[]{:S(2)}) %collective-permute-start.45) | collective-permute-done | bytes 369696 | tf_op jit(solution)/shard_map/ppermute | solution.py:78
  208.1 9.7 %collective-permute-done.50 = bf16[2,152,608]{2,1,0:T(8,128)(2,1)S(1)} collective-permute-done((bf16[2,152,608]{2,1,0:T(8,128)(2,1)S(1)}, bf16[2,152,608]{2,1,0:T(8,128)(2,1)S(1)}, u32[]{:S(2)}, u32[]{:S(2)}) %collective-permute-start.50) | collective-permute-done | bytes 369696 | tf_op jit(solution)/shard_map/ppermute | solution.py:78
  220.2 28.1 %collective-permute-done.44.refs_0_ = bf16[256,2432]{1,0:T(8,128)(2,1)S(1)} collective-permute-done((bf16[256,2432]{1,0:T(8,128)(2,1)S(1)}, bf16[256,2432]{1,0:T(8,128)(2,1)S(1)}, u32[]{:S(2)}, u32[]{:S(2)}) %collective-permute-start.44) | collective-permute-done | bytes 1245216 | tf_op jit(solution)/shard_map/ppermute | solution.py:91
  248.4 2.3 shard_map.227.refs_1_
  250.7 10.6 %collective-permute-done.43.refs_0_ = bf16[128,2432]{1,0:T(8,128)(2,1)S(1)} collective-permute-done((bf16[128,2432]{1,0:T(8,128)(2,1)S(1)}, bf16[128,2432]{1,0:T(8,128)(2,1)S(1)}, u32[]{:S(2)}, u32[]{:S(2)}) %collective-permute-start.43) | collective-permute-done | bytes 622624 | tf_op jit(solution)/shard_map/ppermute | solution.py:91
  261.3 2.1 shard_map.228
  263.4 4.1 %shard_map.229 = bf16[608,2432]{1,0:T(8,128)(2,1)} custom-call(bf16[4,2,152,608]{3,2,1,0:T(8,128)(2,1)S(1)} %pad_maximum_fusion.refs_0_, bf16[4,2,152,608]{3,2,1,0:T(8,128)(2,1)S(1)} %pad_maximum_fusion.1.refs_1_, bf16[4,2,152,608]{3,2,1,0:T(8,128)(2,1)S(1)} %collective-permute-done.52.refs_2_, bf16[4,2,152,608]{3,2,1,0:T(8,128)(2,1)S(1)} %collective-permute-done.53.refs_3_), custom_call_target="tpu_custom_call" | custom-call | tf_op jit(solution)/shard_map/pallas_call | solution.py:56
  267.6 4.1 %shard_map.230 = bf16[608,2432]{1,0:T(8,128)(2,1)} custom-call(bf16[4,2,152,608]{3,2,1,0:T(8,128)(2,1)S(1)} %pad_maximum_fusion.refs_0_, bf16[4,2,152,608]{3,2,1,0:T(8,128)(2,1)S(1)} %pad_maximum_fusion.1.refs_1_, bf16[4,2,152,608]{3,2,1,0:T(8,128)(2,1)S(1)} %collective-permute-done.52.refs_2_, bf16[4,2,152,608]{3,2,1,0:T(8,128)(2,1)S(1)} %collective-permute-done.53.refs_3_), custom_call_target="tpu_custom_call" | custom-call | tf_op jit(solution)/shard_map/pallas_call | solution.py:56
  (178 shorter events, 93.8 us)
Async XLA Ops:
  2.0 17.0 %collective-permute-start.8 = (bf16[608,512]{1,0:T(8,128)(2,1)S(1)}, bf16[608,512]{1,0:T(8,128)(2,1)S(1)}, u32[]{:S(2)}, u32[]{:S(2)}) collective-permute-start(bf16[608,512]{1,0:T(8,128)(2,1)S(1)} %shard_map.204), channel_id=1, source_target_pairs={{0,1},{1,0},{2,3},{3,2},{4,5},{5,4},{6,7},{7,6},{8,9},{9,8},{10,11... | collective-permute-start | bytes 1867784 | tf_op jit(solution)/shard_map/ppermute | solution.py:91
  14.8 35.4 %collective-permute-start.4 = (f32[1216,608]{1,0:T(8,128)S(1)}, f32[1216,608]{1,0:T(8,128)S(1)}, u32[]{:S(2)}, u32[]{:S(2)}) collective-permute-start(f32[1216,608]{1,0:T(8,128)S(1)} %shard_map.208), channel_id=1, source_target_pairs={{0,2},{2,0},{4,6},{6,4},{8,10},{10,8},{12,14},{14,12},{16,18},{18,... | collective-permute-start | bytes 8871944 | tf_op jit(solution)/shard_map/ppermute | solution.py:78
  21.5 32.0 %collective-permute-start.14 = (f32[1216,608]{1,0:T(8,128)S(1)}, f32[1216,608]{1,0:T(8,128)S(1)}, u32[]{:S(2)}, u32[]{:S(2)}) collective-permute-start(f32[1216,608]{1,0:T(8,128)S(1)} %shard_map.211), channel_id=1, source_target_pairs={{0,2},{2,0},{4,6},{6,4},{8,10},{10,8},{12,14},{14,12},{16,18},{18,... | collective-permute-start | bytes 8871944 | tf_op jit(solution)/shard_map/ppermute | solution.py:78
  29.2 17.0 %collective-permute-start.3 = (bf16[2,2,152,512]{3,2,1,0:T(8,128)(2,1)S(1)}, bf16[2,2,152,512]{3,2,1,0:T(8,128)(2,1)S(1)}, u32[]{:S(2)}, u32[]{:S(2)}) collective-permute-start(bf16[2,2,152,512]{3,2,1,0:T(8,128)(2,1)S(1)} %get-tuple-element.234.refs_0_), channel_id=1, source_target_pairs={{0,1},{1,0},{2,3},{3,2},{4,5},{5,4},{6,7},{7,6},{8,9},{9,8},{10,11... | collective-permute-start | bytes 1867784 | tf_op jit(solution)/shard_map/ppermute | solution.py:91
  35.4 93.4 %collective-permute-start = (bf16[2,2,152,512]{3,2,1,0:T(8,128)(2,1)S(1)}, bf16[2,2,152,512]{3,2,1,0:T(8,128)(2,1)S(1)}, u32[]{:S(2)}, u32[]{:S(2)}) collective-permute-start(bf16[2,2,152,512]{3,2,1,0:T(8,128)(2,1)S(1)} %get-tuple-element.295.refs_0_), channel_id=1, source_target_pairs={{0,1},{1,0},{2,3},{3,2},{4,5},{5,4},{6,7},{7,6},{8,9},{9,8},{10,11... | collective-permute-start | bytes 1867784 | tf_op jit(solution)/shard_map/ppermute | solution.py:91
  35.9 41.1 %collective-permute-start.1 = (bf16[2,2,152,512]{3,2,1,0:T(8,128)(2,1)S(1)}, bf16[2,2,152,512]{3,2,1,0:T(8,128)(2,1)S(1)}, u32[]{:S(2)}, u32[]{:S(2)}) collective-permute-start(bf16[2,2,152,512]{3,2,1,0:T(8,128)(2,1)S(1)} %get-tuple-element.252.refs_0_), channel_id=1, source_target_pairs={{0,1},{1,0},{2,3},{3,2},{4,5},{5,4},{6,7},{7,6},{8,9},{9,8},{10,11... | collective-permute-start | bytes 1867784 | tf_op jit(solution)/shard_map/ppermute | solution.py:91
  46.2 46.7 %collective-permute-start.2 = (bf16[2,2,152,512]{3,2,1,0:T(8,128)(2,1)S(1)}, bf16[2,2,152,512]{3,2,1,0:T(8,128)(2,1)S(1)}, u32[]{:S(2)}, u32[]{:S(2)}) collective-permute-start(bf16[2,2,152,512]{3,2,1,0:T(8,128)(2,1)S(1)} %get-tuple-element.268.refs_0_), channel_id=1, source_target_pairs={{0,1},{1,0},{2,3},{3,2},{4,5},{5,4},{6,7},{7,6},{8,9},{9,8},{10,11... | collective-permute-start | bytes 1867784 | tf_op jit(solution)/shard_map/ppermute | solution.py:91
  53.5 25.5 %collective-permute-start.15 = (f32[2,152,608]{2,1,0:T(8,128)S(1)}, f32[2,152,608]{2,1,0:T(8,128)S(1)}, u32[]{:S(2)}, u32[]{:S(2)}) collective-permute-start(f32[2,152,608]{2,1,0:T(8,128)S(1)} %shard_map.213), channel_id=1, source_target_pairs={{0,2},{2,0},{4,6},{6,4},{8,10},{10,8},{12,14},{14,12},{16,18},{18,... | collective-permute-start | bytes 2217992 | tf_op jit(solution)/shard_map/ppermute | solution.py:78
  78.0 18.4 %collective-permute-start.17 = (f32[2,152,608]{2,1,0:T(8,128)S(1)}, f32[2,152,608]{2,1,0:T(8,128)S(1)}, u32[]{:S(2)}, u32[]{:S(2)}) collective-permute-start(f32[2,152,608]{2,1,0:T(8,128)S(1)} %shard_map.216), channel_id=1, source_target_pairs={{0,2},{2,0},{4,6},{6,4},{8,10},{10,8},{12,14},{14,12},{16,18},{18,... | collective-permute-start | bytes 2217992 | tf_op jit(solution)/shard_map/ppermute | solution.py:78
  79.0 11.9 %collective-permute-start.18 = (f16[2,152,608]{2,1,0:T(8,128)(2,1)S(1)}, f16[2,152,608]{2,1,0:T(8,128)(2,1)S(1)}, u32[]{:S(2)}, u32[]{:S(2)}) collective-permute-start(f16[2,152,608]{2,1,0:T(8,128)(2,1)S(1)} %get-tuple-element.375), channel_id=1, source_target_pairs={{0,4},{2,6},{4,0},{6,2},{8,12},{10,14},{12,8},{14,10},{16,20},{18,... | collective-permute-start | bytes 1109000 | tf_op jit(solution)/shard_map/ppermute | solution.py:78
  80.4 16.9 %collective-permute-start.16 = (f16[152,608]{1,0:T(8,128)(2,1)S(1)}, f16[152,608]{1,0:T(8,128)(2,1)S(1)}, u32[]{:S(2)}, u32[]{:S(2)}) collective-permute-start(f16[152,608]{1,0:T(8,128)(2,1)S(1)} %get-tuple-element.396), channel_id=1, source_target_pairs={{0,4},{2,6},{4,0},{6,2},{8,12},{10,14},{12,8},{14,10},{16,20},{18,... | collective-permute-start | bytes 554504 | tf_op jit(solution)/shard_map/ppermute | solution.py:78
  90.9 11.6 %collective-permute-start.23 = (f16[152,608]{1,0:T(8,128)(2,1)S(1)}, f16[152,608]{1,0:T(8,128)(2,1)S(1)}, u32[]{:S(2)}, u32[]{:S(2)}) collective-permute-start(f16[152,608]{1,0:T(8,128)(2,1)S(1)} %get-tuple-element.393), channel_id=1, source_target_pairs={{0,24},{2,26},{4,28},{6,30},{8,0},{10,2},{12,4},{14,6},{16,8},{18,... | collective-permute-start | bytes 554504 | tf_op jit(solution)/shard_map/ppermute | solution.py:78
  96.4 19.2 %collective-permute-start.22 = (f32[2,152,608]{2,1,0:T(8,128)S(1)}, f32[2,152,608]{2,1,0:T(8,128)S(1)}, u32[]{:S(2)}, u32[]{:S(2)}) collective-permute-start(f32[2,152,608]{2,1,0:T(8,128)S(1)} %shard_map.219), channel_id=1, source_target_pairs={{0,2},{2,0},{4,6},{6,4},{8,10},{10,8},{12,14},{14,12},{16,18},{18,... | collective-permute-start | bytes 2217992 | tf_op jit(solution)/shard_map/ppermute | solution.py:78
  97.3 17.5 %collective-permute-start.24 = (f16[152,608]{1,0:T(8,128)(2,1)S(1)}, f16[152,608]{1,0:T(8,128)(2,1)S(1)}, u32[]{:S(2)}, u32[]{:S(2)}) collective-permute-start(f16[152,608]{1,0:T(8,128)(2,1)S(1)} %get-tuple-element.392), channel_id=1, source_target_pairs={{0,16},{2,18},{4,20},{6,22},{8,24},{10,26},{12,28},{14,30},{16,0},... | collective-permute-start | bytes 554504 | tf_op jit(solution)/shard_map/ppermute | solution.py:78
  100.9 22.7 %collective-permute-start.30 = (f16[152,608]{1,0:T(8,128)(2,1)S(1)}, f16[152,608]{1,0:T(8,128)(2,1)S(1)}, u32[]{:S(2)}, u32[]{:S(2)}) collective-permute-start(f16[152,608]{1,0:T(8,128)(2,1)S(1)} %get-tuple-element.385), channel_id=1, source_target_pairs={{0,8},{2,10},{4,12},{6,14},{8,16},{10,18},{12,20},{14,22},{16,24},... | collective-permute-start | bytes 554504 | tf_op jit(solution)/shard_map/ppermute | solution.py:78
  102.5 21.2 %collective-permute-start.28 = (f16[152,608]{1,0:T(8,128)(2,1)S(1)}, f16[152,608]{1,0:T(8,128)(2,1)S(1)}, u32[]{:S(2)}, u32[]{:S(2)}) collective-permute-start(f16[152,608]{1,0:T(8,128)(2,1)S(1)} %get-tuple-element.387), channel_id=1, source_target_pairs={{0,24},{2,26},{4,28},{6,30},{8,0},{10,2},{12,4},{14,6},{16,8},{18,... | collective-permute-start | bytes 554504 | tf_op jit(solution)/shard_map/ppermute | solution.py:78
  114.8 11.6 %collective-permute-start.29 = (f16[152,608]{1,0:T(8,128)(2,1)S(1)}, f16[152,608]{1,0:T(8,128)(2,1)S(1)}, u32[]{:S(2)}, u32[]{:S(2)}) collective-permute-start(f16[152,608]{1,0:T(8,128)(2,1)S(1)} %get-tuple-element.386), channel_id=1, source_target_pairs={{0,16},{2,18},{4,20},{6,22},{8,24},{10,26},{12,28},{14,30},{16,0},... | collective-permute-start | bytes 554504 | tf_op jit(solution)/shard_map/ppermute | solution.py:78
  132.9 20.2 %collective-permute-start.34 = (f32[152,608]{1,0:T(8,128)S(1)}, f32[152,608]{1,0:T(8,128)S(1)}, u32[]{:S(2)}, u32[]{:S(2)}) collective-permute-start(f32[152,608]{1,0:T(8,128)S(1)} %multiply_add_fusion.6), channel_id=1, source_target_pairs={{0,1},{1,0},{2,3},{3,2},{4,5},{5,4},{6,7},{7,6},{8,9},{9,8},{10,11... | collective-permute-start | bytes 1109000 | tf_op jit(solution)/shard_map/ppermute | solution.py:91
  133.4 31.9 %collective-permute-start.42 = (bf16[128,2432]{1,0:T(8,128)(2,1)S(1)}, bf16[128,2432]{1,0:T(8,128)(2,1)S(1)}, u32[]{:S(2)}, u32[]{:S(2)}) collective-permute-start(bf16[128,2432]{1,0:T(8,128)(2,1)S(1)} %slice.154), channel_id=1, source_target_pairs={{0,1},{1,0},{2,3},{3,2},{4,5},{5,4},{6,7},{7,6},{8,9},{9,8},{10,11... | collective-permute-start | bytes 1867784 | tf_op jit(solution)/shard_map/ppermute | solution.py:91
  136.2 16.1 %collective-permute-start.31 = (f16[152,608]{1,0:T(8,128)(2,1)S(1)}, f16[152,608]{1,0:T(8,128)(2,1)S(1)}, u32[]{:S(2)}, u32[]{:S(2)}) collective-permute-start(f16[152,608]{1,0:T(8,128)(2,1)S(1)} %multiply_convert_fusion), channel_id=1, source_target_pairs={{0,16},{2,18},{4,20},{6,22},{8,24},{10,26},{12,28},{14,30},{16,0},... | collective-permute-start | bytes 554504 | tf_op jit(solution)/shard_map/ppermute | solution.py:78
  138.6 14.5 %collective-permute-start.33 = (f16[152,608]{1,0:T(8,128)(2,1)S(1)}, f16[152,608]{1,0:T(8,128)(2,1)S(1)}, u32[]{:S(2)}, u32[]{:S(2)}) collective-permute-start(f16[152,608]{1,0:T(8,128)(2,1)S(1)} %get-tuple-element.383), channel_id=1, source_target_pairs={{0,4},{2,6},{4,0},{6,2},{8,12},{10,14},{12,8},{14,10},{16,20},{18,... | collective-permute-start | bytes 554504 | tf_op jit(solution)/shard_map/ppermute | solution.py:78
  170.3 12.7 %collective-permute-start.47 = (bf16[2,152,608]{2,1,0:T(8,128)(2,1)S(1)}, bf16[2,152,608]{2,1,0:T(8,128)(2,1)S(1)}, u32[]{:S(2)}, u32[]{:S(2)}) collective-permute-start(bf16[2,152,608]{2,1,0:T(8,128)(2,1)S(1)} %get-tuple-element.345), channel_id=1, source_target_pairs={{0,24},{2,26},{4,28},{6,30},{8,0},{10,2},{12,4},{14,6},{16,8},{18,... | collective-permute-start | bytes 1109000 | tf_op jit(solution)/shard_map/ppermute | solution.py:78
  173.5 18.5 %collective-permute-start.49 = (bf16[2,152,608]{2,1,0:T(8,128)(2,1)S(1)}, bf16[2,152,608]{2,1,0:T(8,128)(2,1)S(1)}, u32[]{:S(2)}, u32[]{:S(2)}) collective-permute-start(bf16[2,152,608]{2,1,0:T(8,128)(2,1)S(1)} %get-tuple-element.345), channel_id=1, source_target_pairs={{0,8},{2,10},{4,12},{6,14},{8,16},{10,18},{12,20},{14,22},{16,24},... | collective-permute-start | bytes 1109000 | tf_op jit(solution)/shard_map/ppermute | solution.py:78
  173.5 19.9 %collective-permute-start.46 = (bf16[2,152,608]{2,1,0:T(8,128)(2,1)S(1)}, bf16[2,152,608]{2,1,0:T(8,128)(2,1)S(1)}, u32[]{:S(2)}, u32[]{:S(2)}) collective-permute-start(bf16[2,152,608]{2,1,0:T(8,128)(2,1)S(1)} %get-tuple-element.345), channel_id=1, source_target_pairs={{0,4},{2,6},{4,0},{6,2},{8,12},{10,14},{12,8},{14,10},{16,20},{18,... | collective-permute-start | bytes 1109000 | tf_op jit(solution)/shard_map/ppermute | solution.py:78
  183.0 10.4 %collective-permute-start.48 = (bf16[2,152,608]{2,1,0:T(8,128)(2,1)S(1)}, bf16[2,152,608]{2,1,0:T(8,128)(2,1)S(1)}, u32[]{:S(2)}, u32[]{:S(2)}) collective-permute-start(bf16[2,152,608]{2,1,0:T(8,128)(2,1)S(1)} %collective-permute-done.47), channel_id=1, source_target_pairs={{0,4},{2,6},{4,0},{6,2},{8,12},{10,14},{12,8},{14,10},{16,20},{18,... | collective-permute-start | bytes 1109000 | tf_op jit(solution)/shard_map/ppermute | solution.py:78
  184.4 22.4 %collective-permute-start.45 = (bf16[2,152,608]{2,1,0:T(8,128)(2,1)S(1)}, bf16[2,152,608]{2,1,0:T(8,128)(2,1)S(1)}, u32[]{:S(2)}, u32[]{:S(2)}) collective-permute-start(bf16[2,152,608]{2,1,0:T(8,128)(2,1)S(1)} %get-tuple-element.345), channel_id=1, source_target_pairs={{0,16},{2,18},{4,20},{6,22},{8,24},{10,26},{12,28},{14,30},{16,0},... | collective-permute-start | bytes 1109000 | tf_op jit(solution)/shard_map/ppermute | solution.py:78
  192.0 16.0 %collective-permute-start.51 = (bf16[2,152,608]{2,1,0:T(8,128)(2,1)S(1)}, bf16[2,152,608]{2,1,0:T(8,128)(2,1)S(1)}, u32[]{:S(2)}, u32[]{:S(2)}) collective-permute-start(bf16[2,152,608]{2,1,0:T(8,128)(2,1)S(1)} %collective-permute-done.49), channel_id=1, source_target_pairs={{0,4},{2,6},{4,0},{6,2},{8,12},{10,14},{12,8},{14,10},{16,20},{18,... | collective-permute-start | bytes 1109000 | tf_op jit(solution)/shard_map/ppermute | solution.py:78
  206.8 10.9 %collective-permute-start.50 = (bf16[2,152,608]{2,1,0:T(8,128)(2,1)S(1)}, bf16[2,152,608]{2,1,0:T(8,128)(2,1)S(1)}, u32[]{:S(2)}, u32[]{:S(2)}) collective-permute-start(bf16[2,152,608]{2,1,0:T(8,128)(2,1)S(1)} %collective-permute-done.45), channel_id=1, source_target_pairs={{0,4},{2,6},{4,0},{6,2},{8,12},{10,14},{12,8},{14,10},{16,20},{18,... | collective-permute-start | bytes 1109000 | tf_op jit(solution)/shard_map/ppermute | solution.py:78
  208.1 55.4 %collective-permute-start.52 = (bf16[4,2,152,608]{3,2,1,0:T(8,128)(2,1)S(1)}, bf16[4,2,152,608]{3,2,1,0:T(8,128)(2,1)S(1)}, u32[]{:S(2)}, u32[]{:S(2)}) collective-permute-start(bf16[4,2,152,608]{3,2,1,0:T(8,128)(2,1)S(1)} %pad_maximum_fusion.refs_0_), channel_id=1, source_target_pairs={{0,2},{2,0},{4,6},{6,4},{8,10},{10,8},{12,14},{14,12},{16,18},{18,... | collective-permute-start | bytes 4435976 | tf_op jit(solution)/shard_map/ppermute | solution.py:78
  218.1 45.4 %collective-permute-start.53 = (bf16[4,2,152,608]{3,2,1,0:T(8,128)(2,1)S(1)}, bf16[4,2,152,608]{3,2,1,0:T(8,128)(2,1)S(1)}, u32[]{:S(2)}, u32[]{:S(2)}) collective-permute-start(bf16[4,2,152,608]{3,2,1,0:T(8,128)(2,1)S(1)} %pad_maximum_fusion.1.refs_1_), channel_id=1, source_target_pairs={{0,2},{2,0},{4,6},{6,4},{8,10},{10,8},{12,14},{14,12},{16,18},{18,... | collective-permute-start | bytes 4435976 | tf_op jit(solution)/shard_map/ppermute | solution.py:78
  218.1 30.2 %collective-permute-start.44 = (bf16[256,2432]{1,0:T(8,128)(2,1)S(1)}, bf16[256,2432]{1,0:T(8,128)(2,1)S(1)}, u32[]{:S(2)}, u32[]{:S(2)}) collective-permute-start(bf16[256,2432]{1,0:T(8,128)(2,1)S(1)} %slice.161), channel_id=1, source_target_pairs={{0,1},{1,0},{2,3},{3,2},{4,5},{5,4},{6,7},{7,6},{8,9},{9,8},{10,11... | collective-permute-start | bytes 3735560 | tf_op jit(solution)/shard_map/ppermute | solution.py:91
  219.7 41.5 %collective-permute-start.43 = (bf16[128,2432]{1,0:T(8,128)(2,1)S(1)}, bf16[128,2432]{1,0:T(8,128)(2,1)S(1)}, u32[]{:S(2)}, u32[]{:S(2)}) collective-permute-start(bf16[128,2432]{1,0:T(8,128)(2,1)S(1)} %slice.162), channel_id=1, source_target_pairs={{0,1},{1,0},{2,3},{3,2},{4,5},{5,4},{6,7},{7,6},{8,9},{9,8},{10,11... | collective-permute-start | bytes 1867784 | tf_op jit(solution)/shard_map/ppermute | solution.py:91
  (37 other events, 177.9 us)

commit v5 on v4

--- a/solution.py
+++ b/solution.py
@@ -57,7 +57,7 @@
         kernel,
         out_shape=out_shape,
         compiler_params=pltpu.CompilerParams(vmem_limit_bytes=mib * 1024 * 1024),
-        cost_estimate=pl.CostEstimate(flops=0, bytes_accessed=0, transcendentals=0),
+        cost_estimate=pl.CostEstimate(flops=100 * 10**9, bytes_accessed=0, transcendentals=0),
         **kwargs,
     )(*operands)
 
@@ -134,8 +134,8 @@
     def turn(cot, by_planes):
         r = cot.shape[0]
         step = min(r, TILE)
-        count = OUTER if by_planes else 2
-        lead = (2, inner) if by_planes else (inner, OUTER)
+        count = 2
+        lead = (2, 2, inner) if by_planes else (inner, OUTER)
 
         def kernel(cot_ref, *refs):
             out_refs, (top_ref, wide_ref) = refs[:count], refs[count:]
@@ -159,7 +159,7 @@
             for p in range(n_dp):
                 k, i, other = relative(p)
                 block = wide_ref[p * width : (p + 1) * width, :].astype(jnp.bfloat16)
-                which, at = (k, (other, i)) if by_planes else (other, (i, k))
+                which, at = (1 - (k >> 1), (1 - (k & 1), other, i)) if by_planes else (other, (i, k))
                 for n in range(count):
 
                     @pl.when(which == n)
@@ -172,7 +172,9 @@
             cot,
             grid=(r // step,),
             in_specs=[pl.BlockSpec((step, D), lambda s: (s, 0))],
-            out_specs=[pl.BlockSpec((*lead, width, step), lambda s: (0, 0, 0, s))] * count
+            out_specs=[
+                pl.BlockSpec((*lead, width, step), lambda s: (*(0 for _ in lead), 0, s))
+            ] * count
             + [pl.BlockSpec((8, LANES), lambda s: (0, 0))],
             scratch_shapes=[pltpu.VMEM((D, step), jnp.float32)],
         )
@@ -228,26 +230,25 @@
         )
 
     def multiply_half(other, pieces, scaled):
-        _, _, _, r = pieces[0].shape
-        f = scaled[0].shape[0]
+        r, f = pieces[0].shape[-1], scaled[0].shape[0]
         count = len(pieces)
 
         def kernel(*refs):
             piece_refs, scaled_refs, out_ref = refs[:count], refs[count:-1], refs[-1]
             for i in range(inner):
-                total = dot(piece_refs[0][0, i], scaled_refs[0][...], NT)
+                total = dot(piece_refs[0][0, 0, i], scaled_refs[0][...], NT)
                 for piece_ref, scaled_ref in zip(piece_refs[1:], scaled_refs[1:]):
-                    total = total + dot(piece_ref[0, i], scaled_ref[...], NT)
-                out_ref[i] = total
+                    total = total + dot(piece_ref[0, 0, i], scaled_ref[...], NT)
+                out_ref[0, i] = total
 
         return call(
             kernel,
-            array((inner, width, f), jnp.float32),
+            array((2, inner, width, f), jnp.float32),
             *pieces, *scaled,
-            grid=(1,),
-            in_specs=[pl.BlockSpec((1, inner, width, r), lambda s: (other, 0, 0, 0))] * count
+            grid=(2,),
+            in_specs=[pl.BlockSpec((1, 1, inner, width, r), lambda s: (s, other, 0, 0, 0))] * count
             + [pl.BlockSpec((f, r), lambda s: (0, 0))] * count,
-            out_specs=pl.BlockSpec((inner, width, f), lambda s: (0, 0, 0)),
+            out_specs=pl.BlockSpec((1, inner, width, f), lambda s: (s, 0, 0, 0)),
         )
 
     def scale_rows(act, scales):
@@ -305,7 +306,8 @@
                 for k in range(OUTER):
                     for other in range(2):
                         for i in range(inner):
-                            block = piece_refs[k][other, i].astype(jnp.float32)
+                            block = piece_refs[1 - (k >> 1)][1 - (k & 1), other, i]
+                            block = block.astype(jnp.float32)
                             wide_ref[owner(k, i, other)] = block
                 flat = wide_ref[...].reshape(D, size).astype(jnp.bfloat16)
                 product = dot(weight_ref[...], flat, NN)
@@ -389,10 +391,9 @@
                 if i or o
             ]
 
-        acts = [from_tensor(act, -j) for j, act in enumerate(step(lambda act: cut_acts(act, r), act_fake), 1)]
+        acts = [from_tensor(act, -j) for j, act in enumerate(step(lambda a: cut_acts(a, r), act_fake), 1)]
         planes, top_student = step(lambda cot: turn(cot, True), cot_student)
-        order = (3, 1, 2, 0)
-        others = {k: [from_tensor(planes[k], j) for j in range(1, n_tensor)] for k in order}
+        others = [[from_tensor(planes[0], j) for j in range(1, n_tensor)]]
         cores, top_fake = step(lambda cot: turn(cot, False), cot_fake)
         cores = [core.reshape(-1, r) for core in cores]
 
@@ -403,15 +404,17 @@
             lambda *values: prepare(*values, r),
             act_student, act_fake, top_student, top_fake, scales,
         )
+        pairs = []
         got = gather_planes(bounds)
-        sends, keeps = [], []
-        for j in range(n_tensor):
-            if j:
-                scaled = step(scale_rows, acts[j - 1], scales)
-            sends.append(to_core(step(lambda a, b: multiply_rows([a], [b]), cores[1], scaled)))
-            keeps.append(step(lambda a, b: multiply_rows([a], [b]), cores[0], scaled))
+        scaled_fake = [scaled] + [step(scale_rows, act, scales) for act in acts]
         bounds = reduced(jnp.maximum, bounds, got)
-        bounds = reduced(jnp.maximum, bounds, gather_chips(bounds))
+        got = gather_chips(bounds)
+        for scaled in scaled_fake:
+            send = to_core(step(lambda a, b: multiply_rows([a], [b]), cores[1], scaled))
+            keep = step(lambda a, b: multiply_rows([a], [b]), cores[0], scaled)
+            if not pairs:
+                bounds = reduced(jnp.maximum, bounds, got)
+            pairs.append((keep, send))
 
         def factors(bounds):
             bounds = jnp.maximum(bounds, 1e-30) * (1.01 * count * n_dp / HALF_LIMIT)
@@ -425,74 +428,19 @@
         def widen(value, net):
             return value.astype(jnp.float32) * grow[net]
 
-        halves = ((2, 3), (0, 1))
+        def add_widened(total, values, net):
+            for value in values:
+                total = total + widen(value, net)
+            return total
 
         def fake_middle(keep, send):
             both = (keep + send).reshape(inner, OUTER, width, f)
-            sent = [
-                [shrink(both[i, lo : hi + 1], 1) for i in range(1, inner)] for lo, hi in halves
-            ]
-            return sent, [both[0, lo : hi + 1] for lo, hi in halves]
-
-        def start_middle(keep, send):
-            sent, mine = step(fake_middle, keep, send)
-            return [
-                (own, [to_middle(value, i) for i, value in enumerate(values, 1)])
-                for own, values in zip(mine, sent)
-            ]
-
-        kept, crossing, to_sum = {}, {}, []
-
-        def multiply(k):
-            def half(other, *operands):
-                pieces, scaled = operands[:n_tensor], operands[n_tensor:]
-                return multiply_half(other, pieces, scaled)
-
-            operands = [planes[k], *others[k], *scaled_student]
-            send = to_core(step(functools.partial(half, 1), *operands))
-            kept[k] = step(functools.partial(half, 0), *operands), send
-
-        def cross_middle(k):
-            def work(keep, send):
-                both = keep + send
-                return [shrink(both[i], 0) for i in range(1, inner)], both[0]
-
-            sent, own = step(work, *kept[k])
-            crossing[k] = own, [to_middle(value, i) for i, value in enumerate(sent, 1)]
-
-        def cross_planes(k):
-            def work(own, *got):
-                for value in got:
-                    own = own + widen(value, 0)
-                return shrink(own, 0) if k else own
-
-            own, got = crossing[k]
-            value = step(work, own, *got)
-            to_sum.append(to_plane(value, k) if k else value)
-
-        fake_sums = [[] for _ in range(n_tensor)]
-
-        def fake_planes(j, part):
-            lo, hi = halves[part]
-
-            def work(own, *got):
-                for value in got:
-                    own = own + widen(value, 1)
-                return [shrink(own[k - lo], 1) if k else own[0] for k in range(hi, lo - 1, -1)]
-
-            own, got = middles[j][part]
-            values = step(work, own, *got)
-            for k, value in zip(range(hi, lo - 1, -1), values):
-                fake_sums[j].append(to_plane(value, k) if k else value)
-
-        def fake_total(j):
-            def work(*values):
-                total = values[-1]
-                for value in values[:-1]:
-                    total = total + widen(value, 1)
-                return total
-
-            return step(work, *fake_sums[j])
+            return [shrink(both[i], 1) for i in range(1, inner)], both[0]
+
+        middles = []
+        for keep, send in pairs:
+            sent, own = step(fake_middle, keep, send)
+            middles.append((own, [to_middle(value, i) for i, value in enumerate(sent, 1)]))
 
         def back(whole, net, pieces, j, low, size):
             weight = (weight_student, weight_fake)[net]
@@ -506,66 +454,86 @@
 
             return step(work, weight, *pieces, *has)
 
-        multiply(3)
-        middles = [start_middle(keep, send) for keep, send in zip(keeps, sends)]
-        fake_planes(0, 0)
-        fake_planes(0, 1)
+        fake_sums = {}
+
+        def fake_planes(j):
+            def work(own, *got):
+                own = add_widened(own, got, 1)
+                return [shrink(own[k], 1) for k in (3, 1, 2)], own[0]
+
+            sent, own = step(work, middles[j][0], *middles[j][1])
+            fake_sums[j] = own, [to_plane(value, k) for k, value in zip((3, 1, 2), sent)]
+
+        def fake_total(j):
+            own, got = fake_sums[j]
+            return step(lambda own, *got: add_widened(own, got, 1), own, *got)
+
+        kept = {}
+
+        def multiply(n):
+            def half(other, *operands):
+                return multiply_half(other, operands[:n_tensor], operands[n_tensor:])
+
+            operands = [planes[n], *others[n], *scaled_student]
+            send = to_core(step(functools.partial(half, 1), *operands))
+            kept[n] = step(functools.partial(half, 0), *operands), send
+
+        second = step(lambda value: value, planes[1])
+        others.append([from_tensor(second, j) for j in range(1, n_tensor)])
         back_student = back(None, 0, [cot_student], 0, 0, r)
-        multiply(1)
-        cross_middle(3)
+        back_fake = back(None, 1, [cot_fake], 0, 0, r)
+        multiply(0)
+        fake_planes(0)
+
+        def first_middle(keep, send):
+            both = keep + send
+            return [shrink(both[:, i], 0) for i in range(1, inner)], both[:, 0]
+
+        sent, own = step(first_middle, *kept[0])
+        got = [to_middle(value, i) for i, value in enumerate(sent, 1)]
+        fake_mine = fake_total(0)
         for j in range(1, n_tensor):
-            fake_planes(j, 0)
-        back_fake = back(None, 1, [cot_fake], 0, 0, r)
-        for j in range(1, n_tensor):
-            fake_planes(j, 1)
-        multiply(2)
-        cross_middle(1)
-        cross_planes(3)
+            fake_planes(j)
+
+        def first_planes(own, *got):
+            own = add_widened(own, got, 0)
+            return shrink(own[0], 0), shrink(own[1], 0)
+
+        sent = step(first_planes, own, *got)
+        first_got = [to_plane(value, k) for k, value in zip((3, 2), sent)]
         fake_others = [fake_total(j) for j in range(1, n_tensor)]
         fake_got = [from_tensor(value, j) for j, value in enumerate(fake_others, 1)]
-
-        part = r // 4
-        cuts = ((0, part), (part, 3 * part), (3 * part, r)) if part % LANES == 0 else ((0, r),)
-        raw = []
-
-        def send_raw(lo, hi):
-            rows = step(lambda cot: cot[lo:hi], cot_fake)
-            raw.append([from_tensor(rows, j) for j in range(1, n_tensor)])
-
-        send_raw(*cuts[0])
-        cross_middle(2)
-        cross_planes(1)
-        fake_mine = fake_total(0)
-        cross_planes(2)
-        multiply(0)
-        cross_middle(0)
-
-        def student_partial(*values):
-            total = widen(values[0], 0)
-            for value in values[1:]:
-                total = total + widen(value, 0)
-            return total
-
-        total_student = step(student_partial, *to_sum)
-        to_sum.clear()
+        multiply(1)
+
+        def second_middle(keep, send):
+            both = keep + send
+            sent = [[shrink(both[n, i], 0) for i in range(1, inner)] for n in range(2)]
+            return sent, both[0, 0], both[1, 0]
+
+        sent, own_next, own = step(second_middle, *kept[1])
+        got_next, got = (
+            [to_middle(value, i) for i, value in enumerate(values, 1)] for values in sent
+        )
+        next_sent = step(
+            lambda own, *got: shrink(add_widened(own, got, 0), 0), own_next, *got_next
+        )
+        next_got = to_plane(next_sent, 1)
         total_fake = reduced(jnp.add, fake_mine, fake_got)
-        cross_planes(0)
-        total_student = reduced(jnp.add, total_student, to_sum)
+        total_student = step(
+            lambda own, *got: add_widened(own, got, 0), own, *got, *first_got
+        )
+        total_student = step(
+            lambda own, *got: add_widened(own, got, 0), total_student, next_got
+        )
         squares = step(norms, total_student, total_fake)
+        squares = reduced(
+            jnp.add, squares, [from_tensor(squares, j) for j in range(1, n_tensor)]
+        )
+
+        raw_sent = step(lambda cot: cot, cot_fake)
+        raw = [from_tensor(raw_sent, j) for j in range(1, n_tensor)]
         squares = reduced(jnp.add, squares, gather_planes(squares))
         squares = reduced(jnp.add, squares, gather_chips(squares))
-        got = [from_tensor(squares, j) for j in range(1, n_tensor)]
-        for lo, hi in cuts[1:]:
-            send_raw(lo, hi)
-
-        def back_raw(n):
-            nonlocal back_fake
-            lo, hi = cuts[n]
-            for j in range(1, n_tensor):
-                back_fake = back(back_fake, 1, [raw[n][j - 1]], j, lo, hi - lo)
-
-        back_raw(0)
-        squares = reduced(jnp.add, squares, got)
 
         states = (
             master_student, first_student, second_student, master_fake, first_fake, second_fake,
@@ -580,21 +548,20 @@
         def spread_middle(k, value):
             mine[k] = [value] + [to_middle(value, -i) for i in range(1, inner)]
 
+        spread_middle(0, own)
         planes_got = {k: to_plane(own, -k) for k in (1, 3, 2)}
-        spread_middle(0, own)
         for j in range(1, n_tensor):
-            pieces = [others[k][j - 1] for k in range(OUTER)]
+            pieces = [group[j - 1] for group in others]
             back_student = back(back_student, 0, pieces, j, 0, r)
         spread_middle(1, step(lambda value: value, planes_got[1]))
         spread_middle(3, step(lambda value: value, planes_got[3]))
-
         first_half = step(lambda *values: jnp.stack(values), *mine[0], *mine[1])
         theirs = [to_core(first_half)]
         spread_middle(2, step(lambda value: value, planes_got[2]))
         second_half = step(lambda *values: jnp.stack(values), *mine[2], *mine[3])
         theirs.append(to_core(second_half))
-        for n in range(1, len(cuts)):
-            back_raw(n)
+        for j in range(1, n_tensor):
+            back_fake = back(back_fake, 1, [raw[j - 1]], j, 0, r)
         stacks = [first_half, second_half, *theirs]
         params = [step(lambda *values: spread(values, n), *stacks) for n in range(2)]
 

time: 272 us -> 221 us (0.81)
  waiting for transfers between devices: 141 us -> 79.4 us
  Pallas kernels: 48.7 us -> 58.1 us
  other arithmetic: 19.6 us -> 25.4 us
  starting transfers between devices: 56.3 us -> 53.4 us
    ppermute x10 -> x6, waiting for transfers between devices: 50.5 us -> 8.25 us  [from_tensor(): return lax.ppermute(value, 'tensor', perm)]
    ppermute x44 -> x39, waiting for transfers between devices: 90.3 us -> 71.2 us  [move_dp(): return lax.ppermute(value, 'dp', perm)]
    pallas_call x27 -> x21, Pallas kernels: 48.7 us -> 58.1 us  [call(): pl.pallas_call(kernel, out_shape=out_shape, compiler_params=pltpu.Compile...]
    ppermute x10 -> x6, starting transfers between devices: 12.8 us -> 8.15 us  [from_tensor(): return lax.ppermute(value, 'tensor', perm)]
    slice x0 -> x2, other arithmetic: none -> 4.65 us  [fake_middle(): return ([shrink(both[i], 1) for i in range(1, inner)], both[0])]
    squeeze x6 -> x1, other arithmetic: 4.33 us -> 0.86 us  [first_middle(): return ([shrink(both[:, i], 0) for i in range(1, inner)], both[:, 0])]
    add x12 -> x9, other arithmetic: 6.74 us -> 9.56 us  [the longest x7 9.17 us: add_widened(): total = total + widen(value, net)]
    convert_element_type x7 -> x5, other arithmetic: 7.11 us -> 5.17 us  [shrink(): return (value * fit[net]).astype(jnp.float16)]
  transfers between devices with their start and end apart: 54 -> 45, of which waited for: 25 -> 20; matrix products, arithmetic and copies ran while one was open for 8% -> 11% of each run, Pallas kernels for 14% -> 21%
where the time goes in v5:
time: 221 us
  waiting for transfers between devices  79.4 us (36%)
  Pallas kernels  58.1 us (26%)
  starting transfers between devices  53.4 us (24%)
  other arithmetic  25.4 us (11%)
  local copies, waits for them, and re-layouts  2.91 us (1%)
    ppermute x39, waiting for transfers between devices, move_dp(): return lax.ppermute(value, 'dp', perm)  71.2 us
    pallas_call x21, Pallas kernels, call(): pl.pallas_call(kernel, out_shape=out_shape, compiler_params=pltpu.Compile...  58.1 us
    ppermute x39, starting transfers between devices, move_dp(): return lax.ppermute(value, 'dp', perm)  45.3 us
    add x7, other arithmetic, add_widened(): total = total + widen(value, net)  9.17 us
    ppermute x6, waiting for transfers between devices, from_tensor(): return lax.ppermute(value, 'tensor', perm)  8.25 us
    ppermute x6, starting transfers between devices, from_tensor(): return lax.ppermute(value, 'tensor', perm)  8.15 us
    convert_element_type x5, other arithmetic, shrink(): return (value * fit[net]).astype(jnp.float16)  5.17 us
    slice x2, other arithmetic, fake_middle(): return ([shrink(both[i], 1) for i in range(1, inner)], both[0])  4.65 us
  transfers between devices with their start and end apart: 45, of which 20 were waited for; matrix products, arithmetic and copies ran while one was open for 11% of the time, Pallas kernels for 21%

profile of v5, /device:TPU:0, one launch (start us, length us, event | category | flops | bytes accessed | tf_op | source)
XLA Modules:
  0.0 220.6 jit_solution(3829388115908389193)
XLA Ops:
  3.0 3.0 %collective-permute-start.1 = (bf16[608,512]{1,0:T(8,128)(2,1)}, bf16[608,512]{1,0:T(8,128)(2,1)}, u32[]{:S(2)}, u32[]{:S(2)}) collective-permute-start(bf16[608,512]{1,0:T(8,128)(2,1)} %shard_map.204), channel_id=1, source_target_pairs={{0,1},{1,0},{2,3},{3,2},{4,5},{5,4},{6,7},{7,6},{8,9},{9,8},{10,11... | collective-permute-start | bytes 1867784 | tf_op jit(solution)/shard_map/ppermute | solution.py:91
  6.0 3.2 %shard_map.205 = (bf16[2,2,2,152,512]{4,3,2,1,0:T(8,128)(2,1)}, bf16[2,2,2,152,512]{4,3,2,1,0:T(8,128)(2,1)}, f32[8,128]{1,0:T(8,128)S(1)}) custom-call(bf16[512,2432]{1,0:T(8,128)(2,1)S(1)} %copy-done.4), custom_call_target="tpu_custom_call" | custom-call | flops 99999997952 | tf_op jit(solution)/shard_map/pallas_call | solution.py:56
  9.2 3.7 %shard_map.206 = (bf16[2,4,152,512]{3,2,1,0:T(8,128)(2,1)S(1)}, bf16[2,4,152,512]{3,2,1,0:T(8,128)(2,1)S(1)}, f32[8,128]{1,0:T(8,128)S(1)}) custom-call(bf16[512,2432]{1,0:T(8,128)(2,1)} %refs_0_.1), custom_call_target="tpu_custom_call" | custom-call | flops 99999997952 | tf_op jit(solution)/shard_map/pallas_call | solution.py:56
  16.0 2.6 %collective-permute-start.3 = (f32[8,128]{1,0:T(8,128)S(1)}, f32[8,128]{1,0:T(8,128)S(1)}, u32[]{:S(2)}, u32[]{:S(2)}) collective-permute-start(f32[8,128]{1,0:T(8,128)S(1)} %get-tuple-element.172), channel_id=1, source_target_pairs={{0,16},{2,18},{4,20},{6,22},{8,24},{10,26},{12,28},{14,30},{16,0},... | collective-permute-start | bytes 12296 | tf_op jit(solution)/shard_map/ppermute | solution.py:78
  24.7 3.1 %shard_map.209 = f32[1216,608]{1,0:T(8,128)} custom-call(bf16[1216,512]{1,0:T(8,128)(2,1)S(1)} %bitcast.72, bf16[608,512]{1,0:T(8,128)(2,1)S(1)} %get-tuple-element.180.refs_1_), custom_call_target="tpu_custom_call" | custom-call | flops 99999997952 | tf_op jit(solution)/shard_map/pallas_call | solution.py:56
  46.7 3.2 %shard_map.213.refs_2_ = bf16[608,1024]{1,0:T(8,128)(2,1)} custom-call(f32[2]{0:T(128)S(1)} %copy-done.16, bf16[608,2432]{1,0:T(8,128)(2,1)S(1)} %copy-done, bf16[512,2432]{1,0:T(8,128)(2,1)S(1)} %copy-done.5), custom_call_target="tpu_custom_call" | custom-call | flops 99999997952 | tf_op jit(solution)/shard_map/pallas_call | solution.py:56
  49.9 4.4 %shard_map.214.refs_1_ = bf16[608,1024]{1,0:T(8,128)(2,1)} custom-call(f32[2]{0:T(128)S(1)} %copy-done.16, bf16[608,2432]{1,0:T(8,128)(2,1)S(1)} %copy-done.2, bf16[512,2432]{1,0:T(8,128)(2,1)} %refs_0_.1), custom_call_target="tpu_custom_call" | custom-call | flops 99999997952 | tf_op jit(solution)/shard_map/pallas_call | solution.py:56
  54.2 3.0 %shard_map.215 = f32[2,2,152,608]{3,2,1,0:T(8,128)S(1)} custom-call(bf16[2,2,2,152,512]{4,3,2,1,0:T(8,128)(2,1)} %get-tuple-element.205.refs_0_, bf16[2,2,2,152,512]{4,3,2,1,0:T(8,128)(2,1)} %collective-permute-done.refs_1_.refs_0_, bf16[608,512]{1,0:T(8,128)(2,1)S(1)} %get-tuple-element.231.refs_2_, bf16[608,512]{1,0:T(8,128)(2,1)S(1)} %get-tuple-element.232.refs_3_), custom_call_target="tpu_custom_call" | custom-call | flops 99999997952 | tf_op jit(solution)/shard_map/pallas_call | solution.py:56
  57.5 3.1 %shard_map.216 = f32[2,2,152,608]{3,2,1,0:T(8,128)S(1)} custom-call(bf16[2,2,2,152,512]{4,3,2,1,0:T(8,128)(2,1)} %get-tuple-element.205.refs_0_, bf16[2,2,2,152,512]{4,3,2,1,0:T(8,128)(2,1)} %collective-permute-done.refs_1_.refs_0_, bf16[608,512]{1,0:T(8,128)(2,1)S(1)} %get-tuple-element.231.refs_2_, bf16[608,512]{1,0:T(8,128)(2,1)S(1)} %get-tuple-element.232.refs_3_), custom_call_target="tpu_custom_call" | custom-call | flops 99999997952 | tf_op jit(solution)/shard_map/pallas_call | solution.py:56
  64.0 4.4 %collective-permute-start.13 = (f16[152,608]{1,0:T(8,128)(2,1)S(1)}, f16[152,608]{1,0:T(8,128)(2,1)S(1)}, u32[]{:S(2)}, u32[]{:S(2)}) collective-permute-start(f16[152,608]{1,0:T(8,128)(2,1)S(1)} %get-tuple-element.316), channel_id=1, source_target_pairs={{0,24},{2,26},{4,28},{6,30},{8,0},{10,2},{12,4},{14,6},{16,8},{18,... | collective-permute-start | bytes 554504 | tf_op jit(solution)/shard_map/ppermute | solution.py:78
  70.6 3.1 %collective-permute-done.13 = f16[152,608]{1,0:T(8,128)(2,1)S(1)} collective-permute-done((f16[152,608]{1,0:T(8,128)(2,1)S(1)}, f16[152,608]{1,0:T(8,128)(2,1)S(1)}, u32[]{:S(2)}, u32[]{:S(2)}) %collective-permute-start.13) | collective-permute-done | bytes 184864 | tf_op jit(solution)/shard_map/ppermute | solution.py:78
  75.3 3.6 %collective-permute-done.14 = f16[152,608]{1,0:T(8,128)(2,1)S(1)} collective-permute-done((f16[152,608]{1,0:T(8,128)(2,1)S(1)}, f16[152,608]{1,0:T(8,128)(2,1)S(1)}, u32[]{:S(2)}, u32[]{:S(2)}) %collective-permute-start.14) | collective-permute-done | bytes 184864 | tf_op jit(solution)/shard_map/ppermute | solution.py:78
  78.9 6.2 %collective-permute-done.15 = f16[152,608]{1,0:T(8,128)(2,1)S(1)} collective-permute-done((f16[152,608]{1,0:T(8,128)(2,1)S(1)}, f16[152,608]{1,0:T(8,128)(2,1)S(1)}, u32[]{:S(2)}, u32[]{:S(2)}) %collective-permute-start.15) | collective-permute-done | bytes 184864 | tf_op jit(solution)/shard_map/ppermute | solution.py:78
  89.3 2.8 %collective-permute-start.17 = (f16[152,608]{1,0:T(8,128)(2,1)S(1)}, f16[152,608]{1,0:T(8,128)(2,1)S(1)}, u32[]{:S(2)}, u32[]{:S(2)}) collective-permute-start(f16[152,608]{1,0:T(8,128)(2,1)S(1)} %get-tuple-element.312), channel_id=1, source_target_pairs={{0,24},{2,26},{4,28},{6,30},{8,0},{10,2},{12,4},{14,6},{16,8},{18,... | collective-permute-start | bytes 554504 | tf_op jit(solution)/shard_map/ppermute | solution.py:78
  95.1 6.2 %collective-permute-done.17 = f16[152,608]{1,0:T(8,128)(2,1)S(1)} collective-permute-done((f16[152,608]{1,0:T(8,128)(2,1)S(1)}, f16[152,608]{1,0:T(8,128)(2,1)S(1)}, u32[]{:S(2)}, u32[]{:S(2)}) %collective-permute-start.17) | collective-permute-done | bytes 184864 | tf_op jit(solution)/shard_map/ppermute | solution.py:78
  101.7 5.6 %collective-permute-done.19 = f16[152,608]{1,0:T(8,128)(2,1)S(1)} collective-permute-done((f16[152,608]{1,0:T(8,128)(2,1)S(1)}, f16[152,608]{1,0:T(8,128)(2,1)S(1)}, u32[]{:S(2)}, u32[]{:S(2)}) %collective-permute-start.19) | collective-permute-done | bytes 184864 | tf_op jit(solution)/shard_map/ppermute | solution.py:78
  108.8 3.0 %shard_map.217 = f32[2,2,152,608]{3,2,1,0:T(8,128)S(1)} custom-call(bf16[2,2,2,152,512]{4,3,2,1,0:T(8,128)(2,1)} %get-tuple-element.229.refs_0_, bf16[2,2,2,152,512]{4,3,2,1,0:T(8,128)(2,1)} %collective-permute-done.10.refs_1_, bf16[608,512]{1,0:T(8,128)(2,1)S(1)} %get-tuple-element.231.refs_2_, bf16[608,512]{1,0:T(8,128)(2,1)S(1)} %get-tuple-element.232.refs_3_), custom_call_target="tpu_custom_call" | custom-call | flops 99999997952 | tf_op jit(solution)/shard_map/pallas_call | solution.py:56
  111.9 3.0 %shard_map.218 = f32[2,2,152,608]{3,2,1,0:T(8,128)S(1)} custom-call(bf16[2,2,2,152,512]{4,3,2,1,0:T(8,128)(2,1)} %get-tuple-element.229.refs_0_, bf16[2,2,2,152,512]{4,3,2,1,0:T(8,128)(2,1)} %collective-permute-done.10.refs_1_, bf16[608,512]{1,0:T(8,128)(2,1)S(1)} %get-tuple-element.231.refs_2_, bf16[608,512]{1,0:T(8,128)(2,1)S(1)} %get-tuple-element.232.refs_3_), custom_call_target="tpu_custom_call" | custom-call | flops 99999997952 | tf_op jit(solution)/shard_map/pallas_call | solution.py:56
  118.0 3.5 %collective-permute-start.23 = (f16[152,608]{1,0:T(8,128)(2,1)S(1)}, f16[152,608]{1,0:T(8,128)(2,1)S(1)}, u32[]{:S(2)}, u32[]{:S(2)}) collective-permute-start(f16[152,608]{1,0:T(8,128)(2,1)S(1)} %copy-done.23), channel_id=1, source_target_pairs={{0,24},{2,26},{4,28},{6,30},{8,0},{10,2},{12,4},{14,6},{16,8},{18,... | collective-permute-start | bytes 554504 | tf_op jit(solution)/shard_map/ppermute | solution.py:78
  125.2 3.5 %collective-permute-done.25 = f32[152,608]{1,0:T(8,128)S(1)} collective-permute-done((f32[152,608]{1,0:T(8,128)S(1)}, f32[152,608]{1,0:T(8,128)S(1)}, u32[]{:S(2)}, u32[]{:S(2)}) %collective-permute-start.25) | collective-permute-done | bytes 369696 | tf_op jit(solution)/shard_map/ppermute | solution.py:91
  128.7 8.2 %collective-permute-done.24 = f16[152,608]{1,0:T(8,128)(2,1)S(1)} collective-permute-done((f16[152,608]{1,0:T(8,128)(2,1)S(1)}, f16[152,608]{1,0:T(8,128)(2,1)S(1)}, u32[]{:S(2)}, u32[]{:S(2)}) %collective-permute-start.24) | collective-permute-done | bytes 184864 | tf_op jit(solution)/shard_map/ppermute | solution.py:78
  145.2 2.9 %collective-permute-start.31 = (f32[8,128]{1,0:T(8,128)S(1)}, f32[8,128]{1,0:T(8,128)S(1)}, u32[]{:S(2)}, u32[]{:S(2)}) collective-permute-start(f32[8,128]{1,0:T(8,128)S(1)} %add.101), channel_id=1, source_target_pairs={{0,24},{2,26},{4,28},{6,30},{8,0},{10,2},{12,4},{14,6},{16,8},{18,... | collective-permute-start | bytes 12296 | tf_op jit(solution)/shard_map/ppermute | solution.py:78
  155.3 4.1 %collective-permute-start.38 = (bf16[2,152,608]{2,1,0:T(8,128)(2,1)S(1)}, bf16[2,152,608]{2,1,0:T(8,128)(2,1)S(1)}, u32[]{:S(2)}, u32[]{:S(2)}) collective-permute-start(bf16[2,152,608]{2,1,0:T(8,128)(2,1)S(1)} %get-tuple-element.274), channel_id=1, source_target_pairs={{0,24},{2,26},{4,28},{6,30},{8,0},{10,2},{12,4},{14,6},{16,8},{18,... | collective-permute-start | bytes 1109000 | tf_op jit(solution)/shard_map/ppermute | solution.py:78
  160.9 4.7 %shard_map.221 = bf16[608,1024]{1,0:T(8,128)(2,1)} custom-call(f32[2]{0:T(128)S(1)} %copy-done.17, bf16[608,2432]{1,0:T(8,128)(2,1)S(1)} %copy-done.1, bf16[2,2,2,152,512]{4,3,2,1,0:T(8,128)(2,1)} %collective-permute-done.refs_1_.refs_0_, bf16[2,2,2,152,512]{4,3,2,1,0:T(8,128)(2,1)} %collective-permute-done.10.refs_1_, ...), custom_call_target="tpu_custom_call", output_to_operand_aliasing={{}: (4, {})} | custom-call | flops 99999997952 | tf_op jit(solution)/shard_map/pallas_call | solution.py:56
  165.5 3.3 %collective-permute-done.38 = bf16[2,152,608]{2,1,0:T(8,128)(2,1)S(1)} collective-permute-done((bf16[2,152,608]{2,1,0:T(8,128)(2,1)S(1)}, bf16[2,152,608]{2,1,0:T(8,128)(2,1)S(1)}, u32[]{:S(2)}, u32[]{:S(2)}) %collective-permute-start.38) | collective-permute-done | bytes 369696 | tf_op jit(solution)/shard_map/ppermute | solution.py:78
  171.2 6.4 %collective-permute-done.40 = bf16[2,152,608]{2,1,0:T(8,128)(2,1)S(1)} collective-permute-done((bf16[2,152,608]{2,1,0:T(8,128)(2,1)S(1)}, bf16[2,152,608]{2,1,0:T(8,128)(2,1)S(1)}, u32[]{:S(2)}, u32[]{:S(2)}) %collective-permute-start.40) | collective-permute-done | bytes 369696 | tf_op jit(solution)/shard_map/ppermute | solution.py:78
  179.4 14.3 %collective-permute-done.36 = bf16[2,152,608]{2,1,0:T(8,128)(2,1)S(1)} collective-permute-done((bf16[2,152,608]{2,1,0:T(8,128)(2,1)S(1)}, bf16[2,152,608]{2,1,0:T(8,128)(2,1)S(1)}, u32[]{:S(2)}, u32[]{:S(2)}) %collective-permute-start.36) | collective-permute-done | bytes 369696 | tf_op jit(solution)/shard_map/ppermute | solution.py:78
  195.2 9.4 %collective-permute-done.41 = bf16[2,152,608]{2,1,0:T(8,128)(2,1)S(1)} collective-permute-done((bf16[2,152,608]{2,1,0:T(8,128)(2,1)S(1)}, bf16[2,152,608]{2,1,0:T(8,128)(2,1)S(1)}, u32[]{:S(2)}, u32[]{:S(2)}) %collective-permute-start.41) | collective-permute-done | bytes 369696 | tf_op jit(solution)/shard_map/ppermute | solution.py:78
  205.1 2.8 %collective-permute-done.35.refs_0_ = bf16[512,2432]{1,0:T(8,128)(2,1)} collective-permute-done((bf16[512,2432]{1,0:T(8,128)(2,1)}, bf16[512,2432]{1,0:T(8,128)(2,1)}, u32[]{:S(2)}, u32[]{:S(2)}) %collective-permute-start.35) | collective-permute-done | bytes 2490400 | tf_op jit(solution)/shard_map/ppermute | solution.py:91
  207.9 4.3 %shard_map.222 = bf16[608,1024]{1,0:T(8,128)(2,1)} custom-call(f32[2]{0:T(128)S(1)} %copy-done.17, bf16[608,2432]{1,0:T(8,128)(2,1)S(1)} %copy-done.3, bf16[512,2432]{1,0:T(8,128)(2,1)} %collective-permute-done.35.refs_0_, bf16[608,1024]{1,0:T(8,128)(2,1)} %shard_map.214.refs_1_), custom_call_target="tpu_custom_call", output_to_operand_aliasing={{}: (3, {})} | custom-call | flops 99999997952 | tf_op jit(solution)/shard_map/pallas_call | solution.py:56
  212.3 4.1 %shard_map.223 = bf16[608,2432]{1,0:T(8,128)(2,1)} custom-call(bf16[4,2,152,608]{3,2,1,0:T(8,128)(2,1)S(1)} %pad_maximum_fusion.refs_0_, bf16[4,2,152,608]{3,2,1,0:T(8,128)(2,1)S(1)} %pad_maximum_fusion.1.refs_1_, bf16[4,2,152,608]{3,2,1,0:T(8,128)(2,1)S(1)} %collective-permute-done.43.refs_2_, bf16[4,2,152,608]{3,2,1,0:T(8,128)(2,1)S(1)} %collective-permute-done.44.refs_3_), custom_call_target="tpu_custom_call" | custom-call | flops 99999997952 | tf_op jit(solution)/shard_map/pallas_call | solution.py:56
  216.4 4.1 %shard_map.224 = bf16[608,2432]{1,0:T(8,128)(2,1)} custom-call(bf16[4,2,152,608]{3,2,1,0:T(8,128)(2,1)S(1)} %pad_maximum_fusion.refs_0_, bf16[4,2,152,608]{3,2,1,0:T(8,128)(2,1)S(1)} %pad_maximum_fusion.1.refs_1_, bf16[4,2,152,608]{3,2,1,0:T(8,128)(2,1)S(1)} %collective-permute-done.43.refs_2_, bf16[4,2,152,608]{3,2,1,0:T(8,128)(2,1)S(1)} %collective-permute-done.44.refs_3_), custom_call_target="tpu_custom_call" | custom-call | flops 99999997952 | tf_op jit(solution)/shard_map/pallas_call | solution.py:56
  (165 shorter events, 76.3 us)
Async XLA Ops:
  3.0 17.5 %collective-permute-start.1 = (bf16[608,512]{1,0:T(8,128)(2,1)}, bf16[608,512]{1,0:T(8,128)(2,1)}, u32[]{:S(2)}, u32[]{:S(2)}) collective-permute-start(bf16[608,512]{1,0:T(8,128)(2,1)} %shard_map.204), channel_id=1, source_target_pairs={{0,1},{1,0},{2,3},{3,2},{4,5},{5,4},{6,7},{7,6},{8,9},{9,8},{10,11... | collective-permute-start | bytes 1867784 | tf_op jit(solution)/shard_map/ppermute | solution.py:91
  14.4 7.3 %collective-permute-start.2 = (f32[8,128]{1,0:T(8,128)S(1)}, f32[8,128]{1,0:T(8,128)S(1)}, u32[]{:S(2)}, u32[]{:S(2)}) collective-permute-start(f32[8,128]{1,0:T(8,128)S(1)} %get-tuple-element.172), channel_id=1, source_target_pairs={{0,8},{2,10},{4,12},{6,14},{8,16},{10,18},{12,20},{14,22},{16,24},... | collective-permute-start | bytes 12296 | tf_op jit(solution)/shard_map/ppermute | solution.py:78
  20.0 34.3 %collective-permute-start = (bf16[2,2,2,152,512]{4,3,2,1,0:T(8,128)(2,1)}, bf16[2,2,2,152,512]{4,3,2,1,0:T(8,128)(2,1)}, u32[]{:S(2)}, u32[]{:S(2)}) collective-permute-start(bf16[2,2,2,152,512]{4,3,2,1,0:T(8,128)(2,1)} %get-tuple-element.205.refs_0_), channel_id=1, source_target_pairs={{0,1},{1,0},{2,3},{3,2},{4,5},{5,4},{6,7},{7,6},{8,9},{9,8},{10,11... | collective-permute-start | bytes 3735560 | tf_op jit(solution)/shard_map/ppermute | solution.py:91
  22.8 7.1 %collective-permute-start.6 = (f32[8,128]{1,0:T(8,128)}, f32[8,128]{1,0:T(8,128)}, u32[]{:S(2)}, u32[]{:S(2)}) collective-permute-start(f32[8,128]{1,0:T(8,128)} %maximum_maximum_fusion.1), channel_id=1, source_target_pairs={{0,4},{2,6},{4,0},{6,2},{8,12},{10,14},{12,8},{14,10},{16,20},{18,... | collective-permute-start | bytes 12296 | tf_op jit(solution)/shard_map/ppermute | solution.py:78
  27.8 8.5 %collective-permute-start.9 = (f32[1216,608]{1,0:T(8,128)}, f32[1216,608]{1,0:T(8,128)}, u32[]{:S(2)}, u32[]{:S(2)}) collective-permute-start(f32[1216,608]{1,0:T(8,128)} %shard_map.209), channel_id=1, source_target_pairs={{0,2},{2,0},{4,6},{6,4},{8,10},{10,8},{12,14},{14,12},{16,18},{18,... | collective-permute-start | bytes 8871944 | tf_op jit(solution)/shard_map/ppermute | solution.py:78
  33.0 9.3 %collective-permute-start.8 = (f32[1216,608]{1,0:T(8,128)S(1)}, f32[1216,608]{1,0:T(8,128)S(1)}, u32[]{:S(2)}, u32[]{:S(2)}) collective-permute-start(f32[1216,608]{1,0:T(8,128)S(1)} %shard_map.211), channel_id=1, source_target_pairs={{0,2},{2,0},{4,6},{6,4},{8,10},{10,8},{12,14},{14,12},{16,18},{18,... | collective-permute-start | bytes 8871944 | tf_op jit(solution)/shard_map/ppermute | solution.py:78
  40.8 20.5 %collective-permute-start.12 = (f16[4,152,608]{2,1,0:T(8,128)(2,1)}, f16[4,152,608]{2,1,0:T(8,128)(2,1)}, u32[]{:S(2)}, u32[]{:S(2)}) collective-permute-start(f16[4,152,608]{2,1,0:T(8,128)(2,1)} %bitcast.4), channel_id=1, source_target_pairs={{0,4},{2,6},{4,0},{6,2},{8,12},{10,14},{12,8},{14,10},{16,20},{18,... | collective-permute-start | bytes 2217992 | tf_op jit(solution)/shard_map/ppermute | solution.py:78
  45.0 41.5 %collective-permute-start.11 = (f16[4,152,608]{2,1,0:T(8,128)(2,1)}, f16[4,152,608]{2,1,0:T(8,128)(2,1)}, u32[]{:S(2)}, u32[]{:S(2)}) collective-permute-start(f16[4,152,608]{2,1,0:T(8,128)(2,1)} %bitcast.5), channel_id=1, source_target_pairs={{0,4},{2,6},{4,0},{6,2},{8,12},{10,14},{12,8},{14,10},{16,20},{18,... | collective-permute-start | bytes 2217992 | tf_op jit(solution)/shard_map/ppermute | solution.py:78
  45.5 63.2 %collective-permute-start.10 = (bf16[2,2,2,152,512]{4,3,2,1,0:T(8,128)(2,1)}, bf16[2,2,2,152,512]{4,3,2,1,0:T(8,128)(2,1)}, u32[]{:S(2)}, u32[]{:S(2)}) collective-permute-start(bf16[2,2,2,152,512]{4,3,2,1,0:T(8,128)(2,1)} %get-tuple-element.229.refs_0_), channel_id=1, source_target_pairs={{0,1},{1,0},{2,3},{3,2},{4,5},{5,4},{6,7},{7,6},{8,9},{9,8},{10,11... | collective-permute-start | bytes 3735560 | tf_op jit(solution)/shard_map/ppermute | solution.py:91
  57.4 11.1 %collective-permute-start.16 = (f32[2,2,152,608]{3,2,0,1:T(8,128)S(1)}, f32[2,2,152,608]{3,2,0,1:T(8,128)S(1)}, u32[]{:S(2)}, u32[]{:S(2)}) collective-permute-start(f32[2,2,152,608]{3,2,0,1:T(8,128)S(1)} %copy.27), channel_id=1, source_target_pairs={{0,2},{2,0},{4,6},{6,4},{8,10},{10,8},{12,14},{14,12},{16,18},{18,... | collective-permute-start | bytes 4435976 | tf_op jit(solution)/shard_map/ppermute | solution.py:78
  64.0 9.7 %collective-permute-start.13 = (f16[152,608]{1,0:T(8,128)(2,1)S(1)}, f16[152,608]{1,0:T(8,128)(2,1)S(1)}, u32[]{:S(2)}, u32[]{:S(2)}) collective-permute-start(f16[152,608]{1,0:T(8,128)(2,1)S(1)} %get-tuple-element.316), channel_id=1, source_target_pairs={{0,24},{2,26},{4,28},{6,30},{8,0},{10,2},{12,4},{14,6},{16,8},{18,... | collective-permute-start | bytes 554504 | tf_op jit(solution)/shard_map/ppermute | solution.py:78
  68.5 10.4 %collective-permute-start.14 = (f16[152,608]{1,0:T(8,128)(2,1)S(1)}, f16[152,608]{1,0:T(8,128)(2,1)S(1)}, u32[]{:S(2)}, u32[]{:S(2)}) collective-permute-start(f16[152,608]{1,0:T(8,128)(2,1)S(1)} %get-tuple-element.315), channel_id=1, source_target_pairs={{0,8},{2,10},{4,12},{6,14},{8,16},{10,18},{12,20},{14,22},{16,24},... | collective-permute-start | bytes 554504 | tf_op jit(solution)/shard_map/ppermute | solution.py:78
  68.5 16.6 %collective-permute-start.15 = (f16[152,608]{1,0:T(8,128)(2,1)S(1)}, f16[152,608]{1,0:T(8,128)(2,1)S(1)}, u32[]{:S(2)}, u32[]{:S(2)}) collective-permute-start(f16[152,608]{1,0:T(8,128)(2,1)S(1)} %get-tuple-element.314), channel_id=1, source_target_pairs={{0,16},{2,18},{4,20},{6,22},{8,24},{10,26},{12,28},{14,30},{16,0},... | collective-permute-start | bytes 554504 | tf_op jit(solution)/shard_map/ppermute | solution.py:78
  73.7 19.1 %collective-permute-start.20 = (f16[2,152,608]{2,1,0:T(8,128)(2,1)S(1)}, f16[2,152,608]{2,1,0:T(8,128)(2,1)S(1)}, u32[]{:S(2)}, u32[]{:S(2)}) collective-permute-start(f16[2,152,608]{2,1,0:T(8,128)(2,1)S(1)} %get-tuple-element.309), channel_id=1, source_target_pairs={{0,4},{2,6},{4,0},{6,2},{8,12},{10,14},{12,8},{14,10},{16,20},{18,... | collective-permute-start | bytes 1109000 | tf_op jit(solution)/shard_map/ppermute | solution.py:78
  89.3 11.9 %collective-permute-start.17 = (f16[152,608]{1,0:T(8,128)(2,1)S(1)}, f16[152,608]{1,0:T(8,128)(2,1)S(1)}, u32[]{:S(2)}, u32[]{:S(2)}) collective-permute-start(f16[152,608]{1,0:T(8,128)(2,1)S(1)} %get-tuple-element.312), channel_id=1, source_target_pairs={{0,24},{2,26},{4,28},{6,30},{8,0},{10,2},{12,4},{14,6},{16,8},{18,... | collective-permute-start | bytes 554504 | tf_op jit(solution)/shard_map/ppermute | solution.py:78
  92.1 9.6 %collective-permute-start.18 = (f16[152,608]{1,0:T(8,128)(2,1)S(1)}, f16[152,608]{1,0:T(8,128)(2,1)S(1)}, u32[]{:S(2)}, u32[]{:S(2)}) collective-permute-start(f16[152,608]{1,0:T(8,128)(2,1)S(1)} %get-tuple-element.311), channel_id=1, source_target_pairs={{0,8},{2,10},{4,12},{6,14},{8,16},{10,18},{12,20},{14,22},{16,24},... | collective-permute-start | bytes 554504 | tf_op jit(solution)/shard_map/ppermute | solution.py:78
  92.1 15.2 %collective-permute-start.19 = (f16[152,608]{1,0:T(8,128)(2,1)S(1)}, f16[152,608]{1,0:T(8,128)(2,1)S(1)}, u32[]{:S(2)}, u32[]{:S(2)}) collective-permute-start(f16[152,608]{1,0:T(8,128)(2,1)S(1)} %get-tuple-element.310), channel_id=1, source_target_pairs={{0,16},{2,18},{4,20},{6,22},{8,24},{10,26},{12,28},{14,30},{16,0},... | collective-permute-start | bytes 554504 | tf_op jit(solution)/shard_map/ppermute | solution.py:78
  117.9 10.8 %collective-permute-start.25 = (f32[152,608]{1,0:T(8,128)S(1)}, f32[152,608]{1,0:T(8,128)S(1)}, u32[]{:S(2)}, u32[]{:S(2)}) collective-permute-start(f32[152,608]{1,0:T(8,128)S(1)} %copy-done.21), channel_id=1, source_target_pairs={{0,1},{1,0},{2,3},{3,2},{4,5},{5,4},{6,7},{7,6},{8,9},{9,8},{10,11... | collective-permute-start | bytes 1109000 | tf_op jit(solution)/shard_map/ppermute | solution.py:91
  118.0 10.8 %collective-permute-start.23 = (f16[152,608]{1,0:T(8,128)(2,1)S(1)}, f16[152,608]{1,0:T(8,128)(2,1)S(1)}, u32[]{:S(2)}, u32[]{:S(2)}) collective-permute-start(f16[152,608]{1,0:T(8,128)(2,1)S(1)} %copy-done.23), channel_id=1, source_target_pairs={{0,24},{2,26},{4,28},{6,30},{8,0},{10,2},{12,4},{14,6},{16,8},{18,... | collective-permute-start | bytes 554504 | tf_op jit(solution)/shard_map/ppermute | solution.py:78
  121.4 15.6 %collective-permute-start.24 = (f16[152,608]{1,0:T(8,128)(2,1)S(1)}, f16[152,608]{1,0:T(8,128)(2,1)S(1)}, u32[]{:S(2)}, u32[]{:S(2)}) collective-permute-start(f16[152,608]{1,0:T(8,128)(2,1)S(1)} %copy-done.22), channel_id=1, source_target_pairs={{0,16},{2,18},{4,20},{6,22},{8,24},{10,26},{12,28},{14,30},{16,0},... | collective-permute-start | bytes 554504 | tf_op jit(solution)/shard_map/ppermute | solution.py:78
  121.4 15.6 %collective-permute-start.22 = (f16[152,608]{1,0:T(8,128)(2,1)S(1)}, f16[152,608]{1,0:T(8,128)(2,1)S(1)}, u32[]{:S(2)}, u32[]{:S(2)}) collective-permute-start(f16[152,608]{1,0:T(8,128)(2,1)S(1)} %get-tuple-element.306), channel_id=1, source_target_pairs={{0,4},{2,6},{4,0},{6,2},{8,12},{10,14},{12,8},{14,10},{16,20},{18,... | collective-permute-start | bytes 554504 | tf_op jit(solution)/shard_map/ppermute | solution.py:78
  124.6 13.1 %collective-permute-start.27 = (f16[152,608]{1,0:T(8,128)(2,1)S(1)}, f16[152,608]{1,0:T(8,128)(2,1)S(1)}, u32[]{:S(2)}, u32[]{:S(2)}) collective-permute-start(f16[152,608]{1,0:T(8,128)(2,1)S(1)} %multiply_convert_fusion), channel_id=1, source_target_pairs={{0,8},{2,10},{4,12},{6,14},{8,16},{10,18},{12,20},{14,22},{16,24},... | collective-permute-start | bytes 554504 | tf_op jit(solution)/shard_map/ppermute | solution.py:78
  151.3 56.6 %collective-permute-start.35 = (bf16[512,2432]{1,0:T(8,128)(2,1)}, bf16[512,2432]{1,0:T(8,128)(2,1)}, u32[]{:S(2)}, u32[]{:S(2)}) collective-permute-start(bf16[512,2432]{1,0:T(8,128)(2,1)} %refs_0_.1), channel_id=1, source_target_pairs={{0,1},{1,0},{2,3},{3,2},{4,5},{5,4},{6,7},{7,6},{8,9},{9,8},{10,11... | collective-permute-start | bytes 7471112 | tf_op jit(solution)/shard_map/ppermute | solution.py:91
  155.3 13.6 %collective-permute-start.38 = (bf16[2,152,608]{2,1,0:T(8,128)(2,1)S(1)}, bf16[2,152,608]{2,1,0:T(8,128)(2,1)S(1)}, u32[]{:S(2)}, u32[]{:S(2)}) collective-permute-start(bf16[2,152,608]{2,1,0:T(8,128)(2,1)S(1)} %get-tuple-element.274), channel_id=1, source_target_pairs={{0,24},{2,26},{4,28},{6,30},{8,0},{10,2},{12,4},{14,6},{16,8},{18,... | collective-permute-start | bytes 1109000 | tf_op jit(solution)/shard_map/ppermute | solution.py:78
  159.4 18.3 %collective-permute-start.40 = (bf16[2,152,608]{2,1,0:T(8,128)(2,1)S(1)}, bf16[2,152,608]{2,1,0:T(8,128)(2,1)S(1)}, u32[]{:S(2)}, u32[]{:S(2)}) collective-permute-start(bf16[2,152,608]{2,1,0:T(8,128)(2,1)S(1)} %get-tuple-element.274), channel_id=1, source_target_pairs={{0,8},{2,10},{4,12},{6,14},{8,16},{10,18},{12,20},{14,22},{16,24},... | collective-permute-start | bytes 1109000 | tf_op jit(solution)/shard_map/ppermute | solution.py:78
  159.4 19.7 %collective-permute-start.37 = (bf16[2,152,608]{2,1,0:T(8,128)(2,1)S(1)}, bf16[2,152,608]{2,1,0:T(8,128)(2,1)S(1)}, u32[]{:S(2)}, u32[]{:S(2)}) collective-permute-start(bf16[2,152,608]{2,1,0:T(8,128)(2,1)S(1)} %get-tuple-element.274), channel_id=1, source_target_pairs={{0,4},{2,6},{4,0},{6,2},{8,12},{10,14},{12,8},{14,10},{16,20},{18,... | collective-permute-start | bytes 1109000 | tf_op jit(solution)/shard_map/ppermute | solution.py:78
  168.9 10.2 %collective-permute-start.39 = (bf16[2,152,608]{2,1,0:T(8,128)(2,1)S(1)}, bf16[2,152,608]{2,1,0:T(8,128)(2,1)S(1)}, u32[]{:S(2)}, u32[]{:S(2)}) collective-permute-start(bf16[2,152,608]{2,1,0:T(8,128)(2,1)S(1)} %collective-permute-done.38), channel_id=1, source_target_pairs={{0,4},{2,6},{4,0},{6,2},{8,12},{10,14},{12,8},{14,10},{16,20},{18,... | collective-permute-start | bytes 1109000 | tf_op jit(solution)/shard_map/ppermute | solution.py:78
  170.3 23.4 %collective-permute-start.36 = (bf16[2,152,608]{2,1,0:T(8,128)(2,1)S(1)}, bf16[2,152,608]{2,1,0:T(8,128)(2,1)S(1)}, u32[]{:S(2)}, u32[]{:S(2)}) collective-permute-start(bf16[2,152,608]{2,1,0:T(8,128)(2,1)S(1)} %get-tuple-element.274), channel_id=1, source_target_pairs={{0,16},{2,18},{4,20},{6,22},{8,24},{10,26},{12,28},{14,30},{16,0},... | collective-permute-start | bytes 1109000 | tf_op jit(solution)/shard_map/ppermute | solution.py:78
  177.7 17.6 %collective-permute-start.42 = (bf16[2,152,608]{2,1,0:T(8,128)(2,1)S(1)}, bf16[2,152,608]{2,1,0:T(8,128)(2,1)S(1)}, u32[]{:S(2)}, u32[]{:S(2)}) collective-permute-start(bf16[2,152,608]{2,1,0:T(8,128)(2,1)S(1)} %collective-permute-done.40), channel_id=1, source_target_pairs={{0,4},{2,6},{4,0},{6,2},{8,12},{10,14},{12,8},{14,10},{16,20},{18,... | collective-permute-start | bytes 1109000 | tf_op jit(solution)/shard_map/ppermute | solution.py:78
  193.7 10.9 %collective-permute-start.41 = (bf16[2,152,608]{2,1,0:T(8,128)(2,1)S(1)}, bf16[2,152,608]{2,1,0:T(8,128)(2,1)S(1)}, u32[]{:S(2)}, u32[]{:S(2)}) collective-permute-start(bf16[2,152,608]{2,1,0:T(8,128)(2,1)S(1)} %collective-permute-done.36), channel_id=1, source_target_pairs={{0,4},{2,6},{4,0},{6,2},{8,12},{10,14},{12,8},{14,10},{16,20},{18,... | collective-permute-start | bytes 1109000 | tf_op jit(solution)/shard_map/ppermute | solution.py:78
  195.2 17.0 %collective-permute-start.43 = (bf16[4,2,152,608]{3,2,1,0:T(8,128)(2,1)S(1)}, bf16[4,2,152,608]{3,2,1,0:T(8,128)(2,1)S(1)}, u32[]{:S(2)}, u32[]{:S(2)}) collective-permute-start(bf16[4,2,152,608]{3,2,1,0:T(8,128)(2,1)S(1)} %pad_maximum_fusion.refs_0_), channel_id=1, source_target_pairs={{0,2},{2,0},{4,6},{6,4},{8,10},{10,8},{12,14},{14,12},{16,18},{18,... | collective-permute-start | bytes 4435976 | tf_op jit(solution)/shard_map/ppermute | solution.py:78
  205.0 7.3 %collective-permute-start.44 = (bf16[4,2,152,608]{3,2,1,0:T(8,128)(2,1)S(1)}, bf16[4,2,152,608]{3,2,1,0:T(8,128)(2,1)S(1)}, u32[]{:S(2)}, u32[]{:S(2)}) collective-permute-start(bf16[4,2,152,608]{3,2,1,0:T(8,128)(2,1)S(1)} %pad_maximum_fusion.1.refs_1_), channel_id=1, source_target_pairs={{0,2},{2,0},{4,6},{6,4},{8,10},{10,8},{12,14},{14,12},{16,18},{18,... | collective-permute-start | bytes 4435976 | tf_op jit(solution)/shard_map/ppermute | solution.py:78
  (39 other events, 256.3 us)

commit v6 on v5

--- a/solution.py
+++ b/solution.py
@@ -89,6 +89,15 @@
     def from_tensor(value, k):
         perm = [(s, (s - k) & (n_tensor - 1)) for s in range(n_tensor)]
         return lax.ppermute(value, "tensor", perm)
+
+    def from_diagonal(value, k):
+        perm = []
+        for p in range(n_dp):
+            z, m, c = split(p)
+            for t in range(n_tensor):
+                target = join(z, m, 1 - c) * n_tensor + ((t - k) & (n_tensor - 1))
+                perm.append((p * n_tensor + t, target))
+        return lax.ppermute(value, ("dp", "tensor"), perm)
 
     def my_place():
         return split(lax.axis_index("dp"))
@@ -131,132 +140,125 @@
             scratch_shapes=[pltpu.SemaphoreType.DMA((count,))],
         )
 
+    def bound_of(cots, acts, scales):
+        r, f, count = cots[0].shape[0], acts[0].shape[0], acts[0].shape[1]
+        steps = 4
+
+        def kernel(scale_ref, *refs):
+            ins, (out_ref, most_ref) = refs[:4], refs[4:]
+
+            @pl.when(pl.program_id(0) == 0)
+            def _():
+                most_ref[...] = jnp.zeros_like(most_ref)
+
+            for n, ref in enumerate(ins):
+                value = jnp.abs(ref[...].astype(jnp.float32))
+                rows, cols = value.shape
+                value = jnp.max(value.reshape(rows // 8, 8, cols), axis=0)
+                value = functools.reduce(
+                    jnp.maximum, (value[:, at : at + LANES] for at in range(0, cols, LANES))
+                )
+                most_ref[n] = jnp.maximum(most_ref[n], value)
+
+            @pl.when(pl.program_id(0) == steps - 1)
+            def _():
+                bounds = [
+                    jnp.max(most_ref[net]) * jnp.max(most_ref[2 + net]) * scale_ref[net]
+                    for net in range(2)
+                ]
+                rows = lax.broadcasted_iota(jnp.int32, (8, LANES), 0)
+                out_ref[...] = jnp.where(rows == 0, *bounds)
+
+        return call(
+            kernel, array((8, LANES), jnp.float32), scales, *cots, *acts,
+            grid=(steps,),
+            in_specs=[SMEM]
+            + [pl.BlockSpec((r // steps, D), lambda s: (s, 0))] * 2
+            + [pl.BlockSpec((f, count // steps), lambda s: (0, s))] * 2,
+            out_specs=pl.BlockSpec((8, LANES), lambda s: (0, 0)),
+            scratch_shapes=[pltpu.VMEM((4, 8, LANES), jnp.float32)],
+        )
+
     def turn(cot, by_planes):
         r = cot.shape[0]
         step = min(r, TILE)
-        count = 2
-        lead = (2, 2, inner) if by_planes else (inner, OUTER)
+        count = 4 if by_planes else 2
+        lead = (2, inner) if by_planes else (inner, OUTER)
 
         def kernel(cot_ref, *refs):
-            out_refs, (top_ref, wide_ref) = refs[:count], refs[count:]
+            out_refs, wide_ref = refs[:count], refs[count]
             eye = identity(TILE)
             for start in range(0, D, TILE):
                 size = min(TILE, D - start)
                 wide_ref[start : start + size, :] = dot(
                     eye[:size, :size], cot_ref[:, start : start + size], NT
                 )
-            top = jnp.max(jnp.abs(wide_ref[...]).reshape(D // 8, 8, step), axis=0)
-            top = jnp.broadcast_to(jnp.max(top), (8, LANES))
-
-            @pl.when(pl.program_id(0) == 0)
-            def _():
-                top_ref[...] = top
-
-            @pl.when(pl.program_id(0) > 0)
-            def _():
-                top_ref[...] = jnp.maximum(top_ref[...], top)
-
             for p in range(n_dp):
                 k, i, other = relative(p)
                 block = wide_ref[p * width : (p + 1) * width, :].astype(jnp.bfloat16)
-                which, at = (1 - (k >> 1), (1 - (k & 1), other, i)) if by_planes else (other, (i, k))
+                which, at = other, (i, k)
+                if by_planes:
+                    which, at = 2 - 2 * (k >> 1) + other, (1 - (k & 1), i)
                 for n in range(count):
 
                     @pl.when(which == n)
                     def _(n=n, at=at, block=block):
                         out_refs[n][at] = block
 
-        *outs, top = call(
+        return call(
             kernel,
-            [array((*lead, width, r), jnp.bfloat16)] * count + [array((8, LANES), jnp.float32)],
+            [array((*lead, width, r), jnp.bfloat16)] * count,
             cot,
             grid=(r // step,),
             in_specs=[pl.BlockSpec((step, D), lambda s: (s, 0))],
             out_specs=[
                 pl.BlockSpec((*lead, width, step), lambda s: (*(0 for _ in lead), 0, s))
-            ] * count
-            + [pl.BlockSpec((8, LANES), lambda s: (0, 0))],
+            ] * count,
             scratch_shapes=[pltpu.VMEM((D, step), jnp.float32)],
         )
-        return outs, top
-
-    def prepare(act_s, act_f, top_s, top_f, scales, r):
-        f = act_s.shape[0]
-
-        def kernel(scale_ref, act_s_ref, act_f_ref, top_s_ref, top_f_ref, *refs):
-            bound_ref, fake_ref, *student_refs = refs
-            bounds = []
-            for net, act_ref, top_ref in ((0, act_s_ref, top_s_ref), (1, act_f_ref, top_f_ref)):
-                top = jnp.max(jnp.abs(act_ref[...].astype(jnp.float32)))
-                bounds.append(top_ref[...] * (top * scale_ref[net]))
-            rows = lax.broadcasted_iota(jnp.int32, (8, LANES), 0)
-            bound_ref[...] = jnp.where(rows == 0, *bounds)
-            own = act_f_ref[:, pl.ds(first_row(0, r), r)].astype(jnp.float32)
-            fake_ref[...] = (own * scale_ref[1]).astype(jnp.bfloat16)
-            for j, out_ref in enumerate(student_refs):
-                part = act_s_ref[:, pl.ds(first_row(j, r), r)].astype(jnp.float32)
-                out_ref[...] = (part * scale_ref[0]).astype(jnp.bfloat16)
-
-        return call(
-            kernel,
-            [array((8, LANES), jnp.float32)] + [array((f, r), jnp.bfloat16)] * (1 + n_tensor),
-            scales, act_s, act_f, top_s, top_f,
-            in_specs=[SMEM] + [VMEM] * 4,
-            out_specs=[VMEM] * (2 + n_tensor),
-            mib=16,
-        )
-
-    def multiply_rows(pieces, scaled):
-        rows, r = pieces[0].shape
-        f = scaled[0].shape[0]
+
+    def prepare(net, act, scales, r, places):
+        f = act.shape[0]
+
+        def kernel(scale_ref, act_ref, out_ref):
+            for j in range(places):
+                part = act_ref[:, pl.ds(first_row(j, r), r)].astype(jnp.float32)
+                out_ref[j] = (part * scale_ref[net]).astype(jnp.bfloat16)
+
+        return call(
+            kernel, array((places, f, r), jnp.bfloat16), scales, act,
+            in_specs=[SMEM, VMEM], out_specs=VMEM,
+        )
+
+    def multiply(pieces, scaled, places):
+        lead, r, f = pieces[0].shape[:-1], pieces[0].shape[-1], scaled[0].shape[1]
+        pieces = [piece.reshape(-1, r) for piece in pieces]
+        rows = pieces[0].shape[0]
         step = D // (2 * OUTER)
         count = len(pieces)
 
         def kernel(*refs):
             piece_refs, scaled_refs, out_ref = refs[:count], refs[count:-1], refs[-1]
-            total = dot(piece_refs[0][...], scaled_refs[0][...], NT)
-            for piece_ref, scaled_ref in zip(piece_refs[1:], scaled_refs[1:]):
-                total = total + dot(piece_ref[...], scaled_ref[...], NT)
-            out_ref[...] = total
-
-        return call(
-            kernel,
-            array((rows, f), jnp.float32),
-            *pieces, *scaled,
-            grid=(rows // step,),
-            in_specs=[pl.BlockSpec((step, r), lambda s: (s, 0))] * count
-            + [pl.BlockSpec((f, r), lambda s: (0, 0))] * count,
-            out_specs=pl.BlockSpec((step, f), lambda s: (s, 0)),
-        )
-
-    def multiply_half(other, pieces, scaled):
-        r, f = pieces[0].shape[-1], scaled[0].shape[0]
-        count = len(pieces)
-
-        def kernel(*refs):
-            piece_refs, scaled_refs, out_ref = refs[:count], refs[count:-1], refs[-1]
-            for i in range(inner):
-                total = dot(piece_refs[0][0, 0, i], scaled_refs[0][...], NT)
-                for piece_ref, scaled_ref in zip(piece_refs[1:], scaled_refs[1:]):
-                    total = total + dot(piece_ref[0, 0, i], scaled_ref[...], NT)
-                out_ref[0, i] = total
-
-        return call(
-            kernel,
-            array((2, inner, width, f), jnp.float32),
-            *pieces, *scaled,
-            grid=(2,),
-            in_specs=[pl.BlockSpec((1, 1, inner, width, r), lambda s: (s, other, 0, 0, 0))] * count
-            + [pl.BlockSpec((f, r), lambda s: (0, 0))] * count,
-            out_specs=pl.BlockSpec((1, inner, width, f), lambda s: (s, 0, 0, 0)),
-        )
+            for start in range(0, rows, step):
+                part = slice(start, start + step)
+                total = None
+                for piece_ref, (n, j) in zip(piece_refs, places):
+                    term = dot(piece_ref[part], scaled_refs[n][j], NT)
+                    total = term if total is None else total + term
+                out_ref[part] = total
+
+        out = call(
+            kernel, array((rows, f), jnp.float32), *pieces, *scaled,
+            in_specs=[VMEM] * (count + len(scaled)), out_specs=VMEM,
+        )
+        return out.reshape(*lead, f)
 
     def scale_rows(act, scales):
         def kernel(scale_ref, act_ref, out_ref):
-            out_ref[...] = (act_ref[...].astype(jnp.float32) * scale_ref[1]).astype(jnp.bfloat16)
-
-        return call(
-            kernel, array(act.shape, jnp.bfloat16), scales, act,
+            out_ref[0] = (act_ref[...].astype(jnp.float32) * scale_ref[1]).astype(jnp.bfloat16)
+
+        return call(
+            kernel, array((1, *act.shape), jnp.bfloat16), scales, act,
             in_specs=[SMEM, VMEM], out_specs=VMEM,
         )
 
@@ -306,7 +308,7 @@
                 for k in range(OUTER):
                     for other in range(2):
                         for i in range(inner):
-                            block = piece_refs[1 - (k >> 1)][1 - (k & 1), other, i]
+                            block = piece_refs[2 - 2 * (k >> 1) + other][1 - (k & 1), i]
                             block = block.astype(jnp.float32)
                             wide_ref[owner(k, i, other)] = block
                 flat = wide_ref[...].reshape(D, size).astype(jnp.bfloat16)
@@ -380,47 +382,51 @@
         def reduced(combine, value, got):
             return step(lambda *values: functools.reduce(combine, values), value, *got)
 
-        def gather_planes(value):
-            return [to_plane(value, k) for k in range(1, OUTER)]
-
-        def gather_chips(value):
-            return [
-                move_dp(value, lambda z, m, c, i=i, o=o: (z, (m + i) & (inner - 1), c ^ o))
-                for i in range(inner)
-                for o in range(2)
-                if i or o
-            ]
+        def hops(value, combine):
+            distance = 1
+            while distance < n_dp:
+                perm = [(p, p ^ distance) for p in range(n_dp)]
+                got = lax.ppermute(value, "dp", perm)
+                yield
+                value = step(combine, value, got)
+                distance *= 2
+            yield value
 
         acts = [from_tensor(act, -j) for j, act in enumerate(step(lambda a: cut_acts(a, r), act_fake), 1)]
-        planes, top_student = step(lambda cot: turn(cot, True), cot_student)
-        others = [[from_tensor(planes[0], j) for j in range(1, n_tensor)]]
-        cores, top_fake = step(lambda cot: turn(cot, False), cot_fake)
-        cores = [core.reshape(-1, r) for core in cores]
-
         scales = step(
             lambda steps: 1.0 / (0.1 + steps.astype(jnp.float32) / 1000.0), timesteps[0, :, 0]
         )
-        bounds, scaled, *scaled_student = step(
-            lambda *values: prepare(*values, r),
-            act_student, act_fake, top_student, top_fake, scales,
-        )
-        pairs = []
-        got = gather_planes(bounds)
-        scaled_fake = [scaled] + [step(scale_rows, act, scales) for act in acts]
-        bounds = reduced(jnp.maximum, bounds, got)
-        got = gather_chips(bounds)
-        for scaled in scaled_fake:
-            send = to_core(step(lambda a, b: multiply_rows([a], [b]), cores[1], scaled))
-            keep = step(lambda a, b: multiply_rows([a], [b]), cores[0], scaled)
-            if not pairs:
-                bounds = reduced(jnp.maximum, bounds, got)
-            pairs.append((keep, send))
+        bounds = step(
+            lambda a, b, c, d, scales: bound_of((a, b), (c, d), scales),
+            cot_student, cot_fake, act_student, act_fake, scales,
+        )
+        bounds = hops(bounds, jnp.maximum)
+        next(bounds)
+        fake_blocks = step(lambda cot: turn(cot, False), cot_fake)
+        mate_blocks = to_core(fake_blocks[1])
+        next(bounds)
+        scaled_own = step(lambda act: prepare(1, act, scales, r, 1), act_fake)
+        scaled_fake = [[scaled_own, to_core(scaled_own)]]
+        next(bounds)
+        planes = step(lambda cot: turn(cot, True), cot_student)
+
+        same, diagonal = [], []
+
+        def send_planes(g, own, other):
+            same.append([from_tensor(own, j) for j in range(1, n_tensor)])
+            diagonal.append([from_diagonal(other, j) for j in range(1, n_tensor)])
+
+        send_planes(0, planes[0], planes[1])
+        next(bounds)
+        scaled_student = step(lambda act: prepare(0, act, scales, r, n_tensor), act_student)
+        while (final := next(bounds)) is None:
+            pass
 
         def factors(bounds):
             bounds = jnp.maximum(bounds, 1e-30) * (1.01 * count * n_dp / HALF_LIMIT)
             return bounds[:2, 0], 1.0 / bounds[:2, 0]
 
-        grow, fit = step(factors, bounds)
+        grow, fit = step(factors, final)
 
         def shrink(value, net):
             return (value * fit[net]).astype(jnp.float16)
@@ -433,14 +439,43 @@
                 total = total + widen(value, net)
             return total
 
-        def fake_middle(keep, send):
-            both = (keep + send).reshape(inner, OUTER, width, f)
-            return [shrink(both[i], 1) for i in range(1, inner)], both[0]
-
-        middles = []
-        for keep, send in pairs:
-            sent, own = step(fake_middle, keep, send)
-            middles.append((own, [to_middle(value, i) for i, value in enumerate(sent, 1)]))
+        parts_fake = []
+
+        def multiply_fake(j):
+            parts_fake.append(
+                step(
+                    lambda a, b, c, d: multiply([a, b], [c, d], [(0, 0), (1, 0)]),
+                    fake_blocks[0], mate_blocks, *scaled_fake[j],
+                )
+            )
+
+        for act in acts:
+            scaled_other = step(scale_rows, act, scales)
+            scaled_fake.append([scaled_other, to_core(scaled_other)])
+        multiply_fake(0)
+        mate_student = to_core(scaled_student)
+        mate_planes = [to_core(planes[1]), to_core(planes[3])]
+        for j in range(1, n_tensor):
+            multiply_fake(j)
+        mate_student, *mate_planes = step(lambda *values: values, mate_student, *mate_planes)
+
+        middles = {}
+
+        def fake_middle(j):
+            def work(both):
+                sent = [
+                    [shrink(both[i, lo : lo + 2], 1) for i in range(1, inner)] for lo in (2, 0)
+                ]
+                return sent, both[0, 2:], both[0, :2]
+
+            sent, *mine = step(work, parts_fake[j])
+            middles[j] = [
+                (own, [to_middle(value, i) for i, value in enumerate(values, 1)])
+                for own, values in zip(mine, sent)
+            ]
+
+        for j in range(n_tensor):
+            fake_middle(j)
 
         def back(whole, net, pieces, j, low, size):
             weight = (weight_student, weight_fake)[net]
@@ -454,46 +489,51 @@
 
             return step(work, weight, *pieces, *has)
 
-        fake_sums = {}
-
-        def fake_planes(j):
+        fake_sums = {j: [] for j in range(n_tensor)}
+
+        def fake_planes(j, part):
             def work(own, *got):
                 own = add_widened(own, got, 1)
-                return [shrink(own[k], 1) for k in (3, 1, 2)], own[0]
-
-            sent, own = step(work, middles[j][0], *middles[j][1])
-            fake_sums[j] = own, [to_plane(value, k) for k, value in zip((3, 1, 2), sent)]
+                if part == 0:
+                    return shrink(own[1], 1), shrink(own[0], 1)
+                return shrink(own[1], 1), own[0]
+
+            own, got = middles[j][part]
+            values = step(work, own, *got)
+            for k, value in zip(((3, 2), (1, 0))[part], values):
+                fake_sums[j].append(to_plane(value, k) if k else value)
 
         def fake_total(j):
-            own, got = fake_sums[j]
+            *got, own = fake_sums[j]
             return step(lambda own, *got: add_widened(own, got, 1), own, *got)
 
-        kept = {}
-
-        def multiply(n):
-            def half(other, *operands):
-                return multiply_half(other, operands[:n_tensor], operands[n_tensor:])
-
-            operands = [planes[n], *others[n], *scaled_student]
-            send = to_core(step(functools.partial(half, 1), *operands))
-            kept[n] = step(functools.partial(half, 0), *operands), send
-
-        second = step(lambda value: value, planes[1])
-        others.append([from_tensor(second, j) for j in range(1, n_tensor)])
+        def multiply_student(g):
+            pieces, places = [planes[2 * g], mate_planes[g]], [(0, 0), (1, 0)]
+            for j in range(1, n_tensor):
+                pieces += [same[g][j - 1], diagonal[g][j - 1]]
+                places += [(0, j), (1, j)]
+            return step(
+                lambda *values: multiply(values[:-2], values[-2:], places),
+                *pieces, scaled_student, mate_student,
+            )
+
         back_student = back(None, 0, [cot_student], 0, 0, r)
+        fake_planes(0, 0)
         back_fake = back(None, 1, [cot_fake], 0, 0, r)
-        multiply(0)
-        fake_planes(0)
-
-        def first_middle(keep, send):
-            both = keep + send
+        fake_planes(0, 1)
+        both = multiply_student(0)
+        send_planes(1, *step(lambda a, b: (a, b), planes[2], planes[3]))
+
+        def first_middle(both):
             return [shrink(both[:, i], 0) for i in range(1, inner)], both[:, 0]
 
-        sent, own = step(first_middle, *kept[0])
+        fake_mine = fake_total(0)
+        sent, own = step(first_middle, both)
         got = [to_middle(value, i) for i, value in enumerate(sent, 1)]
-        fake_mine = fake_total(0)
         for j in range(1, n_tensor):
-            fake_planes(j)
+            fake_planes(j, 0)
+        for j in range(1, n_tensor):
+            fake_planes(j, 1)
 
         def first_planes(own, *got):
             own = add_widened(own, got, 0)
@@ -501,19 +541,18 @@
 
         sent = step(first_planes, own, *got)
         first_got = [to_plane(value, k) for k, value in zip((3, 2), sent)]
+        both = multiply_student(1)
+
+        def second_middle(both):
+            sent = [[shrink(both[n, i], 0) for i in range(1, inner)] for n in range(2)]
+            return sent, both[0, 0], both[1, 0]
+
+        sent, own_next, own = step(second_middle, both)
+        got_next, got = (
+            [to_middle(value, i) for i, value in enumerate(values, 1)] for values in sent
+        )
         fake_others = [fake_total(j) for j in range(1, n_tensor)]
         fake_got = [from_tensor(value, j) for j, value in enumerate(fake_others, 1)]
-        multiply(1)
-
-        def second_middle(keep, send):
-            both = keep + send
-            sent = [[shrink(both[n, i], 0) for i in range(1, inner)] for n in range(2)]
-            return sent, both[0, 0], both[1, 0]
-
-        sent, own_next, own = step(second_middle, *kept[1])
-        got_next, got = (
-            [to_middle(value, i) for i, value in enumerate(values, 1)] for values in sent
-        )
         next_sent = step(
             lambda own, *got: shrink(add_widened(own, got, 0), 0), own_next, *got_next
         )
@@ -532,8 +571,11 @@
 
         raw_sent = step(lambda cot: cot, cot_fake)
         raw = [from_tensor(raw_sent, j) for j in range(1, n_tensor)]
-        squares = reduced(jnp.add, squares, gather_planes(squares))
-        squares = reduced(jnp.add, squares, gather_chips(squares))
+        hidden = step(lambda *values: values, *[value for group in diagonal for value in group])
+        mate_others = [to_core(value) for value in hidden]
+        *_, squares = hops(squares, jnp.add)
+        squares, *mate_others = step(lambda *values: values, squares, *mate_others)
+        mate_others = [mate_others[: n_tensor - 1], mate_others[n_tensor - 1 :]]
 
         states = (
             master_student, first_student, second_student, master_fake, first_fake, second_fake,
@@ -551,7 +593,9 @@
         spread_middle(0, own)
         planes_got = {k: to_plane(own, -k) for k in (1, 3, 2)}
         for j in range(1, n_tensor):
-            pieces = [group[j - 1] for group in others]
+            pieces = [
+                piece for g in range(2) for piece in (same[g][j - 1], mate_others[g][j - 1])
+            ]
             back_student = back(back_student, 0, pieces, j, 0, r)
         spread_middle(1, step(lambda value: value, planes_got[1]))
         spread_middle(3, step(lambda value: value, planes_got[3]))

time: 221 us -> 235 us (1.063)
  waiting for transfers between devices: 79.4 us -> 109 us
  starting transfers between devices: 53.4 us -> 44.6 us
  other arithmetic: 25.4 us -> 20.7 us
  Pallas kernels: 58.1 us -> 55.2 us
    ppermute x39 -> x33, starting transfers between devices: 45.3 us -> 26.1 us  [move_dp(): return lax.ppermute(value, 'dp', perm)]
    ppermute x6, waiting for transfers between devices: 8.25 us -> 21.1 us  [from_tensor(): return lax.ppermute(value, 'tensor', perm)]
    ppermute x0 -> x10, waiting for transfers between devices: none -> 10.7 us  [the longest x8 10.7 us: hops(): got = lax.ppermute(value, 'dp', perm)]
    ppermute x0 -> x10, starting transfers between devices: none -> 9.95 us  [the longest x8 9.95 us: hops(): got = lax.ppermute(value, 'dp', perm)]
    ppermute x39 -> x33, waiting for transfers between devices: 71.2 us -> 77.1 us  [move_dp(): return lax.ppermute(value, 'dp', perm)]
    slice x2 -> x0, other arithmetic: 4.65 us -> none  [fake_middle(): return ([shrink(both[i], 1) for i in range(1, inner)], both[0])]
    squeeze x1 -> x4, other arithmetic: 0.86 us -> 4.75 us  [the longest x1 2.62 us: work(): return (sent, both[0, 2:], both[0, :2])]
    pallas_call x21 -> x19, Pallas kernels: 58.1 us -> 55.2 us  [call(): pl.pallas_call(kernel, out_shape=out_shape, compiler_params=pltpu.Compile...]
  transfers between devices with their start and end apart: 45 -> 49, of which waited for: 20 -> 20; matrix products, arithmetic and copies ran while one was open for 11% -> 9% of each run, Pallas kernels for 21% -> 19%
where the time goes in v6:
time: 235 us
  waiting for transfers between devices  109 us (46%)
  Pallas kernels  55.2 us (23%)
  starting transfers between devices  44.6 us (19%)
  other arithmetic  20.7 us (9%)
  local copies, waits for them, and re-layouts  4.04 us (2%)
    ppermute x33, waiting for transfers between devices, move_dp(): return lax.ppermute(value, 'dp', perm)  77.1 us
    pallas_call x19, Pallas kernels, call(): pl.pallas_call(kernel, out_shape=out_shape, compiler_params=pltpu.Compile...  55.2 us
    ppermute x33, starting transfers between devices, move_dp(): return lax.ppermute(value, 'dp', perm)  26.1 us
    ppermute x6, waiting for transfers between devices, from_tensor(): return lax.ppermute(value, 'tensor', perm)  21.1 us
    ppermute x8, waiting for transfers between devices, hops(): got = lax.ppermute(value, 'dp', perm)  10.7 us
    ppermute x8, starting transfers between devices, hops(): got = lax.ppermute(value, 'dp', perm)  9.95 us
    add x9, other arithmetic, add_widened(): total = total + widen(value, net)  9.13 us
    ppermute x6, starting transfers between devices, from_tensor(): return lax.ppermute(value, 'tensor', perm)  8.54 us
  transfers between devices with their start and end apart: 49, of which 20 were waited for; matrix products, arithmetic and copies ran while one was open for 9% of the time, Pallas kernels for 19%

profile of v6, /device:TPU:0, one launch (start us, length us, event | category | flops | bytes accessed | tf_op | source)
XLA Modules:
  0.0 234.8 jit_solution(16826196956110183921)
XLA Ops:
  3.0 3.0 %collective-permute-start.8 = (bf16[608,512]{1,0:T(8,128)(2,1)}, bf16[608,512]{1,0:T(8,128)(2,1)}, u32[]{:S(2)}, u32[]{:S(2)}) collective-permute-start(bf16[608,512]{1,0:T(8,128)(2,1)} %shard_map.204), channel_id=1, source_target_pairs={{0,1},{1,0},{2,3},{3,2},{4,5},{5,4},{6,7},{7,6},{8,9},{9,8},{10,11... | collective-permute-start | bytes 1867784 | tf_op jit(solution)/shard_map/ppermute | solution.py:91
  6.1 3.1 %shard_map.205 = f32[8,128]{1,0:T(8,128)S(1)} custom-call(f32[2]{0:T(128)S(1)} %add_divide_fusion.scale_ref, bf16[512,2432]{1,0:T(8,128)(2,1)S(1)} %copy-done.4, bf16[512,2432]{1,0:T(8,128)(2,1)} %refs_0_.2, bf16[608,1024]{1,0:T(8,128)(2,1)S(1)} %copy-done.8, bf16[608,1024]{1,0:T(8,128)(2,1)S(1)} %copy-done.6), custom_call_target="tpu_custom_call" | custom-call | flops 99999997952 | tf_op jit(solution)/shard_map/pallas_call | solution.py:56
  9.3 3.8 %shard_map.206 = (bf16[2,4,152,512]{3,2,1,0:T(8,128)(2,1)S(1)}, bf16[2,4,152,512]{3,2,1,0:T(8,128)(2,1)}) custom-call(bf16[512,2432]{1,0:T(8,128)(2,1)} %refs_0_.2), custom_call_target="tpu_custom_call" | custom-call | flops 99999997952 | tf_op jit(solution)/shard_map/pallas_call | solution.py:56
  18.8 2.9 %shard_map.208 = (bf16[2,2,152,512]{3,2,1,0:T(8,128)(2,1)}, bf16[2,2,152,512]{3,2,1,0:T(8,128)(2,1)}, bf16[2,2,152,512]{3,2,1,0:T(8,128)(2,1)S(1)}, bf16[2,2,152,512]{3,2,1,0:T(8,128)(2,1)}) custom-call(bf16[512,2432]{1,0:T(8,128)(2,1)S(1)} %copy-done.4), custom_call_target="tpu_custom_call" | custom-call | flops 99999997952 | tf_op jit(solution)/shard_map/pallas_call | solution.py:56
  21.7 2.6 %collective-permute-start.9 = (f32[8,128]{1,0:T(8,128)S(1)}, f32[8,128]{1,0:T(8,128)S(1)}, u32[]{:S(2)}, u32[]{:S(2)}) collective-permute-start(f32[8,128]{1,0:T(8,128)S(1)} %max.20), channel_id=1, source_target_pairs={{0,16},{2,18},{4,20},{6,22},{8,24},{10,26},{12,28},{14,30},{16,0},... | collective-permute-start | bytes 12296 | tf_op jit(solution)/shard_map/ppermute | solution.py:389
  30.5 3.8 %shard_map.211 = f32[1216,608]{1,0:T(8,128)S(1)} custom-call(bf16[1216,512]{1,0:T(8,128)(2,1)S(1)} %bitcast.103, bf16[1216,512]{1,0:T(8,128)(2,1)} %bitcast.2.refs_1_, bf16[1,608,512]{2,1,0:T(8,128)(2,1)} %shard_map.207.refs_2_, bf16[1,608,512]{2,1,0:T(8,128)(2,1)} %collective-permute-done.11.refs_3_), custom_call_target="tpu_custom_call" | custom-call | flops 99999997952 | tf_op jit(solution)/shard_map/pallas_call | solution.py:56
  34.6 3.4 %shard_map.212 = f32[1216,608]{1,0:T(8,128)S(1)} custom-call(bf16[1216,512]{1,0:T(8,128)(2,1)S(1)} %bitcast.104, bf16[1216,512]{1,0:T(8,128)(2,1)} %bitcast.5.refs_1_, bf16[1,608,512]{2,1,0:T(8,128)(2,1)S(1)} %shard_map.210.refs_2_, bf16[1,608,512]{2,1,0:T(8,128)(2,1)S(1)} %collective-permute-done.10.refs_3_), custom_call_target="tpu_custom_call" | custom-call | flops 99999997952 | tf_op jit(solution)/shard_map/pallas_call | solution.py:56
  42.0 2.6 %slice_bitcast_fusion.1 = (f32[2,152,608]{2,1,0:T(8,128)}, f16[2,152,608]{2,1,0:T(8,128)(2,1)}, f32[2,152,608]{2,1,0:T(8,128)}, f16[2,152,608]{2,1,0:T(8,128)(2,1)}) fusion(f32[2,4,152,608]{3,2,1,0:T(8,128)S(1)} %bitcast.90, f32[]{:T(128)} %bitcast.8), kind=kLoop, calls=%fused_computation.8 | loop fusion | flops 739328 | bytes 5175300 | tf_op jit(solution)/shard_map/squeeze | solution.py:469
  46.6 3.2 %shard_map.213.refs_4_ = bf16[608,1024]{1,0:T(8,128)(2,1)} custom-call(f32[2]{0:T(128)S(1)} %copy-done.23, bf16[608,2432]{1,0:T(8,128)(2,1)S(1)} %copy-done, bf16[512,2432]{1,0:T(8,128)(2,1)S(1)} %copy-done.5), custom_call_target="tpu_custom_call" | custom-call | flops 99999997952 | tf_op jit(solution)/shard_map/pallas_call | solution.py:56
  49.8 3.0 %collective-permute-done.14 = f16[2,152,608]{2,1,0:T(8,128)(2,1)S(1)} collective-permute-done((f16[2,152,608]{2,1,0:T(8,128)(2,1)S(1)}, f16[2,152,608]{2,1,0:T(8,128)(2,1)S(1)}, u32[]{:S(2)}, u32[]{:S(2)}) %collective-permute-start.14) | collective-permute-done | bytes 369696 | tf_op jit(solution)/shard_map/ppermute | solution.py:78
  55.7 4.4 %shard_map.214.refs_1_ = bf16[608,1024]{1,0:T(8,128)(2,1)} custom-call(f32[2]{0:T(128)S(1)} %copy-done.23, bf16[608,2432]{1,0:T(8,128)(2,1)S(1)} %copy-done.2, bf16[512,2432]{1,0:T(8,128)(2,1)} %refs_0_.2), custom_call_target="tpu_custom_call" | custom-call | flops 99999997952 | tf_op jit(solution)/shard_map/pallas_call | solution.py:56
  60.1 17.1 %collective-permute-done.13 = f16[2,152,608]{2,1,0:T(8,128)(2,1)S(1)} collective-permute-done((f16[2,152,608]{2,1,0:T(8,128)(2,1)S(1)}, f16[2,152,608]{2,1,0:T(8,128)(2,1)S(1)}, u32[]{:S(2)}, u32[]{:S(2)}) %collective-permute-start.13) | collective-permute-done | bytes 369696 | tf_op jit(solution)/shard_map/ppermute | solution.py:78
  83.5 3.7 %shard_map.215 = f32[608,608]{1,0:T(8,128)S(1)} custom-call(bf16[608,512]{1,0:T(8,128)(2,1)} %bitcast.16.refs_0_, bf16[608,512]{1,0:T(8,128)(2,1)} %bitcast.17.refs_1_, bf16[608,512]{1,0:T(8,128)(2,1)} %bitcast.18.refs_2_, bf16[608,512]{1,0:T(8,128)(2,1)} %bitcast.19.refs_3_, bf16[2,608,512]{2,1,0:T(8,128)(2,1)S(1)} %copy-done.11, ...), custom_call_target="tpu_custom_call" | custom-call | flops 99999997952 | tf_op jit(solution)/shard_map/pallas_call | solution.py:56
  87.2 9.5 %collective-permute-done.18 = f16[152,608]{1,0:T(8,128)(2,1)S(1)} collective-permute-done((f16[152,608]{1,0:T(8,128)(2,1)S(1)}, f16[152,608]{1,0:T(8,128)(2,1)S(1)}, u32[]{:S(2)}, u32[]{:S(2)}) %collective-permute-start.18) | collective-permute-done | bytes 184864 | tf_op jit(solution)/shard_map/ppermute | solution.py:78
  108.0 3.2 %collective-permute-done.20 = f16[2,152,608]{2,1,0:T(8,128)(2,1)S(1)} collective-permute-done((f16[2,152,608]{2,1,0:T(8,128)(2,1)S(1)}, f16[2,152,608]{2,1,0:T(8,128)(2,1)S(1)}, u32[]{:S(2)}, u32[]{:S(2)}) %collective-permute-start.20) | collective-permute-done | bytes 369696 | tf_op jit(solution)/shard_map/ppermute | solution.py:78
  113.3 12.7 %collective-permute-done.15.refs_2_ = bf16[2,2,152,512]{3,2,1,0:T(8,128)(2,1)S(1)} collective-permute-done((bf16[2,2,152,512]{3,2,1,0:T(8,128)(2,1)S(1)}, bf16[2,2,152,512]{3,2,1,0:T(8,128)(2,1)S(1)}, u32[]{:S(2)}, u32[]{:S(2)}) %collective-permute-start.15) | collective-permute-done | bytes 622624 | tf_op jit(solution)/shard_map/ppermute | solution.py:91
  126.0 3.4 %shard_map.216 = f32[608,608]{1,0:T(8,128)S(1)} custom-call(bf16[608,512]{1,0:T(8,128)(2,1)S(1)} %bitcast.95, bf16[608,512]{1,0:T(8,128)(2,1)} %bitcast.34.refs_1_, bf16[608,512]{1,0:T(8,128)(2,1)S(1)} %bitcast.94, bf16[608,512]{1,0:T(8,128)(2,1)S(1)} %bitcast.96, bf16[2,608,512]{2,1,0:T(8,128)(2,1)S(1)} %copy-done.11, bf16[2,608,512]{2,1,0:T(8,128)(2,1)S(1)} %copy-done.13), custom_call_target="tpu_custom_call" | custom-call | flops 99999997952 | tf_op jit(solution)/shard_map/pallas_call | solution.py:56
  134.2 3.8 %collective-permute-done.30 = f16[152,608]{1,0:T(8,128)(2,1)S(1)} collective-permute-done((f16[152,608]{1,0:T(8,128)(2,1)S(1)}, f16[152,608]{1,0:T(8,128)(2,1)S(1)}, u32[]{:S(2)}, u32[]{:S(2)}) %collective-permute-start.30) | collective-permute-done | bytes 184864 | tf_op jit(solution)/shard_map/ppermute | solution.py:78
  139.4 3.8 %collective-permute-done.29 = f32[152,608]{1,0:T(8,128)S(1)} collective-permute-done((f32[152,608]{1,0:T(8,128)S(1)}, f32[152,608]{1,0:T(8,128)S(1)}, u32[]{:S(2)}, u32[]{:S(2)}) %collective-permute-start.29) | collective-permute-done | bytes 369696 | tf_op jit(solution)/shard_map/ppermute | solution.py:91
  143.2 6.8 %collective-permute-done.25 = f16[152,608]{1,0:T(8,128)(2,1)S(1)} collective-permute-done((f16[152,608]{1,0:T(8,128)(2,1)S(1)}, f16[152,608]{1,0:T(8,128)(2,1)S(1)}, u32[]{:S(2)}, u32[]{:S(2)}) %collective-permute-start.25) | collective-permute-done | bytes 184864 | tf_op jit(solution)/shard_map/ppermute | solution.py:78
  159.2 2.8 %collective-permute-done.34 = f32[8,128]{1,0:T(8,128)S(1)} collective-permute-done((f32[8,128]{1,0:T(8,128)S(1)}, f32[8,128]{1,0:T(8,128)S(1)}, u32[]{:S(2)}, u32[]{:S(2)}) %collective-permute-start.34) | collective-permute-done | bytes 4128 | tf_op jit(solution)/shard_map/ppermute | solution.py:389
  162.7 2.9 %collective-permute-done.35 = f32[8,128]{1,0:T(8,128)S(1)} collective-permute-done((f32[8,128]{1,0:T(8,128)S(1)}, f32[8,128]{1,0:T(8,128)S(1)}, u32[]{:S(2)}, u32[]{:S(2)}) %collective-permute-start.35) | collective-permute-done | bytes 4128 | tf_op jit(solution)/shard_map/ppermute | solution.py:389
  165.6 2.6 %collective-permute-start.36 = (f32[8,128]{1,0:T(8,128)S(1)}, f32[8,128]{1,0:T(8,128)S(1)}, u32[]{:S(2)}, u32[]{:S(2)}) collective-permute-start(f32[8,128]{1,0:T(8,128)S(1)} %add.90), channel_id=1, source_target_pairs={{0,16},{2,18},{4,20},{6,22},{8,24},{10,26},{12,28},{14,30},{16,0},... | collective-permute-start | bytes 12296 | tf_op jit(solution)/shard_map/ppermute | solution.py:389
  173.1 3.1 %collective-permute-start.42 = (bf16[2,152,608]{2,1,0:T(8,128)(2,1)S(1)}, bf16[2,152,608]{2,1,0:T(8,128)(2,1)S(1)}, u32[]{:S(2)}, u32[]{:S(2)}) collective-permute-start(bf16[2,152,608]{2,1,0:T(8,128)(2,1)S(1)} %get-tuple-element.280), channel_id=1, source_target_pairs={{0,24},{2,26},{4,28},{6,30},{8,0},{10,2},{12,4},{14,6},{16,8},{18,... | collective-permute-start | bytes 1109000 | tf_op jit(solution)/shard_map/ppermute | solution.py:78
  177.0 4.1 %shard_map.219 = bf16[608,1024]{1,0:T(8,128)(2,1)} custom-call(f32[2]{0:T(128)S(1)} %copy-done.23, bf16[608,2432]{1,0:T(8,128)(2,1)S(1)} %copy-done.1, bf16[2,2,152,512]{3,2,1,0:T(8,128)(2,1)} %collective-permute-done.2.refs_0_, bf16[2,2,152,512]{3,2,1,0:T(8,128)(2,1)S(1)} %collective-permute-done.37.refs_1_, ...), custom_call_target="tpu_custom_call", output_to_operand_aliasing={{}: (6, {})} | custom-call | flops 99999997952 | tf_op jit(solution)/shard_map/pallas_call | solution.py:56
  181.1 8.4 %collective-permute-done.42 = bf16[2,152,608]{2,1,0:T(8,128)(2,1)S(1)} collective-permute-done((bf16[2,152,608]{2,1,0:T(8,128)(2,1)S(1)}, bf16[2,152,608]{2,1,0:T(8,128)(2,1)S(1)}, u32[]{:S(2)}, u32[]{:S(2)}) %collective-permute-start.42) | collective-permute-done | bytes 369696 | tf_op jit(solution)/shard_map/ppermute | solution.py:78
  192.7 8.7 %collective-permute-done.43 = bf16[2,152,608]{2,1,0:T(8,128)(2,1)S(1)} collective-permute-done((bf16[2,152,608]{2,1,0:T(8,128)(2,1)S(1)}, bf16[2,152,608]{2,1,0:T(8,128)(2,1)S(1)}, u32[]{:S(2)}, u32[]{:S(2)}) %collective-permute-start.43) | collective-permute-done | bytes 369696 | tf_op jit(solution)/shard_map/ppermute | solution.py:78
  201.8 7.8 %collective-permute-done.40 = bf16[2,152,608]{2,1,0:T(8,128)(2,1)S(1)} collective-permute-done((bf16[2,152,608]{2,1,0:T(8,128)(2,1)S(1)}, bf16[2,152,608]{2,1,0:T(8,128)(2,1)S(1)}, u32[]{:S(2)}, u32[]{:S(2)}) %collective-permute-start.40) | collective-permute-done | bytes 369696 | tf_op jit(solution)/shard_map/ppermute | solution.py:78
  210.8 8.8 %collective-permute-done.45 = bf16[2,152,608]{2,1,0:T(8,128)(2,1)S(1)} collective-permute-done((bf16[2,152,608]{2,1,0:T(8,128)(2,1)S(1)}, bf16[2,152,608]{2,1,0:T(8,128)(2,1)S(1)}, u32[]{:S(2)}, u32[]{:S(2)}) %collective-permute-start.45) | collective-permute-done | bytes 369696 | tf_op jit(solution)/shard_map/ppermute | solution.py:78
  222.1 4.3 %shard_map.220 = bf16[608,1024]{1,0:T(8,128)(2,1)} custom-call(f32[2]{0:T(128)S(1)} %copy-done.24, bf16[608,2432]{1,0:T(8,128)(2,1)S(1)} %copy-done.3, bf16[512,2432]{1,0:T(8,128)(2,1)} %collective-permute-done.39.refs_0_, bf16[608,1024]{1,0:T(8,128)(2,1)} %shard_map.214.refs_1_), custom_call_target="tpu_custom_call", output_to_operand_aliasing={{}: (3, {})} | custom-call | flops 99999997952 | tf_op jit(solution)/shard_map/pallas_call | solution.py:56
  226.5 4.1 %shard_map.221 = bf16[608,2432]{1,0:T(8,128)(2,1)} custom-call(bf16[4,2,152,608]{3,2,1,0:T(8,128)(2,1)S(1)} %pad_maximum_fusion.refs_0_, bf16[4,2,152,608]{3,2,1,0:T(8,128)(2,1)S(1)} %pad_maximum_fusion.1.refs_1_, bf16[4,2,152,608]{3,2,1,0:T(8,128)(2,1)S(1)} %collective-permute-done.47.refs_2_, bf16[4,2,152,608]{3,2,1,0:T(8,128)(2,1)S(1)} %collective-permute-done.48.refs_3_), custom_call_target="tpu_custom_call" | custom-call | flops 99999997952 | tf_op jit(solution)/shard_map/pallas_call | solution.py:56
  230.6 4.1 %shard_map.222 = bf16[608,2432]{1,0:T(8,128)(2,1)} custom-call(bf16[4,2,152,608]{3,2,1,0:T(8,128)(2,1)S(1)} %pad_maximum_fusion.refs_0_, bf16[4,2,152,608]{3,2,1,0:T(8,128)(2,1)S(1)} %pad_maximum_fusion.1.refs_1_, bf16[4,2,152,608]{3,2,1,0:T(8,128)(2,1)S(1)} %collective-permute-done.47.refs_2_, bf16[4,2,152,608]{3,2,1,0:T(8,128)(2,1)S(1)} %collective-permute-done.48.refs_3_), custom_call_target="tpu_custom_call" | custom-call | flops 99999997952 | tf_op jit(solution)/shard_map/pallas_call | solution.py:56
  (180 shorter events, 71.8 us)
Async XLA Ops:
  3.0 24.5 %collective-permute-start.8 = (bf16[608,512]{1,0:T(8,128)(2,1)}, bf16[608,512]{1,0:T(8,128)(2,1)}, u32[]{:S(2)}, u32[]{:S(2)}) collective-permute-start(bf16[608,512]{1,0:T(8,128)(2,1)} %shard_map.204), channel_id=1, source_target_pairs={{0,1},{1,0},{2,3},{3,2},{4,5},{5,4},{6,7},{7,6},{8,9},{9,8},{10,11... | collective-permute-start | bytes 1867784 | tf_op jit(solution)/shard_map/ppermute | solution.py:91
  13.2 17.1 %collective-permute-start.7 = (bf16[2,4,152,512]{3,2,1,0:T(8,128)(2,1)}, bf16[2,4,152,512]{3,2,1,0:T(8,128)(2,1)}, u32[]{:S(2)}, u32[]{:S(2)}) collective-permute-start(bf16[2,4,152,512]{3,2,1,0:T(8,128)(2,1)} %get-tuple-element.179), channel_id=1, source_target_pairs={{0,2},{2,0},{4,6},{6,4},{8,10},{10,8},{12,14},{14,12},{16,18},{18,... | collective-permute-start | bytes 3735560 | tf_op jit(solution)/shard_map/ppermute | solution.py:78
  16.6 13.4 %collective-permute-start.11 = (bf16[1,608,512]{2,1,0:T(8,128)(2,1)}, bf16[1,608,512]{2,1,0:T(8,128)(2,1)}, u32[]{:S(2)}, u32[]{:S(2)}) collective-permute-start(bf16[1,608,512]{2,1,0:T(8,128)(2,1)} %shard_map.207.refs_2_), channel_id=1, source_target_pairs={{0,2},{2,0},{4,6},{6,4},{8,10},{10,8},{12,14},{14,12},{16,18},{18,... | collective-permute-start | bytes 1867784 | tf_op jit(solution)/shard_map/ppermute | solution.py:78
  21.7 59.6 %collective-permute-start.12 = (bf16[2,2,152,512]{3,2,1,0:T(8,128)(2,1)}, bf16[2,2,152,512]{3,2,1,0:T(8,128)(2,1)}, u32[]{:S(2)}, u32[]{:S(2)}) collective-permute-start(bf16[2,2,152,512]{3,2,1,0:T(8,128)(2,1)} %get-tuple-element.177), channel_id=1, source_target_pairs={{0,3},{1,2},{2,1},{3,0},{4,7},{5,6},{6,5},{7,4},{8,11},{9,10},{10,... | collective-permute-start | bytes 1867784 | tf_op jit(solution)/shard_map/ppermute | solution.py:100
  26.2 11.8 %collective-permute-start.5 = (bf16[2,2,152,512]{3,2,1,0:T(8,128)(2,1)}, bf16[2,2,152,512]{3,2,1,0:T(8,128)(2,1)}, u32[]{:S(2)}, u32[]{:S(2)}) collective-permute-start(bf16[2,2,152,512]{3,2,1,0:T(8,128)(2,1)} %get-tuple-element.177), channel_id=1, source_target_pairs={{0,2},{2,0},{4,6},{6,4},{8,10},{10,8},{12,14},{14,12},{16,18},{18,... | collective-permute-start | bytes 1867784 | tf_op jit(solution)/shard_map/ppermute | solution.py:78
  27.5 54.0 %collective-permute-start.2 = (bf16[2,2,152,512]{3,2,1,0:T(8,128)(2,1)}, bf16[2,2,152,512]{3,2,1,0:T(8,128)(2,1)}, u32[]{:S(2)}, u32[]{:S(2)}) collective-permute-start(bf16[2,2,152,512]{3,2,1,0:T(8,128)(2,1)} %get-tuple-element.205), channel_id=1, source_target_pairs={{0,1},{1,0},{2,3},{3,2},{4,5},{5,4},{6,7},{7,6},{8,9},{9,8},{10,11... | collective-permute-start | bytes 1867784 | tf_op jit(solution)/shard_map/ppermute | solution.py:91
  40.9 11.9 %collective-permute-start.14 = (f16[2,152,608]{2,1,0:T(8,128)(2,1)S(1)}, f16[2,152,608]{2,1,0:T(8,128)(2,1)S(1)}, u32[]{:S(2)}, u32[]{:S(2)}) collective-permute-start(f16[2,152,608]{2,1,0:T(8,128)(2,1)S(1)} %get-tuple-element.310), channel_id=1, source_target_pairs={{0,4},{2,6},{4,0},{6,2},{8,12},{10,14},{12,8},{14,10},{16,20},{18,... | collective-permute-start | bytes 1109000 | tf_op jit(solution)/shard_map/ppermute | solution.py:78
  44.6 56.3 %collective-permute-start.22 = (f16[2,152,608]{2,1,0:T(8,128)(2,1)}, f16[2,152,608]{2,1,0:T(8,128)(2,1)}, u32[]{:S(2)}, u32[]{:S(2)}) collective-permute-start(f16[2,152,608]{2,1,0:T(8,128)(2,1)} %get-tuple-element.309), channel_id=1, source_target_pairs={{0,4},{2,6},{4,0},{6,2},{8,12},{10,14},{12,8},{14,10},{16,20},{18,... | collective-permute-start | bytes 1109000 | tf_op jit(solution)/shard_map/ppermute | solution.py:78
  45.5 57.9 %collective-permute-start.21 = (f16[2,152,608]{2,1,0:T(8,128)(2,1)}, f16[2,152,608]{2,1,0:T(8,128)(2,1)}, u32[]{:S(2)}, u32[]{:S(2)}) collective-permute-start(f16[2,152,608]{2,1,0:T(8,128)(2,1)} %get-tuple-element.307), channel_id=1, source_target_pairs={{0,4},{2,6},{4,0},{6,2},{8,12},{10,14},{12,8},{14,10},{16,20},{18,... | collective-permute-start | bytes 1109000 | tf_op jit(solution)/shard_map/ppermute | solution.py:78
  52.8 24.4 %collective-permute-start.13 = (f16[2,152,608]{2,1,0:T(8,128)(2,1)S(1)}, f16[2,152,608]{2,1,0:T(8,128)(2,1)S(1)}, u32[]{:S(2)}, u32[]{:S(2)}) collective-permute-start(f16[2,152,608]{2,1,0:T(8,128)(2,1)S(1)} %get-tuple-element.312), channel_id=1, source_target_pairs={{0,4},{2,6},{4,0},{6,2},{8,12},{10,14},{12,8},{14,10},{16,20},{18,... | collective-permute-start | bytes 1109000 | tf_op jit(solution)/shard_map/ppermute | solution.py:78
  77.1 19.6 %collective-permute-start.17 = (f16[152,608]{1,0:T(8,128)(2,1)S(1)}, f16[152,608]{1,0:T(8,128)(2,1)S(1)}, u32[]{:S(2)}, u32[]{:S(2)}) collective-permute-start(f16[152,608]{1,0:T(8,128)(2,1)S(1)} %get-tuple-element.327), channel_id=1, source_target_pairs={{0,24},{2,26},{4,28},{6,30},{8,0},{10,2},{12,4},{14,6},{16,8},{18,... | collective-permute-start | bytes 554504 | tf_op jit(solution)/shard_map/ppermute | solution.py:78
  81.2 15.5 %collective-permute-start.18 = (f16[152,608]{1,0:T(8,128)(2,1)S(1)}, f16[152,608]{1,0:T(8,128)(2,1)S(1)}, u32[]{:S(2)}, u32[]{:S(2)}) collective-permute-start(f16[152,608]{1,0:T(8,128)(2,1)S(1)} %get-tuple-element.326), channel_id=1, source_target_pairs={{0,16},{2,18},{4,20},{6,22},{8,24},{10,26},{12,28},{14,30},{16,0},... | collective-permute-start | bytes 554504 | tf_op jit(solution)/shard_map/ppermute | solution.py:78
  81.5 16.4 %collective-permute-start.19 = (f16[152,608]{1,0:T(8,128)(2,1)S(1)}, f16[152,608]{1,0:T(8,128)(2,1)S(1)}, u32[]{:S(2)}, u32[]{:S(2)}) collective-permute-start(f16[152,608]{1,0:T(8,128)(2,1)S(1)} %get-tuple-element.329), channel_id=1, source_target_pairs={{0,8},{2,10},{4,12},{6,14},{8,16},{10,18},{12,20},{14,22},{16,24},... | collective-permute-start | bytes 554504 | tf_op jit(solution)/shard_map/ppermute | solution.py:78
  96.8 16.6 %collective-permute-start.16 = (bf16[2,2,152,512]{3,2,1,0:T(8,128)(2,1)}, bf16[2,2,152,512]{3,2,1,0:T(8,128)(2,1)S(1)}, u32[]{:S(2)}, u32[]{:S(2)}) collective-permute-start(bf16[2,2,152,512]{3,2,1,0:T(8,128)(2,1)} %get-tuple-element.212), channel_id=1, source_target_pairs={{0,3},{1,2},{2,1},{3,0},{4,7},{5,6},{6,5},{7,4},{8,11},{9,10},{10,... | collective-permute-start | bytes 1867784 | tf_op jit(solution)/shard_map/ppermute | solution.py:100
  96.8 29.3 %collective-permute-start.15 = (bf16[2,2,152,512]{3,2,1,0:T(8,128)(2,1)S(1)}, bf16[2,2,152,512]{3,2,1,0:T(8,128)(2,1)S(1)}, u32[]{:S(2)}, u32[]{:S(2)}) collective-permute-start(bf16[2,2,152,512]{3,2,1,0:T(8,128)(2,1)S(1)} %get-tuple-element.224), channel_id=1, source_target_pairs={{0,1},{1,0},{2,3},{3,2},{4,5},{5,4},{6,7},{7,6},{8,9},{9,8},{10,11... | collective-permute-start | bytes 1867784 | tf_op jit(solution)/shard_map/ppermute | solution.py:91
  99.5 11.8 %collective-permute-start.20 = (f16[2,152,608]{2,1,0:T(8,128)(2,1)S(1)}, f16[2,152,608]{2,1,0:T(8,128)(2,1)S(1)}, u32[]{:S(2)}, u32[]{:S(2)}) collective-permute-start(f16[2,152,608]{2,1,0:T(8,128)(2,1)S(1)} %get-tuple-element.318), channel_id=1, source_target_pairs={{0,4},{2,6},{4,0},{6,2},{8,12},{10,14},{12,8},{14,10},{16,20},{18,... | collective-permute-start | bytes 1109000 | tf_op jit(solution)/shard_map/ppermute | solution.py:78
  103.4 28.1 %collective-permute-start.26 = (f16[152,608]{1,0:T(8,128)(2,1)S(1)}, f16[152,608]{1,0:T(8,128)(2,1)S(1)}, u32[]{:S(2)}, u32[]{:S(2)}) collective-permute-start(f16[152,608]{1,0:T(8,128)(2,1)S(1)} %get-tuple-element.321), channel_id=1, source_target_pairs={{0,24},{2,26},{4,28},{6,30},{8,0},{10,2},{12,4},{14,6},{16,8},{18,... | collective-permute-start | bytes 554504 | tf_op jit(solution)/shard_map/ppermute | solution.py:78
  105.9 25.6 %collective-permute-start.28 = (f16[152,608]{1,0:T(8,128)(2,1)S(1)}, f16[152,608]{1,0:T(8,128)(2,1)S(1)}, u32[]{:S(2)}, u32[]{:S(2)}) collective-permute-start(f16[152,608]{1,0:T(8,128)(2,1)S(1)} %get-tuple-element.323), channel_id=1, source_target_pairs={{0,8},{2,10},{4,12},{6,14},{8,16},{10,18},{12,20},{14,22},{16,24},... | collective-permute-start | bytes 554504 | tf_op jit(solution)/shard_map/ppermute | solution.py:78
  111.2 20.3 %collective-permute-start.27 = (f16[152,608]{1,0:T(8,128)(2,1)S(1)}, f16[152,608]{1,0:T(8,128)(2,1)S(1)}, u32[]{:S(2)}, u32[]{:S(2)}) collective-permute-start(f16[152,608]{1,0:T(8,128)(2,1)S(1)} %get-tuple-element.320), channel_id=1, source_target_pairs={{0,16},{2,18},{4,20},{6,22},{8,24},{10,26},{12,28},{14,30},{16,0},... | collective-permute-start | bytes 554504 | tf_op jit(solution)/shard_map/ppermute | solution.py:78
  133.3 16.7 %collective-permute-start.24 = (f16[152,608]{1,0:T(8,128)(2,1)S(1)}, f16[152,608]{1,0:T(8,128)(2,1)S(1)}, u32[]{:S(2)}, u32[]{:S(2)}) collective-permute-start(f16[152,608]{1,0:T(8,128)(2,1)S(1)} %get-tuple-element.325), channel_id=1, source_target_pairs={{0,24},{2,26},{4,28},{6,30},{8,0},{10,2},{12,4},{14,6},{16,8},{18,... | collective-permute-start | bytes 554504 | tf_op jit(solution)/shard_map/ppermute | solution.py:78
  133.6 16.5 %collective-permute-start.25 = (f16[152,608]{1,0:T(8,128)(2,1)S(1)}, f16[152,608]{1,0:T(8,128)(2,1)S(1)}, u32[]{:S(2)}, u32[]{:S(2)}) collective-permute-start(f16[152,608]{1,0:T(8,128)(2,1)S(1)} %get-tuple-element.324), channel_id=1, source_target_pairs={{0,16},{2,18},{4,20},{6,22},{8,24},{10,26},{12,28},{14,30},{16,0},... | collective-permute-start | bytes 554504 | tf_op jit(solution)/shard_map/ppermute | solution.py:78
  133.6 16.5 %collective-permute-start.23 = (f16[152,608]{1,0:T(8,128)(2,1)S(1)}, f16[152,608]{1,0:T(8,128)(2,1)S(1)}, u32[]{:S(2)}, u32[]{:S(2)}) collective-permute-start(f16[152,608]{1,0:T(8,128)(2,1)S(1)} %get-tuple-element.316), channel_id=1, source_target_pairs={{0,4},{2,6},{4,0},{6,2},{8,12},{10,14},{12,8},{14,10},{16,20},{18,... | collective-permute-start | bytes 554504 | tf_op jit(solution)/shard_map/ppermute | solution.py:78
  155.5 14.7 %collective-permute-start.38 = (bf16[2,2,152,512]{3,2,1,0:T(8,128)(2,1)S(1)}, bf16[2,2,152,512]{3,2,1,0:T(8,128)(2,1)S(1)}, u32[]{:S(2)}, u32[]{:S(2)}) collective-permute-start(bf16[2,2,152,512]{3,2,1,0:T(8,128)(2,1)S(1)} %collective-permute-done.16), channel_id=1, source_target_pairs={{0,2},{2,0},{4,6},{6,4},{8,10},{10,8},{12,14},{14,12},{16,18},{18,... | collective-permute-start | bytes 1867784 | tf_op jit(solution)/shard_map/ppermute | solution.py:78
  155.5 14.7 %collective-permute-start.37 = (bf16[2,2,152,512]{3,2,1,0:T(8,128)(2,1)}, bf16[2,2,152,512]{3,2,1,0:T(8,128)(2,1)S(1)}, u32[]{:S(2)}, u32[]{:S(2)}) collective-permute-start(bf16[2,2,152,512]{3,2,1,0:T(8,128)(2,1)} %collective-permute-done.12), channel_id=1, source_target_pairs={{0,2},{2,0},{4,6},{6,4},{8,10},{10,8},{12,14},{14,12},{16,18},{18,... | collective-permute-start | bytes 1867784 | tf_op jit(solution)/shard_map/ppermute | solution.py:78
  168.3 53.8 %collective-permute-start.39 = (bf16[512,2432]{1,0:T(8,128)(2,1)}, bf16[512,2432]{1,0:T(8,128)(2,1)}, u32[]{:S(2)}, u32[]{:S(2)}) collective-permute-start(bf16[512,2432]{1,0:T(8,128)(2,1)} %refs_0_.2), channel_id=1, source_target_pairs={{0,1},{1,0},{2,3},{3,2},{4,5},{5,4},{6,7},{7,6},{8,9},{9,8},{10,11... | collective-permute-start | bytes 7471112 | tf_op jit(solution)/shard_map/ppermute | solution.py:91
  172.3 19.2 %collective-permute-start.44 = (bf16[2,152,608]{2,1,0:T(8,128)(2,1)S(1)}, bf16[2,152,608]{2,1,0:T(8,128)(2,1)S(1)}, u32[]{:S(2)}, u32[]{:S(2)}) collective-permute-start(bf16[2,152,608]{2,1,0:T(8,128)(2,1)S(1)} %get-tuple-element.280), channel_id=1, source_target_pairs={{0,8},{2,10},{4,12},{6,14},{8,16},{10,18},{12,20},{14,22},{16,24},... | collective-permute-start | bytes 1109000 | tf_op jit(solution)/shard_map/ppermute | solution.py:78
  173.1 16.4 %collective-permute-start.42 = (bf16[2,152,608]{2,1,0:T(8,128)(2,1)S(1)}, bf16[2,152,608]{2,1,0:T(8,128)(2,1)S(1)}, u32[]{:S(2)}, u32[]{:S(2)}) collective-permute-start(bf16[2,152,608]{2,1,0:T(8,128)(2,1)S(1)} %get-tuple-element.280), channel_id=1, source_target_pairs={{0,24},{2,26},{4,28},{6,30},{8,0},{10,2},{12,4},{14,6},{16,8},{18,... | collective-permute-start | bytes 1109000 | tf_op jit(solution)/shard_map/ppermute | solution.py:78
  176.2 16.6 %collective-permute-start.41 = (bf16[2,152,608]{2,1,0:T(8,128)(2,1)S(1)}, bf16[2,152,608]{2,1,0:T(8,128)(2,1)S(1)}, u32[]{:S(2)}, u32[]{:S(2)}) collective-permute-start(bf16[2,152,608]{2,1,0:T(8,128)(2,1)S(1)} %get-tuple-element.280), channel_id=1, source_target_pairs={{0,4},{2,6},{4,0},{6,2},{8,12},{10,14},{12,8},{14,10},{16,20},{18,... | collective-permute-start | bytes 1109000 | tf_op jit(solution)/shard_map/ppermute | solution.py:78
  189.5 12.0 %collective-permute-start.43 = (bf16[2,152,608]{2,1,0:T(8,128)(2,1)S(1)}, bf16[2,152,608]{2,1,0:T(8,128)(2,1)S(1)}, u32[]{:S(2)}, u32[]{:S(2)}) collective-permute-start(bf16[2,152,608]{2,1,0:T(8,128)(2,1)S(1)} %collective-permute-done.42), channel_id=1, source_target_pairs={{0,4},{2,6},{4,0},{6,2},{8,12},{10,14},{12,8},{14,10},{16,20},{18,... | collective-permute-start | bytes 1109000 | tf_op jit(solution)/shard_map/ppermute | solution.py:78
  190.3 19.3 %collective-permute-start.40 = (bf16[2,152,608]{2,1,0:T(8,128)(2,1)S(1)}, bf16[2,152,608]{2,1,0:T(8,128)(2,1)S(1)}, u32[]{:S(2)}, u32[]{:S(2)}) collective-permute-start(bf16[2,152,608]{2,1,0:T(8,128)(2,1)S(1)} %get-tuple-element.280), channel_id=1, source_target_pairs={{0,16},{2,18},{4,20},{6,22},{8,24},{10,26},{12,28},{14,30},{16,0},... | collective-permute-start | bytes 1109000 | tf_op jit(solution)/shard_map/ppermute | solution.py:78
  191.5 19.3 %collective-permute-start.46 = (bf16[2,152,608]{2,1,0:T(8,128)(2,1)S(1)}, bf16[2,152,608]{2,1,0:T(8,128)(2,1)S(1)}, u32[]{:S(2)}, u32[]{:S(2)}) collective-permute-start(bf16[2,152,608]{2,1,0:T(8,128)(2,1)S(1)} %collective-permute-done.44), channel_id=1, source_target_pairs={{0,4},{2,6},{4,0},{6,2},{8,12},{10,14},{12,8},{14,10},{16,20},{18,... | collective-permute-start | bytes 1109000 | tf_op jit(solution)/shard_map/ppermute | solution.py:78
  210.8 15.7 %collective-permute-start.47 = (bf16[4,2,152,608]{3,2,1,0:T(8,128)(2,1)S(1)}, bf16[4,2,152,608]{3,2,1,0:T(8,128)(2,1)S(1)}, u32[]{:S(2)}, u32[]{:S(2)}) collective-permute-start(bf16[4,2,152,608]{3,2,1,0:T(8,128)(2,1)S(1)} %pad_maximum_fusion.refs_0_), channel_id=1, source_target_pairs={{0,2},{2,0},{4,6},{6,4},{8,10},{10,8},{12,14},{14,12},{16,18},{18,... | collective-permute-start | bytes 4435976 | tf_op jit(solution)/shard_map/ppermute | solution.py:78
  (46 other events, 347.4 us)

commit v7 on v6

--- a/solution.py
+++ b/solution.py
@@ -57,7 +57,7 @@
         kernel,
         out_shape=out_shape,
         compiler_params=pltpu.CompilerParams(vmem_limit_bytes=mib * 1024 * 1024),
-        cost_estimate=pl.CostEstimate(flops=100 * 10**9, bytes_accessed=0, transcendentals=0),
+        cost_estimate=pl.CostEstimate(flops=0, bytes_accessed=0, transcendentals=0),
         **kwargs,
     )(*operands)
 
@@ -78,7 +78,7 @@
         return lax.ppermute(value, "dp", perm)
 
     def to_plane(value, k):
-        return move_dp(value, lambda z, m, c: ((z + k) & (OUTER - 1), m, c))
+        return move_dp(value, lambda z, m, c: (z ^ k, m, c))
 
     def to_middle(value, k):
         return move_dp(value, lambda z, m, c: (z, (m + k) & (inner - 1), c))
@@ -105,11 +105,11 @@
     def relative(p):
         z, m, c = split(p)
         my_z, my_m, my_c = my_place()
-        return (z - my_z) & (OUTER - 1), (m - my_m) & (inner - 1), c ^ my_c
+        return z ^ my_z, (m - my_m) & (inner - 1), c ^ my_c
 
     def owner(k, i, other):
         z, m, c = my_place()
-        return join((z + k) & (OUTER - 1), (m + i) & (inner - 1), c ^ other)
+        return join(z ^ k, (m + i) & (inner - 1), c ^ other)
 
     def first_row(j, r):
         start = ((lax.axis_index("tensor") + j) & (n_tensor - 1)) * r
@@ -198,7 +198,8 @@
                 block = wide_ref[p * width : (p + 1) * width, :].astype(jnp.bfloat16)
                 which, at = other, (i, k)
                 if by_planes:
-                    which, at = 2 - 2 * (k >> 1) + other, (1 - (k & 1), i)
+                    even = 1 - (k & 1)
+                    which, at = 2 * even + other, ((k >> 1) ^ even, i)
                 for n in range(count):
 
                     @pl.when(which == n)
@@ -308,7 +309,8 @@
                 for k in range(OUTER):
                     for other in range(2):
                         for i in range(inner):
-                            block = piece_refs[2 - 2 * (k >> 1) + other][1 - (k & 1), i]
+                            even = 1 - (k & 1)
+                            block = piece_refs[2 * even + other][(k >> 1) ^ even, i]
                             block = block.astype(jnp.float32)
                             wide_ref[owner(k, i, other)] = block
                 flat = wide_ref[...].reshape(D, size).astype(jnp.bfloat16)
@@ -404,10 +406,8 @@
         next(bounds)
         fake_blocks = step(lambda cot: turn(cot, False), cot_fake)
         mate_blocks = to_core(fake_blocks[1])
-        next(bounds)
         scaled_own = step(lambda act: prepare(1, act, scales, r, 1), act_fake)
         scaled_fake = [[scaled_own, to_core(scaled_own)]]
-        next(bounds)
         planes = step(lambda cot: turn(cot, True), cot_student)
 
         same, diagonal = [], []
@@ -417,65 +417,76 @@
             diagonal.append([from_diagonal(other, j) for j in range(1, n_tensor)])
 
         send_planes(0, planes[0], planes[1])
-        next(bounds)
         scaled_student = step(lambda act: prepare(0, act, scales, r, n_tensor), act_student)
-        while (final := next(bounds)) is None:
-            pass
-
-        def factors(bounds):
-            bounds = jnp.maximum(bounds, 1e-30) * (1.01 * count * n_dp / HALF_LIMIT)
-            return bounds[:2, 0], 1.0 / bounds[:2, 0]
-
-        grow, fit = step(factors, final)
-
-        def shrink(value, net):
-            return (value * fit[net]).astype(jnp.float16)
-
-        def widen(value, net):
-            return value.astype(jnp.float32) * grow[net]
-
-        def add_widened(total, values, net):
-            for value in values:
-                total = total + widen(value, net)
-            return total
-
+        for act in acts:
+            scaled_other = step(scale_rows, act, scales)
+            scaled_fake.append([scaled_other, to_core(scaled_other)])
         parts_fake = []
-
-        def multiply_fake(j):
+        for j in range(n_tensor):
+            if j < 2:
+                next(bounds)
             parts_fake.append(
                 step(
                     lambda a, b, c, d: multiply([a, b], [c, d], [(0, 0), (1, 0)]),
                     fake_blocks[0], mate_blocks, *scaled_fake[j],
                 )
             )
-
-        for act in acts:
-            scaled_other = step(scale_rows, act, scales)
-            scaled_fake.append([scaled_other, to_core(scaled_other)])
-        multiply_fake(0)
+        while (final := next(bounds)) is None:
+            pass
+
+        def factors(bounds):
+            bounds = jnp.maximum(bounds, 1e-30) * (1.01 * count * n_dp / HALF_LIMIT)
+            return bounds[:2, 0], 1.0 / bounds[:2, 0]
+
+        grow, fit = step(factors, final)
+
+        def shrink(value, net):
+            return (value * fit[net]).astype(jnp.float16)
+
+        def widen(value, net):
+            return value.astype(jnp.float32) * grow[net]
+
+        def add_widened(total, values, net):
+            for value in values:
+                total = total + widen(value, net)
+            return total
+
+        fake_own, fake_got = {}, {}
+
+        def fake_middle(j):
+            def work(both):
+                sent = [shrink(both[i], 1) for i in range(1, inner)]
+                return sent, both[0]
+
+            sent, fake_own[j] = step(work, parts_fake[j])
+            fake_got[j] = [to_middle(value, i) for i, value in enumerate(sent, 1)]
+
+        def fake_near(j):
+            def work(own, *got):
+                own = add_widened(own, got, 1)
+                return shrink(own[1::2], 1), own[0::2]
+
+            sent, fake_own[j] = step(work, fake_own[j], *fake_got[j])
+            fake_got[j] = [to_plane(sent, 1)]
+
+        def fake_far(j):
+            def work(own, *got):
+                own = add_widened(own, got, 1)
+                return shrink(own[1], 1), own[0]
+
+            sent, fake_own[j] = step(work, fake_own[j], *fake_got[j])
+            fake_got[j] = [to_plane(sent, 2)]
+
+        def fake_total(j):
+            return step(
+                lambda own, *got: add_widened(own, got, 1), fake_own[j], *fake_got[j]
+            )
+
         mate_student = to_core(scaled_student)
         mate_planes = [to_core(planes[1]), to_core(planes[3])]
-        for j in range(1, n_tensor):
-            multiply_fake(j)
-        mate_student, *mate_planes = step(lambda *values: values, mate_student, *mate_planes)
-
-        middles = {}
-
-        def fake_middle(j):
-            def work(both):
-                sent = [
-                    [shrink(both[i, lo : lo + 2], 1) for i in range(1, inner)] for lo in (2, 0)
-                ]
-                return sent, both[0, 2:], both[0, :2]
-
-            sent, *mine = step(work, parts_fake[j])
-            middles[j] = [
-                (own, [to_middle(value, i) for i, value in enumerate(values, 1)])
-                for own, values in zip(mine, sent)
-            ]
-
         for j in range(n_tensor):
             fake_middle(j)
+        mate_student, *mate_planes = step(lambda *values: values, mate_student, *mate_planes)
 
         def back(whole, net, pieces, j, low, size):
             weight = (weight_student, weight_fake)[net]
@@ -488,24 +499,6 @@
                 )
 
             return step(work, weight, *pieces, *has)
-
-        fake_sums = {j: [] for j in range(n_tensor)}
-
-        def fake_planes(j, part):
-            def work(own, *got):
-                own = add_widened(own, got, 1)
-                if part == 0:
-                    return shrink(own[1], 1), shrink(own[0], 1)
-                return shrink(own[1], 1), own[0]
-
-            own, got = middles[j][part]
-            values = step(work, own, *got)
-            for k, value in zip(((3, 2), (1, 0))[part], values):
-                fake_sums[j].append(to_plane(value, k) if k else value)
-
-        def fake_total(j):
-            *got, own = fake_sums[j]
-            return step(lambda own, *got: add_widened(own, got, 1), own, *got)
 
         def multiply_student(g):
             pieces, places = [planes[2 * g], mate_planes[g]], [(0, 0), (1, 0)]
@@ -518,59 +511,57 @@
             )
 
         back_student = back(None, 0, [cot_student], 0, 0, r)
-        fake_planes(0, 0)
+        send_planes(1, *step(lambda a, b: (a, b), planes[2], planes[3]))
         back_fake = back(None, 1, [cot_fake], 0, 0, r)
-        fake_planes(0, 1)
         both = multiply_student(0)
-        send_planes(1, *step(lambda a, b: (a, b), planes[2], planes[3]))
 
         def first_middle(both):
             return [shrink(both[:, i], 0) for i in range(1, inner)], both[:, 0]
 
-        fake_mine = fake_total(0)
         sent, own = step(first_middle, both)
         got = [to_middle(value, i) for i, value in enumerate(sent, 1)]
-        for j in range(1, n_tensor):
-            fake_planes(j, 0)
-        for j in range(1, n_tensor):
-            fake_planes(j, 1)
+        for j in range(n_tensor):
+            fake_near(j)
 
         def first_planes(own, *got):
-            own = add_widened(own, got, 0)
-            return shrink(own[0], 0), shrink(own[1], 0)
-
-        sent = step(first_planes, own, *got)
-        first_got = [to_plane(value, k) for k, value in zip((3, 2), sent)]
+            return shrink(add_widened(own, got, 0), 0)
+
+        near = to_plane(step(first_planes, own, *got), 1)
+        for j in range(n_tensor):
+            fake_far(j)
         both = multiply_student(1)
 
         def second_middle(both):
             sent = [[shrink(both[n, i], 0) for i in range(1, inner)] for n in range(2)]
             return sent, both[0, 0], both[1, 0]
 
-        sent, own_next, own = step(second_middle, both)
-        got_next, got = (
+        sent, own_far, own = step(second_middle, both)
+        got_far, got = (
             [to_middle(value, i) for i, value in enumerate(values, 1)] for values in sent
         )
+        fake_mine = fake_total(0)
         fake_others = [fake_total(j) for j in range(1, n_tensor)]
-        fake_got = [from_tensor(value, j) for j, value in enumerate(fake_others, 1)]
-        next_sent = step(
-            lambda own, *got: shrink(add_widened(own, got, 0), 0), own_next, *got_next
-        )
-        next_got = to_plane(next_sent, 1)
-        total_fake = reduced(jnp.add, fake_mine, fake_got)
+        others_got = [from_tensor(value, j) for j, value in enumerate(fake_others, 1)]
+
+        def far_plane(own, near, *got):
+            return shrink(add_widened(own, (near[1], *got), 0), 0)
+
+        far = to_plane(step(far_plane, own_far, near, *got_far), 2)
         total_student = step(
-            lambda own, *got: add_widened(own, got, 0), own, *got, *first_got
-        )
+            lambda own, near, *got: add_widened(own, (near[0], *got), 0), own, near, *got
+        )
+        total_fake = reduced(jnp.add, fake_mine, others_got)
         total_student = step(
-            lambda own, *got: add_widened(own, got, 0), total_student, next_got
+            lambda own, got: add_widened(own, (got,), 0), total_student, far
         )
         squares = step(norms, total_student, total_fake)
         squares = reduced(
             jnp.add, squares, [from_tensor(squares, j) for j in range(1, n_tensor)]
         )
 
-        raw_sent = step(lambda cot: cot, cot_fake)
-        raw = [from_tensor(raw_sent, j) for j in range(1, n_tensor)]
+        rows = step(lambda cot: cot, cot_fake)
+        raw = [from_tensor(rows, j) for j in range(1, n_tensor)]
+
         hidden = step(lambda *values: values, *[value for group in diagonal for value in group])
         mate_others = [to_core(value) for value in hidden]
         *_, squares = hops(squares, jnp.add)
@@ -591,7 +582,7 @@
             mine[k] = [value] + [to_middle(value, -i) for i in range(1, inner)]
 
         spread_middle(0, own)
-        planes_got = {k: to_plane(own, -k) for k in (1, 3, 2)}
+        planes_got = {k: to_plane(own, k) for k in (1, 3, 2)}
         for j in range(1, n_tensor):
             pieces = [
                 piece for g in range(2) for piece in (same[g][j - 1], mate_others[g][j - 1])
@@ -599,13 +590,13 @@
             back_student = back(back_student, 0, pieces, j, 0, r)
         spread_middle(1, step(lambda value: value, planes_got[1]))
         spread_middle(3, step(lambda value: value, planes_got[3]))
+        spread_middle(2, step(lambda value: value, planes_got[2]))
         first_half = step(lambda *values: jnp.stack(values), *mine[0], *mine[1])
         theirs = [to_core(first_half)]
-        spread_middle(2, step(lambda value: value, planes_got[2]))
+        for j in range(1, n_tensor):
+            back_fake = back(back_fake, 1, [raw[j - 1]], j, 0, r)
         second_half = step(lambda *values: jnp.stack(values), *mine[2], *mine[3])
         theirs.append(to_core(second_half))
-        for j in range(1, n_tensor):
-            back_fake = back(back_fake, 1, [raw[j - 1]], j, 0, r)
         stacks = [first_half, second_half, *theirs]
         params = [step(lambda *values: spread(values, n), *stacks) for n in range(2)]
 

time: 235 us -> 213 us (0.906)
  Pallas kernels: 55.2 us -> 40.1 us
  other arithmetic: 20.7 us -> 15.7 us
  starting transfers between devices: 44.6 us -> 40 us
  local copies, waits for them, and re-layouts: 4.04 us -> 8.52 us
    pallas_call x19, Pallas kernels: 55.2 us -> 40.1 us  [call(): pl.pallas_call(kernel, out_shape=out_shape, compiler_params=pltpu.Compile...]
    ppermute x33 -> x28, waiting for transfers between devices: 77.1 us -> 62.6 us  [move_dp(): return lax.ppermute(value, 'dp', perm)]
    ppermute x6, waiting for transfers between devices: 21.1 us -> 28.3 us  [from_tensor(): return lax.ppermute(value, 'tensor', perm)]
    ppermute x8, waiting for transfers between devices: 10.7 us -> 15.5 us  [hops(): got = lax.ppermute(value, 'dp', perm)]
    unnamed x58 -> x32, local copies, waits for them, and re-layouts: 2.82 us -> 7.24 us
    ppermute x8, starting transfers between devices: 9.95 us -> 6.79 us  [hops(): got = lax.ppermute(value, 'dp', perm)]
    add x9 -> x8, other arithmetic: 9.13 us -> 6.02 us  [add_widened(): total = total + widen(value, net)]
    ppermute x33 -> x28, starting transfers between devices: 26.1 us -> 25 us  [move_dp(): return lax.ppermute(value, 'dp', perm)]
  transfers between devices with their start and end apart: 49 -> 44, of which waited for: 20 -> 22; matrix products, arithmetic and copies ran while one was open for 9% -> 8% of each run, Pallas kernels for 19% -> 13%
where the time goes in v7:
time: 213 us
  waiting for transfers between devices  107 us (50%)
  Pallas kernels  40.1 us (19%)
  starting transfers between devices  40 us (19%)
  other arithmetic  15.7 us (7%)
  local copies, waits for them, and re-layouts  8.52 us (4%)
    ppermute x28, waiting for transfers between devices, move_dp(): return lax.ppermute(value, 'dp', perm)  62.6 us
    pallas_call x19, Pallas kernels, call(): pl.pallas_call(kernel, out_shape=out_shape, compiler_params=pltpu.Compile...  40.1 us
    ppermute x6, waiting for transfers between devices, from_tensor(): return lax.ppermute(value, 'tensor', perm)  28.3 us
    ppermute x28, starting transfers between devices, move_dp(): return lax.ppermute(value, 'dp', perm)  25 us
    ppermute x8, waiting for transfers between devices, hops(): got = lax.ppermute(value, 'dp', perm)  15.5 us
    ppermute x6, starting transfers between devices, from_tensor(): return lax.ppermute(value, 'tensor', perm)  7.53 us
    unnamed x32, local copies, waits for them, and re-layouts  7.24 us
    ppermute x8, starting transfers between devices, hops(): got = lax.ppermute(value, 'dp', perm)  6.79 us
  transfers between devices with their start and end apart: 44, of which 22 were waited for; matrix products, arithmetic and copies ran while one was open for 8% of the time, Pallas kernels for 13%

profile of v7, /device:TPU:0, one launch (start us, length us, event | category | flops | bytes accessed | tf_op | source)
XLA Modules:
  0.0 212.8 jit_solution(13308601516749100884)
XLA Ops:
  12.1 2.6 %collective-permute-start.5 = (bf16[608,512]{1,0:T(8,128)(2,1)S(1)}, bf16[608,512]{1,0:T(8,128)(2,1)S(1)}, u32[]{:S(2)}, u32[]{:S(2)}) collective-permute-start(bf16[608,512]{1,0:T(8,128)(2,1)S(1)} %shard_map.204), channel_id=1, source_target_pairs={{0,1},{1,0},{2,3},{3,2},{4,5},{5,4},{6,7},{7,6},{8,9},{9,8},{10,11... | collective-permute-start | bytes 1867784 | tf_op jit(solution)/shard_map/ppermute | solution.py:91
  15.6 2.2 %shard_map.208 = (bf16[2,2,152,512]{3,2,1,0:T(8,128)(2,1)S(1)}, bf16[2,2,152,512]{3,2,1,0:T(8,128)(2,1)S(1)}, bf16[2,2,152,512]{3,2,1,0:T(8,128)(2,1)S(1)}, bf16[2,2,152,512]{3,2,1,0:T(8,128)(2,1)S(1)}) custom-call(bf16[512,2432]{1,0:T(8,128)(2,1)S(1)} %copy-done.1), custom_call_target="tpu_custom_call" | custom-call | tf_op jit(solution)/shard_map/pallas_call | solution.py:56
  18.6 10.7 %collective-permute-done.5.act_ref = bf16[608,512]{1,0:T(8,128)(2,1)S(1)} collective-permute-done((bf16[608,512]{1,0:T(8,128)(2,1)S(1)}, bf16[608,512]{1,0:T(8,128)(2,1)S(1)}, u32[]{:S(2)}, u32[]{:S(2)}) %collective-permute-start.5) | collective-permute-done | bytes 622624 | tf_op jit(solution)/shard_map/ppermute | solution.py:91
  33.9 2.1 %shard_map.211 = f32[1216,608]{1,0:T(8,128)S(1)} custom-call(bf16[1216,512]{1,0:T(8,128)(2,1)S(1)} %bitcast.96, bf16[1216,512]{1,0:T(8,128)(2,1)S(1)} %bitcast.98, bf16[1,608,512]{2,1,0:T(8,128)(2,1)S(1)} %shard_map.207.refs_2_, bf16[1,608,512]{2,1,0:T(8,128)(2,1)S(1)} %collective-permute-done.9.refs_3_), custom_call_target="tpu_custom_call" | custom-call | tf_op jit(solution)/shard_map/pallas_call | solution.py:56
  37.7 2.1 %shard_map.212 = f32[1216,608]{1,0:T(8,128)S(1)} custom-call(bf16[1216,512]{1,0:T(8,128)(2,1)S(1)} %bitcast.97, bf16[1216,512]{1,0:T(8,128)(2,1)S(1)} %bitcast.99, bf16[1,608,512]{2,1,0:T(8,128)(2,1)S(1)} %shard_map.210.refs_2_, bf16[1,608,512]{2,1,0:T(8,128)(2,1)S(1)} %collective-permute-done.6.refs_3_), custom_call_target="tpu_custom_call" | custom-call | tf_op jit(solution)/shard_map/pallas_call | solution.py:56
  39.9 2.6 %collective-permute-start.11 = (f32[8,128]{1,0:T(8,128)S(1)}, f32[8,128]{1,0:T(8,128)S(1)}, u32[]{:S(2)}, u32[]{:S(2)}) collective-permute-start(f32[8,128]{1,0:T(8,128)S(1)} %max.20), channel_id=1, source_target_pairs={{0,16},{2,18},{4,20},{6,22},{8,24},{10,26},{12,28},{14,30},{16,0},... | collective-permute-start | bytes 12296 | tf_op jit(solution)/shard_map/ppermute | solution.py:391
  50.0 3.2 %shard_map.213.refs_4_ = bf16[608,1024]{1,0:T(8,128)(2,1)} custom-call(f32[2]{0:T(128)S(1)} %add_divide_fusion.scale_ref, bf16[608,2432]{1,0:T(8,128)(2,1)S(1)} %copy-done.4, bf16[512,2432]{1,0:T(8,128)(2,1)S(1)} %copy-done.1), custom_call_target="tpu_custom_call" | custom-call | tf_op jit(solution)/shard_map/pallas_call | solution.py:56
  54.7 3.2 %shard_map.214.refs_1_ = bf16[608,1024]{1,0:T(8,128)(2,1)} custom-call(f32[2]{0:T(128)S(1)} %add_divide_fusion.scale_ref, bf16[608,2432]{1,0:T(8,128)(2,1)S(1)} %copy-done.5, bf16[512,2432]{1,0:T(8,128)(2,1)S(1)} %copy-done.3), custom_call_target="tpu_custom_call" | custom-call | tf_op jit(solution)/shard_map/pallas_call | solution.py:56
  59.1 13.1 %collective-permute-done.refs_0_ = bf16[2,2,152,512]{3,2,1,0:T(8,128)(2,1)S(1)} collective-permute-done((bf16[2,2,152,512]{3,2,1,0:T(8,128)(2,1)S(1)}, bf16[2,2,152,512]{3,2,1,0:T(8,128)(2,1)S(1)}, u32[]{:S(2)}, u32[]{:S(2)}) %collective-permute-start) | collective-permute-done | bytes 622624 | tf_op jit(solution)/shard_map/ppermute | solution.py:91
  80.1 3.6 %collective-permute-done.14 = f16[4,152,608]{2,1,0:T(8,128)(2,1)S(1)} collective-permute-done((f16[4,152,608]{2,1,0:T(8,128)(2,1)S(1)}, f16[4,152,608]{2,1,0:T(8,128)(2,1)S(1)}, u32[]{:S(2)}, u32[]{:S(2)}) %collective-permute-start.14) | collective-permute-done | bytes 739360 | tf_op jit(solution)/shard_map/ppermute | solution.py:78
  86.7 4.4 %collective-permute-done.19 = f16[2,152,608]{2,1,0:T(8,128)(2,1)S(1)} collective-permute-done((f16[2,152,608]{2,1,0:T(8,128)(2,1)S(1)}, f16[2,152,608]{2,1,0:T(8,128)(2,1)S(1)}, u32[]{:S(2)}, u32[]{:S(2)}) %collective-permute-start.19) | collective-permute-done | bytes 369696 | tf_op jit(solution)/shard_map/ppermute | solution.py:78
  95.5 2.4 %collective-permute-start.24 = (f16[152,608]{1,0:T(8,128)(2,1)S(1)}, f16[152,608]{1,0:T(8,128)(2,1)S(1)}, u32[]{:S(2)}, u32[]{:S(2)}) collective-permute-start(f16[152,608]{1,0:T(8,128)(2,1)S(1)} %get-tuple-element.309), channel_id=1, source_target_pairs={{0,16},{2,18},{4,20},{6,22},{8,24},{10,26},{12,28},{14,30},{16,0},... | collective-permute-start | bytes 554504 | tf_op jit(solution)/shard_map/ppermute | solution.py:78
  97.9 7.4 %collective-permute-done.17 = f16[2,152,608]{2,1,0:T(8,128)(2,1)S(1)} collective-permute-done((f16[2,152,608]{2,1,0:T(8,128)(2,1)S(1)}, f16[2,152,608]{2,1,0:T(8,128)(2,1)S(1)}, u32[]{:S(2)}, u32[]{:S(2)}) %collective-permute-start.17) | collective-permute-done | bytes 369696 | tf_op jit(solution)/shard_map/ppermute | solution.py:78
  106.8 2.1 shard_map.216
  112.5 3.8 %collective-permute-done.23 = f16[152,608]{1,0:T(8,128)(2,1)S(1)} collective-permute-done((f16[152,608]{1,0:T(8,128)(2,1)S(1)}, f16[152,608]{1,0:T(8,128)(2,1)S(1)}, u32[]{:S(2)}, u32[]{:S(2)}) %collective-permute-start.23) | collective-permute-done | bytes 184864 | tf_op jit(solution)/shard_map/ppermute | solution.py:78
  118.9 3.0 %collective-permute-start.25 = (f16[152,608]{1,0:T(8,128)(2,1)S(1)}, f16[152,608]{1,0:T(8,128)(2,1)S(1)}, u32[]{:S(2)}, u32[]{:S(2)}) collective-permute-start(f16[152,608]{1,0:T(8,128)(2,1)S(1)} %fusion.12), channel_id=1, source_target_pairs={{0,16},{2,18},{4,20},{6,22},{8,24},{10,26},{12,28},{14,30},{16,0},... | collective-permute-start | bytes 554504 | tf_op jit(solution)/shard_map/ppermute | solution.py:78
  124.9 3.0 %collective-permute-done.25 = f16[152,608]{1,0:T(8,128)(2,1)S(1)} collective-permute-done((f16[152,608]{1,0:T(8,128)(2,1)S(1)}, f16[152,608]{1,0:T(8,128)(2,1)S(1)}, u32[]{:S(2)}, u32[]{:S(2)}) %collective-permute-start.25) | collective-permute-done | bytes 184864 | tf_op jit(solution)/shard_map/ppermute | solution.py:78
  130.2 2.3 %collective-permute-done.27 = f32[8,128]{1,0:T(8,128)S(1)} collective-permute-done((f32[8,128]{1,0:T(8,128)S(1)}, f32[8,128]{1,0:T(8,128)S(1)}, u32[]{:S(2)}, u32[]{:S(2)}) %collective-permute-start.27) | collective-permute-done | bytes 4128 | tf_op jit(solution)/shard_map/ppermute | solution.py:91
  134.4 2.4 %collective-permute-done.28 = f32[8,128]{1,0:T(8,128)S(1)} collective-permute-done((f32[8,128]{1,0:T(8,128)S(1)}, f32[8,128]{1,0:T(8,128)S(1)}, u32[]{:S(2)}, u32[]{:S(2)}) %collective-permute-start.28) | collective-permute-done | bytes 4128 | tf_op jit(solution)/shard_map/ppermute | solution.py:391
  137.1 3.4 %collective-permute-done.29 = f32[8,128]{1,0:T(8,128)S(1)} collective-permute-done((f32[8,128]{1,0:T(8,128)S(1)}, f32[8,128]{1,0:T(8,128)S(1)}, u32[]{:S(2)}, u32[]{:S(2)}) %collective-permute-start.29) | collective-permute-done | bytes 4128 | tf_op jit(solution)/shard_map/ppermute | solution.py:391
  140.5 3.6 %collective-permute-done.30 = f32[8,128]{1,0:T(8,128)S(1)} collective-permute-done((f32[8,128]{1,0:T(8,128)S(1)}, f32[8,128]{1,0:T(8,128)S(1)}, u32[]{:S(2)}, u32[]{:S(2)}) %collective-permute-start.30) | collective-permute-done | bytes 4128 | tf_op jit(solution)/shard_map/ppermute | solution.py:391
  144.1 4.5 %collective-permute-done.31 = f32[8,128]{1,0:T(8,128)S(1)} collective-permute-done((f32[8,128]{1,0:T(8,128)S(1)}, f32[8,128]{1,0:T(8,128)S(1)}, u32[]{:S(2)}, u32[]{:S(2)}) %collective-permute-start.31) | collective-permute-done | bytes 4128 | tf_op jit(solution)/shard_map/ppermute | solution.py:391
  154.5 3.5 %shard_map.219 = bf16[608,1024]{1,0:T(8,128)(2,1)} custom-call(f32[2]{0:T(128)S(1)} %add_divide_fusion.scale_ref, bf16[608,2432]{1,0:T(8,128)(2,1)S(1)} %copy-done.4, bf16[2,2,152,512]{3,2,1,0:T(8,128)(2,1)S(1)} %collective-permute-done.refs_0_, bf16[2,2,152,512]{3,2,1,0:T(8,128)(2,1)S(1)} %collective-permute-done.32.refs_1_, ...), custom_call_target="tpu_custom_call", output_to_operand_aliasing={{}: (6, {})} | custom-call | tf_op jit(solution)/shard_map/pallas_call | solution.py:56
  158.0 8.4 %collective-permute-done.36 = bf16[2,152,608]{2,1,0:T(8,128)(2,1)S(1)} collective-permute-done((bf16[2,152,608]{2,1,0:T(8,128)(2,1)S(1)}, bf16[2,152,608]{2,1,0:T(8,128)(2,1)S(1)}, u32[]{:S(2)}, u32[]{:S(2)}) %collective-permute-start.36) | collective-permute-done | bytes 369696 | tf_op jit(solution)/shard_map/ppermute | solution.py:78
  166.9 3.7 %collective-permute-done.39 = bf16[2,152,608]{2,1,0:T(8,128)(2,1)S(1)} collective-permute-done((bf16[2,152,608]{2,1,0:T(8,128)(2,1)S(1)}, bf16[2,152,608]{2,1,0:T(8,128)(2,1)S(1)}, u32[]{:S(2)}, u32[]{:S(2)}) %collective-permute-start.39) | collective-permute-done | bytes 369696 | tf_op jit(solution)/shard_map/ppermute | solution.py:78
  170.6 14.6 %collective-permute-done.38 = bf16[2,152,608]{2,1,0:T(8,128)(2,1)S(1)} collective-permute-done((bf16[2,152,608]{2,1,0:T(8,128)(2,1)S(1)}, bf16[2,152,608]{2,1,0:T(8,128)(2,1)S(1)}, u32[]{:S(2)}, u32[]{:S(2)}) %collective-permute-start.38) | collective-permute-done | bytes 369696 | tf_op jit(solution)/shard_map/ppermute | solution.py:78
  187.6 3.2 %shard_map.220 = bf16[608,1024]{1,0:T(8,128)(2,1)} custom-call(f32[2]{0:T(128)S(1)} %add_divide_fusion.scale_ref, bf16[608,2432]{1,0:T(8,128)(2,1)S(1)} %copy-done.5, bf16[512,2432]{1,0:T(8,128)(2,1)S(1)} %collective-permute-done.34.refs_0_, bf16[608,1024]{1,0:T(8,128)(2,1)} %shard_map.214.refs_1_), custom_call_target="tpu_custom_call", output_to_operand_aliasing={{}: (3, {})} | custom-call | tf_op jit(solution)/shard_map/pallas_call | solution.py:56
  190.8 5.8 %collective-permute-done.40 = bf16[2,152,608]{2,1,0:T(8,128)(2,1)S(1)} collective-permute-done((bf16[2,152,608]{2,1,0:T(8,128)(2,1)S(1)}, bf16[2,152,608]{2,1,0:T(8,128)(2,1)S(1)}, u32[]{:S(2)}, u32[]{:S(2)}) %collective-permute-start.40) | collective-permute-done | bytes 369696 | tf_op jit(solution)/shard_map/ppermute | solution.py:78
  196.6 4.2 %collective-permute-done.41 = bf16[2,152,608]{2,1,0:T(8,128)(2,1)S(1)} collective-permute-done((bf16[2,152,608]{2,1,0:T(8,128)(2,1)S(1)}, bf16[2,152,608]{2,1,0:T(8,128)(2,1)S(1)}, u32[]{:S(2)}, u32[]{:S(2)}) %collective-permute-start.41) | collective-permute-done | bytes 369696 | tf_op jit(solution)/shard_map/ppermute | solution.py:78
  201.2 3.4 %collective-permute-done.43.refs_3_ = bf16[4,2,152,608]{3,2,1,0:T(8,128)(2,1)S(1)} collective-permute-done((bf16[4,2,152,608]{3,2,1,0:T(8,128)(2,1)S(1)}, bf16[4,2,152,608]{3,2,1,0:T(8,128)(2,1)S(1)}, u32[]{:S(2)}, u32[]{:S(2)}) %collective-permute-start.43) | collective-permute-done | bytes 1478688 | tf_op jit(solution)/shard_map/ppermute | solution.py:78
  204.6 4.1 %shard_map.221 = bf16[608,2432]{1,0:T(8,128)(2,1)} custom-call(bf16[4,2,152,608]{3,2,1,0:T(8,128)(2,1)S(1)} %pad_maximum_fusion.refs_0_, bf16[4,2,152,608]{3,2,1,0:T(8,128)(2,1)S(1)} %pad_maximum_fusion.1.refs_1_, bf16[4,2,152,608]{3,2,1,0:T(8,128)(2,1)S(1)} %collective-permute-done.42.refs_2_, bf16[4,2,152,608]{3,2,1,0:T(8,128)(2,1)S(1)} %collective-permute-done.43.refs_3_), custom_call_target="tpu_custom_call" | custom-call | tf_op jit(solution)/shard_map/pallas_call | solution.py:56
  208.7 4.1 %shard_map.222 = bf16[608,2432]{1,0:T(8,128)(2,1)} custom-call(bf16[4,2,152,608]{3,2,1,0:T(8,128)(2,1)S(1)} %pad_maximum_fusion.refs_0_, bf16[4,2,152,608]{3,2,1,0:T(8,128)(2,1)S(1)} %pad_maximum_fusion.1.refs_1_, bf16[4,2,152,608]{3,2,1,0:T(8,128)(2,1)S(1)} %collective-permute-done.42.refs_2_, bf16[4,2,152,608]{3,2,1,0:T(8,128)(2,1)S(1)} %collective-permute-done.43.refs_3_), custom_call_target="tpu_custom_call" | custom-call | tf_op jit(solution)/shard_map/pallas_call | solution.py:56
  (144 shorter events, 68.7 us)
Async XLA Ops:
  11.6 22.3 %collective-permute-start.4 = (bf16[2,4,152,512]{3,2,1,0:T(8,128)(2,1)S(1)}, bf16[2,4,152,512]{3,2,1,0:T(8,128)(2,1)S(1)}, u32[]{:S(2)}, u32[]{:S(2)}) collective-permute-start(bf16[2,4,152,512]{3,2,1,0:T(8,128)(2,1)S(1)} %get-tuple-element.168), channel_id=1, source_target_pairs={{0,2},{2,0},{4,6},{6,4},{8,10},{10,8},{12,14},{14,12},{16,18},{18,... | collective-permute-start | bytes 3735560 | tf_op jit(solution)/shard_map/ppermute | solution.py:78
  12.1 17.2 %collective-permute-start.5 = (bf16[608,512]{1,0:T(8,128)(2,1)S(1)}, bf16[608,512]{1,0:T(8,128)(2,1)S(1)}, u32[]{:S(2)}, u32[]{:S(2)}) collective-permute-start(bf16[608,512]{1,0:T(8,128)(2,1)S(1)} %shard_map.204), channel_id=1, source_target_pairs={{0,1},{1,0},{2,3},{3,2},{4,5},{5,4},{6,7},{7,6},{8,9},{9,8},{10,11... | collective-permute-start | bytes 1867784 | tf_op jit(solution)/shard_map/ppermute | solution.py:91
  15.3 18.5 %collective-permute-start.9 = (bf16[1,608,512]{2,1,0:T(8,128)(2,1)S(1)}, bf16[1,608,512]{2,1,0:T(8,128)(2,1)S(1)}, u32[]{:S(2)}, u32[]{:S(2)}) collective-permute-start(bf16[1,608,512]{2,1,0:T(8,128)(2,1)S(1)} %shard_map.207.refs_2_), channel_id=1, source_target_pairs={{0,2},{2,0},{4,6},{6,4},{8,10},{10,8},{12,14},{14,12},{16,18},{18,... | collective-permute-start | bytes 1867784 | tf_op jit(solution)/shard_map/ppermute | solution.py:78
  30.0 7.7 %collective-permute-start.6 = (bf16[1,608,512]{2,1,0:T(8,128)(2,1)S(1)}, bf16[1,608,512]{2,1,0:T(8,128)(2,1)S(1)}, u32[]{:S(2)}, u32[]{:S(2)}) collective-permute-start(bf16[1,608,512]{2,1,0:T(8,128)(2,1)S(1)} %shard_map.210.refs_2_), channel_id=1, source_target_pairs={{0,2},{2,0},{4,6},{6,4},{8,10},{10,8},{12,14},{14,12},{16,18},{18,... | collective-permute-start | bytes 1867784 | tf_op jit(solution)/shard_map/ppermute | solution.py:78
  42.5 16.3 %collective-permute-start.16 = (bf16[2,2,152,512]{3,2,1,0:T(8,128)(2,1)S(1)}, bf16[2,2,152,512]{3,2,1,0:T(8,128)(2,1)S(1)}, u32[]{:S(2)}, u32[]{:S(2)}) collective-permute-start(bf16[2,2,152,512]{3,2,1,0:T(8,128)(2,1)S(1)} %get-tuple-element.166), channel_id=1, source_target_pairs={{0,3},{1,2},{2,1},{3,0},{4,7},{5,6},{6,5},{7,4},{8,11},{9,10},{10,... | collective-permute-start | bytes 1867784 | tf_op jit(solution)/shard_map/ppermute | solution.py:100
  44.1 28.1 %collective-permute-start = (bf16[2,2,152,512]{3,2,1,0:T(8,128)(2,1)S(1)}, bf16[2,2,152,512]{3,2,1,0:T(8,128)(2,1)S(1)}, u32[]{:S(2)}, u32[]{:S(2)}) collective-permute-start(bf16[2,2,152,512]{3,2,1,0:T(8,128)(2,1)S(1)} %get-tuple-element.198), channel_id=1, source_target_pairs={{0,1},{1,0},{2,3},{3,2},{4,5},{5,4},{6,7},{7,6},{8,9},{9,8},{10,11... | collective-permute-start | bytes 1867784 | tf_op jit(solution)/shard_map/ppermute | solution.py:91
  44.6 5.3 %collective-permute-start.1 = (bf16[2,608,512]{2,1,0:T(8,128)(2,1)S(1)}, bf16[2,608,512]{2,1,0:T(8,128)(2,1)S(1)}, u32[]{:S(2)}, u32[]{:S(2)}) collective-permute-start(bf16[2,608,512]{2,1,0:T(8,128)(2,1)S(1)} %shard_map.209.refs_4_), channel_id=1, source_target_pairs={{0,2},{2,0},{4,6},{6,4},{8,10},{10,8},{12,14},{14,12},{16,18},{18,... | collective-permute-start | bytes 3735560 | tf_op jit(solution)/shard_map/ppermute | solution.py:78
  46.8 30.3 %collective-permute-start.15 = (f16[4,152,608]{2,1,0:T(8,128)(2,1)S(1)}, f16[4,152,608]{2,1,0:T(8,128)(2,1)S(1)}, u32[]{:S(2)}, u32[]{:S(2)}) collective-permute-start(f16[4,152,608]{2,1,0:T(8,128)(2,1)S(1)} %get-tuple-element.297), channel_id=1, source_target_pairs={{0,4},{2,6},{4,0},{6,2},{8,12},{10,14},{12,8},{14,10},{16,20},{18,... | collective-permute-start | bytes 2217992 | tf_op jit(solution)/shard_map/ppermute | solution.py:78
  49.1 34.7 %collective-permute-start.14 = (f16[4,152,608]{2,1,0:T(8,128)(2,1)S(1)}, f16[4,152,608]{2,1,0:T(8,128)(2,1)S(1)}, u32[]{:S(2)}, u32[]{:S(2)}) collective-permute-start(f16[4,152,608]{2,1,0:T(8,128)(2,1)S(1)} %get-tuple-element.299), channel_id=1, source_target_pairs={{0,4},{2,6},{4,0},{6,2},{8,12},{10,14},{12,8},{14,10},{16,20},{18,... | collective-permute-start | bytes 2217992 | tf_op jit(solution)/shard_map/ppermute | solution.py:78
  53.1 53.7 %collective-permute-start.12 = (bf16[2,2,152,512]{3,2,1,0:T(8,128)(2,1)S(1)}, bf16[2,2,152,512]{3,2,1,0:T(8,128)(2,1)S(1)}, u32[]{:S(2)}, u32[]{:S(2)}) collective-permute-start(bf16[2,2,152,512]{3,2,1,0:T(8,128)(2,1)S(1)} %get-tuple-element.214), channel_id=1, source_target_pairs={{0,1},{1,0},{2,3},{3,2},{4,5},{5,4},{6,7},{7,6},{8,9},{9,8},{10,11... | collective-permute-start | bytes 1867784 | tf_op jit(solution)/shard_map/ppermute | solution.py:91
  58.8 48.0 %collective-permute-start.13 = (bf16[2,2,152,512]{3,2,1,0:T(8,128)(2,1)S(1)}, bf16[2,2,152,512]{3,2,1,0:T(8,128)(2,1)S(1)}, u32[]{:S(2)}, u32[]{:S(2)}) collective-permute-start(bf16[2,2,152,512]{3,2,1,0:T(8,128)(2,1)S(1)} %get-tuple-element.194), channel_id=1, source_target_pairs={{0,3},{1,2},{2,1},{3,0},{4,7},{5,6},{6,5},{7,4},{8,11},{9,10},{10,... | collective-permute-start | bytes 1867784 | tf_op jit(solution)/shard_map/ppermute | solution.py:100
  75.1 16.0 %collective-permute-start.19 = (f16[2,152,608]{2,1,0:T(8,128)(2,1)S(1)}, f16[2,152,608]{2,1,0:T(8,128)(2,1)S(1)}, u32[]{:S(2)}, u32[]{:S(2)}) collective-permute-start(f16[2,152,608]{2,1,0:T(8,128)(2,1)S(1)} %fusion.4), channel_id=1, source_target_pairs={{0,4},{2,6},{4,0},{6,2},{8,12},{10,14},{12,8},{14,10},{16,20},{18,... | collective-permute-start | bytes 1109000 | tf_op jit(solution)/shard_map/ppermute | solution.py:78
  78.7 15.3 %collective-permute-start.18 = (f16[2,152,608]{2,1,0:T(8,128)(2,1)S(1)}, f16[2,152,608]{2,1,0:T(8,128)(2,1)S(1)}, u32[]{:S(2)}, u32[]{:S(2)}) collective-permute-start(f16[2,152,608]{2,1,0:T(8,128)(2,1)S(1)} %get-tuple-element.305), channel_id=1, source_target_pairs={{0,8},{2,10},{4,12},{6,14},{8,0},{10,2},{12,4},{14,6},{16,24},{18,... | collective-permute-start | bytes 1109000 | tf_op jit(solution)/shard_map/ppermute | solution.py:78
  85.3 20.0 %collective-permute-start.17 = (f16[2,152,608]{2,1,0:T(8,128)(2,1)S(1)}, f16[2,152,608]{2,1,0:T(8,128)(2,1)S(1)}, u32[]{:S(2)}, u32[]{:S(2)}) collective-permute-start(f16[2,152,608]{2,1,0:T(8,128)(2,1)S(1)} %get-tuple-element.306), channel_id=1, source_target_pairs={{0,8},{2,10},{4,12},{6,14},{8,0},{10,2},{12,4},{14,6},{16,24},{18,... | collective-permute-start | bytes 1109000 | tf_op jit(solution)/shard_map/ppermute | solution.py:78
  92.6 24.6 %collective-permute-start.20 = (f16[2,152,608]{2,1,0:T(8,128)(2,1)S(1)}, f16[2,152,608]{2,1,0:T(8,128)(2,1)S(1)}, u32[]{:S(2)}, u32[]{:S(2)}) collective-permute-start(f16[2,152,608]{2,1,0:T(8,128)(2,1)S(1)} %multiply_convert_fusion.2), channel_id=1, source_target_pairs={{0,8},{2,10},{4,12},{6,14},{8,0},{10,2},{12,4},{14,6},{16,24},{18,... | collective-permute-start | bytes 1109000 | tf_op jit(solution)/shard_map/ppermute | solution.py:78
  95.5 16.3 %collective-permute-start.24 = (f16[152,608]{1,0:T(8,128)(2,1)S(1)}, f16[152,608]{1,0:T(8,128)(2,1)S(1)}, u32[]{:S(2)}, u32[]{:S(2)}) collective-permute-start(f16[152,608]{1,0:T(8,128)(2,1)S(1)} %get-tuple-element.309), channel_id=1, source_target_pairs={{0,16},{2,18},{4,20},{6,22},{8,24},{10,26},{12,28},{14,30},{16,0},... | collective-permute-start | bytes 554504 | tf_op jit(solution)/shard_map/ppermute | solution.py:78
  106.7 9.6 %collective-permute-start.23 = (f16[152,608]{1,0:T(8,128)(2,1)S(1)}, f16[152,608]{1,0:T(8,128)(2,1)S(1)}, u32[]{:S(2)}, u32[]{:S(2)}) collective-permute-start(f16[152,608]{1,0:T(8,128)(2,1)S(1)} %get-tuple-element.311), channel_id=1, source_target_pairs={{0,16},{2,18},{4,20},{6,22},{8,24},{10,26},{12,28},{14,30},{16,0},... | collective-permute-start | bytes 554504 | tf_op jit(solution)/shard_map/ppermute | solution.py:78
  109.7 12.2 %collective-permute-start.21 = (f16[152,608]{1,0:T(8,128)(2,1)S(1)}, f16[152,608]{1,0:T(8,128)(2,1)S(1)}, u32[]{:S(2)}, u32[]{:S(2)}) collective-permute-start(f16[152,608]{1,0:T(8,128)(2,1)S(1)} %get-tuple-element.302), channel_id=1, source_target_pairs={{0,4},{2,6},{4,0},{6,2},{8,12},{10,14},{12,8},{14,10},{16,20},{18,... | collective-permute-start | bytes 554504 | tf_op jit(solution)/shard_map/ppermute | solution.py:78
  109.8 7.7 %collective-permute-start.22 = (f16[152,608]{1,0:T(8,128)(2,1)S(1)}, f16[152,608]{1,0:T(8,128)(2,1)S(1)}, u32[]{:S(2)}, u32[]{:S(2)}) collective-permute-start(f16[152,608]{1,0:T(8,128)(2,1)S(1)} %get-tuple-element.300), channel_id=1, source_target_pairs={{0,4},{2,6},{4,0},{6,2},{8,12},{10,14},{12,8},{14,10},{16,20},{18,... | collective-permute-start | bytes 554504 | tf_op jit(solution)/shard_map/ppermute | solution.py:78
  117.0 7.8 %collective-permute-start.26 = (f32[152,608]{1,0:T(8,128)S(1)}, f32[152,608]{1,0:T(8,128)S(1)}, u32[]{:S(2)}, u32[]{:S(2)}) collective-permute-start(f32[152,608]{1,0:T(8,128)S(1)} %multiply_add_fusion.5), channel_id=1, source_target_pairs={{0,1},{1,0},{2,3},{3,2},{4,5},{5,4},{6,7},{7,6},{8,9},{9,8},{10,11... | collective-permute-start | bytes 1109000 | tf_op jit(solution)/shard_map/ppermute | solution.py:91
  118.9 9.0 %collective-permute-start.25 = (f16[152,608]{1,0:T(8,128)(2,1)S(1)}, f16[152,608]{1,0:T(8,128)(2,1)S(1)}, u32[]{:S(2)}, u32[]{:S(2)}) collective-permute-start(f16[152,608]{1,0:T(8,128)(2,1)S(1)} %fusion.12), channel_id=1, source_target_pairs={{0,16},{2,18},{4,20},{6,22},{8,24},{10,26},{12,28},{14,30},{16,0},... | collective-permute-start | bytes 554504 | tf_op jit(solution)/shard_map/ppermute | solution.py:78
  132.6 55.0 %collective-permute-start.34 = (bf16[512,2432]{1,0:T(8,128)(2,1)S(1)}, bf16[512,2432]{1,0:T(8,128)(2,1)S(1)}, u32[]{:S(2)}, u32[]{:S(2)}) collective-permute-start(bf16[512,2432]{1,0:T(8,128)(2,1)S(1)} %copy-done.3), channel_id=1, source_target_pairs={{0,1},{1,0},{2,3},{3,2},{4,5},{5,4},{6,7},{7,6},{8,9},{9,8},{10,11... | collective-permute-start | bytes 7471112 | tf_op jit(solution)/shard_map/ppermute | solution.py:91
  133.9 14.7 %collective-permute-start.33 = (bf16[2,2,152,512]{3,2,1,0:T(8,128)(2,1)S(1)}, bf16[2,2,152,512]{3,2,1,0:T(8,128)(2,1)S(1)}, u32[]{:S(2)}, u32[]{:S(2)}) collective-permute-start(bf16[2,2,152,512]{3,2,1,0:T(8,128)(2,1)S(1)} %collective-permute-done.13), channel_id=1, source_target_pairs={{0,2},{2,0},{4,6},{6,4},{8,10},{10,8},{12,14},{14,12},{16,18},{18,... | collective-permute-start | bytes 1867784 | tf_op jit(solution)/shard_map/ppermute | solution.py:78
  133.9 14.7 %collective-permute-start.32 = (bf16[2,2,152,512]{3,2,1,0:T(8,128)(2,1)S(1)}, bf16[2,2,152,512]{3,2,1,0:T(8,128)(2,1)S(1)}, u32[]{:S(2)}, u32[]{:S(2)}) collective-permute-start(bf16[2,2,152,512]{3,2,1,0:T(8,128)(2,1)S(1)} %collective-permute-done.16), channel_id=1, source_target_pairs={{0,2},{2,0},{4,6},{6,4},{8,10},{10,8},{12,14},{14,12},{16,18},{18,... | collective-permute-start | bytes 1867784 | tf_op jit(solution)/shard_map/ppermute | solution.py:78
  150.8 15.6 %collective-permute-start.36 = (bf16[2,152,608]{2,1,0:T(8,128)(2,1)S(1)}, bf16[2,152,608]{2,1,0:T(8,128)(2,1)S(1)}, u32[]{:S(2)}, u32[]{:S(2)}) collective-permute-start(bf16[2,152,608]{2,1,0:T(8,128)(2,1)S(1)} %get-tuple-element.271), channel_id=1, source_target_pairs={{0,8},{2,10},{4,12},{6,14},{8,0},{10,2},{12,4},{14,6},{16,24},{18,... | collective-permute-start | bytes 1109000 | tf_op jit(solution)/shard_map/ppermute | solution.py:78
  150.8 19.8 %collective-permute-start.39 = (bf16[2,152,608]{2,1,0:T(8,128)(2,1)S(1)}, bf16[2,152,608]{2,1,0:T(8,128)(2,1)S(1)}, u32[]{:S(2)}, u32[]{:S(2)}) collective-permute-start(bf16[2,152,608]{2,1,0:T(8,128)(2,1)S(1)} %get-tuple-element.271), channel_id=1, source_target_pairs={{0,24},{2,26},{4,28},{6,30},{8,16},{10,18},{12,20},{14,22},{16,8},... | collective-permute-start | bytes 1109000 | tf_op jit(solution)/shard_map/ppermute | solution.py:78
  152.2 32.9 %collective-permute-start.38 = (bf16[2,152,608]{2,1,0:T(8,128)(2,1)S(1)}, bf16[2,152,608]{2,1,0:T(8,128)(2,1)S(1)}, u32[]{:S(2)}, u32[]{:S(2)}) collective-permute-start(bf16[2,152,608]{2,1,0:T(8,128)(2,1)S(1)} %get-tuple-element.271), channel_id=1, source_target_pairs={{0,16},{2,18},{4,20},{6,22},{8,24},{10,26},{12,28},{14,30},{16,0},... | collective-permute-start | bytes 1109000 | tf_op jit(solution)/shard_map/ppermute | solution.py:78
  154.3 33.0 %collective-permute-start.35 = (bf16[2,152,608]{2,1,0:T(8,128)(2,1)S(1)}, bf16[2,152,608]{2,1,0:T(8,128)(2,1)S(1)}, u32[]{:S(2)}, u32[]{:S(2)}) collective-permute-start(bf16[2,152,608]{2,1,0:T(8,128)(2,1)S(1)} %get-tuple-element.271), channel_id=1, source_target_pairs={{0,4},{2,6},{4,0},{6,2},{8,12},{10,14},{12,8},{14,10},{16,20},{18,... | collective-permute-start | bytes 1109000 | tf_op jit(solution)/shard_map/ppermute | solution.py:78
  166.4 20.8 %collective-permute-start.37 = (bf16[2,152,608]{2,1,0:T(8,128)(2,1)S(1)}, bf16[2,152,608]{2,1,0:T(8,128)(2,1)S(1)}, u32[]{:S(2)}, u32[]{:S(2)}) collective-permute-start(bf16[2,152,608]{2,1,0:T(8,128)(2,1)S(1)} %collective-permute-done.36), channel_id=1, source_target_pairs={{0,4},{2,6},{4,0},{6,2},{8,12},{10,14},{12,8},{14,10},{16,20},{18,... | collective-permute-start | bytes 1109000 | tf_op jit(solution)/shard_map/ppermute | solution.py:78
  185.2 11.5 %collective-permute-start.40 = (bf16[2,152,608]{2,1,0:T(8,128)(2,1)S(1)}, bf16[2,152,608]{2,1,0:T(8,128)(2,1)S(1)}, u32[]{:S(2)}, u32[]{:S(2)}) collective-permute-start(bf16[2,152,608]{2,1,0:T(8,128)(2,1)S(1)} %collective-permute-done.38), channel_id=1, source_target_pairs={{0,4},{2,6},{4,0},{6,2},{8,12},{10,14},{12,8},{14,10},{16,20},{18,... | collective-permute-start | bytes 1109000 | tf_op jit(solution)/shard_map/ppermute | solution.py:78
  185.5 15.4 %collective-permute-start.41 = (bf16[2,152,608]{2,1,0:T(8,128)(2,1)S(1)}, bf16[2,152,608]{2,1,0:T(8,128)(2,1)S(1)}, u32[]{:S(2)}, u32[]{:S(2)}) collective-permute-start(bf16[2,152,608]{2,1,0:T(8,128)(2,1)S(1)} %collective-permute-done.39), channel_id=1, source_target_pairs={{0,4},{2,6},{4,0},{6,2},{8,12},{10,14},{12,8},{14,10},{16,20},{18,... | collective-permute-start | bytes 1109000 | tf_op jit(solution)/shard_map/ppermute | solution.py:78
  187.5 13.7 %collective-permute-start.42 = (bf16[4,2,152,608]{3,2,1,0:T(8,128)(2,1)S(1)}, bf16[4,2,152,608]{3,2,1,0:T(8,128)(2,1)S(1)}, u32[]{:S(2)}, u32[]{:S(2)}) collective-permute-start(bf16[4,2,152,608]{3,2,1,0:T(8,128)(2,1)S(1)} %pad_maximum_fusion.refs_0_), channel_id=1, source_target_pairs={{0,2},{2,0},{4,6},{6,4},{8,10},{10,8},{12,14},{14,12},{16,18},{18,... | collective-permute-start | bytes 4435976 | tf_op jit(solution)/shard_map/ppermute | solution.py:78
  (28 other events, 223.6 us)

commit v8 on v7

--- a/solution.py
+++ b/solution.py
@@ -16,7 +16,7 @@
 SECOND_CORRECTION = 0.0952078529183
 
 OUTER = 4
-HALF_LIMIT = 60000.0
+HALF_BITS = 15.0
 TILE = 256
 LANES = 128
 
@@ -114,70 +114,6 @@
     def first_row(j, r):
         start = ((lax.axis_index("tensor") + j) & (n_tensor - 1)) * r
         return pl.multiple_of(start, LANES)
-
-    def cut_acts(act, r):
-        count = n_tensor - 1
-
-        def kernel(act_ref, *refs):
-            out_refs, sem = refs[:-1], refs[-1]
-            copies = [
-                pltpu.make_async_copy(
-                    act_ref.at[:, pl.ds(first_row(j + 1, r), r)], out_refs[j], sem.at[j]
-                )
-                for j in range(count)
-            ]
-            for copy in copies:
-                copy.start()
-            for copy in copies:
-                copy.wait()
-
-        return call(
-            kernel,
-            [array((act.shape[0], r), act.dtype)] * count,
-            act,
-            in_specs=[ANY],
-            out_specs=[VMEM] * count,
-            scratch_shapes=[pltpu.SemaphoreType.DMA((count,))],
-        )
-
-    def bound_of(cots, acts, scales):
-        r, f, count = cots[0].shape[0], acts[0].shape[0], acts[0].shape[1]
-        steps = 4
-
-        def kernel(scale_ref, *refs):
-            ins, (out_ref, most_ref) = refs[:4], refs[4:]
-
-            @pl.when(pl.program_id(0) == 0)
-            def _():
-                most_ref[...] = jnp.zeros_like(most_ref)
-
-            for n, ref in enumerate(ins):
-                value = jnp.abs(ref[...].astype(jnp.float32))
-                rows, cols = value.shape
-                value = jnp.max(value.reshape(rows // 8, 8, cols), axis=0)
-                value = functools.reduce(
-                    jnp.maximum, (value[:, at : at + LANES] for at in range(0, cols, LANES))
-                )
-                most_ref[n] = jnp.maximum(most_ref[n], value)
-
-            @pl.when(pl.program_id(0) == steps - 1)
-            def _():
-                bounds = [
-                    jnp.max(most_ref[net]) * jnp.max(most_ref[2 + net]) * scale_ref[net]
-                    for net in range(2)
-                ]
-                rows = lax.broadcasted_iota(jnp.int32, (8, LANES), 0)
-                out_ref[...] = jnp.where(rows == 0, *bounds)
-
-        return call(
-            kernel, array((8, LANES), jnp.float32), scales, *cots, *acts,
-            grid=(steps,),
-            in_specs=[SMEM]
-            + [pl.BlockSpec((r // steps, D), lambda s: (s, 0))] * 2
-            + [pl.BlockSpec((f, count // steps), lambda s: (0, s))] * 2,
-            out_specs=pl.BlockSpec((8, LANES), lambda s: (0, 0)),
-            scratch_shapes=[pltpu.VMEM((4, 8, LANES), jnp.float32)],
-        )
 
     def turn(cot, by_planes):
         r = cot.shape[0]
@@ -218,17 +154,23 @@
             scratch_shapes=[pltpu.VMEM((D, step), jnp.float32)],
         )
 
-    def prepare(net, act, scales, r, places):
+    def prepare(net, act, scales, r, together):
         f = act.shape[0]
-
-        def kernel(scale_ref, act_ref, out_ref):
-            for j in range(places):
+        lead = (n_tensor,) if together else (1,)
+        count = 1 if together else n_tensor
+
+        def kernel(scale_ref, act_ref, *out_refs):
+            for j in range(n_tensor):
                 part = act_ref[:, pl.ds(first_row(j, r), r)].astype(jnp.float32)
-                out_ref[j] = (part * scale_ref[net]).astype(jnp.bfloat16)
+                part = (part * scale_ref[net]).astype(jnp.bfloat16)
+                if together:
+                    out_refs[0][j] = part
+                else:
+                    out_refs[j][0] = part
 
         return call(
-            kernel, array((places, f, r), jnp.bfloat16), scales, act,
-            in_specs=[SMEM, VMEM], out_specs=VMEM,
+            kernel, [array((*lead, f, r), jnp.bfloat16)] * count, scales, act,
+            in_specs=[SMEM, VMEM], out_specs=[VMEM] * count,
         )
 
     def multiply(pieces, scaled, places):
@@ -239,7 +181,9 @@
         count = len(pieces)
 
         def kernel(*refs):
-            piece_refs, scaled_refs, out_ref = refs[:count], refs[count:-1], refs[-1]
+            piece_refs, scaled_refs = refs[:count], refs[count:-2]
+            out_ref, power_ref = refs[-2:]
+            most = jnp.zeros((8, f), jnp.float32)
             for start in range(0, rows, step):
                 part = slice(start, start + step)
                 total = None
@@ -247,21 +191,17 @@
                     term = dot(piece_ref[part], scaled_refs[n][j], NT)
                     total = term if total is None else total + term
                 out_ref[part] = total
-
-        out = call(
-            kernel, array((rows, f), jnp.float32), *pieces, *scaled,
-            in_specs=[VMEM] * (count + len(scaled)), out_specs=VMEM,
-        )
-        return out.reshape(*lead, f)
-
-    def scale_rows(act, scales):
-        def kernel(scale_ref, act_ref, out_ref):
-            out_ref[0] = (act_ref[...].astype(jnp.float32) * scale_ref[1]).astype(jnp.bfloat16)
-
-        return call(
-            kernel, array((1, *act.shape), jnp.bfloat16), scales, act,
-            in_specs=[SMEM, VMEM], out_specs=VMEM,
-        )
+                top = jnp.max(jnp.abs(total).reshape(step // 8, 8, f), axis=0)
+                most = jnp.maximum(most, top)
+            most = jnp.full((8, LANES), jnp.maximum(jnp.max(most), 1e-30))
+            power_ref[...] = jnp.floor(jnp.log2(most)) + 2.0
+
+        out, power = call(
+            kernel, [array((rows, f), jnp.float32), array((8, LANES), jnp.float32)],
+            *pieces, *scaled,
+            in_specs=[VMEM] * (count + len(scaled)), out_specs=[VMEM] * 2,
+        )
+        return out.reshape(*lead, f), power[0, 0]
 
     def norms(total_s, total_f):
         def kernel(s_ref, f_ref, out_ref):
@@ -275,7 +215,7 @@
         )
 
     def update(squares, totals, states):
-        shape = totals[0].shape
+        shape = states[0].shape
 
         def kernel(squares_ref, *refs):
             total_refs, state_refs, (own_ref, *out_refs) = refs[:2], refs[2:8], refs[8:]
@@ -340,27 +280,46 @@
             input_output_aliases=aliases, mib=20,
         )
 
-    def spread(stacks, net):
+    def spread(stacks):
         count, _, _, f = stacks[0].shape
+        tiles = [
+            (net, start, min(TILE, f - start)) for net in range(2) for start in range(0, f, TILE)
+        ]
 
         def kernel(*refs):
-            stack_refs, (out_ref, wide_ref) = refs[:4], refs[4:]
-            lanes = lax.broadcasted_iota(jnp.int32, (width, LANES), 1)
-            inside = lanes + pl.program_id(0) * LANES < f
-            for n, ref in enumerate(stack_refs):
-                for at in range(count):
-                    k, i = divmod((n & 1) * count + at, inner)
-                    block = jnp.where(inside, ref[at, 0].astype(jnp.float32), 0.0)
-                    wide_ref[owner(k, i, n >> 1)] = block
-            flat = wide_ref[...].reshape(D, LANES).astype(jnp.bfloat16)
-            out_ref[...] = dot(identity(LANES), flat, NT).astype(jnp.bfloat16)
+            stack_refs, out_refs, (wide_ref, done_ref, sem) = refs[:4], refs[4:6], refs[6:]
+            eye = identity(TILE)
+            copies = []
+            for step, (net, start, size) in enumerate(tiles):
+                for n, ref in enumerate(stack_refs):
+                    for at in range(count):
+                        k, i = divmod((n & 1) * count + at, inner)
+                        block = ref[at, net, :, start : start + size].astype(jnp.float32)
+                        wide_ref[owner(k, i, n >> 1), :, :size] = block
+                flat = wide_ref[:, :, :size].reshape(D, size).astype(jnp.bfloat16)
+                slot = step & 1
+                if step >= 2:
+                    copies[step - 2].wait()
+                done_ref[slot, :size, :] = dot(eye[:size, :size], flat, NT).astype(jnp.bfloat16)
+                copy = pltpu.make_async_copy(
+                    done_ref.at[slot, pl.ds(0, size)],
+                    out_refs[net].at[pl.ds(start, size)],
+                    sem.at[slot],
+                )
+                copy.start()
+                copies.append(copy)
+            for copy in copies[-2:]:
+                copy.wait()
 
         return call(
-            kernel, array((f, D), jnp.bfloat16), *stacks,
-            grid=(pl.cdiv(f, LANES),),
-            in_specs=[pl.BlockSpec((count, 1, width, LANES), lambda s: (0, net, 0, s))] * 4,
-            out_specs=pl.BlockSpec((LANES, D), lambda s: (s, 0)),
-            scratch_shapes=[pltpu.VMEM((n_dp, width, LANES), jnp.float32)],
+            kernel, [array((f, D), jnp.bfloat16)] * 2, *stacks,
+            in_specs=[VMEM] * 4, out_specs=[ANY] * 2,
+            scratch_shapes=[
+                pltpu.VMEM((n_dp, width, TILE), jnp.float32),
+                pltpu.VMEM((2, TILE, D), jnp.bfloat16),
+                pltpu.SemaphoreType.DMA((2,)),
+            ],
+            mib=24,
         )
 
     def per_device(
@@ -394,20 +353,15 @@
                 distance *= 2
             yield value
 
-        acts = [from_tensor(act, -j) for j, act in enumerate(step(lambda a: cut_acts(a, r), act_fake), 1)]
         scales = step(
             lambda steps: 1.0 / (0.1 + steps.astype(jnp.float32) / 1000.0), timesteps[0, :, 0]
         )
-        bounds = step(
-            lambda a, b, c, d, scales: bound_of((a, b), (c, d), scales),
-            cot_student, cot_fake, act_student, act_fake, scales,
-        )
-        bounds = hops(bounds, jnp.maximum)
-        next(bounds)
+        scaled_own, *sent = step(lambda act: prepare(1, act, scales, r, False), act_fake)
+        acts = [from_tensor(value, -j) for j, value in enumerate(sent, 1)]
+        scaled_fake = [[value, to_core(value)] for value in (scaled_own, *acts)]
         fake_blocks = step(lambda cot: turn(cot, False), cot_fake)
         mate_blocks = to_core(fake_blocks[1])
-        scaled_own = step(lambda act: prepare(1, act, scales, r, 1), act_fake)
-        scaled_fake = [[scaled_own, to_core(scaled_own)]]
+        (scaled_student,) = step(lambda act: prepare(0, act, scales, r, True), act_student)
         planes = step(lambda cot: turn(cot, True), cot_student)
 
         same, diagonal = [], []
@@ -417,69 +371,55 @@
             diagonal.append([from_diagonal(other, j) for j in range(1, n_tensor)])
 
         send_planes(0, planes[0], planes[1])
-        scaled_student = step(lambda act: prepare(0, act, scales, r, n_tensor), act_student)
-        for act in acts:
-            scaled_other = step(scale_rows, act, scales)
-            scaled_fake.append([scaled_other, to_core(scaled_other)])
-        parts_fake = []
-        for j in range(n_tensor):
-            if j < 2:
-                next(bounds)
-            parts_fake.append(
-                step(
-                    lambda a, b, c, d: multiply([a, b], [c, d], [(0, 0), (1, 0)]),
-                    fake_blocks[0], mate_blocks, *scaled_fake[j],
-                )
+
+        def shrink(value, power):
+            scaled = value * jnp.exp2(HALF_BITS - power)
+            width_more = [(0, 0)] * (value.ndim - 1) + [(0, 1)]
+            lanes = lax.broadcasted_iota(jnp.int32, (*value.shape[:-1], f + 1), value.ndim - 1)
+            return jnp.where(lanes == f, power, jnp.pad(scaled, width_more)).astype(jnp.float16)
+
+        def widen(value):
+            power = value.reshape(-1)[f].astype(jnp.float32)
+            return value[..., :f].astype(jnp.float32) * jnp.exp2(power - HALF_BITS), power
+
+        def add(total, power, values):
+            for value in values:
+                value, other = widen(value)
+                total, power = total + value, jnp.maximum(power, other) + 1.0
+            return total, power
+
+        fake_own, fake_got = {}, {}
+
+        def fake_middle(j):
+            def work(both, power):
+                return [shrink(both[i], power) for i in range(1, inner)], (both[0], power)
+
+            both = step(
+                lambda a, b, c, d: multiply([a, b], [c, d], [(0, 0), (1, 0)]),
+                fake_blocks[0], mate_blocks, *scaled_fake[j],
             )
-        while (final := next(bounds)) is None:
-            pass
-
-        def factors(bounds):
-            bounds = jnp.maximum(bounds, 1e-30) * (1.01 * count * n_dp / HALF_LIMIT)
-            return bounds[:2, 0], 1.0 / bounds[:2, 0]
-
-        grow, fit = step(factors, final)
-
-        def shrink(value, net):
-            return (value * fit[net]).astype(jnp.float16)
-
-        def widen(value, net):
-            return value.astype(jnp.float32) * grow[net]
-
-        def add_widened(total, values, net):
-            for value in values:
-                total = total + widen(value, net)
-            return total
-
-        fake_own, fake_got = {}, {}
-
-        def fake_middle(j):
-            def work(both):
-                sent = [shrink(both[i], 1) for i in range(1, inner)]
-                return sent, both[0]
-
-            sent, fake_own[j] = step(work, parts_fake[j])
+            sent, fake_own[j] = step(work, *both)
             fake_got[j] = [to_middle(value, i) for i, value in enumerate(sent, 1)]
 
         def fake_near(j):
-            def work(own, *got):
-                own = add_widened(own, got, 1)
-                return shrink(own[1::2], 1), own[0::2]
-
-            sent, fake_own[j] = step(work, fake_own[j], *fake_got[j])
+            def work(own, power, *got):
+                own, power = add(own, power, got)
+                return shrink(own[1::2], power), (own[0::2], power)
+
+            sent, fake_own[j] = step(work, *fake_own[j], *fake_got[j])
             fake_got[j] = [to_plane(sent, 1)]
 
         def fake_far(j):
-            def work(own, *got):
-                own = add_widened(own, got, 1)
-                return shrink(own[1], 1), own[0]
-
-            sent, fake_own[j] = step(work, fake_own[j], *fake_got[j])
+            def work(own, power, *got):
+                own, power = add(own, power, got)
+                return shrink(own[1], power), (own[0], power)
+
+            sent, fake_own[j] = step(work, *fake_own[j], *fake_got[j])
             fake_got[j] = [to_plane(sent, 2)]
 
         def fake_total(j):
             return step(
-                lambda own, *got: add_widened(own, got, 1), fake_own[j], *fake_got[j]
+                lambda own, power, *got: add(own, power, got)[0], *fake_own[j], *fake_got[j]
             )
 
         mate_student = to_core(scaled_student)
@@ -515,27 +455,25 @@
         back_fake = back(None, 1, [cot_fake], 0, 0, r)
         both = multiply_student(0)
 
-        def first_middle(both):
-            return [shrink(both[:, i], 0) for i in range(1, inner)], both[:, 0]
-
-        sent, own = step(first_middle, both)
+        def first_middle(both, power):
+            return [shrink(both[:, i], power) for i in range(1, inner)], both[:, 0], power
+
+        sent, own, power = step(first_middle, *both)
         got = [to_middle(value, i) for i, value in enumerate(sent, 1)]
         for j in range(n_tensor):
             fake_near(j)
-
-        def first_planes(own, *got):
-            return shrink(add_widened(own, got, 0), 0)
-
-        near = to_plane(step(first_planes, own, *got), 1)
+        near = to_plane(
+            step(lambda own, power, *got: shrink(*add(own, power, got)), own, power, *got), 1
+        )
         for j in range(n_tensor):
             fake_far(j)
         both = multiply_student(1)
 
-        def second_middle(both):
-            sent = [[shrink(both[n, i], 0) for i in range(1, inner)] for n in range(2)]
-            return sent, both[0, 0], both[1, 0]
-
-        sent, own_far, own = step(second_middle, both)
+        def second_middle(both, power):
+            sent = [[shrink(both[n, i], power) for i in range(1, inner)] for n in range(2)]
+            return sent, both[0, 0], both[1, 0], power
+
+        sent, own_far, own, power = step(second_middle, *both)
         got_far, got = (
             [to_middle(value, i) for i, value in enumerate(values, 1)] for values in sent
         )
@@ -543,17 +481,16 @@
         fake_others = [fake_total(j) for j in range(1, n_tensor)]
         others_got = [from_tensor(value, j) for j, value in enumerate(fake_others, 1)]
 
-        def far_plane(own, near, *got):
-            return shrink(add_widened(own, (near[1], *got), 0), 0)
-
-        far = to_plane(step(far_plane, own_far, near, *got_far), 2)
+        def far_plane(own, power, near, *got):
+            return shrink(*add(own, power, [near[1], *got]))
+
+        far = to_plane(step(far_plane, own_far, power, near, *got_far), 2)
         total_student = step(
-            lambda own, near, *got: add_widened(own, (near[0], *got), 0), own, near, *got
+            lambda own, power, near, *got: add(own, power, [near[0], *got])[0],
+            own, power, near, *got,
         )
         total_fake = reduced(jnp.add, fake_mine, others_got)
-        total_student = step(
-            lambda own, got: add_widened(own, (got,), 0), total_student, far
-        )
+        total_student = step(lambda own, got: own + widen(got)[0], total_student, far)
         squares = step(norms, total_student, total_fake)
         squares = reduced(
             jnp.add, squares, [from_tensor(squares, j) for j in range(1, n_tensor)]
@@ -567,7 +504,6 @@
         *_, squares = hops(squares, jnp.add)
         squares, *mate_others = step(lambda *values: values, squares, *mate_others)
         mate_others = [mate_others[: n_tensor - 1], mate_others[n_tensor - 1 :]]
-
         states = (
             master_student, first_student, second_student, master_fake, first_fake, second_fake,
         )
@@ -583,22 +519,22 @@
 
         spread_middle(0, own)
         planes_got = {k: to_plane(own, k) for k in (1, 3, 2)}
+        spread_middle(1, step(lambda value: value, planes_got[1]))
+        spread_middle(3, step(lambda value: value, planes_got[3]))
+        first_half = step(lambda *values: jnp.stack(values), *mine[0], *mine[1])
+        theirs = [to_core(first_half)]
         for j in range(1, n_tensor):
             pieces = [
                 piece for g in range(2) for piece in (same[g][j - 1], mate_others[g][j - 1])
             ]
             back_student = back(back_student, 0, pieces, j, 0, r)
-        spread_middle(1, step(lambda value: value, planes_got[1]))
-        spread_middle(3, step(lambda value: value, planes_got[3]))
         spread_middle(2, step(lambda value: value, planes_got[2]))
-        first_half = step(lambda *values: jnp.stack(values), *mine[0], *mine[1])
-        theirs = [to_core(first_half)]
         for j in range(1, n_tensor):
             back_fake = back(back_fake, 1, [raw[j - 1]], j, 0, r)
         second_half = step(lambda *values: jnp.stack(values), *mine[2], *mine[3])
         theirs.append(to_core(second_half))
         stacks = [first_half, second_half, *theirs]
-        params = [step(lambda *values: spread(values, n), *stacks) for n in range(2)]
+        params = step(lambda *values: spread(values), *stacks)
 
         new_states = [value.T for value in updated]
         return (back_student, back_fake, *new_states, *params)

time: 213 us -> 254 us (1.19)
  waiting for transfers between devices: 107 us -> 56.2 us
  local copies, waits for them, and re-layouts: 8.52 us -> 49.3 us
  other arithmetic: 15.7 us -> 44.5 us
  between operations: 1.17 us -> 15.2 us
  Pallas kernels: 40.1 us -> 44 us
  starting transfers between devices: 40 us -> 42.8 us
    ppermute x28, waiting for transfers between devices: 62.6 us -> 30.8 us  [move_dp(): return lax.ppermute(value, 'dp', perm)]
    reshape x0 -> x10, local copies, waits for them, and re-layouts: none -> 19 us  [widen(): power = value.reshape(-1)[f].astype(jnp.float32)]
    slice x3 -> x18, local copies, waits for them, and re-layouts: 1.23 us -> 16.6 us  [the longest x12 11.2 us: widen(): power = value.reshape(-1)[f].astype(jnp.float32)]
    ppermute x6, waiting for transfers between devices: 28.3 us -> 16.8 us  [from_tensor(): return lax.ppermute(value, 'tensor', perm)]
    squeeze x4 -> x5, other arithmetic: 3.09 us -> 10.6 us  [the longest x2 6.71 us: work(): return ([shrink(both[i], power) for i in range(1, inner)], (both[0], power))]
    ppermute x8 -> x4, waiting for transfers between devices: 15.5 us -> 8.58 us  [hops(): got = lax.ppermute(value, 'dp', perm)]
    add x8, other arithmetic: 6.02 us -> 12.8 us  [the longest x7 11.7 us: add(): total, power = (total + value, jnp.maximum(power, other) + 1.0)]
    convert_element_type x5 -> x10, other arithmetic: 5.07 us -> 11.7 us  [shrink(): jnp.where(lanes == f, power, jnp.pad(scaled, width_more))]
  transfers between devices with their start and end apart: 44 -> 40, of which waited for: 22 -> 13; matrix products, arithmetic and copies ran while one was open for 8% -> 27% of each run, Pallas kernels for 13% -> 14%
where the time goes in v8:
time: 254 us; the launch traced here: 252 us
  waiting for transfers between devices  56.2 us (22%)
  local copies, waits for them, and re-layouts  49.3 us (19%)
  other arithmetic  44.5 us (18%)
  Pallas kernels  44 us (17%)
  starting transfers between devices  42.8 us (17%)
  between operations  15.2 us (6%)
    pallas_call x15, Pallas kernels, call(): pl.pallas_call(kernel, out_shape=out_shape, compiler_params=pltpu.Compile...  44 us
    ppermute x28, waiting for transfers between devices, move_dp(): return lax.ppermute(value, 'dp', perm)  30.8 us
    ppermute x28, starting transfers between devices, move_dp(): return lax.ppermute(value, 'dp', perm)  27.2 us
    reshape x10, local copies, waits for them, and re-layouts, widen(): power = value.reshape(-1)[f].astype(jnp.float32)  19 us
    ppermute x6, waiting for transfers between devices, from_tensor(): return lax.ppermute(value, 'tensor', perm)  16.8 us
    add x7, other arithmetic, add(): total, power = (total + value, jnp.maximum(power, other) + 1.0)  11.7 us
    convert_element_type x10, other arithmetic, shrink(): jnp.where(lanes == f, power, jnp.pad(scaled, width_more))  11.7 us
    unnamed x48, local copies, waits for them, and re-layouts  11.3 us
  transfers between devices with their start and end apart: 40, of which 13 were waited for; matrix products, arithmetic and copies ran while one was open for 27% of the time, Pallas kernels for 14%

profile of v8, /device:TPU:0, one launch (start us, length us, event | category | flops | bytes accessed | tf_op | source)
XLA Modules:
  0.0 252.0 jit_solution(9037429523327462073)
XLA Ops:
  7.4 2.6 %collective-permute-start.5 = (bf16[1,608,512]{2,1,0:T(8,128)(2,1)S(1)}, bf16[1,608,512]{2,1,0:T(8,128)(2,1)}, u32[]{:S(2)}, u32[]{:S(2)}) collective-permute-start(bf16[1,608,512]{2,1,0:T(8,128)(2,1)S(1)} %get-tuple-element.168), channel_id=1, source_target_pairs={{0,1},{1,0},{2,3},{3,2},{4,5},{5,4},{6,7},{7,6},{8,9},{9,8},{10,11... | collective-permute-start | bytes 1867784 | tf_op jit(solution)/shard_map/ppermute | solution.py:91
  10.1 14.6 %collective-permute-done.5.refs_2_ = bf16[1,608,512]{2,1,0:T(8,128)(2,1)} collective-permute-done((bf16[1,608,512]{2,1,0:T(8,128)(2,1)S(1)}, bf16[1,608,512]{2,1,0:T(8,128)(2,1)}, u32[]{:S(2)}, u32[]{:S(2)}) %collective-permute-start.5) | collective-permute-done | bytes 622624 | tf_op jit(solution)/shard_map/ppermute | solution.py:91
  27.0 3.0 %shard_map.207 = (bf16[2,2,152,512]{3,2,1,0:T(8,128)(2,1)}, bf16[2,2,152,512]{3,2,1,0:T(8,128)(2,1)}, bf16[2,2,152,512]{3,2,1,0:T(8,128)(2,1)}, bf16[2,2,152,512]{3,2,1,0:T(8,128)(2,1)}) custom-call(bf16[512,2432]{1,0:T(8,128)(2,1)S(1)} %copy-done.3), custom_call_target="tpu_custom_call" | custom-call | tf_op jit(solution)/shard_map/pallas_call | solution.py:56
  32.1 2.3 shard_map.208
  37.3 3.3 %slice_bitcast_fusion = (f32[4,152,608]{2,1,0:T(8,128)}, f32[4,152,608]{2,1,0:T(8,128)S(1)}) fusion(f32[2,4,152,608]{3,2,1,0:T(8,128)} %bitcast.98, f32[]{:T(128)S(6)} %exp2.155), kind=kLoop, calls=%fused_computation.4 | loop fusion | flops 369664 | bytes 5914628 | tf_op jit(solution)/shard_map/squeeze | solution.py:395
  42.5 3.5 %shard_map.209 = (f32[1216,608]{1,0:T(8,128)S(1)}, f32[8,128]{1,0:T(8,128)S(1)}) custom-call(bf16[1216,512]{1,0:T(8,128)(2,1)S(1)} %bitcast.94, bf16[1216,512]{1,0:T(8,128)(2,1)S(1)} %bitcast.96, bf16[1,608,512]{2,1,0:T(8,128)(2,1)} %collective-permute-done.5.refs_2_, bf16[1,608,512]{2,1,0:T(8,128)(2,1)} %collective-permute-done.6.refs_3_), custom_call_target="tpu_custom_call" | custom-call | tf_op jit(solution)/shard_map/pallas_call | solution.py:56
  48.9 3.4 %slice_bitcast_fusion.1 = (f32[4,152,608]{2,1,0:T(8,128)}, f32[4,152,608]{2,1,0:T(8,128)S(1)}) fusion(f32[2,4,152,608]{3,2,1,0:T(8,128)} %bitcast.97, f32[]{:T(128)S(6)} %exp2.157), kind=kLoop, calls=%fused_computation.5 | loop fusion | flops 369664 | bytes 5914628 | tf_op jit(solution)/shard_map/squeeze | solution.py:395
  56.0 3.2 %shard_map.210.refs_4_ = bf16[608,1024]{1,0:T(8,128)(2,1)} custom-call(f32[2]{0:T(128)S(1)} %divide_bitcast_fusion.scale_ref, bf16[608,2432]{1,0:T(8,128)(2,1)S(1)} %copy-done, bf16[512,2432]{1,0:T(8,128)(2,1)S(1)} %copy-done.4), custom_call_target="tpu_custom_call" | custom-call | tf_op jit(solution)/shard_map/pallas_call | solution.py:56
  61.0 3.2 %shard_map.211.refs_1_ = bf16[608,1024]{1,0:T(8,128)(2,1)} custom-call(f32[2]{0:T(128)S(1)} %divide_bitcast_fusion.scale_ref, bf16[608,2432]{1,0:T(8,128)(2,1)S(1)} %copy-done.1, bf16[512,2432]{1,0:T(8,128)(2,1)S(1)} %copy-done.6), custom_call_target="tpu_custom_call" | custom-call | tf_op jit(solution)/shard_map/pallas_call | solution.py:56
  64.3 4.7 %shard_map.212 = (f32[608,608]{1,0:T(8,128)S(1)}, f32[8,128]{1,0:T(8,128)S(1)}) custom-call(bf16[608,512]{1,0:T(8,128)(2,1)} %bitcast.13.refs_0_, bf16[608,512]{1,0:T(8,128)(2,1)} %bitcast.14.refs_1_, bf16[608,512]{1,0:T(8,128)(2,1)} %bitcast.15.refs_2_, bf16[608,512]{1,0:T(8,128)(2,1)} %bitcast.16.refs_3_, bf16[2,608,512]{2,1,0:T(8,128)(2,1)} %shard_map.206.refs_4_, ...), custom_call_target="tpu_custom_call" | custom-call | tf_op jit(solution)/shard_map/pallas_call | solution.py:56
  71.4 2.3 slice_bitcast_fusion.2
  76.7 3.6 %reshape.174 = f16[370272]{0:T(1024)(128)(2,1)} reshape(f16[4,152,609]{2,1,0:T(8,128)(2,1)} %collective-permute-done.11) | data formatting | bytes 1481088 | tf_op jit(solution)/shard_map/reshape | solution.py:382
  89.4 3.8 %reshape.175 = f16[370272]{0:T(1024)(128)(2,1)} reshape(f16[4,152,609]{2,1,0:T(8,128)(2,1)} %collective-permute-done.10) | data formatting | bytes 1481088 | tf_op jit(solution)/shard_map/reshape | solution.py:382
  113.9 2.8 %collective-permute-start.20 = (f16[152,609]{1,0:T(8,128)(2,1)}, f16[152,609]{1,0:T(8,128)(2,1)S(1)}, u32[]{:S(2)}, u32[]{:S(2)}) collective-permute-start(f16[152,609]{1,0:T(8,128)(2,1)} %select_convert_fusion.10), channel_id=1, source_target_pairs={{0,16},{2,18},{4,20},{6,22},{8,24},{10,26},{12,28},{14,30},{16,0},... | collective-permute-start | bytes 555416 | tf_op jit(solution)/shard_map/ppermute | solution.py:78
  122.8 4.7 %shard_map.213 = (f32[608,608]{1,0:T(8,128)S(1)}, f32[8,128]{1,0:T(8,128)S(1)}) custom-call(bf16[608,512]{1,0:T(8,128)(2,1)} %bitcast.33.refs_0_, bf16[608,512]{1,0:T(8,128)(2,1)} %bitcast.34.refs_1_, bf16[608,512]{1,0:T(8,128)(2,1)} %bitcast.35.refs_2_, bf16[608,512]{1,0:T(8,128)(2,1)} %bitcast.36.refs_3_, bf16[2,608,512]{2,1,0:T(8,128)(2,1)} %shard_map.206.refs_4_, ...), custom_call_target="tpu_custom_call" | custom-call | tf_op jit(solution)/shard_map/pallas_call | solution.py:56
  129.8 2.3 multiply_bitcast_fusion.2
  158.1 2.6 %collective-permute-start.21 = (f16[152,609]{1,0:T(8,128)(2,1)}, f16[152,609]{1,0:T(8,128)(2,1)S(1)}, u32[]{:S(2)}, u32[]{:S(2)}) collective-permute-start(f16[152,609]{1,0:T(8,128)(2,1)} %get-tuple-element.326), channel_id=1, source_target_pairs={{0,16},{2,18},{4,20},{6,22},{8,24},{10,26},{12,28},{14,30},{16,0},... | collective-permute-start | bytes 555416 | tf_op jit(solution)/shard_map/ppermute | solution.py:78
  177.6 2.2 collective-permute-done.23
  183.9 3.1 %collective-permute-done.25 = f32[8,128]{1,0:T(8,128)S(1)} collective-permute-done((f32[8,128]{1,0:T(8,128)S(1)}, f32[8,128]{1,0:T(8,128)S(1)}, u32[]{:S(2)}, u32[]{:S(2)}) %collective-permute-start.25) | collective-permute-done | bytes 4128 | tf_op jit(solution)/shard_map/ppermute | solution.py:350
  188.6 2.0 collective-permute-done.26
  190.6 2.6 %collective-permute-start.27 = (f32[8,128]{1,0:T(8,128)S(1)}, f32[8,128]{1,0:T(8,128)S(1)}, u32[]{:S(2)}, u32[]{:S(2)}) collective-permute-start(f32[8,128]{1,0:T(8,128)S(1)} %add.142), channel_id=1, source_target_pairs={{0,16},{2,18},{4,20},{6,22},{8,24},{10,26},{12,28},{14,30},{16,0},... | collective-permute-start | bytes 12296 | tf_op jit(solution)/shard_map/ppermute | solution.py:350
  197.2 2.1 shard_map.215
  200.8 2.5 collective-permute-start.33
  203.8 6.9 %collective-permute-done.31 = bf16[2,152,608]{2,1,0:T(8,128)(2,1)S(1)} collective-permute-done((bf16[2,152,608]{2,1,0:T(8,128)(2,1)S(1)}, bf16[2,152,608]{2,1,0:T(8,128)(2,1)S(1)}, u32[]{:S(2)}, u32[]{:S(2)}) %collective-permute-start.31) | collective-permute-done | bytes 369696 | tf_op jit(solution)/shard_map/ppermute | solution.py:78
  210.8 4.6 %collective-permute-start.35 = (bf16[2,152,608]{2,1,0:T(8,128)(2,1)S(1)}, bf16[2,152,608]{2,1,0:T(8,128)(2,1)S(1)}, u32[]{:S(2)}, u32[]{:S(2)}) collective-permute-start(bf16[2,152,608]{2,1,0:T(8,128)(2,1)S(1)} %get-tuple-element.274), channel_id=1, source_target_pairs={{0,16},{2,18},{4,20},{6,22},{8,24},{10,26},{12,28},{14,30},{16,0},... | collective-permute-start | bytes 1109000 | tf_op jit(solution)/shard_map/ppermute | solution.py:78
  215.4 6.3 %collective-permute-done.33 = bf16[2,152,608]{2,1,0:T(8,128)(2,1)S(1)} collective-permute-done((bf16[2,152,608]{2,1,0:T(8,128)(2,1)S(1)}, bf16[2,152,608]{2,1,0:T(8,128)(2,1)S(1)}, u32[]{:S(2)}, u32[]{:S(2)}) %collective-permute-start.33) | collective-permute-done | bytes 369696 | tf_op jit(solution)/shard_map/ppermute | solution.py:78
  222.8 4.4 %shard_map.216 = bf16[608,1024]{1,0:T(8,128)(2,1)} custom-call(f32[2]{0:T(128)S(1)} %divide_bitcast_fusion.scale_ref, bf16[608,2432]{1,0:T(8,128)(2,1)S(1)} %copy-done, bf16[2,2,152,512]{3,2,1,0:T(8,128)(2,1)} %collective-permute-done.refs_0_, bf16[2,2,152,512]{3,2,1,0:T(8,128)(2,1)S(1)} %collective-permute-done.28.refs_1_, ...), custom_call_target="tpu_custom_call", output_to_operand_aliasing={{}: (6, {})} | custom-call | tf_op jit(solution)/shard_map/pallas_call | solution.py:56
  227.2 7.4 %collective-permute-done.35 = bf16[2,152,608]{2,1,0:T(8,128)(2,1)S(1)} collective-permute-done((bf16[2,152,608]{2,1,0:T(8,128)(2,1)S(1)}, bf16[2,152,608]{2,1,0:T(8,128)(2,1)S(1)}, u32[]{:S(2)}, u32[]{:S(2)}) %collective-permute-start.35) | collective-permute-done | bytes 369696 | tf_op jit(solution)/shard_map/ppermute | solution.py:78
  235.2 3.2 %shard_map.217 = bf16[608,1024]{1,0:T(8,128)(2,1)} custom-call(f32[2]{0:T(128)S(1)} %divide_bitcast_fusion.scale_ref, bf16[608,2432]{1,0:T(8,128)(2,1)S(1)} %copy-done.2, bf16[512,2432]{1,0:T(8,128)(2,1)S(1)} %collective-permute-done.34.refs_0_, bf16[608,1024]{1,0:T(8,128)(2,1)} %shard_map.211.refs_1_), custom_call_target="tpu_custom_call", output_to_operand_aliasing={{}: (3, {})} | custom-call | tf_op jit(solution)/shard_map/pallas_call | solution.py:56
  238.4 4.4 %collective-permute-done.36 = bf16[2,152,608]{2,1,0:T(8,128)(2,1)S(1)} collective-permute-done((bf16[2,152,608]{2,1,0:T(8,128)(2,1)S(1)}, bf16[2,152,608]{2,1,0:T(8,128)(2,1)S(1)}, u32[]{:S(2)}, u32[]{:S(2)}) %collective-permute-start.36) | collective-permute-done | bytes 369696 | tf_op jit(solution)/shard_map/ppermute | solution.py:78
  243.2 3.4 %collective-permute-done.39.refs_3_ = bf16[4,2,152,608]{3,2,1,0:T(8,128)(2,1)S(1)} collective-permute-done((bf16[4,2,152,608]{3,2,1,0:T(8,128)(2,1)S(1)}, bf16[4,2,152,608]{3,2,1,0:T(8,128)(2,1)S(1)}, u32[]{:S(2)}, u32[]{:S(2)}) %collective-permute-start.39) | collective-permute-done | bytes 1478688 | tf_op jit(solution)/shard_map/ppermute | solution.py:78
  246.6 5.2 %shard_map.218 = (bf16[608,2432]{1,0:T(8,128)(2,1)}, bf16[608,2432]{1,0:T(8,128)(2,1)}) custom-call(bf16[4,2,152,608]{3,2,1,0:T(8,128)(2,1)S(1)} %pad_maximum_fusion.refs_0_, bf16[4,2,152,608]{3,2,1,0:T(8,128)(2,1)S(1)} %pad_maximum_fusion.1.refs_1_, bf16[4,2,152,608]{3,2,1,0:T(8,128)(2,1)S(1)} %collective-permute-done.38.refs_2_, ...), custom_call_target="tpu_custom_call" | custom-call | tf_op jit(solution)/shard_map/pallas_call | solution.py:56
  (179 shorter events, 110.6 us)
Async XLA Ops:
  6.8 25.0 %collective-permute-start.4 = (bf16[2,4,152,512]{3,2,1,0:T(8,128)(2,1)S(1)}, bf16[2,4,152,512]{3,2,1,0:T(8,128)(2,1)S(1)}, u32[]{:S(2)}, u32[]{:S(2)}) collective-permute-start(bf16[2,4,152,512]{3,2,1,0:T(8,128)(2,1)S(1)} %get-tuple-element.167), channel_id=1, source_target_pairs={{0,2},{2,0},{4,6},{6,4},{8,10},{10,8},{12,14},{14,12},{16,18},{18,... | collective-permute-start | bytes 3735560 | tf_op jit(solution)/shard_map/ppermute | solution.py:78
  7.4 17.3 %collective-permute-start.5 = (bf16[1,608,512]{2,1,0:T(8,128)(2,1)S(1)}, bf16[1,608,512]{2,1,0:T(8,128)(2,1)}, u32[]{:S(2)}, u32[]{:S(2)}) collective-permute-start(bf16[1,608,512]{2,1,0:T(8,128)(2,1)S(1)} %get-tuple-element.168), channel_id=1, source_target_pairs={{0,1},{1,0},{2,3},{3,2},{4,5},{5,4},{6,7},{7,6},{8,9},{9,8},{10,11... | collective-permute-start | bytes 1867784 | tf_op jit(solution)/shard_map/ppermute | solution.py:91
  9.9 21.4 %collective-permute-start.7 = (bf16[1,608,512]{2,1,0:T(8,128)(2,1)S(1)}, bf16[1,608,512]{2,1,0:T(8,128)(2,1)S(1)}, u32[]{:S(2)}, u32[]{:S(2)}) collective-permute-start(bf16[1,608,512]{2,1,0:T(8,128)(2,1)S(1)} %get-tuple-element.171.refs_2_), channel_id=1, source_target_pairs={{0,2},{2,0},{4,6},{6,4},{8,10},{10,8},{12,14},{14,12},{16,18},{18,... | collective-permute-start | bytes 1867784 | tf_op jit(solution)/shard_map/ppermute | solution.py:78
  24.7 15.9 %collective-permute-start.6 = (bf16[1,608,512]{2,1,0:T(8,128)(2,1)}, bf16[1,608,512]{2,1,0:T(8,128)(2,1)}, u32[]{:S(2)}, u32[]{:S(2)}) collective-permute-start(bf16[1,608,512]{2,1,0:T(8,128)(2,1)} %collective-permute-done.5.refs_2_), channel_id=1, source_target_pairs={{0,2},{2,0},{4,6},{6,4},{8,10},{10,8},{12,14},{14,12},{16,18},{18,... | collective-permute-start | bytes 1867784 | tf_op jit(solution)/shard_map/ppermute | solution.py:78
  26.5 29.5 %collective-permute-start.1 = (bf16[2,608,512]{2,1,0:T(8,128)(2,1)}, bf16[2,608,512]{2,1,0:T(8,128)(2,1)}, u32[]{:S(2)}, u32[]{:S(2)}) collective-permute-start(bf16[2,608,512]{2,1,0:T(8,128)(2,1)} %shard_map.206.refs_4_), channel_id=1, source_target_pairs={{0,2},{2,0},{4,6},{6,4},{8,10},{10,8},{12,14},{14,12},{16,18},{18,... | collective-permute-start | bytes 3735560 | tf_op jit(solution)/shard_map/ppermute | solution.py:78
  30.0 34.3 %collective-permute-start.12 = (bf16[2,2,152,512]{3,2,1,0:T(8,128)(2,1)}, bf16[2,2,152,512]{3,2,1,0:T(8,128)(2,1)}, u32[]{:S(2)}, u32[]{:S(2)}) collective-permute-start(bf16[2,2,152,512]{3,2,1,0:T(8,128)(2,1)} %get-tuple-element.165), channel_id=1, source_target_pairs={{0,3},{1,2},{2,1},{3,0},{4,7},{5,6},{6,5},{7,4},{8,11},{9,10},{10,... | collective-permute-start | bytes 1867784 | tf_op jit(solution)/shard_map/ppermute | solution.py:100
  31.4 20.9 %collective-permute-start.2 = (bf16[2,2,152,512]{3,2,1,0:T(8,128)(2,1)}, bf16[2,2,152,512]{3,2,1,0:T(8,128)(2,1)}, u32[]{:S(2)}, u32[]{:S(2)}) collective-permute-start(bf16[2,2,152,512]{3,2,1,0:T(8,128)(2,1)} %get-tuple-element.165), channel_id=1, source_target_pairs={{0,2},{2,0},{4,6},{6,4},{8,10},{10,8},{12,14},{14,12},{16,18},{18,... | collective-permute-start | bytes 1867784 | tf_op jit(solution)/shard_map/ppermute | solution.py:78
  31.9 32.5 %collective-permute-start = (bf16[2,2,152,512]{3,2,1,0:T(8,128)(2,1)}, bf16[2,2,152,512]{3,2,1,0:T(8,128)(2,1)}, u32[]{:S(2)}, u32[]{:S(2)}) collective-permute-start(bf16[2,2,152,512]{3,2,1,0:T(8,128)(2,1)} %get-tuple-element.194), channel_id=1, source_target_pairs={{0,1},{1,0},{2,3},{3,2},{4,5},{5,4},{6,7},{7,6},{8,9},{9,8},{10,11... | collective-permute-start | bytes 1867784 | tf_op jit(solution)/shard_map/ppermute | solution.py:91
  40.6 15.2 %collective-permute-start.3 = (bf16[2,2,152,512]{3,2,1,0:T(8,128)(2,1)}, bf16[2,2,152,512]{3,2,1,0:T(8,128)(2,1)}, u32[]{:S(2)}, u32[]{:S(2)}) collective-permute-start(bf16[2,2,152,512]{3,2,1,0:T(8,128)(2,1)} %get-tuple-element.190), channel_id=1, source_target_pairs={{0,2},{2,0},{4,6},{6,4},{8,10},{10,8},{12,14},{14,12},{16,18},{18,... | collective-permute-start | bytes 1867784 | tf_op jit(solution)/shard_map/ppermute | solution.py:78
  52.3 24.4 %collective-permute-start.11 = (f16[4,152,609]{2,1,0:T(8,128)(2,1)}, f16[4,152,609]{2,1,0:T(8,128)(2,1)}, u32[]{:S(2)}, u32[]{:S(2)}) collective-permute-start(f16[4,152,609]{2,1,0:T(8,128)(2,1)} %select_convert_fusion.1), channel_id=1, source_target_pairs={{0,4},{2,6},{4,0},{6,2},{8,12},{10,14},{12,8},{14,10},{16,20},{18,... | collective-permute-start | bytes 2221640 | tf_op jit(solution)/shard_map/ppermute | solution.py:78
  55.8 33.7 %collective-permute-start.10 = (f16[4,152,609]{2,1,0:T(8,128)(2,1)}, f16[4,152,609]{2,1,0:T(8,128)(2,1)}, u32[]{:S(2)}, u32[]{:S(2)}) collective-permute-start(f16[4,152,609]{2,1,0:T(8,128)(2,1)} %select_convert_fusion), channel_id=1, source_target_pairs={{0,4},{2,6},{4,0},{6,2},{8,12},{10,14},{12,8},{14,10},{16,20},{18,... | collective-permute-start | bytes 2221640 | tf_op jit(solution)/shard_map/ppermute | solution.py:78
  59.2 63.6 %collective-permute-start.8 = (bf16[2,2,152,512]{3,2,1,0:T(8,128)(2,1)}, bf16[2,2,152,512]{3,2,1,0:T(8,128)(2,1)}, u32[]{:S(2)}, u32[]{:S(2)}) collective-permute-start(bf16[2,2,152,512]{3,2,1,0:T(8,128)(2,1)} %get-tuple-element.219), channel_id=1, source_target_pairs={{0,1},{1,0},{2,3},{3,2},{4,5},{5,4},{6,7},{7,6},{8,9},{9,8},{10,11... | collective-permute-start | bytes 1867784 | tf_op jit(solution)/shard_map/ppermute | solution.py:91
  64.2 58.6 %collective-permute-start.9 = (bf16[2,2,152,512]{3,2,1,0:T(8,128)(2,1)}, bf16[2,2,152,512]{3,2,1,0:T(8,128)(2,1)}, u32[]{:S(2)}, u32[]{:S(2)}) collective-permute-start(bf16[2,2,152,512]{3,2,1,0:T(8,128)(2,1)} %get-tuple-element.190), channel_id=1, source_target_pairs={{0,3},{1,2},{2,1},{3,0},{4,7},{5,6},{6,5},{7,4},{8,11},{9,10},{10,... | collective-permute-start | bytes 1867784 | tf_op jit(solution)/shard_map/ppermute | solution.py:100
  75.2 26.1 %collective-permute-start.15 = (f16[2,152,609]{2,1,0:T(8,128)(2,1)}, f16[2,152,609]{2,1,0:T(8,128)(2,1)S(1)}, u32[]{:S(2)}, u32[]{:S(2)}) collective-permute-start(f16[2,152,609]{2,1,0:T(8,128)(2,1)} %select_convert_fusion.5), channel_id=1, source_target_pairs={{0,4},{2,6},{4,0},{6,2},{8,12},{10,14},{12,8},{14,10},{16,20},{18,... | collective-permute-start | bytes 1110824 | tf_op jit(solution)/shard_map/ppermute | solution.py:78
  86.5 21.3 %collective-permute-start.14 = (f16[2,152,609]{2,1,0:T(8,128)(2,1)}, f16[2,152,609]{2,1,0:T(8,128)(2,1)}, u32[]{:S(2)}, u32[]{:S(2)}) collective-permute-start(f16[2,152,609]{2,1,0:T(8,128)(2,1)} %select_convert_fusion.4), channel_id=1, source_target_pairs={{0,8},{2,10},{4,12},{6,14},{8,0},{10,2},{12,4},{14,6},{16,24},{18,... | collective-permute-start | bytes 1110824 | tf_op jit(solution)/shard_map/ppermute | solution.py:78
  99.5 17.2 %collective-permute-start.13 = (f16[2,152,609]{2,1,0:T(8,128)(2,1)}, f16[2,152,609]{2,1,0:T(8,128)(2,1)}, u32[]{:S(2)}, u32[]{:S(2)}) collective-permute-start(f16[2,152,609]{2,1,0:T(8,128)(2,1)} %select_convert_fusion.3), channel_id=1, source_target_pairs={{0,8},{2,10},{4,12},{6,14},{8,0},{10,2},{12,4},{14,6},{16,24},{18,... | collective-permute-start | bytes 1110824 | tf_op jit(solution)/shard_map/ppermute | solution.py:78
  107.6 37.0 %collective-permute-start.16 = (f16[2,152,609]{2,1,0:T(8,128)(2,1)}, f16[2,152,609]{2,1,0:T(8,128)(2,1)}, u32[]{:S(2)}, u32[]{:S(2)}) collective-permute-start(f16[2,152,609]{2,1,0:T(8,128)(2,1)} %select_convert_fusion.2), channel_id=1, source_target_pairs={{0,8},{2,10},{4,12},{6,14},{8,0},{10,2},{12,4},{14,6},{16,24},{18,... | collective-permute-start | bytes 1110824 | tf_op jit(solution)/shard_map/ppermute | solution.py:78
  113.9 21.4 %collective-permute-start.20 = (f16[152,609]{1,0:T(8,128)(2,1)}, f16[152,609]{1,0:T(8,128)(2,1)S(1)}, u32[]{:S(2)}, u32[]{:S(2)}) collective-permute-start(f16[152,609]{1,0:T(8,128)(2,1)} %select_convert_fusion.10), channel_id=1, source_target_pairs={{0,16},{2,18},{4,20},{6,22},{8,24},{10,26},{12,28},{14,30},{16,0},... | collective-permute-start | bytes 555416 | tf_op jit(solution)/shard_map/ppermute | solution.py:78
  122.7 17.4 %collective-permute-start.19 = (f16[152,609]{1,0:T(8,128)(2,1)}, f16[152,609]{1,0:T(8,128)(2,1)}, u32[]{:S(2)}, u32[]{:S(2)}) collective-permute-start(f16[152,609]{1,0:T(8,128)(2,1)} %select_convert_fusion.9), channel_id=1, source_target_pairs={{0,16},{2,18},{4,20},{6,22},{8,24},{10,26},{12,28},{14,30},{16,0},... | collective-permute-start | bytes 555416 | tf_op jit(solution)/shard_map/ppermute | solution.py:78
  133.5 11.1 %collective-permute-start.18 = (f16[152,609]{1,0:T(8,128)(2,1)}, f16[152,609]{1,0:T(8,128)(2,1)}, u32[]{:S(2)}, u32[]{:S(2)}) collective-permute-start(f16[152,609]{1,0:T(8,128)(2,1)} %select_convert_fusion.7), channel_id=1, source_target_pairs={{0,4},{2,6},{4,0},{6,2},{8,12},{10,14},{12,8},{14,10},{16,20},{18,... | collective-permute-start | bytes 555416 | tf_op jit(solution)/shard_map/ppermute | solution.py:78
  156.4 14.0 %collective-permute-start.22 = (f32[152,608]{1,0:T(8,128)}, f32[152,608]{1,0:T(8,128)}, u32[]{:S(2)}, u32[]{:S(2)}) collective-permute-start(f32[152,608]{1,0:T(8,128)} %multiply_add_fusion.6), channel_id=1, source_target_pairs={{0,1},{1,0},{2,3},{3,2},{4,5},{5,4},{6,7},{7,6},{8,9},{9,8},{10,11... | collective-permute-start | bytes 1109000 | tf_op jit(solution)/shard_map/ppermute | solution.py:91
  158.1 13.4 %collective-permute-start.21 = (f16[152,609]{1,0:T(8,128)(2,1)}, f16[152,609]{1,0:T(8,128)(2,1)S(1)}, u32[]{:S(2)}, u32[]{:S(2)}) collective-permute-start(f16[152,609]{1,0:T(8,128)(2,1)} %get-tuple-element.326), channel_id=1, source_target_pairs={{0,16},{2,18},{4,20},{6,22},{8,24},{10,26},{12,28},{14,30},{16,0},... | collective-permute-start | bytes 555416 | tf_op jit(solution)/shard_map/ppermute | solution.py:78
  179.9 55.3 %collective-permute-start.34 = (bf16[512,2432]{1,0:T(8,128)(2,1)}, bf16[512,2432]{1,0:T(8,128)(2,1)S(1)}, u32[]{:S(2)}, u32[]{:S(2)}) collective-permute-start(bf16[512,2432]{1,0:T(8,128)(2,1)} %refs_0_.1), channel_id=1, source_target_pairs={{0,1},{1,0},{2,3},{3,2},{4,5},{5,4},{6,7},{7,6},{8,9},{9,8},{10,11... | collective-permute-start | bytes 7471112 | tf_op jit(solution)/shard_map/ppermute | solution.py:91
  181.3 13.8 %collective-permute-start.29 = (bf16[2,2,152,512]{3,2,1,0:T(8,128)(2,1)}, bf16[2,2,152,512]{3,2,1,0:T(8,128)(2,1)S(1)}, u32[]{:S(2)}, u32[]{:S(2)}) collective-permute-start(bf16[2,2,152,512]{3,2,1,0:T(8,128)(2,1)} %collective-permute-done.9), channel_id=1, source_target_pairs={{0,2},{2,0},{4,6},{6,4},{8,10},{10,8},{12,14},{14,12},{16,18},{18,... | collective-permute-start | bytes 1867784 | tf_op jit(solution)/shard_map/ppermute | solution.py:78
  181.3 13.8 %collective-permute-start.28 = (bf16[2,2,152,512]{3,2,1,0:T(8,128)(2,1)}, bf16[2,2,152,512]{3,2,1,0:T(8,128)(2,1)S(1)}, u32[]{:S(2)}, u32[]{:S(2)}) collective-permute-start(bf16[2,2,152,512]{3,2,1,0:T(8,128)(2,1)} %collective-permute-done.12), channel_id=1, source_target_pairs={{0,2},{2,0},{4,6},{6,4},{8,10},{10,8},{12,14},{14,12},{16,18},{18,... | collective-permute-start | bytes 1867784 | tf_op jit(solution)/shard_map/ppermute | solution.py:78
  199.3 11.4 %collective-permute-start.31 = (bf16[2,152,608]{2,1,0:T(8,128)(2,1)S(1)}, bf16[2,152,608]{2,1,0:T(8,128)(2,1)S(1)}, u32[]{:S(2)}, u32[]{:S(2)}) collective-permute-start(bf16[2,152,608]{2,1,0:T(8,128)(2,1)S(1)} %get-tuple-element.274), channel_id=1, source_target_pairs={{0,8},{2,10},{4,12},{6,14},{8,0},{10,2},{12,4},{14,6},{16,24},{18,... | collective-permute-start | bytes 1109000 | tf_op jit(solution)/shard_map/ppermute | solution.py:78
  200.8 20.9 %collective-permute-start.33 = (bf16[2,152,608]{2,1,0:T(8,128)(2,1)S(1)}, bf16[2,152,608]{2,1,0:T(8,128)(2,1)S(1)}, u32[]{:S(2)}, u32[]{:S(2)}) collective-permute-start(bf16[2,152,608]{2,1,0:T(8,128)(2,1)S(1)} %get-tuple-element.274), channel_id=1, source_target_pairs={{0,24},{2,26},{4,28},{6,30},{8,16},{10,18},{12,20},{14,22},{16,8},... | collective-permute-start | bytes 1109000 | tf_op jit(solution)/shard_map/ppermute | solution.py:78
  203.3 18.9 %collective-permute-start.30 = (bf16[2,152,608]{2,1,0:T(8,128)(2,1)S(1)}, bf16[2,152,608]{2,1,0:T(8,128)(2,1)S(1)}, u32[]{:S(2)}, u32[]{:S(2)}) collective-permute-start(bf16[2,152,608]{2,1,0:T(8,128)(2,1)S(1)} %get-tuple-element.274), channel_id=1, source_target_pairs={{0,4},{2,6},{4,0},{6,2},{8,12},{10,14},{12,8},{14,10},{16,20},{18,... | collective-permute-start | bytes 1109000 | tf_op jit(solution)/shard_map/ppermute | solution.py:78
  210.7 11.5 %collective-permute-start.32 = (bf16[2,152,608]{2,1,0:T(8,128)(2,1)S(1)}, bf16[2,152,608]{2,1,0:T(8,128)(2,1)S(1)}, u32[]{:S(2)}, u32[]{:S(2)}) collective-permute-start(bf16[2,152,608]{2,1,0:T(8,128)(2,1)S(1)} %collective-permute-done.31), channel_id=1, source_target_pairs={{0,4},{2,6},{4,0},{6,2},{8,12},{10,14},{12,8},{14,10},{16,20},{18,... | collective-permute-start | bytes 1109000 | tf_op jit(solution)/shard_map/ppermute | solution.py:78
  210.8 23.8 %collective-permute-start.35 = (bf16[2,152,608]{2,1,0:T(8,128)(2,1)S(1)}, bf16[2,152,608]{2,1,0:T(8,128)(2,1)S(1)}, u32[]{:S(2)}, u32[]{:S(2)}) collective-permute-start(bf16[2,152,608]{2,1,0:T(8,128)(2,1)S(1)} %get-tuple-element.274), channel_id=1, source_target_pairs={{0,16},{2,18},{4,20},{6,22},{8,24},{10,26},{12,28},{14,30},{16,0},... | collective-permute-start | bytes 1109000 | tf_op jit(solution)/shard_map/ppermute | solution.py:78
  221.7 16.6 %collective-permute-start.37 = (bf16[2,152,608]{2,1,0:T(8,128)(2,1)S(1)}, bf16[2,152,608]{2,1,0:T(8,128)(2,1)S(1)}, u32[]{:S(2)}, u32[]{:S(2)}) collective-permute-start(bf16[2,152,608]{2,1,0:T(8,128)(2,1)S(1)} %collective-permute-done.33), channel_id=1, source_target_pairs={{0,4},{2,6},{4,0},{6,2},{8,12},{10,14},{12,8},{14,10},{16,20},{18,... | collective-permute-start | bytes 1109000 | tf_op jit(solution)/shard_map/ppermute | solution.py:78
  234.6 8.2 %collective-permute-start.36 = (bf16[2,152,608]{2,1,0:T(8,128)(2,1)S(1)}, bf16[2,152,608]{2,1,0:T(8,128)(2,1)S(1)}, u32[]{:S(2)}, u32[]{:S(2)}) collective-permute-start(bf16[2,152,608]{2,1,0:T(8,128)(2,1)S(1)} %collective-permute-done.35), channel_id=1, source_target_pairs={{0,4},{2,6},{4,0},{6,2},{8,12},{10,14},{12,8},{14,10},{16,20},{18,... | collective-permute-start | bytes 1109000 | tf_op jit(solution)/shard_map/ppermute | solution.py:78
  (32 other events, 246.8 us)

commit v9 on v8

--- a/solution.py
+++ b/solution.py
@@ -16,7 +16,7 @@
 SECOND_CORRECTION = 0.0952078529183
 
 OUTER = 4
-HALF_BITS = 15.0
+HALF_LIMIT = 60000.0
 TILE = 256
 LANES = 128
 
@@ -122,13 +122,24 @@
         lead = (2, inner) if by_planes else (inner, OUTER)
 
         def kernel(cot_ref, *refs):
-            out_refs, wide_ref = refs[:count], refs[count]
+            out_refs, (top_ref, wide_ref) = refs[:count], refs[count:]
             eye = identity(TILE)
             for start in range(0, D, TILE):
                 size = min(TILE, D - start)
                 wide_ref[start : start + size, :] = dot(
                     eye[:size, :size], cot_ref[:, start : start + size], NT
                 )
+            top = jnp.max(jnp.abs(wide_ref[...]).reshape(D // 8, 8, step), axis=0)
+            top = jnp.broadcast_to(jnp.max(top), (8, LANES))
+
+            @pl.when(pl.program_id(0) == 0)
+            def _():
+                top_ref[...] = top
+
+            @pl.when(pl.program_id(0) > 0)
+            def _():
+                top_ref[...] = jnp.maximum(top_ref[...], top)
+
             for p in range(n_dp):
                 k, i, other = relative(p)
                 block = wide_ref[p * width : (p + 1) * width, :].astype(jnp.bfloat16)
@@ -142,35 +153,56 @@
                     def _(n=n, at=at, block=block):
                         out_refs[n][at] = block
 
-        return call(
+        *outs, top = call(
             kernel,
-            [array((*lead, width, r), jnp.bfloat16)] * count,
+            [array((*lead, width, r), jnp.bfloat16)] * count + [array((8, LANES), jnp.float32)],
             cot,
             grid=(r // step,),
             in_specs=[pl.BlockSpec((step, D), lambda s: (s, 0))],
             out_specs=[
                 pl.BlockSpec((*lead, width, step), lambda s: (*(0 for _ in lead), 0, s))
-            ] * count,
+            ] * count
+            + [pl.BlockSpec((8, LANES), lambda s: (0, 0))],
             scratch_shapes=[pltpu.VMEM((D, step), jnp.float32)],
         )
-
-    def prepare(net, act, scales, r, together):
+        return outs, top
+
+    def prepare_fake(act, scales, r):
         f = act.shape[0]
-        lead = (n_tensor,) if together else (1,)
-        count = 1 if together else n_tensor
-
-        def kernel(scale_ref, act_ref, *out_refs):
+
+        def kernel(scale_ref, act_ref, top_ref, *out_refs):
+            most = jnp.max(jnp.abs(act_ref[...].astype(jnp.float32)))
+            top_ref[...] = jnp.full((8, LANES), most * scale_ref[1])
+            for j, out_ref in enumerate(out_refs):
+                part = act_ref[:, pl.ds(first_row(j, r), r)].astype(jnp.float32)
+                out_ref[0] = (part * scale_ref[1]).astype(jnp.bfloat16)
+
+        return call(
+            kernel,
+            [array((8, LANES), jnp.float32)] + [array((1, f, r), jnp.bfloat16)] * n_tensor,
+            scales, act,
+            in_specs=[SMEM, VMEM], out_specs=[VMEM] * (1 + n_tensor),
+        )
+
+    def prepare_student(act, top_s, top_f, top_act_f, scales, r):
+        f = act.shape[0]
+
+        def kernel(scale_ref, act_ref, top_s_ref, top_f_ref, top_act_f_ref, top_ref, out_ref):
+            most = jnp.max(jnp.abs(act_ref[...].astype(jnp.float32)))
+            most = jnp.full((8, LANES), most * scale_ref[0])
+            rows = lax.broadcasted_iota(jnp.int32, (8, LANES), 0)
+            tops = jnp.where(rows == 0, top_s_ref[...], most)
+            tops = jnp.where(rows == 2, top_f_ref[...], tops)
+            top_ref[...] = jnp.where(rows == 3, top_act_f_ref[...], tops)
             for j in range(n_tensor):
                 part = act_ref[:, pl.ds(first_row(j, r), r)].astype(jnp.float32)
-                part = (part * scale_ref[net]).astype(jnp.bfloat16)
-                if together:
-                    out_refs[0][j] = part
-                else:
-                    out_refs[j][0] = part
+                out_ref[j] = (part * scale_ref[0]).astype(jnp.bfloat16)
 
         return call(
-            kernel, [array((*lead, f, r), jnp.bfloat16)] * count, scales, act,
-            in_specs=[SMEM, VMEM], out_specs=[VMEM] * count,
+            kernel,
+            [array((8, LANES), jnp.float32), array((n_tensor, f, r), jnp.bfloat16)],
+            scales, act, top_s, top_f, top_act_f,
+            in_specs=[SMEM] + [VMEM] * 4, out_specs=[VMEM] * 2,
         )
 
     def multiply(pieces, scaled, places):
@@ -181,9 +213,7 @@
         count = len(pieces)
 
         def kernel(*refs):
-            piece_refs, scaled_refs = refs[:count], refs[count:-2]
-            out_ref, power_ref = refs[-2:]
-            most = jnp.zeros((8, f), jnp.float32)
+            piece_refs, scaled_refs, out_ref = refs[:count], refs[count:-1], refs[-1]
             for start in range(0, rows, step):
                 part = slice(start, start + step)
                 total = None
@@ -191,17 +221,12 @@
                     term = dot(piece_ref[part], scaled_refs[n][j], NT)
                     total = term if total is None else total + term
                 out_ref[part] = total
-                top = jnp.max(jnp.abs(total).reshape(step // 8, 8, f), axis=0)
-                most = jnp.maximum(most, top)
-            most = jnp.full((8, LANES), jnp.maximum(jnp.max(most), 1e-30))
-            power_ref[...] = jnp.floor(jnp.log2(most)) + 2.0
-
-        out, power = call(
-            kernel, [array((rows, f), jnp.float32), array((8, LANES), jnp.float32)],
-            *pieces, *scaled,
-            in_specs=[VMEM] * (count + len(scaled)), out_specs=[VMEM] * 2,
-        )
-        return out.reshape(*lead, f), power[0, 0]
+
+        out = call(
+            kernel, array((rows, f), jnp.float32), *pieces, *scaled,
+            in_specs=[VMEM] * (count + len(scaled)), out_specs=VMEM,
+        )
+        return out.reshape(*lead, f)
 
     def norms(total_s, total_f):
         def kernel(s_ref, f_ref, out_ref):
@@ -215,7 +240,7 @@
         )
 
     def update(squares, totals, states):
-        shape = states[0].shape
+        shape = totals[0].shape
 
         def kernel(squares_ref, *refs):
             total_refs, state_refs, (own_ref, *out_refs) = refs[:2], refs[2:8], refs[8:]
@@ -343,26 +368,26 @@
         def reduced(combine, value, got):
             return step(lambda *values: functools.reduce(combine, values), value, *got)
 
-        def hops(value, combine):
-            distance = 1
-            while distance < n_dp:
-                perm = [(p, p ^ distance) for p in range(n_dp)]
-                got = lax.ppermute(value, "dp", perm)
-                yield
-                value = step(combine, value, got)
-                distance *= 2
+        def hops(value, combine, *axes):
+            for axis in axes:
+                distance = 1
+                while distance < mesh.shape[axis]:
+                    perm = [(p, p ^ distance) for p in range(mesh.shape[axis])]
+                    got = lax.ppermute(value, axis, perm)
+                    yield
+                    value = step(combine, value, got)
+                    distance *= 2
             yield value
 
         scales = step(
             lambda steps: 1.0 / (0.1 + steps.astype(jnp.float32) / 1000.0), timesteps[0, :, 0]
         )
-        scaled_own, *sent = step(lambda act: prepare(1, act, scales, r, False), act_fake)
+        top_act, scaled_own, *sent = step(lambda act: prepare_fake(act, scales, r), act_fake)
         acts = [from_tensor(value, -j) for j, value in enumerate(sent, 1)]
-        scaled_fake = [[value, to_core(value)] for value in (scaled_own, *acts)]
-        fake_blocks = step(lambda cot: turn(cot, False), cot_fake)
+        scaled_fake = [[scaled_own, to_core(scaled_own)]]
+        fake_blocks, top_fake = step(lambda cot: turn(cot, False), cot_fake)
         mate_blocks = to_core(fake_blocks[1])
-        (scaled_student,) = step(lambda act: prepare(0, act, scales, r, True), act_student)
-        planes = step(lambda cot: turn(cot, True), cot_student)
+        planes, top_student = step(lambda cot: turn(cot, True), cot_student)
 
         same, diagonal = [], []
 
@@ -370,56 +395,80 @@
             same.append([from_tensor(own, j) for j in range(1, n_tensor)])
             diagonal.append([from_diagonal(other, j) for j in range(1, n_tensor)])
 
+        tops, scaled_student = step(
+            lambda *values: prepare_student(*values, scales, r),
+            act_student, top_student, top_fake, top_act,
+        )
+        tops = hops(tops, jnp.maximum, "tensor", "dp")
+        next(tops)
         send_planes(0, planes[0], planes[1])
-
-        def shrink(value, power):
-            scaled = value * jnp.exp2(HALF_BITS - power)
-            width_more = [(0, 0)] * (value.ndim - 1) + [(0, 1)]
-            lanes = lax.broadcasted_iota(jnp.int32, (*value.shape[:-1], f + 1), value.ndim - 1)
-            return jnp.where(lanes == f, power, jnp.pad(scaled, width_more)).astype(jnp.float16)
-
-        def widen(value):
-            power = value.reshape(-1)[f].astype(jnp.float32)
-            return value[..., :f].astype(jnp.float32) * jnp.exp2(power - HALF_BITS), power
-
-        def add(total, power, values):
+        parts_fake = []
+
+        def multiply_fake(j):
+            parts_fake.append(
+                step(
+                    lambda a, b, c, d: multiply([a, b], [c, d], [(0, 0), (1, 0)]),
+                    fake_blocks[0], mate_blocks, *scaled_fake[j],
+                )
+            )
+
+        multiply_fake(0)
+        acts = step(lambda *values: values, *acts)
+        scaled_fake += [[act, to_core(act)] for act in acts]
+        next(tops)
+        next(tops)
+        for j in range(1, n_tensor):
+            multiply_fake(j)
+        while (final := next(tops)) is None:
+            pass
+
+        def factors(tops):
+            bounds = tops[0:3:2, 0] * tops[1:4:2, 0]
+            bounds = jnp.maximum(bounds, 1e-30) * (1.01 * count * n_dp / HALF_LIMIT)
+            return bounds, 1.0 / bounds
+
+        grow, fit = step(factors, final)
+
+        def shrink(value, net):
+            return (value * fit[net]).astype(jnp.float16)
+
+        def widen(value, net):
+            return value.astype(jnp.float32) * grow[net]
+
+        def add_widened(total, values, net):
             for value in values:
-                value, other = widen(value)
-                total, power = total + value, jnp.maximum(power, other) + 1.0
-            return total, power
+                total = total + widen(value, net)
+            return total
 
         fake_own, fake_got = {}, {}
 
         def fake_middle(j):
-            def work(both, power):
-                return [shrink(both[i], power) for i in range(1, inner)], (both[0], power)
-
-            both = step(
-                lambda a, b, c, d: multiply([a, b], [c, d], [(0, 0), (1, 0)]),
-                fake_blocks[0], mate_blocks, *scaled_fake[j],
-            )
-            sent, fake_own[j] = step(work, *both)
+            def work(both):
+                sent = [shrink(both[i], 1) for i in range(1, inner)]
+                return sent, both[0]
+
+            sent, fake_own[j] = step(work, parts_fake[j])
             fake_got[j] = [to_middle(value, i) for i, value in enumerate(sent, 1)]
 
         def fake_near(j):
-            def work(own, power, *got):
-                own, power = add(own, power, got)
-                return shrink(own[1::2], power), (own[0::2], power)
-
-            sent, fake_own[j] = step(work, *fake_own[j], *fake_got[j])
+            def work(own, *got):
+                own = add_widened(own, got, 1)
+                return shrink(own[1::2], 1), own[0::2]
+
+            sent, fake_own[j] = step(work, fake_own[j], *fake_got[j])
             fake_got[j] = [to_plane(sent, 1)]
 
         def fake_far(j):
-            def work(own, power, *got):
-                own, power = add(own, power, got)
-                return shrink(own[1], power), (own[0], power)
-
-            sent, fake_own[j] = step(work, *fake_own[j], *fake_got[j])
+            def work(own, *got):
+                own = add_widened(own, got, 1)
+                return shrink(own[1], 1), own[0]
+
+            sent, fake_own[j] = step(work, fake_own[j], *fake_got[j])
             fake_got[j] = [to_plane(sent, 2)]
 
         def fake_total(j):
             return step(
-                lambda own, power, *got: add(own, power, got)[0], *fake_own[j], *fake_got[j]
+                lambda own, *got: add_widened(own, got, 1), fake_own[j], *fake_got[j]
             )
 
         mate_student = to_core(scaled_student)
@@ -455,25 +504,27 @@
         back_fake = back(None, 1, [cot_fake], 0, 0, r)
         both = multiply_student(0)
 
-        def first_middle(both, power):
-            return [shrink(both[:, i], power) for i in range(1, inner)], both[:, 0], power
-
-        sent, own, power = step(first_middle, *both)
+        def first_middle(both):
+            return [shrink(both[:, i], 0) for i in range(1, inner)], both[:, 0]
+
+        sent, own = step(first_middle, both)
         got = [to_middle(value, i) for i, value in enumerate(sent, 1)]
         for j in range(n_tensor):
             fake_near(j)
-        near = to_plane(
-            step(lambda own, power, *got: shrink(*add(own, power, got)), own, power, *got), 1
-        )
+
+        def first_planes(own, *got):
+            return shrink(add_widened(own, got, 0), 0)
+
+        near = to_plane(step(first_planes, own, *got), 1)
         for j in range(n_tensor):
             fake_far(j)
         both = multiply_student(1)
 
-        def second_middle(both, power):
-            sent = [[shrink(both[n, i], power) for i in range(1, inner)] for n in range(2)]
-            return sent, both[0, 0], both[1, 0], power
-
-        sent, own_far, own, power = step(second_middle, *both)
+        def second_middle(both):
+            sent = [[shrink(both[n, i], 0) for i in range(1, inner)] for n in range(2)]
+            return sent, both[0, 0], both[1, 0]
+
+        sent, own_far, own = step(second_middle, both)
         got_far, got = (
             [to_middle(value, i) for i, value in enumerate(values, 1)] for values in sent
         )
@@ -481,16 +532,17 @@
         fake_others = [fake_total(j) for j in range(1, n_tensor)]
         others_got = [from_tensor(value, j) for j, value in enumerate(fake_others, 1)]
 
-        def far_plane(own, power, near, *got):
-            return shrink(*add(own, power, [near[1], *got]))
-
-        far = to_plane(step(far_plane, own_far, power, near, *got_far), 2)
+        def far_plane(own, near, *got):
+            return shrink(add_widened(own, (near[1], *got), 0), 0)
+
+        far = to_plane(step(far_plane, own_far, near, *got_far), 2)
         total_student = step(
-            lambda own, power, near, *got: add(own, power, [near[0], *got])[0],
-            own, power, near, *got,
+            lambda own, near, *got: add_widened(own, (near[0], *got), 0), own, near, *got
         )
         total_fake = reduced(jnp.add, fake_mine, others_got)
-        total_student = step(lambda own, got: own + widen(got)[0], total_student, far)
+        total_student = step(
+            lambda own, got: add_widened(own, (got,), 0), total_student, far
+        )
         squares = step(norms, total_student, total_fake)
         squares = reduced(
             jnp.add, squares, [from_tensor(squares, j) for j in range(1, n_tensor)]
@@ -499,11 +551,7 @@
         rows = step(lambda cot: cot, cot_fake)
         raw = [from_tensor(rows, j) for j in range(1, n_tensor)]
 
-        hidden = step(lambda *values: values, *[value for group in diagonal for value in group])
-        mate_others = [to_core(value) for value in hidden]
-        *_, squares = hops(squares, jnp.add)
-        squares, *mate_others = step(lambda *values: values, squares, *mate_others)
-        mate_others = [mate_others[: n_tensor - 1], mate_others[n_tensor - 1 :]]
+        *_, squares = hops(squares, jnp.add, "dp")
         states = (
             master_student, first_student, second_student, master_fake, first_fake, second_fake,
         )
@@ -521,14 +569,20 @@
         planes_got = {k: to_plane(own, k) for k in (1, 3, 2)}
         spread_middle(1, step(lambda value: value, planes_got[1]))
         spread_middle(3, step(lambda value: value, planes_got[3]))
+        early = [value for k in (0, 1, 3) for value in mine[k]]
+        early = step(lambda *values: values, *early)
+        mine = {k: list(early[n * inner : (n + 1) * inner]) for n, k in enumerate((0, 1, 3))}
+        spread_middle(2, step(lambda value: value, planes_got[2]))
         first_half = step(lambda *values: jnp.stack(values), *mine[0], *mine[1])
         theirs = [to_core(first_half)]
+        hidden = step(lambda *values: values, *[value for group in diagonal for value in group])
+        mate_others = [to_core(value) for value in hidden]
+        mate_others = [mate_others[: n_tensor - 1], mate_others[n_tensor - 1 :]]
         for j in range(1, n_tensor):
             pieces = [
                 piece for g in range(2) for piece in (same[g][j - 1], mate_others[g][j - 1])
             ]
             back_student = back(back_student, 0, pieces, j, 0, r)
-        spread_middle(2, step(lambda value: value, planes_got[2]))
         for j in range(1, n_tensor):
             back_fake = back(back_fake, 1, [raw[j - 1]], j, 0, r)
         second_half = step(lambda *values: jnp.stack(values), *mine[2], *mine[3])

time: 254 us -> 211 us (0.83)
  local copies, waits for them, and re-layouts: 49.3 us -> 6.35 us
  waiting for transfers between devices: 56.2 us -> 90.7 us
  other arithmetic: 44.5 us -> 17.2 us
  between operations: 15.2 us -> 1.32 us
  starting transfers between devices: 42.8 us -> 52 us
    ppermute x28, waiting for transfers between devices: 30.8 us -> 54.3 us  [move_dp(): return lax.ppermute(value, 'dp', perm)]
    reshape x10 -> x0, local copies, waits for them, and re-layouts: 19 us -> none  [widen(): power = value.reshape(-1)[f].astype(jnp.float32)]
    slice x18 -> x4, local copies, waits for them, and re-layouts: 16.6 us -> 1.15 us  [the longest x1 0.59 us: shrink(): return (value * fit[net]).astype(jnp.float16)]
    squeeze x5 -> x4, other arithmetic: 10.6 us -> 3.62 us  [the longest x2 2.23 us: work(): return (sent, both[0])]
    ppermute x4 -> x9, starting transfers between devices: 4.69 us -> 11.6 us  [hops(): got = lax.ppermute(value, axis, perm)]
    convert_element_type x10 -> x5, other arithmetic: 11.7 us -> 5.07 us  [shrink(): return (value * fit[net]).astype(jnp.float16)]
    add x8, other arithmetic: 12.8 us -> 6.27 us  [add_widened(): total = total + widen(value, net)]
    unnamed x48 -> x36, local copies, waits for them, and re-layouts: 11.3 us -> 5.14 us
  transfers between devices with their start and end apart: 40 -> 45, of which waited for: 13 -> 26; matrix products, arithmetic and copies ran while one was open for 27% -> 8% of each run, Pallas kernels for 14% -> 16%
where the time goes in v9:
time: 211 us; the launch traced here: 210 us
  waiting for transfers between devices  90.7 us (43%)
  starting transfers between devices  52 us (25%)
  Pallas kernels  42.9 us (20%)
  other arithmetic  17.2 us (8%)
  local copies, waits for them, and re-layouts  6.35 us (3%)
    ppermute x28, waiting for transfers between devices, move_dp(): return lax.ppermute(value, 'dp', perm)  54.3 us
    pallas_call x15, Pallas kernels, call(): pl.pallas_call(kernel, out_shape=out_shape, compiler_params=pltpu.Compile...  42.9 us
    ppermute x28, starting transfers between devices, move_dp(): return lax.ppermute(value, 'dp', perm)  27.1 us
    ppermute x6, waiting for transfers between devices, from_tensor(): return lax.ppermute(value, 'tensor', perm)  21 us
    ppermute x9, waiting for transfers between devices, hops(): got = lax.ppermute(value, axis, perm)  14 us
    ppermute x9, starting transfers between devices, hops(): got = lax.ppermute(value, axis, perm)  11.6 us
    ppermute x6, starting transfers between devices, from_tensor(): return lax.ppermute(value, 'tensor', perm)  9.64 us
    add x8, other arithmetic, add_widened(): total = total + widen(value, net)  6.27 us
  transfers between devices with their start and end apart: 45, of which 26 were waited for; matrix products, arithmetic and copies ran while one was open for 8% of the time, Pallas kernels for 16%

profile of v9, /device:TPU:0, one launch (start us, length us, event | category | flops | bytes accessed | tf_op | source)
XLA Modules:
  0.0 210.5 jit_solution(18189923043595692398)
XLA Ops:
  5.6 2.2 %shard_map.205 = (bf16[2,4,152,512]{3,2,1,0:T(8,128)(2,1)S(1)}, bf16[2,4,152,512]{3,2,1,0:T(8,128)(2,1)S(1)}, f32[8,128]{1,0:T(8,128)S(1)}) custom-call(bf16[512,2432]{1,0:T(8,128)(2,1)S(1)} %copy-done.6), custom_call_target="tpu_custom_call" | custom-call | tf_op jit(solution)/shard_map/pallas_call | solution.py:56
  8.5 2.9 %collective-permute-start.6 = (bf16[1,608,512]{2,1,0:T(8,128)(2,1)S(1)}, bf16[1,608,512]{2,1,0:T(8,128)(2,1)S(1)}, u32[]{:S(2)}, u32[]{:S(2)}) collective-permute-start(bf16[1,608,512]{2,1,0:T(8,128)(2,1)S(1)} %get-tuple-element.176), channel_id=1, source_target_pairs={{0,1},{1,0},{2,3},{3,2},{4,5},{5,4},{6,7},{7,6},{8,9},{9,8},{10,11... | collective-permute-start | bytes 1867784 | tf_op jit(solution)/shard_map/ppermute | solution.py:91
  11.4 3.4 %shard_map.206 = (bf16[2,2,152,512]{3,2,1,0:T(8,128)(2,1)}, bf16[2,2,152,512]{3,2,1,0:T(8,128)(2,1)}, bf16[2,2,152,512]{3,2,1,0:T(8,128)(2,1)S(1)}, bf16[2,2,152,512]{3,2,1,0:T(8,128)(2,1)}, f32[8,128]{1,0:T(8,128)S(1)}) custom-call(bf16[512,2432]{1,0:T(8,128)(2,1)S(1)} %copy-done.4), custom_call_target="tpu_custom_call" | custom-call | tf_op jit(solution)/shard_map/pallas_call | solution.py:56
  14.7 2.2 %shard_map.207 = (f32[8,128]{1,0:T(8,128)S(1)}, bf16[2,608,512]{2,1,0:T(8,128)(2,1)}) custom-call(f32[2]{0:T(128)S(1)} %divide_bitcast_fusion.scale_ref, bf16[608,1024]{1,0:T(8,128)(2,1)S(1)} %copy-done.9, f32[8,128]{1,0:T(8,128)S(1)} %get-tuple-element.171.top_s_ref, f32[8,128]{1,0:T(8,128)S(1)} %get-tuple-element.172.top_f_ref, ...), custom_call_target="tpu_custom_call" | custom-call | tf_op jit(solution)/shard_map/pallas_call | solution.py:56
  17.0 2.1 %shard_map.208 = f32[1216,608]{1,0:T(8,128)S(1)} custom-call(bf16[1216,512]{1,0:T(8,128)(2,1)S(1)} %bitcast.97, bf16[1216,512]{1,0:T(8,128)(2,1)S(1)} %bitcast.99, bf16[1,608,512]{2,1,0:T(8,128)(2,1)S(1)} %get-tuple-element.181.refs_2_, bf16[1,608,512]{2,1,0:T(8,128)(2,1)S(1)} %collective-permute-done.7.refs_3_), custom_call_target="tpu_custom_call" | custom-call | tf_op jit(solution)/shard_map/pallas_call | solution.py:56
  19.1 6.6 %collective-permute-done.6.refs_2_ = bf16[1,608,512]{2,1,0:T(8,128)(2,1)S(1)} collective-permute-done((bf16[1,608,512]{2,1,0:T(8,128)(2,1)S(1)}, bf16[1,608,512]{2,1,0:T(8,128)(2,1)S(1)}, u32[]{:S(2)}, u32[]{:S(2)}) %collective-permute-start.6) | collective-permute-done | bytes 622624 | tf_op jit(solution)/shard_map/ppermute | solution.py:91
  32.7 2.1 %shard_map.209 = f32[1216,608]{1,0:T(8,128)S(1)} custom-call(bf16[1216,512]{1,0:T(8,128)(2,1)S(1)} %bitcast.98, bf16[1216,512]{1,0:T(8,128)(2,1)S(1)} %bitcast.100, bf16[1,608,512]{2,1,0:T(8,128)(2,1)S(1)} %collective-permute-done.6.refs_2_, bf16[1,608,512]{2,1,0:T(8,128)(2,1)S(1)} %collective-permute-done.8.refs_3_), custom_call_target="tpu_custom_call" | custom-call | tf_op jit(solution)/shard_map/pallas_call | solution.py:56
  40.1 2.6 %collective-permute-start.13 = (f32[8,128]{1,0:T(8,128)S(1)}, f32[8,128]{1,0:T(8,128)S(1)}, u32[]{:S(2)}, u32[]{:S(2)}) collective-permute-start(f32[8,128]{1,0:T(8,128)S(1)} %max.22), channel_id=1, source_target_pairs={{0,16},{2,18},{4,20},{6,22},{8,24},{10,26},{12,28},{14,30},{16,0},... | collective-permute-start | bytes 12296 | tf_op jit(solution)/shard_map/ppermute | solution.py:376
  49.7 3.2 %shard_map.210.refs_4_ = bf16[608,1024]{1,0:T(8,128)(2,1)} custom-call(f32[2]{0:T(128)S(1)} %divide_bitcast_fusion.scale_ref, bf16[608,2432]{1,0:T(8,128)(2,1)S(1)} %copy-done.2, bf16[512,2432]{1,0:T(8,128)(2,1)S(1)} %copy-done.5), custom_call_target="tpu_custom_call" | custom-call | tf_op jit(solution)/shard_map/pallas_call | solution.py:56
  54.5 3.2 %shard_map.211.refs_1_ = bf16[608,1024]{1,0:T(8,128)(2,1)} custom-call(f32[2]{0:T(128)S(1)} %divide_bitcast_fusion.scale_ref, bf16[608,2432]{1,0:T(8,128)(2,1)S(1)} %copy-done.3, bf16[512,2432]{1,0:T(8,128)(2,1)S(1)} %copy-done.7), custom_call_target="tpu_custom_call" | custom-call | tf_op jit(solution)/shard_map/pallas_call | solution.py:56
  59.0 2.1 collective-permute-start.14
  61.1 12.2 %collective-permute-done.refs_0_ = bf16[2,2,152,512]{3,2,1,0:T(8,128)(2,1)} collective-permute-done((bf16[2,2,152,512]{3,2,1,0:T(8,128)(2,1)}, bf16[2,2,152,512]{3,2,1,0:T(8,128)(2,1)}, u32[]{:S(2)}, u32[]{:S(2)}) %collective-permute-start) | collective-permute-done | bytes 622624 | tf_op jit(solution)/shard_map/ppermute | solution.py:91
  73.3 4.5 %shard_map.212 = f32[608,608]{1,0:T(8,128)S(1)} custom-call(bf16[608,512]{1,0:T(8,128)(2,1)} %bitcast.12.refs_0_, bf16[608,512]{1,0:T(8,128)(2,1)} %bitcast.13.refs_1_, bf16[608,512]{1,0:T(8,128)(2,1)} %bitcast.14.refs_2_, bf16[608,512]{1,0:T(8,128)(2,1)} %bitcast.15.refs_3_, bf16[2,608,512]{2,1,0:T(8,128)(2,1)} %get-tuple-element.229.refs_4_, ...), custom_call_target="tpu_custom_call" | custom-call | tf_op jit(solution)/shard_map/pallas_call | solution.py:56
  86.8 4.7 %collective-permute-done.20 = f16[2,152,608]{2,1,0:T(8,128)(2,1)S(1)} collective-permute-done((f16[2,152,608]{2,1,0:T(8,128)(2,1)S(1)}, f16[2,152,608]{2,1,0:T(8,128)(2,1)S(1)}, u32[]{:S(2)}, u32[]{:S(2)}) %collective-permute-start.20) | collective-permute-done | bytes 369696 | tf_op jit(solution)/shard_map/ppermute | solution.py:78
  96.1 2.4 %collective-permute-start.25 = (f16[152,608]{1,0:T(8,128)(2,1)S(1)}, f16[152,608]{1,0:T(8,128)(2,1)S(1)}, u32[]{:S(2)}, u32[]{:S(2)}) collective-permute-start(f16[152,608]{1,0:T(8,128)(2,1)S(1)} %get-tuple-element.323), channel_id=1, source_target_pairs={{0,16},{2,18},{4,20},{6,22},{8,24},{10,26},{12,28},{14,30},{16,0},... | collective-permute-start | bytes 554504 | tf_op jit(solution)/shard_map/ppermute | solution.py:78
  98.5 9.5 %collective-permute-done.18 = f16[2,152,608]{2,1,0:T(8,128)(2,1)S(1)} collective-permute-done((f16[2,152,608]{2,1,0:T(8,128)(2,1)S(1)}, f16[2,152,608]{2,1,0:T(8,128)(2,1)S(1)}, u32[]{:S(2)}, u32[]{:S(2)}) %collective-permute-start.18) | collective-permute-done | bytes 369696 | tf_op jit(solution)/shard_map/ppermute | solution.py:78
  109.5 4.0 %shard_map.213 = f32[608,608]{1,0:T(8,128)S(1)} custom-call(bf16[608,512]{1,0:T(8,128)(2,1)S(1)} %bitcast.103, bf16[608,512]{1,0:T(8,128)(2,1)} %bitcast.25.refs_1_, bf16[608,512]{1,0:T(8,128)(2,1)S(1)} %bitcast.101, bf16[608,512]{1,0:T(8,128)(2,1)S(1)} %bitcast.102, bf16[2,608,512]{2,1,0:T(8,128)(2,1)} %get-tuple-element.229.refs_4_, ...), custom_call_target="tpu_custom_call" | custom-call | tf_op jit(solution)/shard_map/pallas_call | solution.py:56
  123.5 3.0 %collective-permute-start.26 = (f16[152,608]{1,0:T(8,128)(2,1)S(1)}, f16[152,608]{1,0:T(8,128)(2,1)S(1)}, u32[]{:S(2)}, u32[]{:S(2)}) collective-permute-start(f16[152,608]{1,0:T(8,128)(2,1)S(1)} %fusion.12), channel_id=1, source_target_pairs={{0,16},{2,18},{4,20},{6,22},{8,24},{10,26},{12,28},{14,30},{16,0},... | collective-permute-start | bytes 554504 | tf_op jit(solution)/shard_map/ppermute | solution.py:78
  127.5 4.6 %collective-permute-done.26 = f16[152,608]{1,0:T(8,128)(2,1)S(1)} collective-permute-done((f16[152,608]{1,0:T(8,128)(2,1)S(1)}, f16[152,608]{1,0:T(8,128)(2,1)S(1)}, u32[]{:S(2)}, u32[]{:S(2)}) %collective-permute-start.26) | collective-permute-done | bytes 184864 | tf_op jit(solution)/shard_map/ppermute | solution.py:78
  134.7 2.2 %collective-permute-done.28 = f32[8,128]{1,0:T(8,128)S(1)} collective-permute-done((f32[8,128]{1,0:T(8,128)S(1)}, f32[8,128]{1,0:T(8,128)S(1)}, u32[]{:S(2)}, u32[]{:S(2)}) %collective-permute-start.28) | collective-permute-done | bytes 4128 | tf_op jit(solution)/shard_map/ppermute | solution.py:91
  143.6 3.1 %collective-permute-done.31 = f32[8,128]{1,0:T(8,128)S(1)} collective-permute-done((f32[8,128]{1,0:T(8,128)S(1)}, f32[8,128]{1,0:T(8,128)S(1)}, u32[]{:S(2)}, u32[]{:S(2)}) %collective-permute-start.31) | collective-permute-done | bytes 4128 | tf_op jit(solution)/shard_map/ppermute | solution.py:376
  148.7 2.6 %collective-permute-done.32 = f32[8,128]{1,0:T(8,128)S(1)} collective-permute-done((f32[8,128]{1,0:T(8,128)S(1)}, f32[8,128]{1,0:T(8,128)S(1)}, u32[]{:S(2)}, u32[]{:S(2)}) %collective-permute-start.32) | collective-permute-done | bytes 4128 | tf_op jit(solution)/shard_map/ppermute | solution.py:376
  151.3 2.1 shard_map.215
  154.5 2.4 %collective-permute-start.36 = (bf16[2,152,608]{2,1,0:T(8,128)(2,1)S(1)}, bf16[2,152,608]{2,1,0:T(8,128)(2,1)S(1)}, u32[]{:S(2)}, u32[]{:S(2)}) collective-permute-start(bf16[2,152,608]{2,1,0:T(8,128)(2,1)S(1)} %get-tuple-element.275), channel_id=1, source_target_pairs={{0,24},{2,26},{4,28},{6,30},{8,16},{10,18},{12,20},{14,22},{16,8},... | collective-permute-start | bytes 1109000 | tf_op jit(solution)/shard_map/ppermute | solution.py:78
  158.8 5.1 %collective-permute-done.34 = bf16[2,152,608]{2,1,0:T(8,128)(2,1)S(1)} collective-permute-done((bf16[2,152,608]{2,1,0:T(8,128)(2,1)S(1)}, bf16[2,152,608]{2,1,0:T(8,128)(2,1)S(1)}, u32[]{:S(2)}, u32[]{:S(2)}) %collective-permute-start.34) | collective-permute-done | bytes 369696 | tf_op jit(solution)/shard_map/ppermute | solution.py:78
  163.9 8.1 %collective-permute-done.36 = bf16[2,152,608]{2,1,0:T(8,128)(2,1)S(1)} collective-permute-done((bf16[2,152,608]{2,1,0:T(8,128)(2,1)S(1)}, bf16[2,152,608]{2,1,0:T(8,128)(2,1)S(1)}, u32[]{:S(2)}, u32[]{:S(2)}) %collective-permute-start.36) | collective-permute-done | bytes 369696 | tf_op jit(solution)/shard_map/ppermute | solution.py:78
  176.0 8.0 %collective-permute-done.37 = bf16[2,152,608]{2,1,0:T(8,128)(2,1)S(1)} collective-permute-done((bf16[2,152,608]{2,1,0:T(8,128)(2,1)S(1)}, bf16[2,152,608]{2,1,0:T(8,128)(2,1)S(1)}, u32[]{:S(2)}, u32[]{:S(2)}) %collective-permute-start.37) | collective-permute-done | bytes 369696 | tf_op jit(solution)/shard_map/ppermute | solution.py:78
  184.0 4.2 %collective-permute-done.35 = bf16[2,152,608]{2,1,0:T(8,128)(2,1)S(1)} collective-permute-done((bf16[2,152,608]{2,1,0:T(8,128)(2,1)S(1)}, bf16[2,152,608]{2,1,0:T(8,128)(2,1)S(1)}, u32[]{:S(2)}, u32[]{:S(2)}) %collective-permute-start.35) | collective-permute-done | bytes 369696 | tf_op jit(solution)/shard_map/ppermute | solution.py:78
  192.9 4.1 %shard_map.216 = bf16[608,1024]{1,0:T(8,128)(2,1)} custom-call(f32[2]{0:T(128)S(1)} %divide_bitcast_fusion.scale_ref, bf16[608,2432]{1,0:T(8,128)(2,1)S(1)} %copy-done.2, bf16[2,2,152,512]{3,2,1,0:T(8,128)(2,1)} %collective-permute-done.refs_0_, bf16[2,2,152,512]{3,2,1,0:T(8,128)(2,1)S(1)} %collective-permute-done.39.refs_1_, ...), custom_call_target="tpu_custom_call", output_to_operand_aliasing={{}: (6, {})} | custom-call | tf_op jit(solution)/shard_map/pallas_call | solution.py:56
  197.0 3.2 %shard_map.217 = bf16[608,1024]{1,0:T(8,128)(2,1)} custom-call(f32[2]{0:T(128)S(1)} %divide_bitcast_fusion.scale_ref, bf16[608,2432]{1,0:T(8,128)(2,1)S(1)} %copy-done.3, bf16[512,2432]{1,0:T(8,128)(2,1)S(1)} %collective-permute-done.41.refs_0_, bf16[608,1024]{1,0:T(8,128)(2,1)} %shard_map.211.refs_1_), custom_call_target="tpu_custom_call", output_to_operand_aliasing={{}: (3, {})} | custom-call | tf_op jit(solution)/shard_map/pallas_call | solution.py:56
  201.7 3.4 %collective-permute-done.44.refs_3_ = bf16[4,2,152,608]{3,2,1,0:T(8,128)(2,1)S(1)} collective-permute-done((bf16[4,2,152,608]{3,2,1,0:T(8,128)(2,1)S(1)}, bf16[4,2,152,608]{3,2,1,0:T(8,128)(2,1)S(1)}, u32[]{:S(2)}, u32[]{:S(2)}) %collective-permute-start.44) | collective-permute-done | bytes 1478688 | tf_op jit(solution)/shard_map/ppermute | solution.py:78
  205.1 5.2 %shard_map.218 = (bf16[608,2432]{1,0:T(8,128)(2,1)}, bf16[608,2432]{1,0:T(8,128)(2,1)}) custom-call(bf16[4,2,152,608]{3,2,1,0:T(8,128)(2,1)S(1)} %pad_maximum_fusion.refs_0_, bf16[4,2,152,608]{3,2,1,0:T(8,128)(2,1)S(1)} %pad_maximum_fusion.1.refs_1_, bf16[4,2,152,608]{3,2,1,0:T(8,128)(2,1)S(1)} %collective-permute-done.43.refs_2_, ...), custom_call_target="tpu_custom_call" | custom-call | tf_op jit(solution)/shard_map/pallas_call | solution.py:56
  (148 shorter events, 78.0 us)
Async XLA Ops:
  7.9 9.1 %collective-permute-start.5 = (bf16[2,4,152,512]{3,2,1,0:T(8,128)(2,1)S(1)}, bf16[2,4,152,512]{3,2,1,0:T(8,128)(2,1)S(1)}, u32[]{:S(2)}, u32[]{:S(2)}) collective-permute-start(bf16[2,4,152,512]{3,2,1,0:T(8,128)(2,1)S(1)} %get-tuple-element.175), channel_id=1, source_target_pairs={{0,2},{2,0},{4,6},{6,4},{8,10},{10,8},{12,14},{14,12},{16,18},{18,... | collective-permute-start | bytes 3735560 | tf_op jit(solution)/shard_map/ppermute | solution.py:78
  8.4 8.6 %collective-permute-start.7 = (bf16[1,608,512]{2,1,0:T(8,128)(2,1)S(1)}, bf16[1,608,512]{2,1,0:T(8,128)(2,1)S(1)}, u32[]{:S(2)}, u32[]{:S(2)}) collective-permute-start(bf16[1,608,512]{2,1,0:T(8,128)(2,1)S(1)} %get-tuple-element.181.refs_2_), channel_id=1, source_target_pairs={{0,2},{2,0},{4,6},{6,4},{8,10},{10,8},{12,14},{14,12},{16,18},{18,... | collective-permute-start | bytes 1867784 | tf_op jit(solution)/shard_map/ppermute | solution.py:78
  8.5 17.2 %collective-permute-start.6 = (bf16[1,608,512]{2,1,0:T(8,128)(2,1)S(1)}, bf16[1,608,512]{2,1,0:T(8,128)(2,1)S(1)}, u32[]{:S(2)}, u32[]{:S(2)}) collective-permute-start(bf16[1,608,512]{2,1,0:T(8,128)(2,1)S(1)} %get-tuple-element.176), channel_id=1, source_target_pairs={{0,1},{1,0},{2,3},{3,2},{4,5},{5,4},{6,7},{7,6},{8,9},{9,8},{10,11... | collective-permute-start | bytes 1867784 | tf_op jit(solution)/shard_map/ppermute | solution.py:91
  25.7 7.1 %collective-permute-start.8 = (bf16[1,608,512]{2,1,0:T(8,128)(2,1)S(1)}, bf16[1,608,512]{2,1,0:T(8,128)(2,1)S(1)}, u32[]{:S(2)}, u32[]{:S(2)}) collective-permute-start(bf16[1,608,512]{2,1,0:T(8,128)(2,1)S(1)} %collective-permute-done.6.refs_2_), channel_id=1, source_target_pairs={{0,2},{2,0},{4,6},{6,4},{8,10},{10,8},{12,14},{14,12},{16,18},{18,... | collective-permute-start | bytes 1867784 | tf_op jit(solution)/shard_map/ppermute | solution.py:78
  25.7 24.0 %collective-permute-start.2 = (bf16[2,608,512]{2,1,0:T(8,128)(2,1)}, bf16[2,608,512]{2,1,0:T(8,128)(2,1)}, u32[]{:S(2)}, u32[]{:S(2)}) collective-permute-start(bf16[2,608,512]{2,1,0:T(8,128)(2,1)} %get-tuple-element.229.refs_4_), channel_id=1, source_target_pairs={{0,2},{2,0},{4,6},{6,4},{8,10},{10,8},{12,14},{14,12},{16,18},{18,... | collective-permute-start | bytes 3735560 | tf_op jit(solution)/shard_map/ppermute | solution.py:78
  30.9 5.5 %collective-permute-start.11 = (f32[8,128]{1,0:T(8,128)S(1)}, f32[8,128]{1,0:T(8,128)S(1)}, u32[]{:S(2)}, u32[]{:S(2)}) collective-permute-start(f32[8,128]{1,0:T(8,128)S(1)} %max.20), channel_id=1, source_target_pairs={{0,4},{2,6},{4,0},{6,2},{8,12},{10,14},{12,8},{14,10},{16,20},{18,... | collective-permute-start | bytes 12296 | tf_op jit(solution)/shard_map/ppermute | solution.py:376
  40.1 4.7 %collective-permute-start.13 = (f32[8,128]{1,0:T(8,128)S(1)}, f32[8,128]{1,0:T(8,128)S(1)}, u32[]{:S(2)}, u32[]{:S(2)}) collective-permute-start(f32[8,128]{1,0:T(8,128)S(1)} %max.22), channel_id=1, source_target_pairs={{0,16},{2,18},{4,20},{6,22},{8,24},{10,26},{12,28},{14,30},{16,0},... | collective-permute-start | bytes 12296 | tf_op jit(solution)/shard_map/ppermute | solution.py:376
  42.7 16.3 %collective-permute-start.1 = (bf16[2,2,152,512]{3,2,1,0:T(8,128)(2,1)}, bf16[2,2,152,512]{3,2,1,0:T(8,128)(2,1)}, u32[]{:S(2)}, u32[]{:S(2)}) collective-permute-start(bf16[2,2,152,512]{3,2,1,0:T(8,128)(2,1)} %get-tuple-element.165), channel_id=1, source_target_pairs={{0,3},{1,2},{2,1},{3,0},{4,7},{5,6},{6,5},{7,4},{8,11},{9,10},{10,... | collective-permute-start | bytes 1867784 | tf_op jit(solution)/shard_map/ppermute | solution.py:100
  44.3 29.0 %collective-permute-start = (bf16[2,2,152,512]{3,2,1,0:T(8,128)(2,1)}, bf16[2,2,152,512]{3,2,1,0:T(8,128)(2,1)}, u32[]{:S(2)}, u32[]{:S(2)}) collective-permute-start(bf16[2,2,152,512]{3,2,1,0:T(8,128)(2,1)} %get-tuple-element.209), channel_id=1, source_target_pairs={{0,1},{1,0},{2,3},{3,2},{4,5},{5,4},{6,7},{7,6},{8,9},{9,8},{10,11... | collective-permute-start | bytes 1867784 | tf_op jit(solution)/shard_map/ppermute | solution.py:91
  46.6 33.1 %collective-permute-start.17 = (f16[4,152,608]{2,1,0:T(8,128)(2,1)S(1)}, f16[4,152,608]{2,1,0:T(8,128)(2,1)S(1)}, u32[]{:S(2)}, u32[]{:S(2)}) collective-permute-start(f16[4,152,608]{2,1,0:T(8,128)(2,1)S(1)} %get-tuple-element.311), channel_id=1, source_target_pairs={{0,4},{2,6},{4,0},{6,2},{8,12},{10,14},{12,8},{14,10},{16,20},{18,... | collective-permute-start | bytes 2217992 | tf_op jit(solution)/shard_map/ppermute | solution.py:78
  48.8 34.8 %collective-permute-start.16 = (f16[4,152,608]{2,1,0:T(8,128)(2,1)S(1)}, f16[4,152,608]{2,1,0:T(8,128)(2,1)S(1)}, u32[]{:S(2)}, u32[]{:S(2)}) collective-permute-start(f16[4,152,608]{2,1,0:T(8,128)(2,1)S(1)} %get-tuple-element.313), channel_id=1, source_target_pairs={{0,4},{2,6},{4,0},{6,2},{8,12},{10,14},{12,8},{14,10},{16,20},{18,... | collective-permute-start | bytes 2217992 | tf_op jit(solution)/shard_map/ppermute | solution.py:78
  52.9 56.6 %collective-permute-start.15 = (bf16[2,2,152,512]{3,2,1,0:T(8,128)(2,1)S(1)}, bf16[2,2,152,512]{3,2,1,0:T(8,128)(2,1)S(1)}, u32[]{:S(2)}, u32[]{:S(2)}) collective-permute-start(bf16[2,2,152,512]{3,2,1,0:T(8,128)(2,1)S(1)} %copy-done.11), channel_id=1, source_target_pairs={{0,1},{1,0},{2,3},{3,2},{4,5},{5,4},{6,7},{7,6},{8,9},{9,8},{10,11... | collective-permute-start | bytes 1867784 | tf_op jit(solution)/shard_map/ppermute | solution.py:91
  59.0 50.5 %collective-permute-start.14 = (bf16[2,2,152,512]{3,2,1,0:T(8,128)(2,1)}, bf16[2,2,152,512]{3,2,1,0:T(8,128)(2,1)S(1)}, u32[]{:S(2)}, u32[]{:S(2)}) collective-permute-start(bf16[2,2,152,512]{3,2,1,0:T(8,128)(2,1)} %get-tuple-element.203), channel_id=1, source_target_pairs={{0,3},{1,2},{2,1},{3,0},{4,7},{5,6},{6,5},{7,4},{8,11},{9,10},{10,... | collective-permute-start | bytes 1867784 | tf_op jit(solution)/shard_map/ppermute | solution.py:100
  78.6 12.9 %collective-permute-start.20 = (f16[2,152,608]{2,1,0:T(8,128)(2,1)S(1)}, f16[2,152,608]{2,1,0:T(8,128)(2,1)S(1)}, u32[]{:S(2)}, u32[]{:S(2)}) collective-permute-start(f16[2,152,608]{2,1,0:T(8,128)(2,1)S(1)} %fusion.4), channel_id=1, source_target_pairs={{0,4},{2,6},{4,0},{6,2},{8,12},{10,14},{12,8},{14,10},{16,20},{18,... | collective-permute-start | bytes 1109000 | tf_op jit(solution)/shard_map/ppermute | solution.py:78
  81.3 13.3 %collective-permute-start.19 = (f16[2,152,608]{2,1,0:T(8,128)(2,1)S(1)}, f16[2,152,608]{2,1,0:T(8,128)(2,1)S(1)}, u32[]{:S(2)}, u32[]{:S(2)}) collective-permute-start(f16[2,152,608]{2,1,0:T(8,128)(2,1)S(1)} %get-tuple-element.319), channel_id=1, source_target_pairs={{0,8},{2,10},{4,12},{6,14},{8,0},{10,2},{12,4},{14,6},{16,24},{18,... | collective-permute-start | bytes 1109000 | tf_op jit(solution)/shard_map/ppermute | solution.py:78
  85.2 22.8 %collective-permute-start.18 = (f16[2,152,608]{2,1,0:T(8,128)(2,1)S(1)}, f16[2,152,608]{2,1,0:T(8,128)(2,1)S(1)}, u32[]{:S(2)}, u32[]{:S(2)}) collective-permute-start(f16[2,152,608]{2,1,0:T(8,128)(2,1)S(1)} %get-tuple-element.320), channel_id=1, source_target_pairs={{0,8},{2,10},{4,12},{6,14},{8,0},{10,2},{12,4},{14,6},{16,24},{18,... | collective-permute-start | bytes 1109000 | tf_op jit(solution)/shard_map/ppermute | solution.py:78
  93.0 27.1 %collective-permute-start.21 = (f16[2,152,608]{2,1,0:T(8,128)(2,1)S(1)}, f16[2,152,608]{2,1,0:T(8,128)(2,1)S(1)}, u32[]{:S(2)}, u32[]{:S(2)}) collective-permute-start(f16[2,152,608]{2,1,0:T(8,128)(2,1)S(1)} %multiply_convert_fusion.2), channel_id=1, source_target_pairs={{0,8},{2,10},{4,12},{6,14},{8,0},{10,2},{12,4},{14,6},{16,24},{18,... | collective-permute-start | bytes 1109000 | tf_op jit(solution)/shard_map/ppermute | solution.py:78
  96.1 20.3 %collective-permute-start.25 = (f16[152,608]{1,0:T(8,128)(2,1)S(1)}, f16[152,608]{1,0:T(8,128)(2,1)S(1)}, u32[]{:S(2)}, u32[]{:S(2)}) collective-permute-start(f16[152,608]{1,0:T(8,128)(2,1)S(1)} %get-tuple-element.323), channel_id=1, source_target_pairs={{0,16},{2,18},{4,20},{6,22},{8,24},{10,26},{12,28},{14,30},{16,0},... | collective-permute-start | bytes 554504 | tf_op jit(solution)/shard_map/ppermute | solution.py:78
  109.4 8.3 %collective-permute-start.24 = (f16[152,608]{1,0:T(8,128)(2,1)S(1)}, f16[152,608]{1,0:T(8,128)(2,1)S(1)}, u32[]{:S(2)}, u32[]{:S(2)}) collective-permute-start(f16[152,608]{1,0:T(8,128)(2,1)S(1)} %get-tuple-element.325), channel_id=1, source_target_pairs={{0,16},{2,18},{4,20},{6,22},{8,24},{10,26},{12,28},{14,30},{16,0},... | collective-permute-start | bytes 554504 | tf_op jit(solution)/shard_map/ppermute | solution.py:78
  114.2 12.2 %collective-permute-start.22 = (f16[152,608]{1,0:T(8,128)(2,1)S(1)}, f16[152,608]{1,0:T(8,128)(2,1)S(1)}, u32[]{:S(2)}, u32[]{:S(2)}) collective-permute-start(f16[152,608]{1,0:T(8,128)(2,1)S(1)} %get-tuple-element.316), channel_id=1, source_target_pairs={{0,4},{2,6},{4,0},{6,2},{8,12},{10,14},{12,8},{14,10},{16,20},{18,... | collective-permute-start | bytes 554504 | tf_op jit(solution)/shard_map/ppermute | solution.py:78
  115.8 6.2 %collective-permute-start.23 = (f16[152,608]{1,0:T(8,128)(2,1)S(1)}, f16[152,608]{1,0:T(8,128)(2,1)S(1)}, u32[]{:S(2)}, u32[]{:S(2)}) collective-permute-start(f16[152,608]{1,0:T(8,128)(2,1)S(1)} %get-tuple-element.314), channel_id=1, source_target_pairs={{0,4},{2,6},{4,0},{6,2},{8,12},{10,14},{12,8},{14,10},{16,20},{18,... | collective-permute-start | bytes 554504 | tf_op jit(solution)/shard_map/ppermute | solution.py:78
  118.5 9.0 %collective-permute-start.27 = (f32[152,608]{1,0:T(8,128)S(1)}, f32[152,608]{1,0:T(8,128)S(1)}, u32[]{:S(2)}, u32[]{:S(2)}) collective-permute-start(f32[152,608]{1,0:T(8,128)S(1)} %multiply_add_fusion.5), channel_id=1, source_target_pairs={{0,1},{1,0},{2,3},{3,2},{4,5},{5,4},{6,7},{7,6},{8,9},{9,8},{10,11... | collective-permute-start | bytes 1109000 | tf_op jit(solution)/shard_map/ppermute | solution.py:91
  123.5 8.7 %collective-permute-start.26 = (f16[152,608]{1,0:T(8,128)(2,1)S(1)}, f16[152,608]{1,0:T(8,128)(2,1)S(1)}, u32[]{:S(2)}, u32[]{:S(2)}) collective-permute-start(f16[152,608]{1,0:T(8,128)(2,1)S(1)} %fusion.12), channel_id=1, source_target_pairs={{0,16},{2,18},{4,20},{6,22},{8,24},{10,26},{12,28},{14,30},{16,0},... | collective-permute-start | bytes 554504 | tf_op jit(solution)/shard_map/ppermute | solution.py:78
  136.9 60.1 %collective-permute-start.41 = (bf16[512,2432]{1,0:T(8,128)(2,1)S(1)}, bf16[512,2432]{1,0:T(8,128)(2,1)S(1)}, u32[]{:S(2)}, u32[]{:S(2)}) collective-permute-start(bf16[512,2432]{1,0:T(8,128)(2,1)S(1)} %copy-done.7), channel_id=1, source_target_pairs={{0,1},{1,0},{2,3},{3,2},{4,5},{5,4},{6,7},{7,6},{8,9},{9,8},{10,11... | collective-permute-start | bytes 7471112 | tf_op jit(solution)/shard_map/ppermute | solution.py:91
  153.4 10.5 %collective-permute-start.34 = (bf16[2,152,608]{2,1,0:T(8,128)(2,1)S(1)}, bf16[2,152,608]{2,1,0:T(8,128)(2,1)S(1)}, u32[]{:S(2)}, u32[]{:S(2)}) collective-permute-start(bf16[2,152,608]{2,1,0:T(8,128)(2,1)S(1)} %get-tuple-element.275), channel_id=1, source_target_pairs={{0,8},{2,10},{4,12},{6,14},{8,0},{10,2},{12,4},{14,6},{16,24},{18,... | collective-permute-start | bytes 1109000 | tf_op jit(solution)/shard_map/ppermute | solution.py:78
  154.5 17.6 %collective-permute-start.36 = (bf16[2,152,608]{2,1,0:T(8,128)(2,1)S(1)}, bf16[2,152,608]{2,1,0:T(8,128)(2,1)S(1)}, u32[]{:S(2)}, u32[]{:S(2)}) collective-permute-start(bf16[2,152,608]{2,1,0:T(8,128)(2,1)S(1)} %get-tuple-element.275), channel_id=1, source_target_pairs={{0,24},{2,26},{4,28},{6,30},{8,16},{10,18},{12,20},{14,22},{16,8},... | collective-permute-start | bytes 1109000 | tf_op jit(solution)/shard_map/ppermute | solution.py:78
  156.8 19.2 %collective-permute-start.33 = (bf16[2,152,608]{2,1,0:T(8,128)(2,1)S(1)}, bf16[2,152,608]{2,1,0:T(8,128)(2,1)S(1)}, u32[]{:S(2)}, u32[]{:S(2)}) collective-permute-start(bf16[2,152,608]{2,1,0:T(8,128)(2,1)S(1)} %get-tuple-element.275), channel_id=1, source_target_pairs={{0,4},{2,6},{4,0},{6,2},{8,12},{10,14},{12,8},{14,10},{16,20},{18,... | collective-permute-start | bytes 1109000 | tf_op jit(solution)/shard_map/ppermute | solution.py:78
  172.0 12.0 %collective-permute-start.37 = (bf16[2,152,608]{2,1,0:T(8,128)(2,1)S(1)}, bf16[2,152,608]{2,1,0:T(8,128)(2,1)S(1)}, u32[]{:S(2)}, u32[]{:S(2)}) collective-permute-start(bf16[2,152,608]{2,1,0:T(8,128)(2,1)S(1)} %collective-permute-done.36), channel_id=1, source_target_pairs={{0,4},{2,6},{4,0},{6,2},{8,12},{10,14},{12,8},{14,10},{16,20},{18,... | collective-permute-start | bytes 1109000 | tf_op jit(solution)/shard_map/ppermute | solution.py:78
  173.8 14.4 %collective-permute-start.35 = (bf16[2,152,608]{2,1,0:T(8,128)(2,1)S(1)}, bf16[2,152,608]{2,1,0:T(8,128)(2,1)S(1)}, u32[]{:S(2)}, u32[]{:S(2)}) collective-permute-start(bf16[2,152,608]{2,1,0:T(8,128)(2,1)S(1)} %collective-permute-done.34), channel_id=1, source_target_pairs={{0,4},{2,6},{4,0},{6,2},{8,12},{10,14},{12,8},{14,10},{16,20},{18,... | collective-permute-start | bytes 1109000 | tf_op jit(solution)/shard_map/ppermute | solution.py:78
  174.1 15.3 %collective-permute-start.38 = (bf16[2,152,608]{2,1,0:T(8,128)(2,1)S(1)}, bf16[2,152,608]{2,1,0:T(8,128)(2,1)S(1)}, u32[]{:S(2)}, u32[]{:S(2)}) collective-permute-start(bf16[2,152,608]{2,1,0:T(8,128)(2,1)S(1)} %get-tuple-element.275), channel_id=1, source_target_pairs={{0,16},{2,18},{4,20},{6,22},{8,24},{10,26},{12,28},{14,30},{16,0},... | collective-permute-start | bytes 1109000 | tf_op jit(solution)/shard_map/ppermute | solution.py:78
  190.3 11.0 %collective-permute-start.42 = (bf16[2,152,608]{2,1,0:T(8,128)(2,1)S(1)}, bf16[2,152,608]{2,1,0:T(8,128)(2,1)S(1)}, u32[]{:S(2)}, u32[]{:S(2)}) collective-permute-start(bf16[2,152,608]{2,1,0:T(8,128)(2,1)S(1)} %collective-permute-done.38), channel_id=1, source_target_pairs={{0,4},{2,6},{4,0},{6,2},{8,12},{10,14},{12,8},{14,10},{16,20},{18,... | collective-permute-start | bytes 1109000 | tf_op jit(solution)/shard_map/ppermute | solution.py:78
  191.7 9.9 %collective-permute-start.43 = (bf16[4,2,152,608]{3,2,1,0:T(8,128)(2,1)S(1)}, bf16[4,2,152,608]{3,2,1,0:T(8,128)(2,1)S(1)}, u32[]{:S(2)}, u32[]{:S(2)}) collective-permute-start(bf16[4,2,152,608]{3,2,1,0:T(8,128)(2,1)S(1)} %pad_maximum_fusion.refs_0_), channel_id=1, source_target_pairs={{0,2},{2,0},{4,6},{6,4},{8,10},{10,8},{12,14},{14,12},{16,18},{18,... | collective-permute-start | bytes 4435976 | tf_op jit(solution)/shard_map/ppermute | solution.py:78
  (31 other events, 230.5 us)

commit v10 on v9

--- a/solution.py
+++ b/solution.py
@@ -344,7 +344,7 @@
                 pltpu.VMEM((2, TILE, D), jnp.bfloat16),
                 pltpu.SemaphoreType.DMA((2,)),
             ],
-            mib=24,
+            mib=20,
         )
 
     def per_device(
@@ -399,7 +399,7 @@
             lambda *values: prepare_student(*values, scales, r),
             act_student, top_student, top_fake, top_act,
         )
-        tops = hops(tops, jnp.maximum, "tensor", "dp")
+        tops = hops(tops, jnp.maximum, "dp")
         next(tops)
         send_planes(0, planes[0], planes[1])
         parts_fake = []
@@ -413,27 +413,26 @@
             )
 
         multiply_fake(0)
+        next(tops)
+        next(tops)
+        next(tops)
         acts = step(lambda *values: values, *acts)
         scaled_fake += [[act, to_core(act)] for act in acts]
-        next(tops)
-        next(tops)
-        for j in range(1, n_tensor):
-            multiply_fake(j)
-        while (final := next(tops)) is None:
+        while (tops_own := next(tops)) is None:
             pass
 
-        def factors(tops):
-            bounds = tops[0:3:2, 0] * tops[1:4:2, 0]
-            bounds = jnp.maximum(bounds, 1e-30) * (1.01 * count * n_dp / HALF_LIMIT)
-            return bounds, 1.0 / bounds
-
-        grow, fit = step(factors, final)
+        def factor(tops, net):
+            bound = jnp.maximum(tops[2 * net, 0] * tops[2 * net + 1, 0], 1e-30)
+            bound = bound * (1.01 * count * n_dp / HALF_LIMIT)
+            return bound, 1.0 / bound
+
+        factors = {"own": step(lambda tops: factor(tops, 1), tops_own)}
 
         def shrink(value, net):
-            return (value * fit[net]).astype(jnp.float16)
+            return (value * factors[net][1]).astype(jnp.float16)
 
         def widen(value, net):
-            return value.astype(jnp.float32) * grow[net]
+            return value.astype(jnp.float32) * factors[net][0]
 
         def add_widened(total, values, net):
             for value in values:
@@ -442,9 +441,12 @@
 
         fake_own, fake_got = {}, {}
 
+        def which(j):
+            return 1 if j else "own"
+
         def fake_middle(j):
             def work(both):
-                sent = [shrink(both[i], 1) for i in range(1, inner)]
+                sent = [shrink(both[i], which(j)) for i in range(1, inner)]
                 return sent, both[0]
 
             sent, fake_own[j] = step(work, parts_fake[j])
@@ -452,29 +454,32 @@
 
         def fake_near(j):
             def work(own, *got):
-                own = add_widened(own, got, 1)
-                return shrink(own[1::2], 1), own[0::2]
+                own = add_widened(own, got, which(j))
+                return shrink(own[1::2], which(j)), own[0::2]
 
             sent, fake_own[j] = step(work, fake_own[j], *fake_got[j])
             fake_got[j] = [to_plane(sent, 1)]
 
         def fake_far(j):
             def work(own, *got):
-                own = add_widened(own, got, 1)
-                return shrink(own[1], 1), own[0]
+                own = add_widened(own, got, which(j))
+                return shrink(own[1], which(j)), own[0]
 
             sent, fake_own[j] = step(work, fake_own[j], *fake_got[j])
             fake_got[j] = [to_plane(sent, 2)]
 
         def fake_total(j):
             return step(
-                lambda own, *got: add_widened(own, got, 1), fake_own[j], *fake_got[j]
+                lambda own, *got: add_widened(own, got, which(j)), fake_own[j], *fake_got[j]
             )
 
+        fake_middle(0)
+        for j in range(1, n_tensor):
+            multiply_fake(j)
         mate_student = to_core(scaled_student)
         mate_planes = [to_core(planes[1]), to_core(planes[3])]
-        for j in range(n_tensor):
-            fake_middle(j)
+        tops = hops(tops_own, jnp.maximum, "tensor")
+        next(tops)
         mate_student, *mate_planes = step(lambda *values: values, mate_student, *mate_planes)
 
         def back(whole, net, pieces, j, low, size):
@@ -502,6 +507,11 @@
         back_student = back(None, 0, [cot_student], 0, 0, r)
         send_planes(1, *step(lambda a, b: (a, b), planes[2], planes[3]))
         back_fake = back(None, 1, [cot_fake], 0, 0, r)
+        while (tops_all := next(tops)) is None:
+            pass
+        factors[0], factors[1] = step(lambda tops: (factor(tops, 0), factor(tops, 1)), tops_all)
+        for j in range(1, n_tensor):
+            fake_middle(j)
         both = multiply_student(0)
 
         def first_middle(both):
@@ -551,7 +561,15 @@
         rows = step(lambda cot: cot, cot_fake)
         raw = [from_tensor(rows, j) for j in range(1, n_tensor)]
 
-        *_, squares = hops(squares, jnp.add, "dp")
+        got = [to_plane(squares, k) for k in range(1, OUTER)]
+        squares = reduced(jnp.add, squares, got)
+        got = [
+            move_dp(squares, lambda z, m, c, i=i, o=o: (z, (m + i) & (inner - 1), c ^ o))
+            for i in range(inner)
+            for o in range(2)
+            if i or o
+        ]
+        squares = reduced(jnp.add, squares, got)
         states = (
             master_student, first_student, second_student, master_fake, first_fake, second_fake,
         )

time: 211 us -> 210 us (level)
  waiting for transfers between devices: 90.7 us -> 103 us
  other arithmetic: 17.2 us -> 6.13 us
  starting transfers between devices: 52 us -> 44.8 us
  between operations: 1.32 us -> 5.41 us
    ppermute x28 -> x34, waiting for transfers between devices: 54.3 us -> 74.4 us  [move_dp(): return lax.ppermute(value, 'dp', perm)]
    ppermute x6, waiting for transfers between devices: 21 us -> 11.8 us  [from_tensor(): return lax.ppermute(value, 'tensor', perm)]
    convert_element_type x5 -> x6, other arithmetic: 5.07 us -> 0.76 us  [shrink(): return (value * factors[net][1]).astype(jnp.float16)]
    add x8, other arithmetic: 6.27 us -> 2.15 us  [add_widened(): total = total + widen(value, net)]
    ppermute x28 -> x34, starting transfers between devices: 27.1 us -> 30.8 us  [move_dp(): return lax.ppermute(value, 'dp', perm)]
    ppermute x9 -> x5, starting transfers between devices: 11.6 us -> 7.9 us  [hops(): got = lax.ppermute(value, axis, perm)]
    ppermute x2, starting transfers between devices: 3.7 us -> 0.07 us  [from_diagonal(): return lax.ppermute(value, ('dp', 'tensor'), perm)]
    ppermute x6, starting transfers between devices: 9.64 us -> 6.03 us  [from_tensor(): return lax.ppermute(value, 'tensor', perm)]
  transfers between devices with their start and end apart: 45 -> 47, of which waited for: 26 -> 23; matrix products, arithmetic and copies ran while one was open for 8% -> 3% of each run, Pallas kernels for 16% -> 17%
where the time goes in v10:
time: 210 us
  waiting for transfers between devices  103 us (49%)
  Pallas kernels  44.8 us (21%)
  starting transfers between devices  44.8 us (21%)
  other arithmetic  6.13 us (3%)
  between operations  5.41 us (3%)
  local copies, waits for them, and re-layouts  5.09 us (2%)
    ppermute x34, waiting for transfers between devices, move_dp(): return lax.ppermute(value, 'dp', perm)  74.4 us
    pallas_call x15, Pallas kernels, call(): pl.pallas_call(kernel, out_shape=out_shape, compiler_params=pltpu.Compile...  44.8 us
    ppermute x34, starting transfers between devices, move_dp(): return lax.ppermute(value, 'dp', perm)  30.8 us
    ppermute x5, waiting for transfers between devices, hops(): got = lax.ppermute(value, axis, perm)  17.2 us
    ppermute x6, waiting for transfers between devices, from_tensor(): return lax.ppermute(value, 'tensor', perm)  11.8 us
    ppermute x5, starting transfers between devices, hops(): got = lax.ppermute(value, axis, perm)  7.9 us
    ppermute x6, starting transfers between devices, from_tensor(): return lax.ppermute(value, 'tensor', perm)  6.03 us
  transfers between devices with their start and end apart: 47, of which 23 were waited for; matrix products, arithmetic and copies ran while one was open for 3% of the time, Pallas kernels for 17%

profile of v10, /device:TPU:0, one launch (start us, length us, event | category | flops | bytes accessed | tf_op | source)
XLA Modules:
  0.0 209.7 jit_solution(251053055191668938)
XLA Ops:
  5.6 2.2 %shard_map.205 = (bf16[2,4,152,512]{3,2,1,0:T(8,128)(2,1)S(1)}, bf16[2,4,152,512]{3,2,1,0:T(8,128)(2,1)S(1)}, f32[8,128]{1,0:T(8,128)S(1)}) custom-call(bf16[512,2432]{1,0:T(8,128)(2,1)S(1)} %copy-done.6), custom_call_target="tpu_custom_call" | custom-call | tf_op jit(solution)/shard_map/pallas_call | solution.py:56
  8.5 2.9 %collective-permute-start.6 = (bf16[1,608,512]{2,1,0:T(8,128)(2,1)S(1)}, bf16[1,608,512]{2,1,0:T(8,128)(2,1)}, u32[]{:S(2)}, u32[]{:S(2)}) collective-permute-start(bf16[1,608,512]{2,1,0:T(8,128)(2,1)S(1)} %get-tuple-element.177), channel_id=1, source_target_pairs={{0,1},{1,0},{2,3},{3,2},{4,5},{5,4},{6,7},{7,6},{8,9},{9,8},{10,11... | collective-permute-start | bytes 1867784 | tf_op jit(solution)/shard_map/ppermute | solution.py:91
  11.4 3.4 %shard_map.206 = (bf16[2,2,152,512]{3,2,1,0:T(8,128)(2,1)}, bf16[2,2,152,512]{3,2,1,0:T(8,128)(2,1)}, bf16[2,2,152,512]{3,2,1,0:T(8,128)(2,1)S(1)}, bf16[2,2,152,512]{3,2,1,0:T(8,128)(2,1)}, f32[8,128]{1,0:T(8,128)S(1)}) custom-call(bf16[512,2432]{1,0:T(8,128)(2,1)S(1)} %copy-done.4), custom_call_target="tpu_custom_call" | custom-call | tf_op jit(solution)/shard_map/pallas_call | solution.py:56
  14.8 2.2 %shard_map.207 = (f32[8,128]{1,0:T(8,128)S(1)}, bf16[2,608,512]{2,1,0:T(8,128)(2,1)}) custom-call(f32[2]{0:T(128)S(1)} %divide_bitcast_fusion.scale_ref, bf16[608,1024]{1,0:T(8,128)(2,1)S(1)} %copy-done.14, f32[8,128]{1,0:T(8,128)S(1)} %get-tuple-element.172.top_s_ref, f32[8,128]{1,0:T(8,128)S(1)} %get-tuple-element.173.top_f_ref, ...), custom_call_target="tpu_custom_call" | custom-call | tf_op jit(solution)/shard_map/pallas_call | solution.py:56
  17.6 2.1 %shard_map.208 = f32[1216,608]{1,0:T(8,128)S(1)} custom-call(bf16[1216,512]{1,0:T(8,128)(2,1)S(1)} %bitcast.96, bf16[1216,512]{1,0:T(8,128)(2,1)S(1)} %bitcast.98, bf16[1,608,512]{2,1,0:T(8,128)(2,1)S(1)} %get-tuple-element.182.refs_2_, bf16[1,608,512]{2,1,0:T(8,128)(2,1)S(1)} %collective-permute-done.8.refs_3_), custom_call_target="tpu_custom_call" | custom-call | tf_op jit(solution)/shard_map/pallas_call | solution.py:56
  21.4 2.1 collective-permute-done.9
  27.6 2.6 %collective-permute-start.12 = (f32[8,128]{1,0:T(8,128)S(1)}, f32[8,128]{1,0:T(8,128)S(1)}, u32[]{:S(2)}, u32[]{:S(2)}) collective-permute-start(f32[8,128]{1,0:T(8,128)S(1)} %max.29), channel_id=1, source_target_pairs={{0,16},{2,18},{4,20},{6,22},{8,24},{10,26},{12,28},{14,30},{16,0},... | collective-permute-start | bytes 12296 | tf_op jit(solution)/shard_map/ppermute | solution.py:376
  37.8 3.5 %shard_map.209 = f32[1216,608]{1,0:T(8,128)S(1)} custom-call(bf16[1216,512]{1,0:T(8,128)(2,1)S(1)} %bitcast.97, bf16[1216,512]{1,0:T(8,128)(2,1)S(1)} %bitcast.99, bf16[1,608,512]{2,1,0:T(8,128)(2,1)} %collective-permute-done.6.refs_2_, bf16[1,608,512]{2,1,0:T(8,128)(2,1)} %collective-permute-done.11.refs_3_), custom_call_target="tpu_custom_call" | custom-call | tf_op jit(solution)/shard_map/pallas_call | solution.py:56
  43.0 3.2 %shard_map.210.refs_4_ = bf16[608,1024]{1,0:T(8,128)(2,1)} custom-call(f32[2]{0:T(128)S(1)} %divide_bitcast_fusion.scale_ref, bf16[608,2432]{1,0:T(8,128)(2,1)S(1)} %copy-done, bf16[512,2432]{1,0:T(8,128)(2,1)S(1)} %copy-done.5), custom_call_target="tpu_custom_call" | custom-call | tf_op jit(solution)/shard_map/pallas_call | solution.py:56
  46.2 3.2 %shard_map.211.refs_1_ = bf16[608,1024]{1,0:T(8,128)(2,1)} custom-call(f32[2]{0:T(128)S(1)} %divide_bitcast_fusion.scale_ref, bf16[608,2432]{1,0:T(8,128)(2,1)S(1)} %copy-done.2, bf16[512,2432]{1,0:T(8,128)(2,1)S(1)} %copy-done.7), custom_call_target="tpu_custom_call" | custom-call | tf_op jit(solution)/shard_map/pallas_call | solution.py:56
  49.4 11.2 %collective-permute-done.15 = f32[8,128]{1,0:T(8,128)S(1)} collective-permute-done((f32[8,128]{1,0:T(8,128)S(1)}, f32[8,128]{1,0:T(8,128)S(1)}, u32[]{:S(2)}, u32[]{:S(2)}) %collective-permute-start.15) | collective-permute-done | bytes 4128 | tf_op jit(solution)/shard_map/ppermute | solution.py:376
  66.2 4.5 %shard_map.212 = f32[608,608]{1,0:T(8,128)S(1)} custom-call(bf16[608,512]{1,0:T(8,128)(2,1)} %bitcast.14.refs_0_, bf16[608,512]{1,0:T(8,128)(2,1)} %bitcast.15.refs_1_, bf16[608,512]{1,0:T(8,128)(2,1)} %bitcast.16.refs_2_, bf16[608,512]{1,0:T(8,128)(2,1)} %bitcast.17.refs_3_, bf16[2,608,512]{2,1,0:T(8,128)(2,1)} %get-tuple-element.231.refs_4_, ...), custom_call_target="tpu_custom_call" | custom-call | tf_op jit(solution)/shard_map/pallas_call | solution.py:56
  75.2 9.7 %collective-permute-done.16 = f16[4,152,608]{2,1,0:T(8,128)(2,1)S(1)} collective-permute-done((f16[4,152,608]{2,1,0:T(8,128)(2,1)S(1)}, f16[4,152,608]{2,1,0:T(8,128)(2,1)S(1)}, u32[]{:S(2)}, u32[]{:S(2)}) %collective-permute-start.16) | collective-permute-done | bytes 739360 | tf_op jit(solution)/shard_map/ppermute | solution.py:78
  86.9 3.2 %collective-permute-done.20 = f16[2,152,608]{2,1,0:T(8,128)(2,1)S(1)} collective-permute-done((f16[2,152,608]{2,1,0:T(8,128)(2,1)S(1)}, f16[2,152,608]{2,1,0:T(8,128)(2,1)S(1)}, u32[]{:S(2)}, u32[]{:S(2)}) %collective-permute-start.20) | collective-permute-done | bytes 369696 | tf_op jit(solution)/shard_map/ppermute | solution.py:78
  92.1 2.7 %collective-permute-start.25 = (f16[152,608]{1,0:T(8,128)(2,1)S(1)}, f16[152,608]{1,0:T(8,128)(2,1)S(1)}, u32[]{:S(2)}, u32[]{:S(2)}) collective-permute-start(f16[152,608]{1,0:T(8,128)(2,1)S(1)} %get-tuple-element.323), channel_id=1, source_target_pairs={{0,16},{2,18},{4,20},{6,22},{8,24},{10,26},{12,28},{14,30},{16,0},... | collective-permute-start | bytes 554504 | tf_op jit(solution)/shard_map/ppermute | solution.py:78
  94.7 8.7 %collective-permute-done.18 = f16[2,152,608]{2,1,0:T(8,128)(2,1)S(1)} collective-permute-done((f16[2,152,608]{2,1,0:T(8,128)(2,1)S(1)}, f16[2,152,608]{2,1,0:T(8,128)(2,1)S(1)}, u32[]{:S(2)}, u32[]{:S(2)}) %collective-permute-start.18) | collective-permute-done | bytes 369696 | tf_op jit(solution)/shard_map/ppermute | solution.py:78
  105.4 4.2 %shard_map.213 = f32[608,608]{1,0:T(8,128)S(1)} custom-call(bf16[608,512]{1,0:T(8,128)(2,1)S(1)} %bitcast.101, bf16[608,512]{1,0:T(8,128)(2,1)} %bitcast.24.refs_1_, bf16[608,512]{1,0:T(8,128)(2,1)} %bitcast.25.refs_2_, bf16[608,512]{1,0:T(8,128)(2,1)S(1)} %bitcast.100, bf16[2,608,512]{2,1,0:T(8,128)(2,1)} %get-tuple-element.231.refs_4_, ...), custom_call_target="tpu_custom_call" | custom-call | tf_op jit(solution)/shard_map/pallas_call | solution.py:56
  111.9 6.8 %collective-permute-done.24 = f16[152,608]{1,0:T(8,128)(2,1)S(1)} collective-permute-done((f16[152,608]{1,0:T(8,128)(2,1)S(1)}, f16[152,608]{1,0:T(8,128)(2,1)S(1)}, u32[]{:S(2)}, u32[]{:S(2)}) %collective-permute-start.24) | collective-permute-done | bytes 184864 | tf_op jit(solution)/shard_map/ppermute | solution.py:78
  120.1 8.7 %collective-permute-done.27 = f32[152,608]{1,0:T(8,128)S(1)} collective-permute-done((f32[152,608]{1,0:T(8,128)S(1)}, f32[152,608]{1,0:T(8,128)S(1)}, u32[]{:S(2)}, u32[]{:S(2)}) %collective-permute-start.27) | collective-permute-done | bytes 369696 | tf_op jit(solution)/shard_map/ppermute | solution.py:91
  129.9 3.1 %collective-permute-done.28 = f32[8,128]{1,0:T(8,128)S(1)} collective-permute-done((f32[8,128]{1,0:T(8,128)S(1)}, f32[8,128]{1,0:T(8,128)S(1)}, u32[]{:S(2)}, u32[]{:S(2)}) %collective-permute-start.28) | collective-permute-done | bytes 4128 | tf_op jit(solution)/shard_map/ppermute | solution.py:91
  135.4 2.6 %collective-permute-start.31 = (f32[8,128]{1,0:T(8,128)S(1)}, f32[8,128]{1,0:T(8,128)S(1)}, u32[]{:S(2)}, u32[]{:S(2)}) collective-permute-start(f32[8,128]{1,0:T(8,128)S(1)} %add.78), channel_id=1, source_target_pairs={{0,24},{2,26},{4,28},{6,30},{8,16},{10,18},{12,20},{14,22},{16,8},... | collective-permute-start | bytes 12296 | tf_op jit(solution)/shard_map/ppermute | solution.py:78
  138.2 2.7 %collective-permute-done.31 = f32[8,128]{1,0:T(8,128)S(1)} collective-permute-done((f32[8,128]{1,0:T(8,128)S(1)}, f32[8,128]{1,0:T(8,128)S(1)}, u32[]{:S(2)}, u32[]{:S(2)}) %collective-permute-start.31) | collective-permute-done | bytes 4128 | tf_op jit(solution)/shard_map/ppermute | solution.py:78
  145.6 2.1 shard_map.215
  147.7 2.5 %collective-permute-start.38 = (bf16[2,152,608]{2,1,0:T(8,128)(2,1)S(1)}, bf16[2,152,608]{2,1,0:T(8,128)(2,1)S(1)}, u32[]{:S(2)}, u32[]{:S(2)}) collective-permute-start(bf16[2,152,608]{2,1,0:T(8,128)(2,1)S(1)} %get-tuple-element.277), channel_id=1, source_target_pairs={{0,24},{2,26},{4,28},{6,30},{8,16},{10,18},{12,20},{14,22},{16,8},... | collective-permute-start | bytes 1109000 | tf_op jit(solution)/shard_map/ppermute | solution.py:78
  150.8 8.3 %collective-permute-done.36 = bf16[2,152,608]{2,1,0:T(8,128)(2,1)S(1)} collective-permute-done((bf16[2,152,608]{2,1,0:T(8,128)(2,1)S(1)}, bf16[2,152,608]{2,1,0:T(8,128)(2,1)S(1)}, u32[]{:S(2)}, u32[]{:S(2)}) %collective-permute-start.36) | collective-permute-done | bytes 369696 | tf_op jit(solution)/shard_map/ppermute | solution.py:78
  159.1 9.2 %collective-permute-done.38 = bf16[2,152,608]{2,1,0:T(8,128)(2,1)S(1)} collective-permute-done((bf16[2,152,608]{2,1,0:T(8,128)(2,1)S(1)}, bf16[2,152,608]{2,1,0:T(8,128)(2,1)S(1)}, u32[]{:S(2)}, u32[]{:S(2)}) %collective-permute-start.38) | collective-permute-done | bytes 369696 | tf_op jit(solution)/shard_map/ppermute | solution.py:78
  172.3 8.0 %collective-permute-done.39 = bf16[2,152,608]{2,1,0:T(8,128)(2,1)S(1)} collective-permute-done((bf16[2,152,608]{2,1,0:T(8,128)(2,1)S(1)}, bf16[2,152,608]{2,1,0:T(8,128)(2,1)S(1)}, u32[]{:S(2)}, u32[]{:S(2)}) %collective-permute-start.39) | collective-permute-done | bytes 369696 | tf_op jit(solution)/shard_map/ppermute | solution.py:78
  180.2 7.2 %collective-permute-done.37 = bf16[2,152,608]{2,1,0:T(8,128)(2,1)S(1)} collective-permute-done((bf16[2,152,608]{2,1,0:T(8,128)(2,1)S(1)}, bf16[2,152,608]{2,1,0:T(8,128)(2,1)S(1)}, u32[]{:S(2)}, u32[]{:S(2)}) %collective-permute-start.37) | collective-permute-done | bytes 369696 | tf_op jit(solution)/shard_map/ppermute | solution.py:78
  191.9 4.4 %shard_map.216 = bf16[608,1024]{1,0:T(8,128)(2,1)} custom-call(f32[2]{0:T(128)S(1)} %divide_bitcast_fusion.scale_ref, bf16[608,2432]{1,0:T(8,128)(2,1)S(1)} %copy-done.1, bf16[2,2,152,512]{3,2,1,0:T(8,128)(2,1)} %collective-permute-done.refs_0_, bf16[2,2,152,512]{3,2,1,0:T(8,128)(2,1)S(1)} %collective-permute-done.41.refs_1_, ...), custom_call_target="tpu_custom_call", output_to_operand_aliasing={{}: (6, {})} | custom-call | tf_op jit(solution)/shard_map/pallas_call | solution.py:56
  196.3 3.2 %shard_map.217 = bf16[608,1024]{1,0:T(8,128)(2,1)} custom-call(f32[2]{0:T(128)S(1)} %divide_bitcast_fusion.scale_ref, bf16[608,2432]{1,0:T(8,128)(2,1)S(1)} %copy-done.3, bf16[512,2432]{1,0:T(8,128)(2,1)S(1)} %collective-permute-done.43.refs_0_, bf16[608,1024]{1,0:T(8,128)(2,1)} %shard_map.211.refs_1_), custom_call_target="tpu_custom_call", output_to_operand_aliasing={{}: (3, {})} | custom-call | tf_op jit(solution)/shard_map/pallas_call | solution.py:56
  200.9 3.4 %collective-permute-done.46.refs_3_ = bf16[4,2,152,608]{3,2,1,0:T(8,128)(2,1)S(1)} collective-permute-done((bf16[4,2,152,608]{3,2,1,0:T(8,128)(2,1)S(1)}, bf16[4,2,152,608]{3,2,1,0:T(8,128)(2,1)S(1)}, u32[]{:S(2)}, u32[]{:S(2)}) %collective-permute-start.46) | collective-permute-done | bytes 1478688 | tf_op jit(solution)/shard_map/ppermute | solution.py:78
  204.3 5.2 %shard_map.218 = (bf16[608,2432]{1,0:T(8,128)(2,1)}, bf16[608,2432]{1,0:T(8,128)(2,1)}) custom-call(bf16[4,2,152,608]{3,2,1,0:T(8,128)(2,1)S(1)} %pad_maximum_fusion.refs_0_, bf16[4,2,152,608]{3,2,1,0:T(8,128)(2,1)S(1)} %pad_maximum_fusion.1.refs_1_, bf16[4,2,152,608]{3,2,1,0:T(8,128)(2,1)S(1)} %collective-permute-done.45.refs_2_, ...), custom_call_target="tpu_custom_call" | custom-call | tf_op jit(solution)/shard_map/pallas_call | solution.py:56
  (158 shorter events, 55.4 us)
Async XLA Ops:
  7.9 9.7 %collective-permute-start.5 = (bf16[2,4,152,512]{3,2,1,0:T(8,128)(2,1)S(1)}, bf16[2,4,152,512]{3,2,1,0:T(8,128)(2,1)S(1)}, u32[]{:S(2)}, u32[]{:S(2)}) collective-permute-start(bf16[2,4,152,512]{3,2,1,0:T(8,128)(2,1)S(1)} %get-tuple-element.176), channel_id=1, source_target_pairs={{0,2},{2,0},{4,6},{6,4},{8,10},{10,8},{12,14},{14,12},{16,18},{18,... | collective-permute-start | bytes 3735560 | tf_op jit(solution)/shard_map/ppermute | solution.py:78
  8.4 9.2 %collective-permute-start.8 = (bf16[1,608,512]{2,1,0:T(8,128)(2,1)S(1)}, bf16[1,608,512]{2,1,0:T(8,128)(2,1)S(1)}, u32[]{:S(2)}, u32[]{:S(2)}) collective-permute-start(bf16[1,608,512]{2,1,0:T(8,128)(2,1)S(1)} %get-tuple-element.182.refs_2_), channel_id=1, source_target_pairs={{0,2},{2,0},{4,6},{6,4},{8,10},{10,8},{12,14},{14,12},{16,18},{18,... | collective-permute-start | bytes 1867784 | tf_op jit(solution)/shard_map/ppermute | solution.py:78
  8.5 18.6 %collective-permute-start.6 = (bf16[1,608,512]{2,1,0:T(8,128)(2,1)S(1)}, bf16[1,608,512]{2,1,0:T(8,128)(2,1)}, u32[]{:S(2)}, u32[]{:S(2)}) collective-permute-start(bf16[1,608,512]{2,1,0:T(8,128)(2,1)S(1)} %get-tuple-element.177), channel_id=1, source_target_pairs={{0,1},{1,0},{2,3},{3,2},{4,5},{5,4},{6,7},{7,6},{8,9},{9,8},{10,11... | collective-permute-start | bytes 1867784 | tf_op jit(solution)/shard_map/ppermute | solution.py:91
  17.0 25.9 %collective-permute-start.2 = (bf16[2,608,512]{2,1,0:T(8,128)(2,1)}, bf16[2,608,512]{2,1,0:T(8,128)(2,1)}, u32[]{:S(2)}, u32[]{:S(2)}) collective-permute-start(bf16[2,608,512]{2,1,0:T(8,128)(2,1)} %get-tuple-element.231.refs_4_), channel_id=1, source_target_pairs={{0,2},{2,0},{4,6},{6,4},{8,10},{10,8},{12,14},{14,12},{16,18},{18,... | collective-permute-start | bytes 3735560 | tf_op jit(solution)/shard_map/ppermute | solution.py:78
  25.0 9.4 %collective-permute-start.3 = (bf16[2,2,152,512]{3,2,1,0:T(8,128)(2,1)}, bf16[2,2,152,512]{3,2,1,0:T(8,128)(2,1)}, u32[]{:S(2)}, u32[]{:S(2)}) collective-permute-start(bf16[2,2,152,512]{3,2,1,0:T(8,128)(2,1)} %get-tuple-element.166), channel_id=1, source_target_pairs={{0,2},{2,0},{4,6},{6,4},{8,10},{10,8},{12,14},{14,12},{16,18},{18,... | collective-permute-start | bytes 1867784 | tf_op jit(solution)/shard_map/ppermute | solution.py:78
  27.1 14.3 %collective-permute-start.4 = (bf16[2,2,152,512]{3,2,1,0:T(8,128)(2,1)}, bf16[2,2,152,512]{3,2,1,0:T(8,128)(2,1)}, u32[]{:S(2)}, u32[]{:S(2)}) collective-permute-start(bf16[2,2,152,512]{3,2,1,0:T(8,128)(2,1)} %get-tuple-element.202), channel_id=1, source_target_pairs={{0,2},{2,0},{4,6},{6,4},{8,10},{10,8},{12,14},{14,12},{16,18},{18,... | collective-permute-start | bytes 1867784 | tf_op jit(solution)/shard_map/ppermute | solution.py:78
  32.1 34.1 %collective-permute-start = (bf16[2,2,152,512]{3,2,1,0:T(8,128)(2,1)}, bf16[2,2,152,512]{3,2,1,0:T(8,128)(2,1)}, u32[]{:S(2)}, u32[]{:S(2)}) collective-permute-start(bf16[2,2,152,512]{3,2,1,0:T(8,128)(2,1)} %get-tuple-element.211), channel_id=1, source_target_pairs={{0,1},{1,0},{2,3},{3,2},{4,5},{5,4},{6,7},{7,6},{8,9},{9,8},{10,11... | collective-permute-start | bytes 1867784 | tf_op jit(solution)/shard_map/ppermute | solution.py:91
  34.4 31.8 %collective-permute-start.1 = (bf16[2,2,152,512]{3,2,1,0:T(8,128)(2,1)}, bf16[2,2,152,512]{3,2,1,0:T(8,128)(2,1)}, u32[]{:S(2)}, u32[]{:S(2)}) collective-permute-start(bf16[2,2,152,512]{3,2,1,0:T(8,128)(2,1)} %get-tuple-element.166), channel_id=1, source_target_pairs={{0,3},{1,2},{2,1},{3,0},{4,7},{5,6},{6,5},{7,4},{8,11},{9,10},{10,... | collective-permute-start | bytes 1867784 | tf_op jit(solution)/shard_map/ppermute | solution.py:100
  34.5 26.1 %collective-permute-start.15 = (f32[8,128]{1,0:T(8,128)S(1)}, f32[8,128]{1,0:T(8,128)S(1)}, u32[]{:S(2)}, u32[]{:S(2)}) collective-permute-start(f32[8,128]{1,0:T(8,128)S(1)} %max.30), channel_id=1, source_target_pairs={{0,1},{1,0},{2,3},{3,2},{4,5},{5,4},{6,7},{7,6},{8,9},{9,8},{10,11... | collective-permute-start | bytes 12296 | tf_op jit(solution)/shard_map/ppermute | solution.py:376
  41.4 30.0 %collective-permute-start.17 = (f16[4,152,608]{2,1,0:T(8,128)(2,1)}, f16[4,152,608]{2,1,0:T(8,128)(2,1)}, u32[]{:S(2)}, u32[]{:S(2)}) collective-permute-start(f16[4,152,608]{2,1,0:T(8,128)(2,1)} %get-tuple-element.311), channel_id=1, source_target_pairs={{0,4},{2,6},{4,0},{6,2},{8,12},{10,14},{12,8},{14,10},{16,20},{18,... | collective-permute-start | bytes 2217992 | tf_op jit(solution)/shard_map/ppermute | solution.py:78
  62.5 43.0 %collective-permute-start.14 = (bf16[2,2,152,512]{3,2,1,0:T(8,128)(2,1)}, bf16[2,2,152,512]{3,2,1,0:T(8,128)(2,1)}, u32[]{:S(2)}, u32[]{:S(2)}) collective-permute-start(bf16[2,2,152,512]{3,2,1,0:T(8,128)(2,1)} %copy-done.15), channel_id=1, source_target_pairs={{0,1},{1,0},{2,3},{3,2},{4,5},{5,4},{6,7},{7,6},{8,9},{9,8},{10,11... | collective-permute-start | bytes 1867784 | tf_op jit(solution)/shard_map/ppermute | solution.py:91
  64.5 20.4 %collective-permute-start.16 = (f16[4,152,608]{2,1,0:T(8,128)(2,1)S(1)}, f16[4,152,608]{2,1,0:T(8,128)(2,1)S(1)}, u32[]{:S(2)}, u32[]{:S(2)}) collective-permute-start(f16[4,152,608]{2,1,0:T(8,128)(2,1)S(1)} %get-tuple-element.312), channel_id=1, source_target_pairs={{0,4},{2,6},{4,0},{6,2},{8,12},{10,14},{12,8},{14,10},{16,20},{18,... | collective-permute-start | bytes 2217992 | tf_op jit(solution)/shard_map/ppermute | solution.py:78
  70.8 19.3 %collective-permute-start.20 = (f16[2,152,608]{2,1,0:T(8,128)(2,1)S(1)}, f16[2,152,608]{2,1,0:T(8,128)(2,1)S(1)}, u32[]{:S(2)}, u32[]{:S(2)}) collective-permute-start(f16[2,152,608]{2,1,0:T(8,128)(2,1)S(1)} %fusion.4), channel_id=1, source_target_pairs={{0,4},{2,6},{4,0},{6,2},{8,12},{10,14},{12,8},{14,10},{16,20},{18,... | collective-permute-start | bytes 1109000 | tf_op jit(solution)/shard_map/ppermute | solution.py:78
  71.3 34.1 %collective-permute-start.13 = (bf16[2,2,152,512]{3,2,1,0:T(8,128)(2,1)}, bf16[2,2,152,512]{3,2,1,0:T(8,128)(2,1)S(1)}, u32[]{:S(2)}, u32[]{:S(2)}) collective-permute-start(bf16[2,2,152,512]{3,2,1,0:T(8,128)(2,1)} %get-tuple-element.202), channel_id=1, source_target_pairs={{0,3},{1,2},{2,1},{3,0},{4,7},{5,6},{6,5},{7,4},{8,11},{9,10},{10,... | collective-permute-start | bytes 1867784 | tf_op jit(solution)/shard_map/ppermute | solution.py:100
  73.6 18.3 %collective-permute-start.19 = (f16[2,152,608]{2,1,0:T(8,128)(2,1)S(1)}, f16[2,152,608]{2,1,0:T(8,128)(2,1)S(1)}, u32[]{:S(2)}, u32[]{:S(2)}) collective-permute-start(f16[2,152,608]{2,1,0:T(8,128)(2,1)S(1)} %get-tuple-element.319), channel_id=1, source_target_pairs={{0,8},{2,10},{4,12},{6,14},{8,0},{10,2},{12,4},{14,6},{16,24},{18,... | collective-permute-start | bytes 1109000 | tf_op jit(solution)/shard_map/ppermute | solution.py:78
  85.2 18.3 %collective-permute-start.18 = (f16[2,152,608]{2,1,0:T(8,128)(2,1)S(1)}, f16[2,152,608]{2,1,0:T(8,128)(2,1)S(1)}, u32[]{:S(2)}, u32[]{:S(2)}) collective-permute-start(f16[2,152,608]{2,1,0:T(8,128)(2,1)S(1)} %get-tuple-element.320), channel_id=1, source_target_pairs={{0,8},{2,10},{4,12},{6,14},{8,0},{10,2},{12,4},{14,6},{16,24},{18,... | collective-permute-start | bytes 1109000 | tf_op jit(solution)/shard_map/ppermute | solution.py:78
  90.2 29.3 %collective-permute-start.21 = (f16[2,152,608]{2,1,0:T(8,128)(2,1)S(1)}, f16[2,152,608]{2,1,0:T(8,128)(2,1)S(1)}, u32[]{:S(2)}, u32[]{:S(2)}) collective-permute-start(f16[2,152,608]{2,1,0:T(8,128)(2,1)S(1)} %multiply_convert_fusion.2), channel_id=1, source_target_pairs={{0,8},{2,10},{4,12},{6,14},{8,0},{10,2},{12,4},{14,6},{16,24},{18,... | collective-permute-start | bytes 1109000 | tf_op jit(solution)/shard_map/ppermute | solution.py:78
  92.1 18.6 %collective-permute-start.25 = (f16[152,608]{1,0:T(8,128)(2,1)S(1)}, f16[152,608]{1,0:T(8,128)(2,1)S(1)}, u32[]{:S(2)}, u32[]{:S(2)}) collective-permute-start(f16[152,608]{1,0:T(8,128)(2,1)S(1)} %get-tuple-element.323), channel_id=1, source_target_pairs={{0,16},{2,18},{4,20},{6,22},{8,24},{10,26},{12,28},{14,30},{16,0},... | collective-permute-start | bytes 554504 | tf_op jit(solution)/shard_map/ppermute | solution.py:78
  103.6 15.1 %collective-permute-start.24 = (f16[152,608]{1,0:T(8,128)(2,1)S(1)}, f16[152,608]{1,0:T(8,128)(2,1)S(1)}, u32[]{:S(2)}, u32[]{:S(2)}) collective-permute-start(f16[152,608]{1,0:T(8,128)(2,1)S(1)} %get-tuple-element.325), channel_id=1, source_target_pairs={{0,16},{2,18},{4,20},{6,22},{8,24},{10,26},{12,28},{14,30},{16,0},... | collective-permute-start | bytes 554504 | tf_op jit(solution)/shard_map/ppermute | solution.py:78
  109.7 9.8 %collective-permute-start.23 = (f16[152,608]{1,0:T(8,128)(2,1)S(1)}, f16[152,608]{1,0:T(8,128)(2,1)S(1)}, u32[]{:S(2)}, u32[]{:S(2)}) collective-permute-start(f16[152,608]{1,0:T(8,128)(2,1)S(1)} %get-tuple-element.314), channel_id=1, source_target_pairs={{0,4},{2,6},{4,0},{6,2},{8,12},{10,14},{12,8},{14,10},{16,20},{18,... | collective-permute-start | bytes 554504 | tf_op jit(solution)/shard_map/ppermute | solution.py:78
  110.7 9.1 %collective-permute-start.22 = (f16[152,608]{1,0:T(8,128)(2,1)S(1)}, f16[152,608]{1,0:T(8,128)(2,1)S(1)}, u32[]{:S(2)}, u32[]{:S(2)}) collective-permute-start(f16[152,608]{1,0:T(8,128)(2,1)S(1)} %get-tuple-element.316), channel_id=1, source_target_pairs={{0,4},{2,6},{4,0},{6,2},{8,12},{10,14},{12,8},{14,10},{16,20},{18,... | collective-permute-start | bytes 554504 | tf_op jit(solution)/shard_map/ppermute | solution.py:78
  118.8 10.1 %collective-permute-start.27 = (f32[152,608]{1,0:T(8,128)S(1)}, f32[152,608]{1,0:T(8,128)S(1)}, u32[]{:S(2)}, u32[]{:S(2)}) collective-permute-start(f32[152,608]{1,0:T(8,128)S(1)} %multiply_add_fusion.5), channel_id=1, source_target_pairs={{0,1},{1,0},{2,3},{3,2},{4,5},{5,4},{6,7},{7,6},{8,9},{9,8},{10,11... | collective-permute-start | bytes 1109000 | tf_op jit(solution)/shard_map/ppermute | solution.py:91
  119.7 9.2 %collective-permute-start.26 = (f16[152,608]{1,0:T(8,128)(2,1)S(1)}, f16[152,608]{1,0:T(8,128)(2,1)S(1)}, u32[]{:S(2)}, u32[]{:S(2)}) collective-permute-start(f16[152,608]{1,0:T(8,128)(2,1)S(1)} %fusion.12), channel_id=1, source_target_pairs={{0,16},{2,18},{4,20},{6,22},{8,24},{10,26},{12,28},{14,30},{16,0},... | collective-permute-start | bytes 554504 | tf_op jit(solution)/shard_map/ppermute | solution.py:78
  133.0 63.3 %collective-permute-start.43 = (bf16[512,2432]{1,0:T(8,128)(2,1)S(1)}, bf16[512,2432]{1,0:T(8,128)(2,1)S(1)}, u32[]{:S(2)}, u32[]{:S(2)}) collective-permute-start(bf16[512,2432]{1,0:T(8,128)(2,1)S(1)} %copy-done.8), channel_id=1, source_target_pairs={{0,1},{1,0},{2,3},{3,2},{4,5},{5,4},{6,7},{7,6},{8,9},{9,8},{10,11... | collective-permute-start | bytes 7471112 | tf_op jit(solution)/shard_map/ppermute | solution.py:91
  147.7 11.4 %collective-permute-start.36 = (bf16[2,152,608]{2,1,0:T(8,128)(2,1)S(1)}, bf16[2,152,608]{2,1,0:T(8,128)(2,1)S(1)}, u32[]{:S(2)}, u32[]{:S(2)}) collective-permute-start(bf16[2,152,608]{2,1,0:T(8,128)(2,1)S(1)} %get-tuple-element.277), channel_id=1, source_target_pairs={{0,8},{2,10},{4,12},{6,14},{8,0},{10,2},{12,4},{14,6},{16,24},{18,... | collective-permute-start | bytes 1109000 | tf_op jit(solution)/shard_map/ppermute | solution.py:78
  147.7 20.6 %collective-permute-start.38 = (bf16[2,152,608]{2,1,0:T(8,128)(2,1)S(1)}, bf16[2,152,608]{2,1,0:T(8,128)(2,1)S(1)}, u32[]{:S(2)}, u32[]{:S(2)}) collective-permute-start(bf16[2,152,608]{2,1,0:T(8,128)(2,1)S(1)} %get-tuple-element.277), channel_id=1, source_target_pairs={{0,24},{2,26},{4,28},{6,30},{8,16},{10,18},{12,20},{14,22},{16,8},... | collective-permute-start | bytes 1109000 | tf_op jit(solution)/shard_map/ppermute | solution.py:78
  150.2 22.0 %collective-permute-start.35 = (bf16[2,152,608]{2,1,0:T(8,128)(2,1)S(1)}, bf16[2,152,608]{2,1,0:T(8,128)(2,1)S(1)}, u32[]{:S(2)}, u32[]{:S(2)}) collective-permute-start(bf16[2,152,608]{2,1,0:T(8,128)(2,1)S(1)} %get-tuple-element.277), channel_id=1, source_target_pairs={{0,4},{2,6},{4,0},{6,2},{8,12},{10,14},{12,8},{14,10},{16,20},{18,... | collective-permute-start | bytes 1109000 | tf_op jit(solution)/shard_map/ppermute | solution.py:78
  168.3 11.9 %collective-permute-start.39 = (bf16[2,152,608]{2,1,0:T(8,128)(2,1)S(1)}, bf16[2,152,608]{2,1,0:T(8,128)(2,1)S(1)}, u32[]{:S(2)}, u32[]{:S(2)}) collective-permute-start(bf16[2,152,608]{2,1,0:T(8,128)(2,1)S(1)} %collective-permute-done.38), channel_id=1, source_target_pairs={{0,4},{2,6},{4,0},{6,2},{8,12},{10,14},{12,8},{14,10},{16,20},{18,... | collective-permute-start | bytes 1109000 | tf_op jit(solution)/shard_map/ppermute | solution.py:78
  168.8 18.6 %collective-permute-start.37 = (bf16[2,152,608]{2,1,0:T(8,128)(2,1)S(1)}, bf16[2,152,608]{2,1,0:T(8,128)(2,1)S(1)}, u32[]{:S(2)}, u32[]{:S(2)}) collective-permute-start(bf16[2,152,608]{2,1,0:T(8,128)(2,1)S(1)} %collective-permute-done.36), channel_id=1, source_target_pairs={{0,4},{2,6},{4,0},{6,2},{8,12},{10,14},{12,8},{14,10},{16,20},{18,... | collective-permute-start | bytes 1109000 | tf_op jit(solution)/shard_map/ppermute | solution.py:78
  170.3 18.3 %collective-permute-start.40 = (bf16[2,152,608]{2,1,0:T(8,128)(2,1)S(1)}, bf16[2,152,608]{2,1,0:T(8,128)(2,1)S(1)}, u32[]{:S(2)}, u32[]{:S(2)}) collective-permute-start(bf16[2,152,608]{2,1,0:T(8,128)(2,1)S(1)} %get-tuple-element.277), channel_id=1, source_target_pairs={{0,16},{2,18},{4,20},{6,22},{8,24},{10,26},{12,28},{14,30},{16,0},... | collective-permute-start | bytes 1109000 | tf_op jit(solution)/shard_map/ppermute | solution.py:78
  189.5 11.0 %collective-permute-start.44 = (bf16[2,152,608]{2,1,0:T(8,128)(2,1)S(1)}, bf16[2,152,608]{2,1,0:T(8,128)(2,1)S(1)}, u32[]{:S(2)}, u32[]{:S(2)}) collective-permute-start(bf16[2,152,608]{2,1,0:T(8,128)(2,1)S(1)} %collective-permute-done.40), channel_id=1, source_target_pairs={{0,4},{2,6},{4,0},{6,2},{8,12},{10,14},{12,8},{14,10},{16,20},{18,... | collective-permute-start | bytes 1109000 | tf_op jit(solution)/shard_map/ppermute | solution.py:78
  189.9 11.0 %collective-permute-start.45 = (bf16[4,2,152,608]{3,2,1,0:T(8,128)(2,1)S(1)}, bf16[4,2,152,608]{3,2,1,0:T(8,128)(2,1)S(1)}, u32[]{:S(2)}, u32[]{:S(2)}) collective-permute-start(bf16[4,2,152,608]{3,2,1,0:T(8,128)(2,1)S(1)} %pad_maximum_fusion.refs_0_), channel_id=1, source_target_pairs={{0,2},{2,0},{4,6},{6,4},{8,10},{10,8},{12,14},{14,12},{16,18},{18,... | collective-permute-start | bytes 4435976 | tf_op jit(solution)/shard_map/ppermute | solution.py:78
  (39 other events, 294.7 us)

commit v11 on v10

--- a/solution.py
+++ b/solution.py
@@ -305,22 +305,22 @@
             input_output_aliases=aliases, mib=20,
         )
 
-    def spread(stacks):
-        count, _, _, f = stacks[0].shape
+    def spread(blocks, *arrays):
+        f = arrays[0].shape[-1]
         tiles = [
             (net, start, min(TILE, f - start)) for net in range(2) for start in range(0, f, TILE)
         ]
 
         def kernel(*refs):
-            stack_refs, out_refs, (wide_ref, done_ref, sem) = refs[:4], refs[4:6], refs[6:]
+            array_refs, refs = refs[: len(arrays)], refs[len(arrays) :]
+            out_refs, (wide_ref, done_ref, sem) = refs[:2], refs[2:]
             eye = identity(TILE)
             copies = []
             for step, (net, start, size) in enumerate(tiles):
-                for n, ref in enumerate(stack_refs):
-                    for at in range(count):
-                        k, i = divmod((n & 1) * count + at, inner)
-                        block = ref[at, net, :, start : start + size].astype(jnp.float32)
-                        wide_ref[owner(k, i, n >> 1), :, :size] = block
+                for (k, i, other), (n, at) in blocks.items():
+                    ref = array_refs[n] if at is None else array_refs[n].at[at]
+                    block = ref[net, :, start : start + size].astype(jnp.float32)
+                    wide_ref[owner(k, i, other), :, :size] = block
                 flat = wide_ref[:, :, :size].reshape(D, size).astype(jnp.bfloat16)
                 slot = step & 1
                 if step >= 2:
@@ -337,8 +337,8 @@
                 copy.wait()
 
         return call(
-            kernel, [array((f, D), jnp.bfloat16)] * 2, *stacks,
-            in_specs=[VMEM] * 4, out_specs=[ANY] * 2,
+            kernel, [array((f, D), jnp.bfloat16)] * 2, *arrays,
+            in_specs=[VMEM] * len(arrays), out_specs=[ANY] * 2,
             scratch_shapes=[
                 pltpu.VMEM((n_dp, width, TILE), jnp.float32),
                 pltpu.VMEM((2, TILE, D), jnp.bfloat16),
@@ -526,8 +526,7 @@
             return shrink(add_widened(own, got, 0), 0)
 
         near = to_plane(step(first_planes, own, *got), 1)
-        for j in range(n_tensor):
-            fake_far(j)
+        fake_far(0)
         both = multiply_student(1)
 
         def second_middle(both):
@@ -538,6 +537,8 @@
         got_far, got = (
             [to_middle(value, i) for i, value in enumerate(values, 1)] for values in sent
         )
+        for j in range(1, n_tensor):
+            fake_far(j)
         fake_mine = fake_total(0)
         fake_others = [fake_total(j) for j in range(1, n_tensor)]
         others_got = [from_tensor(value, j) for j, value in enumerate(fake_others, 1)]
@@ -584,15 +585,18 @@
             mine[k] = [value] + [to_middle(value, -i) for i in range(1, inner)]
 
         spread_middle(0, own)
-        planes_got = {k: to_plane(own, k) for k in (1, 3, 2)}
-        spread_middle(1, step(lambda value: value, planes_got[1]))
-        spread_middle(3, step(lambda value: value, planes_got[3]))
-        early = [value for k in (0, 1, 3) for value in mine[k]]
-        early = step(lambda *values: values, *early)
-        mine = {k: list(early[n * inner : (n + 1) * inner]) for n, k in enumerate((0, 1, 3))}
-        spread_middle(2, step(lambda value: value, planes_got[2]))
-        first_half = step(lambda *values: jnp.stack(values), *mine[0], *mine[1])
-        theirs = [to_core(first_half)]
+        far_got, near_got = to_plane(own, 2), to_plane(own, 1)
+        spread_middle(1, step(lambda value: value, near_got))
+        value = step(lambda value: value, far_got)
+        spread_middle(2, value)
+        passed_on = to_plane(value, 1)
+        arrays = [step(lambda *values: jnp.stack(values), *mine[0], *mine[1])]
+        arrays.append(to_core(arrays[0]))
+        spread_middle(3, step(lambda value: value, passed_on))
+        arrays.append(step(lambda *values: jnp.stack(values), *mine[2]))
+        arrays.append(to_core(arrays[2]))
+        mine[3] = step(lambda *values: values, *mine[3])
+        raw = step(lambda *values: values, *raw)
         hidden = step(lambda *values: values, *[value for group in diagonal for value in group])
         mate_others = [to_core(value) for value in hidden]
         mate_others = [mate_others[: n_tensor - 1], mate_others[n_tensor - 1 :]]
@@ -603,10 +607,16 @@
             back_student = back(back_student, 0, pieces, j, 0, r)
         for j in range(1, n_tensor):
             back_fake = back(back_fake, 1, [raw[j - 1]], j, 0, r)
-        second_half = step(lambda *values: jnp.stack(values), *mine[2], *mine[3])
-        theirs.append(to_core(second_half))
-        stacks = [first_half, second_half, *theirs]
-        params = step(lambda *values: spread(values), *stacks)
+        blocks = {}
+        for other in range(2):
+            for i in range(inner):
+                for k in range(2):
+                    blocks[k, i, other] = other, k * inner + i
+                blocks[2, i, other] = 2 + other, i
+        for i, value in enumerate(mine[3]):
+            blocks[3, i, 0], blocks[3, i, 1] = (len(arrays), None), (len(arrays) + 1, None)
+            arrays += [value, to_core(value)]
+        params = step(lambda *values: spread(blocks, *values), *arrays)
 
         new_states = [value.T for value in updated]
         return (back_student, back_fake, *new_states, *params)

time: 210 us -> 211 us (level)
  waiting for transfers between devices: 103 us -> 107 us
  starting transfers between devices: 44.8 us -> 42.3 us
    ppermute x34 -> x36, waiting for transfers between devices: 74.4 us -> 78.3 us  [move_dp(): return lax.ppermute(value, 'dp', perm)]
    ppermute x34 -> x36, starting transfers between devices: 30.8 us -> 28.3 us  [move_dp(): return lax.ppermute(value, 'dp', perm)]
  transfers between devices with their start and end apart: 47 -> 49, of which waited for: 23 -> 23; matrix products, arithmetic and copies ran while one was open for 3% -> 3% of each run, Pallas kernels for 17% -> 17%
where the time goes in v11:
time: 211 us
  waiting for transfers between devices  107 us (51%)
  Pallas kernels  44.9 us (21%)
  starting transfers between devices  42.3 us (20%)
  other arithmetic  5.9 us (3%)
  between operations  5.43 us (3%)
  local copies, waits for them, and re-layouts  5.09 us (2%)
    ppermute x36, waiting for transfers between devices, move_dp(): return lax.ppermute(value, 'dp', perm)  78.3 us
    pallas_call x15, Pallas kernels, call(): pl.pallas_call(kernel, out_shape=out_shape, compiler_params=pltpu.Compile...  44.9 us
    ppermute x36, starting transfers between devices, move_dp(): return lax.ppermute(value, 'dp', perm)  28.3 us
    ppermute x5, waiting for transfers between devices, hops(): got = lax.ppermute(value, axis, perm)  17.2 us
    ppermute x6, waiting for transfers between devices, from_tensor(): return lax.ppermute(value, 'tensor', perm)  11.5 us
    ppermute x5, starting transfers between devices, hops(): got = lax.ppermute(value, axis, perm)  7.86 us
    ppermute x6, starting transfers between devices, from_tensor(): return lax.ppermute(value, 'tensor', perm)  6.06 us
  transfers between devices with their start and end apart: 49, of which 23 were waited for; matrix products, arithmetic and copies ran while one was open for 3% of the time, Pallas kernels for 17%

profile of v11, /device:TPU:0, one launch (start us, length us, event | category | flops | bytes accessed | tf_op | source)
XLA Modules:
  0.0 210.6 jit_solution(2741180016043216795)
XLA Ops:
  5.6 2.2 %shard_map.205 = (bf16[2,4,152,512]{3,2,1,0:T(8,128)(2,1)S(1)}, bf16[2,4,152,512]{3,2,1,0:T(8,128)(2,1)S(1)}, f32[8,128]{1,0:T(8,128)S(1)}) custom-call(bf16[512,2432]{1,0:T(8,128)(2,1)S(1)} %copy-done.6), custom_call_target="tpu_custom_call" | custom-call | tf_op jit(solution)/shard_map/pallas_call | solution.py:56
  8.5 2.9 %collective-permute-start.6 = (bf16[1,608,512]{2,1,0:T(8,128)(2,1)S(1)}, bf16[1,608,512]{2,1,0:T(8,128)(2,1)}, u32[]{:S(2)}, u32[]{:S(2)}) collective-permute-start(bf16[1,608,512]{2,1,0:T(8,128)(2,1)S(1)} %get-tuple-element.176), channel_id=1, source_target_pairs={{0,1},{1,0},{2,3},{3,2},{4,5},{5,4},{6,7},{7,6},{8,9},{9,8},{10,11... | collective-permute-start | bytes 1867784 | tf_op jit(solution)/shard_map/ppermute | solution.py:91
  11.4 3.4 %shard_map.206 = (bf16[2,2,152,512]{3,2,1,0:T(8,128)(2,1)}, bf16[2,2,152,512]{3,2,1,0:T(8,128)(2,1)}, bf16[2,2,152,512]{3,2,1,0:T(8,128)(2,1)S(1)}, bf16[2,2,152,512]{3,2,1,0:T(8,128)(2,1)}, f32[8,128]{1,0:T(8,128)S(1)}) custom-call(bf16[512,2432]{1,0:T(8,128)(2,1)S(1)} %copy-done.4), custom_call_target="tpu_custom_call" | custom-call | tf_op jit(solution)/shard_map/pallas_call | solution.py:56
  14.8 2.2 %shard_map.207 = (f32[8,128]{1,0:T(8,128)S(1)}, bf16[2,608,512]{2,1,0:T(8,128)(2,1)}) custom-call(f32[2]{0:T(128)S(1)} %divide_bitcast_fusion.scale_ref, bf16[608,1024]{1,0:T(8,128)(2,1)S(1)} %copy-done.14, f32[8,128]{1,0:T(8,128)S(1)} %get-tuple-element.171.top_s_ref, f32[8,128]{1,0:T(8,128)S(1)} %get-tuple-element.172.top_f_ref, ...), custom_call_target="tpu_custom_call" | custom-call | tf_op jit(solution)/shard_map/pallas_call | solution.py:56
  17.5 2.1 %shard_map.208 = f32[1216,608]{1,0:T(8,128)S(1)} custom-call(bf16[1216,512]{1,0:T(8,128)(2,1)S(1)} %bitcast.94, bf16[1216,512]{1,0:T(8,128)(2,1)S(1)} %bitcast.96, bf16[1,608,512]{2,1,0:T(8,128)(2,1)S(1)} %get-tuple-element.181.refs_2_, bf16[1,608,512]{2,1,0:T(8,128)(2,1)S(1)} %collective-permute-done.8.refs_3_), custom_call_target="tpu_custom_call" | custom-call | tf_op jit(solution)/shard_map/pallas_call | solution.py:56
  27.5 2.6 %collective-permute-start.12 = (f32[8,128]{1,0:T(8,128)S(1)}, f32[8,128]{1,0:T(8,128)S(1)}, u32[]{:S(2)}, u32[]{:S(2)}) collective-permute-start(f32[8,128]{1,0:T(8,128)S(1)} %max.29), channel_id=1, source_target_pairs={{0,16},{2,18},{4,20},{6,22},{8,24},{10,26},{12,28},{14,30},{16,0},... | collective-permute-start | bytes 12296 | tf_op jit(solution)/shard_map/ppermute | solution.py:376
  37.8 3.6 %shard_map.209 = f32[1216,608]{1,0:T(8,128)S(1)} custom-call(bf16[1216,512]{1,0:T(8,128)(2,1)S(1)} %bitcast.95, bf16[1216,512]{1,0:T(8,128)(2,1)S(1)} %bitcast.97, bf16[1,608,512]{2,1,0:T(8,128)(2,1)} %collective-permute-done.6.refs_2_, bf16[1,608,512]{2,1,0:T(8,128)(2,1)} %collective-permute-done.11.refs_3_), custom_call_target="tpu_custom_call" | custom-call | tf_op jit(solution)/shard_map/pallas_call | solution.py:56
  43.0 3.2 %shard_map.210.refs_4_ = bf16[608,1024]{1,0:T(8,128)(2,1)} custom-call(f32[2]{0:T(128)S(1)} %divide_bitcast_fusion.scale_ref, bf16[608,2432]{1,0:T(8,128)(2,1)S(1)} %copy-done, bf16[512,2432]{1,0:T(8,128)(2,1)S(1)} %copy-done.5), custom_call_target="tpu_custom_call" | custom-call | tf_op jit(solution)/shard_map/pallas_call | solution.py:56
  46.2 3.2 %shard_map.211.refs_1_ = bf16[608,1024]{1,0:T(8,128)(2,1)} custom-call(f32[2]{0:T(128)S(1)} %divide_bitcast_fusion.scale_ref, bf16[608,2432]{1,0:T(8,128)(2,1)S(1)} %copy-done.2, bf16[512,2432]{1,0:T(8,128)(2,1)S(1)} %copy-done.7), custom_call_target="tpu_custom_call" | custom-call | tf_op jit(solution)/shard_map/pallas_call | solution.py:56
  49.4 11.2 %collective-permute-done.16 = f32[8,128]{1,0:T(8,128)S(1)} collective-permute-done((f32[8,128]{1,0:T(8,128)S(1)}, f32[8,128]{1,0:T(8,128)S(1)}, u32[]{:S(2)}, u32[]{:S(2)}) %collective-permute-start.16) | collective-permute-done | bytes 4128 | tf_op jit(solution)/shard_map/ppermute | solution.py:376
  66.2 4.5 %shard_map.212 = f32[608,608]{1,0:T(8,128)S(1)} custom-call(bf16[608,512]{1,0:T(8,128)(2,1)} %bitcast.13.refs_0_, bf16[608,512]{1,0:T(8,128)(2,1)} %bitcast.14.refs_1_, bf16[608,512]{1,0:T(8,128)(2,1)} %bitcast.15.refs_2_, bf16[608,512]{1,0:T(8,128)(2,1)} %bitcast.16.refs_3_, bf16[2,608,512]{2,1,0:T(8,128)(2,1)} %get-tuple-element.228.refs_4_, ...), custom_call_target="tpu_custom_call" | custom-call | tf_op jit(solution)/shard_map/pallas_call | solution.py:56
  75.1 9.7 %collective-permute-done.19 = f16[4,152,608]{2,1,0:T(8,128)(2,1)S(1)} collective-permute-done((f16[4,152,608]{2,1,0:T(8,128)(2,1)S(1)}, f16[4,152,608]{2,1,0:T(8,128)(2,1)S(1)}, u32[]{:S(2)}, u32[]{:S(2)}) %collective-permute-start.19) | collective-permute-done | bytes 739360 | tf_op jit(solution)/shard_map/ppermute | solution.py:78
  86.8 3.2 %collective-permute-done.18 = f16[2,152,608]{2,1,0:T(8,128)(2,1)S(1)} collective-permute-done((f16[2,152,608]{2,1,0:T(8,128)(2,1)S(1)}, f16[2,152,608]{2,1,0:T(8,128)(2,1)S(1)}, u32[]{:S(2)}, u32[]{:S(2)}) %collective-permute-start.18) | collective-permute-done | bytes 369696 | tf_op jit(solution)/shard_map/ppermute | solution.py:78
  92.0 2.7 %collective-permute-start.25 = (f16[152,608]{1,0:T(8,128)(2,1)S(1)}, f16[152,608]{1,0:T(8,128)(2,1)S(1)}, u32[]{:S(2)}, u32[]{:S(2)}) collective-permute-start(f16[152,608]{1,0:T(8,128)(2,1)S(1)} %get-tuple-element.321), channel_id=1, source_target_pairs={{0,16},{2,18},{4,20},{6,22},{8,24},{10,26},{12,28},{14,30},{16,0},... | collective-permute-start | bytes 554504 | tf_op jit(solution)/shard_map/ppermute | solution.py:78
  94.7 4.2 %shard_map.213 = f32[608,608]{1,0:T(8,128)S(1)} custom-call(bf16[608,512]{1,0:T(8,128)(2,1)S(1)} %bitcast.99, bf16[608,512]{1,0:T(8,128)(2,1)} %bitcast.23.refs_1_, bf16[608,512]{1,0:T(8,128)(2,1)} %bitcast.24.refs_2_, bf16[608,512]{1,0:T(8,128)(2,1)S(1)} %bitcast.98, bf16[2,608,512]{2,1,0:T(8,128)(2,1)} %get-tuple-element.228.refs_4_, ...), custom_call_target="tpu_custom_call" | custom-call | tf_op jit(solution)/shard_map/pallas_call | solution.py:56
  102.3 2.1 %collective-permute-start.24 = (f16[152,608]{1,0:T(8,128)(2,1)S(1)}, f16[152,608]{1,0:T(8,128)(2,1)S(1)}, u32[]{:S(2)}, u32[]{:S(2)}) collective-permute-start(f16[152,608]{1,0:T(8,128)(2,1)S(1)} %get-tuple-element.322), channel_id=1, source_target_pairs={{0,16},{2,18},{4,20},{6,22},{8,24},{10,26},{12,28},{14,30},{16,0},... | collective-permute-start | bytes 554504 | tf_op jit(solution)/shard_map/ppermute | solution.py:78
  104.5 3.0 %collective-permute-done.25 = f16[152,608]{1,0:T(8,128)(2,1)S(1)} collective-permute-done((f16[152,608]{1,0:T(8,128)(2,1)S(1)}, f16[152,608]{1,0:T(8,128)(2,1)S(1)}, u32[]{:S(2)}, u32[]{:S(2)}) %collective-permute-start.25) | collective-permute-done | bytes 184864 | tf_op jit(solution)/shard_map/ppermute | solution.py:78
  107.5 10.3 %collective-permute-done.24 = f16[152,608]{1,0:T(8,128)(2,1)S(1)} collective-permute-done((f16[152,608]{1,0:T(8,128)(2,1)S(1)}, f16[152,608]{1,0:T(8,128)(2,1)S(1)}, u32[]{:S(2)}, u32[]{:S(2)}) %collective-permute-start.24) | collective-permute-done | bytes 184864 | tf_op jit(solution)/shard_map/ppermute | solution.py:78
  119.2 8.5 %collective-permute-done.27 = f32[152,608]{1,0:T(8,128)S(1)} collective-permute-done((f32[152,608]{1,0:T(8,128)S(1)}, f32[152,608]{1,0:T(8,128)S(1)}, u32[]{:S(2)}, u32[]{:S(2)}) %collective-permute-start.27) | collective-permute-done | bytes 369696 | tf_op jit(solution)/shard_map/ppermute | solution.py:91
  128.8 3.1 %collective-permute-done.28 = f32[8,128]{1,0:T(8,128)S(1)} collective-permute-done((f32[8,128]{1,0:T(8,128)S(1)}, f32[8,128]{1,0:T(8,128)S(1)}, u32[]{:S(2)}, u32[]{:S(2)}) %collective-permute-start.28) | collective-permute-done | bytes 4128 | tf_op jit(solution)/shard_map/ppermute | solution.py:91
  132.5 2.3 %collective-permute-start.31 = (f32[8,128]{1,0:T(8,128)S(1)}, f32[8,128]{1,0:T(8,128)S(1)}, u32[]{:S(2)}, u32[]{:S(2)}) collective-permute-start(f32[8,128]{1,0:T(8,128)S(1)} %add.78), channel_id=1, source_target_pairs={{0,16},{2,18},{4,20},{6,22},{8,24},{10,26},{12,28},{14,30},{16,0},... | collective-permute-start | bytes 12296 | tf_op jit(solution)/shard_map/ppermute | solution.py:78
  137.0 3.2 %collective-permute-done.32 = f32[8,128]{1,0:T(8,128)S(1)} collective-permute-done((f32[8,128]{1,0:T(8,128)S(1)}, f32[8,128]{1,0:T(8,128)S(1)}, u32[]{:S(2)}, u32[]{:S(2)}) %collective-permute-start.32) | collective-permute-done | bytes 4128 | tf_op jit(solution)/shard_map/ppermute | solution.py:78
  140.2 2.3 %collective-permute-start.34 = (f32[8,128]{1,0:T(8,128)S(1)}, f32[8,128]{1,0:T(8,128)S(1)}, u32[]{:S(2)}, u32[]{:S(2)}) collective-permute-start(f32[8,128]{1,0:T(8,128)S(1)} %add_add_fusion.1), channel_id=1, source_target_pairs={{0,4},{2,6},{4,0},{6,2},{8,12},{10,14},{12,8},{14,10},{16,20},{18,... | collective-permute-start | bytes 12296 | tf_op jit(solution)/shard_map/ppermute | solution.py:78
  145.6 2.1 shard_map.215
  150.2 16.0 %collective-permute-done.37 = bf16[2,152,608]{2,1,0:T(8,128)(2,1)S(1)} collective-permute-done((bf16[2,152,608]{2,1,0:T(8,128)(2,1)S(1)}, bf16[2,152,608]{2,1,0:T(8,128)(2,1)S(1)}, u32[]{:S(2)}, u32[]{:S(2)}) %collective-permute-start.37) | collective-permute-done | bytes 369696 | tf_op jit(solution)/shard_map/ppermute | solution.py:78
  168.7 9.4 %collective-permute-done.40 = bf16[2,152,608]{2,1,0:T(8,128)(2,1)S(1)} collective-permute-done((bf16[2,152,608]{2,1,0:T(8,128)(2,1)S(1)}, bf16[2,152,608]{2,1,0:T(8,128)(2,1)S(1)}, u32[]{:S(2)}, u32[]{:S(2)}) %collective-permute-start.40) | collective-permute-done | bytes 369696 | tf_op jit(solution)/shard_map/ppermute | solution.py:78
  179.1 7.3 %collective-permute-done.42 = bf16[2,152,608]{2,1,0:T(8,128)(2,1)S(1)} collective-permute-done((bf16[2,152,608]{2,1,0:T(8,128)(2,1)S(1)}, bf16[2,152,608]{2,1,0:T(8,128)(2,1)S(1)}, u32[]{:S(2)}, u32[]{:S(2)}) %collective-permute-start.42) | collective-permute-done | bytes 369696 | tf_op jit(solution)/shard_map/ppermute | solution.py:78
  186.6 6.9 %collective-permute-done.41.refs_6_ = bf16[2,152,608]{2,1,0:T(8,128)(2,1)S(1)} collective-permute-done((bf16[2,152,608]{2,1,0:T(8,128)(2,1)S(1)}, bf16[2,152,608]{2,1,0:T(8,128)(2,1)S(1)}, u32[]{:S(2)}, u32[]{:S(2)}) %collective-permute-start.41) | collective-permute-done | bytes 369696 | tf_op jit(solution)/shard_map/ppermute | solution.py:78
  194.5 2.1 collective-permute-done.43.refs_1_
  197.5 4.4 %shard_map.216 = bf16[608,1024]{1,0:T(8,128)(2,1)} custom-call(f32[2]{0:T(128)S(1)} %divide_bitcast_fusion.scale_ref, bf16[608,2432]{1,0:T(8,128)(2,1)S(1)} %copy-done.1, bf16[2,2,152,512]{3,2,1,0:T(8,128)(2,1)} %collective-permute-done.refs_0_, bf16[2,2,152,512]{3,2,1,0:T(8,128)(2,1)S(1)} %collective-permute-done.43.refs_1_, ...), custom_call_target="tpu_custom_call", output_to_operand_aliasing={{}: (6, {})} | custom-call | tf_op jit(solution)/shard_map/pallas_call | solution.py:56
  202.0 3.2 %shard_map.217 = bf16[608,1024]{1,0:T(8,128)(2,1)} custom-call(f32[2]{0:T(128)S(1)} %divide_bitcast_fusion.scale_ref, bf16[608,2432]{1,0:T(8,128)(2,1)S(1)} %copy-done.3, bf16[512,2432]{1,0:T(8,128)(2,1)S(1)} %collective-permute-done.29.refs_0_, bf16[608,1024]{1,0:T(8,128)(2,1)} %shard_map.211.refs_1_), custom_call_target="tpu_custom_call", output_to_operand_aliasing={{}: (3, {})} | custom-call | tf_op jit(solution)/shard_map/pallas_call | solution.py:56
  205.2 5.2 %shard_map.218 = (bf16[608,2432]{1,0:T(8,128)(2,1)}, bf16[608,2432]{1,0:T(8,128)(2,1)}) custom-call(bf16[4,2,152,608]{3,2,1,0:T(8,128)(2,1)S(1)} %pad_maximum_fusion.refs_0_, bf16[4,2,152,608]{3,2,1,0:T(8,128)(2,1)S(1)} %collective-permute-done.45.refs_1_, bf16[2,2,152,608]{3,2,1,0:T(8,128)(2,1)S(1)} %pad_maximum_fusion.1.refs_2_, ...), custom_call_target="tpu_custom_call" | custom-call | tf_op jit(solution)/shard_map/pallas_call | solution.py:56
  (162 shorter events, 53.0 us)
Async XLA Ops:
  7.9 9.7 %collective-permute-start.5 = (bf16[2,4,152,512]{3,2,1,0:T(8,128)(2,1)S(1)}, bf16[2,4,152,512]{3,2,1,0:T(8,128)(2,1)S(1)}, u32[]{:S(2)}, u32[]{:S(2)}) collective-permute-start(bf16[2,4,152,512]{3,2,1,0:T(8,128)(2,1)S(1)} %get-tuple-element.175), channel_id=1, source_target_pairs={{0,2},{2,0},{4,6},{6,4},{8,10},{10,8},{12,14},{14,12},{16,18},{18,... | collective-permute-start | bytes 3735560 | tf_op jit(solution)/shard_map/ppermute | solution.py:78
  8.5 18.5 %collective-permute-start.6 = (bf16[1,608,512]{2,1,0:T(8,128)(2,1)S(1)}, bf16[1,608,512]{2,1,0:T(8,128)(2,1)}, u32[]{:S(2)}, u32[]{:S(2)}) collective-permute-start(bf16[1,608,512]{2,1,0:T(8,128)(2,1)S(1)} %get-tuple-element.176), channel_id=1, source_target_pairs={{0,1},{1,0},{2,3},{3,2},{4,5},{5,4},{6,7},{7,6},{8,9},{9,8},{10,11... | collective-permute-start | bytes 1867784 | tf_op jit(solution)/shard_map/ppermute | solution.py:91
  17.0 25.9 %collective-permute-start.2 = (bf16[2,608,512]{2,1,0:T(8,128)(2,1)}, bf16[2,608,512]{2,1,0:T(8,128)(2,1)}, u32[]{:S(2)}, u32[]{:S(2)}) collective-permute-start(bf16[2,608,512]{2,1,0:T(8,128)(2,1)} %get-tuple-element.228.refs_4_), channel_id=1, source_target_pairs={{0,2},{2,0},{4,6},{6,4},{8,10},{10,8},{12,14},{14,12},{16,18},{18,... | collective-permute-start | bytes 3735560 | tf_op jit(solution)/shard_map/ppermute | solution.py:78
  25.0 9.4 %collective-permute-start.3 = (bf16[2,2,152,512]{3,2,1,0:T(8,128)(2,1)}, bf16[2,2,152,512]{3,2,1,0:T(8,128)(2,1)}, u32[]{:S(2)}, u32[]{:S(2)}) collective-permute-start(bf16[2,2,152,512]{3,2,1,0:T(8,128)(2,1)} %get-tuple-element.165), channel_id=1, source_target_pairs={{0,2},{2,0},{4,6},{6,4},{8,10},{10,8},{12,14},{14,12},{16,18},{18,... | collective-permute-start | bytes 1867784 | tf_op jit(solution)/shard_map/ppermute | solution.py:78
  27.0 14.3 %collective-permute-start.4 = (bf16[2,2,152,512]{3,2,1,0:T(8,128)(2,1)}, bf16[2,2,152,512]{3,2,1,0:T(8,128)(2,1)}, u32[]{:S(2)}, u32[]{:S(2)}) collective-permute-start(bf16[2,2,152,512]{3,2,1,0:T(8,128)(2,1)} %get-tuple-element.201), channel_id=1, source_target_pairs={{0,2},{2,0},{4,6},{6,4},{8,10},{10,8},{12,14},{14,12},{16,18},{18,... | collective-permute-start | bytes 1867784 | tf_op jit(solution)/shard_map/ppermute | solution.py:78
  32.0 34.1 %collective-permute-start = (bf16[2,2,152,512]{3,2,1,0:T(8,128)(2,1)}, bf16[2,2,152,512]{3,2,1,0:T(8,128)(2,1)}, u32[]{:S(2)}, u32[]{:S(2)}) collective-permute-start(bf16[2,2,152,512]{3,2,1,0:T(8,128)(2,1)} %get-tuple-element.210), channel_id=1, source_target_pairs={{0,1},{1,0},{2,3},{3,2},{4,5},{5,4},{6,7},{7,6},{8,9},{9,8},{10,11... | collective-permute-start | bytes 1867784 | tf_op jit(solution)/shard_map/ppermute | solution.py:91
  34.4 31.7 %collective-permute-start.1 = (bf16[2,2,152,512]{3,2,1,0:T(8,128)(2,1)}, bf16[2,2,152,512]{3,2,1,0:T(8,128)(2,1)}, u32[]{:S(2)}, u32[]{:S(2)}) collective-permute-start(bf16[2,2,152,512]{3,2,1,0:T(8,128)(2,1)} %get-tuple-element.165), channel_id=1, source_target_pairs={{0,3},{1,2},{2,1},{3,0},{4,7},{5,6},{6,5},{7,4},{8,11},{9,10},{10,... | collective-permute-start | bytes 1867784 | tf_op jit(solution)/shard_map/ppermute | solution.py:100
  34.5 26.0 %collective-permute-start.16 = (f32[8,128]{1,0:T(8,128)S(1)}, f32[8,128]{1,0:T(8,128)S(1)}, u32[]{:S(2)}, u32[]{:S(2)}) collective-permute-start(f32[8,128]{1,0:T(8,128)S(1)} %max.30), channel_id=1, source_target_pairs={{0,1},{1,0},{2,3},{3,2},{4,5},{5,4},{6,7},{7,6},{8,9},{9,8},{10,11... | collective-permute-start | bytes 12296 | tf_op jit(solution)/shard_map/ppermute | solution.py:376
  41.3 30.0 %collective-permute-start.15 = (f16[4,152,608]{2,1,0:T(8,128)(2,1)}, f16[4,152,608]{2,1,0:T(8,128)(2,1)}, u32[]{:S(2)}, u32[]{:S(2)}) collective-permute-start(f16[4,152,608]{2,1,0:T(8,128)(2,1)} %get-tuple-element.311), channel_id=1, source_target_pairs={{0,4},{2,6},{4,0},{6,2},{8,12},{10,14},{12,8},{14,10},{16,20},{18,... | collective-permute-start | bytes 2217992 | tf_op jit(solution)/shard_map/ppermute | solution.py:78
  62.4 32.3 %collective-permute-start.14 = (bf16[2,2,152,512]{3,2,1,0:T(8,128)(2,1)}, bf16[2,2,152,512]{3,2,1,0:T(8,128)(2,1)}, u32[]{:S(2)}, u32[]{:S(2)}) collective-permute-start(bf16[2,2,152,512]{3,2,1,0:T(8,128)(2,1)} %copy-done.15), channel_id=1, source_target_pairs={{0,1},{1,0},{2,3},{3,2},{4,5},{5,4},{6,7},{7,6},{8,9},{9,8},{10,11... | collective-permute-start | bytes 1867784 | tf_op jit(solution)/shard_map/ppermute | solution.py:91
  64.5 20.4 %collective-permute-start.19 = (f16[4,152,608]{2,1,0:T(8,128)(2,1)S(1)}, f16[4,152,608]{2,1,0:T(8,128)(2,1)S(1)}, u32[]{:S(2)}, u32[]{:S(2)}) collective-permute-start(f16[4,152,608]{2,1,0:T(8,128)(2,1)S(1)} %get-tuple-element.309), channel_id=1, source_target_pairs={{0,4},{2,6},{4,0},{6,2},{8,12},{10,14},{12,8},{14,10},{16,20},{18,... | collective-permute-start | bytes 2217992 | tf_op jit(solution)/shard_map/ppermute | solution.py:78
  70.8 19.2 %collective-permute-start.18 = (f16[2,152,608]{2,1,0:T(8,128)(2,1)S(1)}, f16[2,152,608]{2,1,0:T(8,128)(2,1)S(1)}, u32[]{:S(2)}, u32[]{:S(2)}) collective-permute-start(f16[2,152,608]{2,1,0:T(8,128)(2,1)S(1)} %fusion.4), channel_id=1, source_target_pairs={{0,4},{2,6},{4,0},{6,2},{8,12},{10,14},{12,8},{14,10},{16,20},{18,... | collective-permute-start | bytes 1109000 | tf_op jit(solution)/shard_map/ppermute | solution.py:78
  71.3 23.4 %collective-permute-start.13 = (bf16[2,2,152,512]{3,2,1,0:T(8,128)(2,1)}, bf16[2,2,152,512]{3,2,1,0:T(8,128)(2,1)S(1)}, u32[]{:S(2)}, u32[]{:S(2)}) collective-permute-start(bf16[2,2,152,512]{3,2,1,0:T(8,128)(2,1)} %get-tuple-element.201), channel_id=1, source_target_pairs={{0,3},{1,2},{2,1},{3,0},{4,7},{5,6},{6,5},{7,4},{8,11},{9,10},{10,... | collective-permute-start | bytes 1867784 | tf_op jit(solution)/shard_map/ppermute | solution.py:100
  73.5 18.4 %collective-permute-start.17 = (f16[2,152,608]{2,1,0:T(8,128)(2,1)S(1)}, f16[2,152,608]{2,1,0:T(8,128)(2,1)S(1)}, u32[]{:S(2)}, u32[]{:S(2)}) collective-permute-start(f16[2,152,608]{2,1,0:T(8,128)(2,1)S(1)} %get-tuple-element.318), channel_id=1, source_target_pairs={{0,8},{2,10},{4,12},{6,14},{8,0},{10,2},{12,4},{14,6},{16,24},{18,... | collective-permute-start | bytes 1109000 | tf_op jit(solution)/shard_map/ppermute | solution.py:78
  85.1 17.0 %collective-permute-start.23 = (f16[2,152,608]{2,1,0:T(8,128)(2,1)S(1)}, f16[2,152,608]{2,1,0:T(8,128)(2,1)S(1)}, u32[]{:S(2)}, u32[]{:S(2)}) collective-permute-start(f16[2,152,608]{2,1,0:T(8,128)(2,1)S(1)} %get-tuple-element.313), channel_id=1, source_target_pairs={{0,8},{2,10},{4,12},{6,14},{8,0},{10,2},{12,4},{14,6},{16,24},{18,... | collective-permute-start | bytes 1109000 | tf_op jit(solution)/shard_map/ppermute | solution.py:78
  90.2 28.5 %collective-permute-start.20 = (f16[2,152,608]{2,1,0:T(8,128)(2,1)S(1)}, f16[2,152,608]{2,1,0:T(8,128)(2,1)S(1)}, u32[]{:S(2)}, u32[]{:S(2)}) collective-permute-start(f16[2,152,608]{2,1,0:T(8,128)(2,1)S(1)} %multiply_convert_fusion.2), channel_id=1, source_target_pairs={{0,8},{2,10},{4,12},{6,14},{8,0},{10,2},{12,4},{14,6},{16,24},{18,... | collective-permute-start | bytes 1109000 | tf_op jit(solution)/shard_map/ppermute | solution.py:78
  92.0 15.4 %collective-permute-start.25 = (f16[152,608]{1,0:T(8,128)(2,1)S(1)}, f16[152,608]{1,0:T(8,128)(2,1)S(1)}, u32[]{:S(2)}, u32[]{:S(2)}) collective-permute-start(f16[152,608]{1,0:T(8,128)(2,1)S(1)} %get-tuple-element.321), channel_id=1, source_target_pairs={{0,16},{2,18},{4,20},{6,22},{8,24},{10,26},{12,28},{14,30},{16,0},... | collective-permute-start | bytes 554504 | tf_op jit(solution)/shard_map/ppermute | solution.py:78
  99.0 19.6 %collective-permute-start.22 = (f16[152,608]{1,0:T(8,128)(2,1)S(1)}, f16[152,608]{1,0:T(8,128)(2,1)S(1)}, u32[]{:S(2)}, u32[]{:S(2)}) collective-permute-start(f16[152,608]{1,0:T(8,128)(2,1)S(1)} %get-tuple-element.314), channel_id=1, source_target_pairs={{0,4},{2,6},{4,0},{6,2},{8,12},{10,14},{12,8},{14,10},{16,20},{18,... | collective-permute-start | bytes 554504 | tf_op jit(solution)/shard_map/ppermute | solution.py:78
  100.6 18.3 %collective-permute-start.21 = (f16[152,608]{1,0:T(8,128)(2,1)S(1)}, f16[152,608]{1,0:T(8,128)(2,1)S(1)}, u32[]{:S(2)}, u32[]{:S(2)}) collective-permute-start(f16[152,608]{1,0:T(8,128)(2,1)S(1)} %get-tuple-element.316), channel_id=1, source_target_pairs={{0,4},{2,6},{4,0},{6,2},{8,12},{10,14},{12,8},{14,10},{16,20},{18,... | collective-permute-start | bytes 554504 | tf_op jit(solution)/shard_map/ppermute | solution.py:78
  102.3 15.5 %collective-permute-start.24 = (f16[152,608]{1,0:T(8,128)(2,1)S(1)}, f16[152,608]{1,0:T(8,128)(2,1)S(1)}, u32[]{:S(2)}, u32[]{:S(2)}) collective-permute-start(f16[152,608]{1,0:T(8,128)(2,1)S(1)} %get-tuple-element.322), channel_id=1, source_target_pairs={{0,16},{2,18},{4,20},{6,22},{8,24},{10,26},{12,28},{14,30},{16,0},... | collective-permute-start | bytes 554504 | tf_op jit(solution)/shard_map/ppermute | solution.py:78
  117.9 9.8 %collective-permute-start.27 = (f32[152,608]{1,0:T(8,128)S(1)}, f32[152,608]{1,0:T(8,128)S(1)}, u32[]{:S(2)}, u32[]{:S(2)}) collective-permute-start(f32[152,608]{1,0:T(8,128)S(1)} %multiply_add_fusion.5), channel_id=1, source_target_pairs={{0,1},{1,0},{2,3},{3,2},{4,5},{5,4},{6,7},{7,6},{8,9},{9,8},{10,11... | collective-permute-start | bytes 1109000 | tf_op jit(solution)/shard_map/ppermute | solution.py:91
  131.8 61.6 %collective-permute-start.29 = (bf16[512,2432]{1,0:T(8,128)(2,1)S(1)}, bf16[512,2432]{1,0:T(8,128)(2,1)S(1)}, u32[]{:S(2)}, u32[]{:S(2)}) collective-permute-start(bf16[512,2432]{1,0:T(8,128)(2,1)S(1)} %copy-done.8), channel_id=1, source_target_pairs={{0,1},{1,0},{2,3},{3,2},{4,5},{5,4},{6,7},{7,6},{8,9},{9,8},{10,11... | collective-permute-start | bytes 7471112 | tf_op jit(solution)/shard_map/ppermute | solution.py:91
  147.7 18.5 %collective-permute-start.37 = (bf16[2,152,608]{2,1,0:T(8,128)(2,1)S(1)}, bf16[2,152,608]{2,1,0:T(8,128)(2,1)S(1)}, u32[]{:S(2)}, u32[]{:S(2)}) collective-permute-start(bf16[2,152,608]{2,1,0:T(8,128)(2,1)S(1)} %get-tuple-element.271), channel_id=1, source_target_pairs={{0,8},{2,10},{4,12},{6,14},{8,0},{10,2},{12,4},{14,6},{16,24},{18,... | collective-permute-start | bytes 1109000 | tf_op jit(solution)/shard_map/ppermute | solution.py:78
  147.7 20.7 %collective-permute-start.36 = (bf16[2,152,608]{2,1,0:T(8,128)(2,1)S(1)}, bf16[2,152,608]{2,1,0:T(8,128)(2,1)S(1)}, u32[]{:S(2)}, u32[]{:S(2)}) collective-permute-start(bf16[2,152,608]{2,1,0:T(8,128)(2,1)S(1)} %get-tuple-element.271), channel_id=1, source_target_pairs={{0,16},{2,18},{4,20},{6,22},{8,24},{10,26},{12,28},{14,30},{16,0},... | collective-permute-start | bytes 1109000 | tf_op jit(solution)/shard_map/ppermute | solution.py:78
  149.6 19.1 %collective-permute-start.39 = (bf16[2,152,608]{2,1,0:T(8,128)(2,1)S(1)}, bf16[2,152,608]{2,1,0:T(8,128)(2,1)S(1)}, u32[]{:S(2)}, u32[]{:S(2)}) collective-permute-start(bf16[2,152,608]{2,1,0:T(8,128)(2,1)S(1)} %get-tuple-element.271), channel_id=1, source_target_pairs={{0,4},{2,6},{4,0},{6,2},{8,12},{10,14},{12,8},{14,10},{16,20},{18,... | collective-permute-start | bytes 1109000 | tf_op jit(solution)/shard_map/ppermute | solution.py:78
  166.2 11.9 %collective-permute-start.40 = (bf16[2,152,608]{2,1,0:T(8,128)(2,1)S(1)}, bf16[2,152,608]{2,1,0:T(8,128)(2,1)S(1)}, u32[]{:S(2)}, u32[]{:S(2)}) collective-permute-start(bf16[2,152,608]{2,1,0:T(8,128)(2,1)S(1)} %collective-permute-done.37), channel_id=1, source_target_pairs={{0,4},{2,6},{4,0},{6,2},{8,12},{10,14},{12,8},{14,10},{16,20},{18,... | collective-permute-start | bytes 1109000 | tf_op jit(solution)/shard_map/ppermute | solution.py:78
  168.4 10.6 %collective-permute-start.38 = (bf16[2,152,608]{2,1,0:T(8,128)(2,1)S(1)}, bf16[2,152,608]{2,1,0:T(8,128)(2,1)S(1)}, u32[]{:S(2)}, u32[]{:S(2)}) collective-permute-start(bf16[2,152,608]{2,1,0:T(8,128)(2,1)S(1)} %collective-permute-done.36), channel_id=1, source_target_pairs={{0,8},{2,10},{4,12},{6,14},{8,0},{10,2},{12,4},{14,6},{16,24},{18,... | collective-permute-start | bytes 1109000 | tf_op jit(solution)/shard_map/ppermute | solution.py:78
  168.4 18.1 %collective-permute-start.42 = (bf16[2,152,608]{2,1,0:T(8,128)(2,1)S(1)}, bf16[2,152,608]{2,1,0:T(8,128)(2,1)S(1)}, u32[]{:S(2)}, u32[]{:S(2)}) collective-permute-start(bf16[2,152,608]{2,1,0:T(8,128)(2,1)S(1)} %collective-permute-done.36), channel_id=1, source_target_pairs={{0,4},{2,6},{4,0},{6,2},{8,12},{10,14},{12,8},{14,10},{16,20},{18,... | collective-permute-start | bytes 1109000 | tf_op jit(solution)/shard_map/ppermute | solution.py:78
  178.5 26.8 %collective-permute-start.45 = (bf16[4,2,152,608]{3,2,1,0:T(8,128)(2,1)S(1)}, bf16[4,2,152,608]{3,2,1,0:T(8,128)(2,1)S(1)}, u32[]{:S(2)}, u32[]{:S(2)}) collective-permute-start(bf16[4,2,152,608]{3,2,1,0:T(8,128)(2,1)S(1)} %pad_maximum_fusion.refs_0_), channel_id=1, source_target_pairs={{0,2},{2,0},{4,6},{6,4},{8,10},{10,8},{12,14},{14,12},{16,18},{18,... | collective-permute-start | bytes 4435976 | tf_op jit(solution)/shard_map/ppermute | solution.py:78
  179.0 14.5 %collective-permute-start.41 = (bf16[2,152,608]{2,1,0:T(8,128)(2,1)S(1)}, bf16[2,152,608]{2,1,0:T(8,128)(2,1)S(1)}, u32[]{:S(2)}, u32[]{:S(2)}) collective-permute-start(bf16[2,152,608]{2,1,0:T(8,128)(2,1)S(1)} %collective-permute-done.38.refs_4_), channel_id=1, source_target_pairs={{0,4},{2,6},{4,0},{6,2},{8,12},{10,14},{12,8},{14,10},{16,20},{18,... | collective-permute-start | bytes 1109000 | tf_op jit(solution)/shard_map/ppermute | solution.py:78
  193.5 11.7 %collective-permute-start.46 = (bf16[2,2,152,608]{3,2,1,0:T(8,128)(2,1)S(1)}, bf16[2,2,152,608]{3,2,1,0:T(8,128)(2,1)S(1)}, u32[]{:S(2)}, u32[]{:S(2)}) collective-permute-start(bf16[2,2,152,608]{3,2,1,0:T(8,128)(2,1)S(1)} %pad_maximum_fusion.1.refs_2_), channel_id=1, source_target_pairs={{0,2},{2,0},{4,6},{6,4},{8,10},{10,8},{12,14},{14,12},{16,18},{18,... | collective-permute-start | bytes 2217992 | tf_op jit(solution)/shard_map/ppermute | solution.py:78
  194.0 11.2 %collective-permute-start.47 = (bf16[2,152,608]{2,1,0:T(8,128)(2,1)S(1)}, bf16[2,152,608]{2,1,0:T(8,128)(2,1)S(1)}, u32[]{:S(2)}, u32[]{:S(2)}) collective-permute-start(bf16[2,152,608]{2,1,0:T(8,128)(2,1)S(1)} %collective-permute-done.38.refs_4_), channel_id=1, source_target_pairs={{0,2},{2,0},{4,6},{6,4},{8,10},{10,8},{12,14},{14,12},{16,18},{18,... | collective-permute-start | bytes 1109000 | tf_op jit(solution)/shard_map/ppermute | solution.py:78
  (41 other events, 341.8 us)

commit v12 on v11

--- a/solution.py
+++ b/solution.py
@@ -595,8 +595,6 @@
         spread_middle(3, step(lambda value: value, passed_on))
         arrays.append(step(lambda *values: jnp.stack(values), *mine[2]))
         arrays.append(to_core(arrays[2]))
-        mine[3] = step(lambda *values: values, *mine[3])
-        raw = step(lambda *values: values, *raw)
         hidden = step(lambda *values: values, *[value for group in diagonal for value in group])
         mate_others = [to_core(value) for value in hidden]
         mate_others = [mate_others[: n_tensor - 1], mate_others[n_tensor - 1 :]]
@@ -607,6 +605,7 @@
             back_student = back(back_student, 0, pieces, j, 0, r)
         for j in range(1, n_tensor):
             back_fake = back(back_fake, 1, [raw[j - 1]], j, 0, r)
+        mine[3] = step(lambda *values: values, *mine[3])
         blocks = {}
         for other in range(2):
             for i in range(inner):

time: 211 us -> 205 us (0.972)
  waiting for transfers between devices: 107 us -> 101 us
    ppermute x36, waiting for transfers between devices: 78.3 us -> 72.2 us  [move_dp(): return lax.ppermute(value, 'dp', perm)]
  transfers between devices with their start and end apart: 49 -> 49, of which waited for: 23 -> 25; matrix products, arithmetic and copies ran while one was open for 3% -> 3% of each run, Pallas kernels for 17% -> 18%
where the time goes in v12:
time: 205 us; the launch traced here: 204 us
  waiting for transfers between devices  101 us (49%)
  Pallas kernels  44.9 us (22%)
  starting transfers between devices  42.1 us (21%)
  other arithmetic  5.94 us (3%)
  between operations  5.42 us (3%)
  local copies, waits for them, and re-layouts  5.09 us (2%)
    ppermute x36, waiting for transfers between devices, move_dp(): return lax.ppermute(value, 'dp', perm)  72.2 us
    pallas_call x15, Pallas kernels, call(): pl.pallas_call(kernel, out_shape=out_shape, compiler_params=pltpu.Compile...  44.9 us
    ppermute x36, starting transfers between devices, move_dp(): return lax.ppermute(value, 'dp', perm)  28.3 us
    ppermute x5, waiting for transfers between devices, hops(): got = lax.ppermute(value, axis, perm)  17.2 us
    ppermute x6, waiting for transfers between devices, from_tensor(): return lax.ppermute(value, 'tensor', perm)  11.7 us
    ppermute x5, starting transfers between devices, hops(): got = lax.ppermute(value, axis, perm)  7.86 us
    ppermute x6, starting transfers between devices, from_tensor(): return lax.ppermute(value, 'tensor', perm)  5.84 us
  transfers between devices with their start and end apart: 49, of which 25 were waited for; matrix products, arithmetic and copies ran while one was open for 3% of the time, Pallas kernels for 18%

profile of v12, /device:TPU:0, one launch (start us, length us, event | category | flops | bytes accessed | tf_op | source)
XLA Modules:
  0.0 204.5 jit_solution(10038469240676899134)
XLA Ops:
  5.6 2.2 %shard_map.205 = (bf16[2,4,152,512]{3,2,1,0:T(8,128)(2,1)S(1)}, bf16[2,4,152,512]{3,2,1,0:T(8,128)(2,1)S(1)}, f32[8,128]{1,0:T(8,128)S(1)}) custom-call(bf16[512,2432]{1,0:T(8,128)(2,1)S(1)} %copy-done.6), custom_call_target="tpu_custom_call" | custom-call | tf_op jit(solution)/shard_map/pallas_call | solution.py:56
  8.5 2.9 %collective-permute-start.6 = (bf16[1,608,512]{2,1,0:T(8,128)(2,1)S(1)}, bf16[1,608,512]{2,1,0:T(8,128)(2,1)}, u32[]{:S(2)}, u32[]{:S(2)}) collective-permute-start(bf16[1,608,512]{2,1,0:T(8,128)(2,1)S(1)} %get-tuple-element.175), channel_id=1, source_target_pairs={{0,1},{1,0},{2,3},{3,2},{4,5},{5,4},{6,7},{7,6},{8,9},{9,8},{10,11... | collective-permute-start | bytes 1867784 | tf_op jit(solution)/shard_map/ppermute | solution.py:91
  11.4 3.4 %shard_map.206 = (bf16[2,2,152,512]{3,2,1,0:T(8,128)(2,1)}, bf16[2,2,152,512]{3,2,1,0:T(8,128)(2,1)}, bf16[2,2,152,512]{3,2,1,0:T(8,128)(2,1)S(1)}, bf16[2,2,152,512]{3,2,1,0:T(8,128)(2,1)}, f32[8,128]{1,0:T(8,128)S(1)}) custom-call(bf16[512,2432]{1,0:T(8,128)(2,1)S(1)} %copy-done.4), custom_call_target="tpu_custom_call" | custom-call | tf_op jit(solution)/shard_map/pallas_call | solution.py:56
  14.8 2.2 %shard_map.207 = (f32[8,128]{1,0:T(8,128)S(1)}, bf16[2,608,512]{2,1,0:T(8,128)(2,1)}) custom-call(f32[2]{0:T(128)S(1)} %divide_bitcast_fusion.scale_ref, bf16[608,1024]{1,0:T(8,128)(2,1)S(1)} %copy-done.14, f32[8,128]{1,0:T(8,128)S(1)} %get-tuple-element.170.top_s_ref, f32[8,128]{1,0:T(8,128)S(1)} %get-tuple-element.171.top_f_ref, ...), custom_call_target="tpu_custom_call" | custom-call | tf_op jit(solution)/shard_map/pallas_call | solution.py:56
  17.5 2.1 %shard_map.208 = f32[1216,608]{1,0:T(8,128)S(1)} custom-call(bf16[1216,512]{1,0:T(8,128)(2,1)S(1)} %bitcast.94, bf16[1216,512]{1,0:T(8,128)(2,1)S(1)} %bitcast.96, bf16[1,608,512]{2,1,0:T(8,128)(2,1)S(1)} %get-tuple-element.180.refs_2_, bf16[1,608,512]{2,1,0:T(8,128)(2,1)S(1)} %collective-permute-done.8.refs_3_), custom_call_target="tpu_custom_call" | custom-call | tf_op jit(solution)/shard_map/pallas_call | solution.py:56
  21.3 2.1 %collective-permute-done.9 = f32[8,128]{1,0:T(8,128)S(1)} collective-permute-done((f32[8,128]{1,0:T(8,128)S(1)}, f32[8,128]{1,0:T(8,128)S(1)}, u32[]{:S(2)}, u32[]{:S(2)}) %collective-permute-start.9) | collective-permute-done | bytes 4128 | tf_op jit(solution)/shard_map/ppermute | solution.py:376
  25.0 2.0 collective-permute-done.10
  27.5 2.6 %collective-permute-start.12 = (f32[8,128]{1,0:T(8,128)S(1)}, f32[8,128]{1,0:T(8,128)S(1)}, u32[]{:S(2)}, u32[]{:S(2)}) collective-permute-start(f32[8,128]{1,0:T(8,128)S(1)} %max.29), channel_id=1, source_target_pairs={{0,16},{2,18},{4,20},{6,22},{8,24},{10,26},{12,28},{14,30},{16,0},... | collective-permute-start | bytes 12296 | tf_op jit(solution)/shard_map/ppermute | solution.py:376
  37.8 3.6 %shard_map.209 = f32[1216,608]{1,0:T(8,128)S(1)} custom-call(bf16[1216,512]{1,0:T(8,128)(2,1)S(1)} %bitcast.95, bf16[1216,512]{1,0:T(8,128)(2,1)S(1)} %bitcast.97, bf16[1,608,512]{2,1,0:T(8,128)(2,1)} %collective-permute-done.6.refs_2_, bf16[1,608,512]{2,1,0:T(8,128)(2,1)} %collective-permute-done.11.refs_3_), custom_call_target="tpu_custom_call" | custom-call | tf_op jit(solution)/shard_map/pallas_call | solution.py:56
  43.0 3.2 %shard_map.210.refs_4_ = bf16[608,1024]{1,0:T(8,128)(2,1)} custom-call(f32[2]{0:T(128)S(1)} %divide_bitcast_fusion.scale_ref, bf16[608,2432]{1,0:T(8,128)(2,1)S(1)} %copy-done, bf16[512,2432]{1,0:T(8,128)(2,1)S(1)} %copy-done.5), custom_call_target="tpu_custom_call" | custom-call | tf_op jit(solution)/shard_map/pallas_call | solution.py:56
  46.2 3.2 %shard_map.211.refs_1_ = bf16[608,1024]{1,0:T(8,128)(2,1)} custom-call(f32[2]{0:T(128)S(1)} %divide_bitcast_fusion.scale_ref, bf16[608,2432]{1,0:T(8,128)(2,1)S(1)} %copy-done.2, bf16[512,2432]{1,0:T(8,128)(2,1)S(1)} %copy-done.7), custom_call_target="tpu_custom_call" | custom-call | tf_op jit(solution)/shard_map/pallas_call | solution.py:56
  49.4 11.2 %collective-permute-done.16 = f32[8,128]{1,0:T(8,128)S(1)} collective-permute-done((f32[8,128]{1,0:T(8,128)S(1)}, f32[8,128]{1,0:T(8,128)S(1)}, u32[]{:S(2)}, u32[]{:S(2)}) %collective-permute-start.16) | collective-permute-done | bytes 4128 | tf_op jit(solution)/shard_map/ppermute | solution.py:376
  66.2 4.5 %shard_map.212 = f32[608,608]{1,0:T(8,128)S(1)} custom-call(bf16[608,512]{1,0:T(8,128)(2,1)} %bitcast.13.refs_0_, bf16[608,512]{1,0:T(8,128)(2,1)} %bitcast.14.refs_1_, bf16[608,512]{1,0:T(8,128)(2,1)} %bitcast.15.refs_2_, bf16[608,512]{1,0:T(8,128)(2,1)} %bitcast.16.refs_3_, bf16[2,608,512]{2,1,0:T(8,128)(2,1)} %get-tuple-element.227.refs_4_, ...), custom_call_target="tpu_custom_call" | custom-call | tf_op jit(solution)/shard_map/pallas_call | solution.py:56
  75.1 9.7 %collective-permute-done.19 = f16[4,152,608]{2,1,0:T(8,128)(2,1)S(1)} collective-permute-done((f16[4,152,608]{2,1,0:T(8,128)(2,1)S(1)}, f16[4,152,608]{2,1,0:T(8,128)(2,1)S(1)}, u32[]{:S(2)}, u32[]{:S(2)}) %collective-permute-start.19) | collective-permute-done | bytes 739360 | tf_op jit(solution)/shard_map/ppermute | solution.py:78
  86.9 3.1 %collective-permute-done.18 = f16[2,152,608]{2,1,0:T(8,128)(2,1)S(1)} collective-permute-done((f16[2,152,608]{2,1,0:T(8,128)(2,1)S(1)}, f16[2,152,608]{2,1,0:T(8,128)(2,1)S(1)}, u32[]{:S(2)}, u32[]{:S(2)}) %collective-permute-start.18) | collective-permute-done | bytes 369696 | tf_op jit(solution)/shard_map/ppermute | solution.py:78
  92.0 2.7 %collective-permute-start.25 = (f16[152,608]{1,0:T(8,128)(2,1)S(1)}, f16[152,608]{1,0:T(8,128)(2,1)S(1)}, u32[]{:S(2)}, u32[]{:S(2)}) collective-permute-start(f16[152,608]{1,0:T(8,128)(2,1)S(1)} %get-tuple-element.319), channel_id=1, source_target_pairs={{0,16},{2,18},{4,20},{6,22},{8,24},{10,26},{12,28},{14,30},{16,0},... | collective-permute-start | bytes 554504 | tf_op jit(solution)/shard_map/ppermute | solution.py:78
  94.7 4.2 %shard_map.213 = f32[608,608]{1,0:T(8,128)S(1)} custom-call(bf16[608,512]{1,0:T(8,128)(2,1)S(1)} %bitcast.99, bf16[608,512]{1,0:T(8,128)(2,1)} %bitcast.23.refs_1_, bf16[608,512]{1,0:T(8,128)(2,1)} %bitcast.24.refs_2_, bf16[608,512]{1,0:T(8,128)(2,1)S(1)} %bitcast.98, bf16[2,608,512]{2,1,0:T(8,128)(2,1)} %get-tuple-element.227.refs_4_, ...), custom_call_target="tpu_custom_call" | custom-call | tf_op jit(solution)/shard_map/pallas_call | solution.py:56
  102.4 2.2 %collective-permute-start.24 = (f16[152,608]{1,0:T(8,128)(2,1)S(1)}, f16[152,608]{1,0:T(8,128)(2,1)S(1)}, u32[]{:S(2)}, u32[]{:S(2)}) collective-permute-start(f16[152,608]{1,0:T(8,128)(2,1)S(1)} %get-tuple-element.320), channel_id=1, source_target_pairs={{0,16},{2,18},{4,20},{6,22},{8,24},{10,26},{12,28},{14,30},{16,0},... | collective-permute-start | bytes 554504 | tf_op jit(solution)/shard_map/ppermute | solution.py:78
  104.6 2.9 %collective-permute-done.25 = f16[152,608]{1,0:T(8,128)(2,1)S(1)} collective-permute-done((f16[152,608]{1,0:T(8,128)(2,1)S(1)}, f16[152,608]{1,0:T(8,128)(2,1)S(1)}, u32[]{:S(2)}, u32[]{:S(2)}) %collective-permute-start.25) | collective-permute-done | bytes 184864 | tf_op jit(solution)/shard_map/ppermute | solution.py:78
  107.5 10.3 %collective-permute-done.24 = f16[152,608]{1,0:T(8,128)(2,1)S(1)} collective-permute-done((f16[152,608]{1,0:T(8,128)(2,1)S(1)}, f16[152,608]{1,0:T(8,128)(2,1)S(1)}, u32[]{:S(2)}, u32[]{:S(2)}) %collective-permute-start.24) | collective-permute-done | bytes 184864 | tf_op jit(solution)/shard_map/ppermute | solution.py:78
  119.2 8.5 %collective-permute-done.27 = f32[152,608]{1,0:T(8,128)S(1)} collective-permute-done((f32[152,608]{1,0:T(8,128)S(1)}, f32[152,608]{1,0:T(8,128)S(1)}, u32[]{:S(2)}, u32[]{:S(2)}) %collective-permute-start.27) | collective-permute-done | bytes 369696 | tf_op jit(solution)/shard_map/ppermute | solution.py:91
  128.7 3.2 %collective-permute-done.28 = f32[8,128]{1,0:T(8,128)S(1)} collective-permute-done((f32[8,128]{1,0:T(8,128)S(1)}, f32[8,128]{1,0:T(8,128)S(1)}, u32[]{:S(2)}, u32[]{:S(2)}) %collective-permute-start.28) | collective-permute-done | bytes 4128 | tf_op jit(solution)/shard_map/ppermute | solution.py:91
  132.4 2.6 %collective-permute-start.30 = (f32[8,128]{1,0:T(8,128)S(1)}, f32[8,128]{1,0:T(8,128)S(1)}, u32[]{:S(2)}, u32[]{:S(2)}) collective-permute-start(f32[8,128]{1,0:T(8,128)S(1)} %add.78), channel_id=1, source_target_pairs={{0,16},{2,18},{4,20},{6,22},{8,24},{10,26},{12,28},{14,30},{16,0},... | collective-permute-start | bytes 12296 | tf_op jit(solution)/shard_map/ppermute | solution.py:78
  136.9 3.5 %collective-permute-done.31 = f32[8,128]{1,0:T(8,128)S(1)} collective-permute-done((f32[8,128]{1,0:T(8,128)S(1)}, f32[8,128]{1,0:T(8,128)S(1)}, u32[]{:S(2)}, u32[]{:S(2)}) %collective-permute-start.31) | collective-permute-done | bytes 4128 | tf_op jit(solution)/shard_map/ppermute | solution.py:78
  140.4 2.2 %collective-permute-start.33 = (f32[8,128]{1,0:T(8,128)S(1)}, f32[8,128]{1,0:T(8,128)S(1)}, u32[]{:S(2)}, u32[]{:S(2)}) collective-permute-start(f32[8,128]{1,0:T(8,128)S(1)} %add_add_fusion.1), channel_id=1, source_target_pairs={{0,4},{2,6},{4,0},{6,2},{8,12},{10,14},{12,8},{14,10},{16,20},{18,... | collective-permute-start | bytes 12296 | tf_op jit(solution)/shard_map/ppermute | solution.py:78
  145.7 2.1 %shard_map.215 = (bf16[2,152,608]{2,1,0:T(8,128)(2,1)S(1)}, f32[152,608]{1,0:T(8,128)}, f32[152,608]{1,0:T(8,128)}, f32[152,608]{1,0:T(8,128)}, f32[152,608]{1,0...) custom-call(f32[8,128]{1,0:T(8,128)S(1)} %add_add_fusion.squares_ref, ...), custom_call_target="tpu_custom_call" | custom-call | tf_op jit(solution)/shard_map/pallas_call | solution.py:56
  150.2 16.0 %collective-permute-done.36 = bf16[2,152,608]{2,1,0:T(8,128)(2,1)S(1)} collective-permute-done((bf16[2,152,608]{2,1,0:T(8,128)(2,1)S(1)}, bf16[2,152,608]{2,1,0:T(8,128)(2,1)S(1)}, u32[]{:S(2)}, u32[]{:S(2)}) %collective-permute-start.36) | collective-permute-done | bytes 369696 | tf_op jit(solution)/shard_map/ppermute | solution.py:78
  168.7 9.3 %collective-permute-done.40 = bf16[2,152,608]{2,1,0:T(8,128)(2,1)S(1)} collective-permute-done((bf16[2,152,608]{2,1,0:T(8,128)(2,1)S(1)}, bf16[2,152,608]{2,1,0:T(8,128)(2,1)S(1)}, u32[]{:S(2)}, u32[]{:S(2)}) %collective-permute-start.40) | collective-permute-done | bytes 369696 | tf_op jit(solution)/shard_map/ppermute | solution.py:78
  179.0 6.0 %collective-permute-done.37 = bf16[2,152,608]{2,1,0:T(8,128)(2,1)S(1)} collective-permute-done((bf16[2,152,608]{2,1,0:T(8,128)(2,1)S(1)}, bf16[2,152,608]{2,1,0:T(8,128)(2,1)S(1)}, u32[]{:S(2)}, u32[]{:S(2)}) %collective-permute-start.37) | collective-permute-done | bytes 369696 | tf_op jit(solution)/shard_map/ppermute | solution.py:78
  188.2 4.4 %shard_map.216 = bf16[608,1024]{1,0:T(8,128)(2,1)} custom-call(f32[2]{0:T(128)S(1)} %divide_bitcast_fusion.scale_ref, bf16[608,2432]{1,0:T(8,128)(2,1)S(1)} %copy-done.1, bf16[2,2,152,512]{3,2,1,0:T(8,128)(2,1)} %collective-permute-done.refs_0_, bf16[2,2,152,512]{3,2,1,0:T(8,128)(2,1)S(1)} %collective-permute-done.41.refs_1_, ...), custom_call_target="tpu_custom_call", output_to_operand_aliasing={{}: (6, {})} | custom-call | tf_op jit(solution)/shard_map/pallas_call | solution.py:56
  192.6 3.2 %shard_map.217 = bf16[608,1024]{1,0:T(8,128)(2,1)} custom-call(f32[2]{0:T(128)S(1)} %divide_bitcast_fusion.scale_ref, bf16[608,2432]{1,0:T(8,128)(2,1)S(1)} %copy-done.3, bf16[512,2432]{1,0:T(8,128)(2,1)S(1)} %collective-permute-done.43.refs_0_, bf16[608,1024]{1,0:T(8,128)(2,1)} %shard_map.211.refs_1_), custom_call_target="tpu_custom_call", output_to_operand_aliasing={{}: (3, {})} | custom-call | tf_op jit(solution)/shard_map/pallas_call | solution.py:56
  199.0 5.2 %shard_map.218 = (bf16[608,2432]{1,0:T(8,128)(2,1)}, bf16[608,2432]{1,0:T(8,128)(2,1)}) custom-call(bf16[4,2,152,608]{3,2,1,0:T(8,128)(2,1)S(1)} %pad_maximum_fusion.refs_0_, bf16[4,2,152,608]{3,2,1,0:T(8,128)(2,1)S(1)} %collective-permute-done.44.refs_1_, bf16[2,2,152,608]{3,2,1,0:T(8,128)(2,1)S(1)} %pad_maximum_fusion.1.refs_2_, ...), custom_call_target="tpu_custom_call" | custom-call | tf_op jit(solution)/shard_map/pallas_call | solution.py:56
  (162 shorter events, 52.7 us)
Async XLA Ops:
  7.9 9.7 %collective-permute-start.5 = (bf16[2,4,152,512]{3,2,1,0:T(8,128)(2,1)S(1)}, bf16[2,4,152,512]{3,2,1,0:T(8,128)(2,1)S(1)}, u32[]{:S(2)}, u32[]{:S(2)}) collective-permute-start(bf16[2,4,152,512]{3,2,1,0:T(8,128)(2,1)S(1)} %get-tuple-element.174), channel_id=1, source_target_pairs={{0,2},{2,0},{4,6},{6,4},{8,10},{10,8},{12,14},{14,12},{16,18},{18,... | collective-permute-start | bytes 3735560 | tf_op jit(solution)/shard_map/ppermute | solution.py:78
  8.4 9.1 %collective-permute-start.8 = (bf16[1,608,512]{2,1,0:T(8,128)(2,1)S(1)}, bf16[1,608,512]{2,1,0:T(8,128)(2,1)S(1)}, u32[]{:S(2)}, u32[]{:S(2)}) collective-permute-start(bf16[1,608,512]{2,1,0:T(8,128)(2,1)S(1)} %get-tuple-element.180.refs_2_), channel_id=1, source_target_pairs={{0,2},{2,0},{4,6},{6,4},{8,10},{10,8},{12,14},{14,12},{16,18},{18,... | collective-permute-start | bytes 1867784 | tf_op jit(solution)/shard_map/ppermute | solution.py:78
  8.5 18.5 %collective-permute-start.6 = (bf16[1,608,512]{2,1,0:T(8,128)(2,1)S(1)}, bf16[1,608,512]{2,1,0:T(8,128)(2,1)}, u32[]{:S(2)}, u32[]{:S(2)}) collective-permute-start(bf16[1,608,512]{2,1,0:T(8,128)(2,1)S(1)} %get-tuple-element.175), channel_id=1, source_target_pairs={{0,1},{1,0},{2,3},{3,2},{4,5},{5,4},{6,7},{7,6},{8,9},{9,8},{10,11... | collective-permute-start | bytes 1867784 | tf_op jit(solution)/shard_map/ppermute | solution.py:91
  17.0 25.9 %collective-permute-start.2 = (bf16[2,608,512]{2,1,0:T(8,128)(2,1)}, bf16[2,608,512]{2,1,0:T(8,128)(2,1)}, u32[]{:S(2)}, u32[]{:S(2)}) collective-permute-start(bf16[2,608,512]{2,1,0:T(8,128)(2,1)} %get-tuple-element.227.refs_4_), channel_id=1, source_target_pairs={{0,2},{2,0},{4,6},{6,4},{8,10},{10,8},{12,14},{14,12},{16,18},{18,... | collective-permute-start | bytes 3735560 | tf_op jit(solution)/shard_map/ppermute | solution.py:78
  25.0 9.4 %collective-permute-start.3 = (bf16[2,2,152,512]{3,2,1,0:T(8,128)(2,1)}, bf16[2,2,152,512]{3,2,1,0:T(8,128)(2,1)}, u32[]{:S(2)}, u32[]{:S(2)}) collective-permute-start(bf16[2,2,152,512]{3,2,1,0:T(8,128)(2,1)} %get-tuple-element.164), channel_id=1, source_target_pairs={{0,2},{2,0},{4,6},{6,4},{8,10},{10,8},{12,14},{14,12},{16,18},{18,... | collective-permute-start | bytes 1867784 | tf_op jit(solution)/shard_map/ppermute | solution.py:78
  27.0 14.3 %collective-permute-start.4 = (bf16[2,2,152,512]{3,2,1,0:T(8,128)(2,1)}, bf16[2,2,152,512]{3,2,1,0:T(8,128)(2,1)}, u32[]{:S(2)}, u32[]{:S(2)}) collective-permute-start(bf16[2,2,152,512]{3,2,1,0:T(8,128)(2,1)} %get-tuple-element.200), channel_id=1, source_target_pairs={{0,2},{2,0},{4,6},{6,4},{8,10},{10,8},{12,14},{14,12},{16,18},{18,... | collective-permute-start | bytes 1867784 | tf_op jit(solution)/shard_map/ppermute | solution.py:78
  32.0 34.1 %collective-permute-start = (bf16[2,2,152,512]{3,2,1,0:T(8,128)(2,1)}, bf16[2,2,152,512]{3,2,1,0:T(8,128)(2,1)}, u32[]{:S(2)}, u32[]{:S(2)}) collective-permute-start(bf16[2,2,152,512]{3,2,1,0:T(8,128)(2,1)} %get-tuple-element.209), channel_id=1, source_target_pairs={{0,1},{1,0},{2,3},{3,2},{4,5},{5,4},{6,7},{7,6},{8,9},{9,8},{10,11... | collective-permute-start | bytes 1867784 | tf_op jit(solution)/shard_map/ppermute | solution.py:91
  34.4 31.7 %collective-permute-start.1 = (bf16[2,2,152,512]{3,2,1,0:T(8,128)(2,1)}, bf16[2,2,152,512]{3,2,1,0:T(8,128)(2,1)}, u32[]{:S(2)}, u32[]{:S(2)}) collective-permute-start(bf16[2,2,152,512]{3,2,1,0:T(8,128)(2,1)} %get-tuple-element.164), channel_id=1, source_target_pairs={{0,3},{1,2},{2,1},{3,0},{4,7},{5,6},{6,5},{7,4},{8,11},{9,10},{10,... | collective-permute-start | bytes 1867784 | tf_op jit(solution)/shard_map/ppermute | solution.py:100
  34.5 26.0 %collective-permute-start.16 = (f32[8,128]{1,0:T(8,128)S(1)}, f32[8,128]{1,0:T(8,128)S(1)}, u32[]{:S(2)}, u32[]{:S(2)}) collective-permute-start(f32[8,128]{1,0:T(8,128)S(1)} %max.30), channel_id=1, source_target_pairs={{0,1},{1,0},{2,3},{3,2},{4,5},{5,4},{6,7},{7,6},{8,9},{9,8},{10,11... | collective-permute-start | bytes 12296 | tf_op jit(solution)/shard_map/ppermute | solution.py:376
  41.3 30.0 %collective-permute-start.15 = (f16[4,152,608]{2,1,0:T(8,128)(2,1)}, f16[4,152,608]{2,1,0:T(8,128)(2,1)}, u32[]{:S(2)}, u32[]{:S(2)}) collective-permute-start(f16[4,152,608]{2,1,0:T(8,128)(2,1)} %get-tuple-element.309), channel_id=1, source_target_pairs={{0,4},{2,6},{4,0},{6,2},{8,12},{10,14},{12,8},{14,10},{16,20},{18,... | collective-permute-start | bytes 2217992 | tf_op jit(solution)/shard_map/ppermute | solution.py:78
  62.4 32.3 %collective-permute-start.14 = (bf16[2,2,152,512]{3,2,1,0:T(8,128)(2,1)}, bf16[2,2,152,512]{3,2,1,0:T(8,128)(2,1)}, u32[]{:S(2)}, u32[]{:S(2)}) collective-permute-start(bf16[2,2,152,512]{3,2,1,0:T(8,128)(2,1)} %copy-done.15), channel_id=1, source_target_pairs={{0,1},{1,0},{2,3},{3,2},{4,5},{5,4},{6,7},{7,6},{8,9},{9,8},{10,11... | collective-permute-start | bytes 1867784 | tf_op jit(solution)/shard_map/ppermute | solution.py:91
  64.5 20.4 %collective-permute-start.19 = (f16[4,152,608]{2,1,0:T(8,128)(2,1)S(1)}, f16[4,152,608]{2,1,0:T(8,128)(2,1)S(1)}, u32[]{:S(2)}, u32[]{:S(2)}) collective-permute-start(f16[4,152,608]{2,1,0:T(8,128)(2,1)S(1)} %get-tuple-element.307), channel_id=1, source_target_pairs={{0,4},{2,6},{4,0},{6,2},{8,12},{10,14},{12,8},{14,10},{16,20},{18,... | collective-permute-start | bytes 2217992 | tf_op jit(solution)/shard_map/ppermute | solution.py:78
  70.8 19.2 %collective-permute-start.18 = (f16[2,152,608]{2,1,0:T(8,128)(2,1)S(1)}, f16[2,152,608]{2,1,0:T(8,128)(2,1)S(1)}, u32[]{:S(2)}, u32[]{:S(2)}) collective-permute-start(f16[2,152,608]{2,1,0:T(8,128)(2,1)S(1)} %fusion.4), channel_id=1, source_target_pairs={{0,4},{2,6},{4,0},{6,2},{8,12},{10,14},{12,8},{14,10},{16,20},{18,... | collective-permute-start | bytes 1109000 | tf_op jit(solution)/shard_map/ppermute | solution.py:78
  71.3 23.4 %collective-permute-start.13 = (bf16[2,2,152,512]{3,2,1,0:T(8,128)(2,1)}, bf16[2,2,152,512]{3,2,1,0:T(8,128)(2,1)S(1)}, u32[]{:S(2)}, u32[]{:S(2)}) collective-permute-start(bf16[2,2,152,512]{3,2,1,0:T(8,128)(2,1)} %get-tuple-element.200), channel_id=1, source_target_pairs={{0,3},{1,2},{2,1},{3,0},{4,7},{5,6},{6,5},{7,4},{8,11},{9,10},{10,... | collective-permute-start | bytes 1867784 | tf_op jit(solution)/shard_map/ppermute | solution.py:100
  73.5 18.4 %collective-permute-start.17 = (f16[2,152,608]{2,1,0:T(8,128)(2,1)S(1)}, f16[2,152,608]{2,1,0:T(8,128)(2,1)S(1)}, u32[]{:S(2)}, u32[]{:S(2)}) collective-permute-start(f16[2,152,608]{2,1,0:T(8,128)(2,1)S(1)} %get-tuple-element.316), channel_id=1, source_target_pairs={{0,8},{2,10},{4,12},{6,14},{8,0},{10,2},{12,4},{14,6},{16,24},{18,... | collective-permute-start | bytes 1109000 | tf_op jit(solution)/shard_map/ppermute | solution.py:78
  85.2 17.0 %collective-permute-start.23 = (f16[2,152,608]{2,1,0:T(8,128)(2,1)S(1)}, f16[2,152,608]{2,1,0:T(8,128)(2,1)S(1)}, u32[]{:S(2)}, u32[]{:S(2)}) collective-permute-start(f16[2,152,608]{2,1,0:T(8,128)(2,1)S(1)} %get-tuple-element.311), channel_id=1, source_target_pairs={{0,8},{2,10},{4,12},{6,14},{8,0},{10,2},{12,4},{14,6},{16,24},{18,... | collective-permute-start | bytes 1109000 | tf_op jit(solution)/shard_map/ppermute | solution.py:78
  90.2 28.4 %collective-permute-start.20 = (f16[2,152,608]{2,1,0:T(8,128)(2,1)S(1)}, f16[2,152,608]{2,1,0:T(8,128)(2,1)S(1)}, u32[]{:S(2)}, u32[]{:S(2)}) collective-permute-start(f16[2,152,608]{2,1,0:T(8,128)(2,1)S(1)} %multiply_convert_fusion.2), channel_id=1, source_target_pairs={{0,8},{2,10},{4,12},{6,14},{8,0},{10,2},{12,4},{14,6},{16,24},{18,... | collective-permute-start | bytes 1109000 | tf_op jit(solution)/shard_map/ppermute | solution.py:78
  92.0 15.4 %collective-permute-start.25 = (f16[152,608]{1,0:T(8,128)(2,1)S(1)}, f16[152,608]{1,0:T(8,128)(2,1)S(1)}, u32[]{:S(2)}, u32[]{:S(2)}) collective-permute-start(f16[152,608]{1,0:T(8,128)(2,1)S(1)} %get-tuple-element.319), channel_id=1, source_target_pairs={{0,16},{2,18},{4,20},{6,22},{8,24},{10,26},{12,28},{14,30},{16,0},... | collective-permute-start | bytes 554504 | tf_op jit(solution)/shard_map/ppermute | solution.py:78
  99.0 19.6 %collective-permute-start.22 = (f16[152,608]{1,0:T(8,128)(2,1)S(1)}, f16[152,608]{1,0:T(8,128)(2,1)S(1)}, u32[]{:S(2)}, u32[]{:S(2)}) collective-permute-start(f16[152,608]{1,0:T(8,128)(2,1)S(1)} %get-tuple-element.312), channel_id=1, source_target_pairs={{0,4},{2,6},{4,0},{6,2},{8,12},{10,14},{12,8},{14,10},{16,20},{18,... | collective-permute-start | bytes 554504 | tf_op jit(solution)/shard_map/ppermute | solution.py:78
  100.6 18.2 %collective-permute-start.21 = (f16[152,608]{1,0:T(8,128)(2,1)S(1)}, f16[152,608]{1,0:T(8,128)(2,1)S(1)}, u32[]{:S(2)}, u32[]{:S(2)}) collective-permute-start(f16[152,608]{1,0:T(8,128)(2,1)S(1)} %get-tuple-element.314), channel_id=1, source_target_pairs={{0,4},{2,6},{4,0},{6,2},{8,12},{10,14},{12,8},{14,10},{16,20},{18,... | collective-permute-start | bytes 554504 | tf_op jit(solution)/shard_map/ppermute | solution.py:78
  102.4 15.5 %collective-permute-start.24 = (f16[152,608]{1,0:T(8,128)(2,1)S(1)}, f16[152,608]{1,0:T(8,128)(2,1)S(1)}, u32[]{:S(2)}, u32[]{:S(2)}) collective-permute-start(f16[152,608]{1,0:T(8,128)(2,1)S(1)} %get-tuple-element.320), channel_id=1, source_target_pairs={{0,16},{2,18},{4,20},{6,22},{8,24},{10,26},{12,28},{14,30},{16,0},... | collective-permute-start | bytes 554504 | tf_op jit(solution)/shard_map/ppermute | solution.py:78
  117.9 9.8 %collective-permute-start.27 = (f32[152,608]{1,0:T(8,128)S(1)}, f32[152,608]{1,0:T(8,128)S(1)}, u32[]{:S(2)}, u32[]{:S(2)}) collective-permute-start(f32[152,608]{1,0:T(8,128)S(1)} %multiply_add_fusion.5), channel_id=1, source_target_pairs={{0,1},{1,0},{2,3},{3,2},{4,5},{5,4},{6,7},{7,6},{8,9},{9,8},{10,11... | collective-permute-start | bytes 1109000 | tf_op jit(solution)/shard_map/ppermute | solution.py:91
  131.9 60.8 %collective-permute-start.43 = (bf16[512,2432]{1,0:T(8,128)(2,1)S(1)}, bf16[512,2432]{1,0:T(8,128)(2,1)S(1)}, u32[]{:S(2)}, u32[]{:S(2)}) collective-permute-start(bf16[512,2432]{1,0:T(8,128)(2,1)S(1)} %copy-done.8), channel_id=1, source_target_pairs={{0,1},{1,0},{2,3},{3,2},{4,5},{5,4},{6,7},{7,6},{8,9},{9,8},{10,11... | collective-permute-start | bytes 7471112 | tf_op jit(solution)/shard_map/ppermute | solution.py:91
  147.7 18.4 %collective-permute-start.36 = (bf16[2,152,608]{2,1,0:T(8,128)(2,1)S(1)}, bf16[2,152,608]{2,1,0:T(8,128)(2,1)S(1)}, u32[]{:S(2)}, u32[]{:S(2)}) collective-permute-start(bf16[2,152,608]{2,1,0:T(8,128)(2,1)S(1)} %get-tuple-element.270), channel_id=1, source_target_pairs={{0,8},{2,10},{4,12},{6,14},{8,0},{10,2},{12,4},{14,6},{16,24},{18,... | collective-permute-start | bytes 1109000 | tf_op jit(solution)/shard_map/ppermute | solution.py:78
  147.7 20.7 %collective-permute-start.35 = (bf16[2,152,608]{2,1,0:T(8,128)(2,1)S(1)}, bf16[2,152,608]{2,1,0:T(8,128)(2,1)S(1)}, u32[]{:S(2)}, u32[]{:S(2)}) collective-permute-start(bf16[2,152,608]{2,1,0:T(8,128)(2,1)S(1)} %get-tuple-element.270), channel_id=1, source_target_pairs={{0,16},{2,18},{4,20},{6,22},{8,24},{10,26},{12,28},{14,30},{16,0},... | collective-permute-start | bytes 1109000 | tf_op jit(solution)/shard_map/ppermute | solution.py:78
  149.5 19.2 %collective-permute-start.39 = (bf16[2,152,608]{2,1,0:T(8,128)(2,1)S(1)}, bf16[2,152,608]{2,1,0:T(8,128)(2,1)S(1)}, u32[]{:S(2)}, u32[]{:S(2)}) collective-permute-start(bf16[2,152,608]{2,1,0:T(8,128)(2,1)S(1)} %get-tuple-element.270), channel_id=1, source_target_pairs={{0,4},{2,6},{4,0},{6,2},{8,12},{10,14},{12,8},{14,10},{16,20},{18,... | collective-permute-start | bytes 1109000 | tf_op jit(solution)/shard_map/ppermute | solution.py:78
  166.1 11.9 %collective-permute-start.40 = (bf16[2,152,608]{2,1,0:T(8,128)(2,1)S(1)}, bf16[2,152,608]{2,1,0:T(8,128)(2,1)S(1)}, u32[]{:S(2)}, u32[]{:S(2)}) collective-permute-start(bf16[2,152,608]{2,1,0:T(8,128)(2,1)S(1)} %collective-permute-done.36), channel_id=1, source_target_pairs={{0,4},{2,6},{4,0},{6,2},{8,12},{10,14},{12,8},{14,10},{16,20},{18,... | collective-permute-start | bytes 1109000 | tf_op jit(solution)/shard_map/ppermute | solution.py:78
  168.4 10.6 %collective-permute-start.38 = (bf16[2,152,608]{2,1,0:T(8,128)(2,1)S(1)}, bf16[2,152,608]{2,1,0:T(8,128)(2,1)S(1)}, u32[]{:S(2)}, u32[]{:S(2)}) collective-permute-start(bf16[2,152,608]{2,1,0:T(8,128)(2,1)S(1)} %collective-permute-done.35), channel_id=1, source_target_pairs={{0,8},{2,10},{4,12},{6,14},{8,0},{10,2},{12,4},{14,6},{16,24},{18,... | collective-permute-start | bytes 1109000 | tf_op jit(solution)/shard_map/ppermute | solution.py:78
  168.4 16.6 %collective-permute-start.37 = (bf16[2,152,608]{2,1,0:T(8,128)(2,1)S(1)}, bf16[2,152,608]{2,1,0:T(8,128)(2,1)S(1)}, u32[]{:S(2)}, u32[]{:S(2)}) collective-permute-start(bf16[2,152,608]{2,1,0:T(8,128)(2,1)S(1)} %collective-permute-done.35), channel_id=1, source_target_pairs={{0,4},{2,6},{4,0},{6,2},{8,12},{10,14},{12,8},{14,10},{16,20},{18,... | collective-permute-start | bytes 1109000 | tf_op jit(solution)/shard_map/ppermute | solution.py:78
  178.4 18.9 %collective-permute-start.44 = (bf16[4,2,152,608]{3,2,1,0:T(8,128)(2,1)S(1)}, bf16[4,2,152,608]{3,2,1,0:T(8,128)(2,1)S(1)}, u32[]{:S(2)}, u32[]{:S(2)}) collective-permute-start(bf16[4,2,152,608]{3,2,1,0:T(8,128)(2,1)S(1)} %pad_maximum_fusion.refs_0_), channel_id=1, source_target_pairs={{0,2},{2,0},{4,6},{6,4},{8,10},{10,8},{12,14},{14,12},{16,18},{18,... | collective-permute-start | bytes 4435976 | tf_op jit(solution)/shard_map/ppermute | solution.py:78
  185.8 11.0 %collective-permute-start.46 = (bf16[2,152,608]{2,1,0:T(8,128)(2,1)S(1)}, bf16[2,152,608]{2,1,0:T(8,128)(2,1)S(1)}, u32[]{:S(2)}, u32[]{:S(2)}) collective-permute-start(bf16[2,152,608]{2,1,0:T(8,128)(2,1)S(1)} %collective-permute-done.38.refs_4_), channel_id=1, source_target_pairs={{0,4},{2,6},{4,0},{6,2},{8,12},{10,14},{12,8},{14,10},{16,20},{18,... | collective-permute-start | bytes 1109000 | tf_op jit(solution)/shard_map/ppermute | solution.py:78
  187.6 9.7 %collective-permute-start.45 = (bf16[2,2,152,608]{3,2,1,0:T(8,128)(2,1)S(1)}, bf16[2,2,152,608]{3,2,1,0:T(8,128)(2,1)S(1)}, u32[]{:S(2)}, u32[]{:S(2)}) collective-permute-start(bf16[2,2,152,608]{3,2,1,0:T(8,128)(2,1)S(1)} %pad_maximum_fusion.1.refs_2_), channel_id=1, source_target_pairs={{0,2},{2,0},{4,6},{6,4},{8,10},{10,8},{12,14},{14,12},{16,18},{18,... | collective-permute-start | bytes 2217992 | tf_op jit(solution)/shard_map/ppermute | solution.py:78
  (41 other events, 317.9 us)

commit v13 on v12

--- a/solution.py
+++ b/solution.py
@@ -539,14 +539,14 @@
         )
         for j in range(1, n_tensor):
             fake_far(j)
-        fake_mine = fake_total(0)
+
+        def far_plane(own, near, *got):
+            return shrink(add_widened(own, (near[1], *got), 0), 0)
+
+        far = to_plane(step(far_plane, own_far, near, *got_far), 2)
         fake_others = [fake_total(j) for j in range(1, n_tensor)]
         others_got = [from_tensor(value, j) for j, value in enumerate(fake_others, 1)]
-
-        def far_plane(own, near, *got):
-            return shrink(add_widened(own, (near[1], *got), 0), 0)
-
-        far = to_plane(step(far_plane, own_far, near, *got_far), 2)
+        fake_mine = fake_total(0)
         total_student = step(
             lambda own, near, *got: add_widened(own, (near[0], *got), 0), own, near, *got
         )

time: 205 us -> 206 us (level)
  transfers between devices with their start and end apart: 49 -> 49, of which waited for: 25 -> 26; matrix products, arithmetic and copies ran while one was open for 3% -> 3% of each run, Pallas kernels for 18% -> 18%
where the time goes in v13:
time: 206 us; the launch traced here: 205 us
  waiting for transfers between devices  102 us (50%)
  Pallas kernels  44.9 us (22%)
  starting transfers between devices  42.3 us (21%)
  other arithmetic  5.94 us (3%)
  between operations  5.4 us (3%)
  local copies, waits for them, and re-layouts  5.08 us (2%)
    ppermute x36, waiting for transfers between devices, move_dp(): return lax.ppermute(value, 'dp', perm)  73.8 us
    pallas_call x15, Pallas kernels, call(): pl.pallas_call(kernel, out_shape=out_shape, compiler_params=pltpu.Compile...  44.9 us
    ppermute x36, starting transfers between devices, move_dp(): return lax.ppermute(value, 'dp', perm)  28.6 us
    ppermute x5, waiting for transfers between devices, hops(): got = lax.ppermute(value, axis, perm)  17.2 us
    ppermute x6, waiting for transfers between devices, from_tensor(): return lax.ppermute(value, 'tensor', perm)  10.8 us
    ppermute x5, starting transfers between devices, hops(): got = lax.ppermute(value, axis, perm)  7.86 us
    ppermute x6, starting transfers between devices, from_tensor(): return lax.ppermute(value, 'tensor', perm)  5.71 us
  transfers between devices with their start and end apart: 49, of which 26 were waited for; matrix products, arithmetic and copies ran while one was open for 3% of the time, Pallas kernels for 18%

profile of v13, /device:TPU:0, one launch (start us, length us, event | category | flops | bytes accessed | tf_op | source)
XLA Modules:
  0.0 205.4 jit_solution(2058507982844096903)
XLA Ops:
  5.6 2.2 %shard_map.205 = (bf16[2,4,152,512]{3,2,1,0:T(8,128)(2,1)S(1)}, bf16[2,4,152,512]{3,2,1,0:T(8,128)(2,1)S(1)}, f32[8,128]{1,0:T(8,128)S(1)}) custom-call(bf16[512,2432]{1,0:T(8,128)(2,1)S(1)} %copy-done.6), custom_call_target="tpu_custom_call" | custom-call | tf_op jit(solution)/shard_map/pallas_call | solution.py:56
  8.5 2.9 %collective-permute-start.6 = (bf16[1,608,512]{2,1,0:T(8,128)(2,1)S(1)}, bf16[1,608,512]{2,1,0:T(8,128)(2,1)}, u32[]{:S(2)}, u32[]{:S(2)}) collective-permute-start(bf16[1,608,512]{2,1,0:T(8,128)(2,1)S(1)} %get-tuple-element.175), channel_id=1, source_target_pairs={{0,1},{1,0},{2,3},{3,2},{4,5},{5,4},{6,7},{7,6},{8,9},{9,8},{10,11... | collective-permute-start | bytes 1867784 | tf_op jit(solution)/shard_map/ppermute | solution.py:91
  11.4 3.4 %shard_map.206 = (bf16[2,2,152,512]{3,2,1,0:T(8,128)(2,1)}, bf16[2,2,152,512]{3,2,1,0:T(8,128)(2,1)}, bf16[2,2,152,512]{3,2,1,0:T(8,128)(2,1)S(1)}, bf16[2,2,152,512]{3,2,1,0:T(8,128)(2,1)}, f32[8,128]{1,0:T(8,128)S(1)}) custom-call(bf16[512,2432]{1,0:T(8,128)(2,1)S(1)} %copy-done.4), custom_call_target="tpu_custom_call" | custom-call | tf_op jit(solution)/shard_map/pallas_call | solution.py:56
  14.8 2.2 %shard_map.207 = (f32[8,128]{1,0:T(8,128)S(1)}, bf16[2,608,512]{2,1,0:T(8,128)(2,1)}) custom-call(f32[2]{0:T(128)S(1)} %divide_bitcast_fusion.scale_ref, bf16[608,1024]{1,0:T(8,128)(2,1)S(1)} %copy-done.14, f32[8,128]{1,0:T(8,128)S(1)} %get-tuple-element.170.top_s_ref, f32[8,128]{1,0:T(8,128)S(1)} %get-tuple-element.171.top_f_ref, ...), custom_call_target="tpu_custom_call" | custom-call | tf_op jit(solution)/shard_map/pallas_call | solution.py:56
  17.5 2.1 %shard_map.208 = f32[1216,608]{1,0:T(8,128)S(1)} custom-call(bf16[1216,512]{1,0:T(8,128)(2,1)S(1)} %bitcast.94, bf16[1216,512]{1,0:T(8,128)(2,1)S(1)} %bitcast.96, bf16[1,608,512]{2,1,0:T(8,128)(2,1)S(1)} %get-tuple-element.180.refs_2_, bf16[1,608,512]{2,1,0:T(8,128)(2,1)S(1)} %collective-permute-done.8.refs_3_), custom_call_target="tpu_custom_call" | custom-call | tf_op jit(solution)/shard_map/pallas_call | solution.py:56
  21.3 2.1 %collective-permute-done.9 = f32[8,128]{1,0:T(8,128)S(1)} collective-permute-done((f32[8,128]{1,0:T(8,128)S(1)}, f32[8,128]{1,0:T(8,128)S(1)}, u32[]{:S(2)}, u32[]{:S(2)}) %collective-permute-start.9) | collective-permute-done | bytes 4128 | tf_op jit(solution)/shard_map/ppermute | solution.py:376
  25.0 2.0 collective-permute-done.10
  27.5 2.6 %collective-permute-start.12 = (f32[8,128]{1,0:T(8,128)S(1)}, f32[8,128]{1,0:T(8,128)S(1)}, u32[]{:S(2)}, u32[]{:S(2)}) collective-permute-start(f32[8,128]{1,0:T(8,128)S(1)} %max.29), channel_id=1, source_target_pairs={{0,16},{2,18},{4,20},{6,22},{8,24},{10,26},{12,28},{14,30},{16,0},... | collective-permute-start | bytes 12296 | tf_op jit(solution)/shard_map/ppermute | solution.py:376
  37.8 3.6 %shard_map.209 = f32[1216,608]{1,0:T(8,128)S(1)} custom-call(bf16[1216,512]{1,0:T(8,128)(2,1)S(1)} %bitcast.95, bf16[1216,512]{1,0:T(8,128)(2,1)S(1)} %bitcast.97, bf16[1,608,512]{2,1,0:T(8,128)(2,1)} %collective-permute-done.6.refs_2_, bf16[1,608,512]{2,1,0:T(8,128)(2,1)} %collective-permute-done.11.refs_3_), custom_call_target="tpu_custom_call" | custom-call | tf_op jit(solution)/shard_map/pallas_call | solution.py:56
  43.0 3.2 %shard_map.210.refs_4_ = bf16[608,1024]{1,0:T(8,128)(2,1)} custom-call(f32[2]{0:T(128)S(1)} %divide_bitcast_fusion.scale_ref, bf16[608,2432]{1,0:T(8,128)(2,1)S(1)} %copy-done, bf16[512,2432]{1,0:T(8,128)(2,1)S(1)} %copy-done.5), custom_call_target="tpu_custom_call" | custom-call | tf_op jit(solution)/shard_map/pallas_call | solution.py:56
  46.2 3.2 %shard_map.211.refs_1_ = bf16[608,1024]{1,0:T(8,128)(2,1)} custom-call(f32[2]{0:T(128)S(1)} %divide_bitcast_fusion.scale_ref, bf16[608,2432]{1,0:T(8,128)(2,1)S(1)} %copy-done.2, bf16[512,2432]{1,0:T(8,128)(2,1)S(1)} %copy-done.7), custom_call_target="tpu_custom_call" | custom-call | tf_op jit(solution)/shard_map/pallas_call | solution.py:56
  49.4 11.2 %collective-permute-done.16 = f32[8,128]{1,0:T(8,128)S(1)} collective-permute-done((f32[8,128]{1,0:T(8,128)S(1)}, f32[8,128]{1,0:T(8,128)S(1)}, u32[]{:S(2)}, u32[]{:S(2)}) %collective-permute-start.16) | collective-permute-done | bytes 4128 | tf_op jit(solution)/shard_map/ppermute | solution.py:376
  66.2 4.5 %shard_map.212 = f32[608,608]{1,0:T(8,128)S(1)} custom-call(bf16[608,512]{1,0:T(8,128)(2,1)} %bitcast.13.refs_0_, bf16[608,512]{1,0:T(8,128)(2,1)} %bitcast.14.refs_1_, bf16[608,512]{1,0:T(8,128)(2,1)} %bitcast.15.refs_2_, bf16[608,512]{1,0:T(8,128)(2,1)} %bitcast.16.refs_3_, bf16[2,608,512]{2,1,0:T(8,128)(2,1)} %get-tuple-element.227.refs_4_, ...), custom_call_target="tpu_custom_call" | custom-call | tf_op jit(solution)/shard_map/pallas_call | solution.py:56
  75.1 9.7 %collective-permute-done.19 = f16[4,152,608]{2,1,0:T(8,128)(2,1)S(1)} collective-permute-done((f16[4,152,608]{2,1,0:T(8,128)(2,1)S(1)}, f16[4,152,608]{2,1,0:T(8,128)(2,1)S(1)}, u32[]{:S(2)}, u32[]{:S(2)}) %collective-permute-start.19) | collective-permute-done | bytes 739360 | tf_op jit(solution)/shard_map/ppermute | solution.py:78
  86.9 3.1 %collective-permute-done.18 = f16[2,152,608]{2,1,0:T(8,128)(2,1)S(1)} collective-permute-done((f16[2,152,608]{2,1,0:T(8,128)(2,1)S(1)}, f16[2,152,608]{2,1,0:T(8,128)(2,1)S(1)}, u32[]{:S(2)}, u32[]{:S(2)}) %collective-permute-start.18) | collective-permute-done | bytes 369696 | tf_op jit(solution)/shard_map/ppermute | solution.py:78
  92.0 2.7 %collective-permute-start.22 = (f16[152,608]{1,0:T(8,128)(2,1)S(1)}, f16[152,608]{1,0:T(8,128)(2,1)S(1)}, u32[]{:S(2)}, u32[]{:S(2)}) collective-permute-start(f16[152,608]{1,0:T(8,128)(2,1)S(1)} %get-tuple-element.321), channel_id=1, source_target_pairs={{0,16},{2,18},{4,20},{6,22},{8,24},{10,26},{12,28},{14,30},{16,0},... | collective-permute-start | bytes 554504 | tf_op jit(solution)/shard_map/ppermute | solution.py:78
  94.7 4.2 %shard_map.213 = f32[608,608]{1,0:T(8,128)S(1)} custom-call(bf16[608,512]{1,0:T(8,128)(2,1)S(1)} %bitcast.99, bf16[608,512]{1,0:T(8,128)(2,1)} %bitcast.23.refs_1_, bf16[608,512]{1,0:T(8,128)(2,1)} %bitcast.24.refs_2_, bf16[608,512]{1,0:T(8,128)(2,1)S(1)} %bitcast.98, bf16[2,608,512]{2,1,0:T(8,128)(2,1)} %get-tuple-element.227.refs_4_, ...), custom_call_target="tpu_custom_call" | custom-call | tf_op jit(solution)/shard_map/pallas_call | solution.py:56
  102.4 2.2 %collective-permute-start.24 = (f16[152,608]{1,0:T(8,128)(2,1)S(1)}, f16[152,608]{1,0:T(8,128)(2,1)S(1)}, u32[]{:S(2)}, u32[]{:S(2)}) collective-permute-start(f16[152,608]{1,0:T(8,128)(2,1)S(1)} %get-tuple-element.318), channel_id=1, source_target_pairs={{0,16},{2,18},{4,20},{6,22},{8,24},{10,26},{12,28},{14,30},{16,0},... | collective-permute-start | bytes 554504 | tf_op jit(solution)/shard_map/ppermute | solution.py:78
  104.7 4.1 %collective-permute-done.20 = f16[2,152,608]{2,1,0:T(8,128)(2,1)S(1)} collective-permute-done((f16[2,152,608]{2,1,0:T(8,128)(2,1)S(1)}, f16[2,152,608]{2,1,0:T(8,128)(2,1)S(1)}, u32[]{:S(2)}, u32[]{:S(2)}) %collective-permute-start.20) | collective-permute-done | bytes 369696 | tf_op jit(solution)/shard_map/ppermute | solution.py:78
  110.3 9.6 %collective-permute-done.24 = f16[152,608]{1,0:T(8,128)(2,1)S(1)} collective-permute-done((f16[152,608]{1,0:T(8,128)(2,1)S(1)}, f16[152,608]{1,0:T(8,128)(2,1)S(1)}, u32[]{:S(2)}, u32[]{:S(2)}) %collective-permute-start.24) | collective-permute-done | bytes 184864 | tf_op jit(solution)/shard_map/ppermute | solution.py:78
  121.1 7.6 %collective-permute-done.27 = f32[152,608]{1,0:T(8,128)S(1)} collective-permute-done((f32[152,608]{1,0:T(8,128)S(1)}, f32[152,608]{1,0:T(8,128)S(1)}, u32[]{:S(2)}, u32[]{:S(2)}) %collective-permute-start.27) | collective-permute-done | bytes 369696 | tf_op jit(solution)/shard_map/ppermute | solution.py:91
  129.6 3.2 %collective-permute-done.28 = f32[8,128]{1,0:T(8,128)S(1)} collective-permute-done((f32[8,128]{1,0:T(8,128)S(1)}, f32[8,128]{1,0:T(8,128)S(1)}, u32[]{:S(2)}, u32[]{:S(2)}) %collective-permute-start.28) | collective-permute-done | bytes 4128 | tf_op jit(solution)/shard_map/ppermute | solution.py:91
  134.0 3.4 %collective-permute-start.30 = (f32[8,128]{1,0:T(8,128)S(1)}, f32[8,128]{1,0:T(8,128)S(1)}, u32[]{:S(2)}, u32[]{:S(2)}) collective-permute-start(f32[8,128]{1,0:T(8,128)S(1)} %add.78), channel_id=1, source_target_pairs={{0,16},{2,18},{4,20},{6,22},{8,24},{10,26},{12,28},{14,30},{16,0},... | collective-permute-start | bytes 12296 | tf_op jit(solution)/shard_map/ppermute | solution.py:78
  139.0 3.8 %collective-permute-done.31 = f32[8,128]{1,0:T(8,128)S(1)} collective-permute-done((f32[8,128]{1,0:T(8,128)S(1)}, f32[8,128]{1,0:T(8,128)S(1)}, u32[]{:S(2)}, u32[]{:S(2)}) %collective-permute-start.31) | collective-permute-done | bytes 4128 | tf_op jit(solution)/shard_map/ppermute | solution.py:78
  147.5 2.1 %shard_map.215 = (bf16[2,152,608]{2,1,0:T(8,128)(2,1)S(1)}, f32[152,608]{1,0:T(8,128)}, f32[152,608]{1,0:T(8,128)}, f32[152,608]{1,0:T(8,128)}, f32[152,608]{1,0...) custom-call(f32[8,128]{1,0:T(8,128)S(1)} %add_add_fusion.squares_ref, ...), custom_call_target="tpu_custom_call" | custom-call | tf_op jit(solution)/shard_map/pallas_call | solution.py:56
  151.1 16.0 %collective-permute-done.36 = bf16[2,152,608]{2,1,0:T(8,128)(2,1)S(1)} collective-permute-done((bf16[2,152,608]{2,1,0:T(8,128)(2,1)S(1)}, bf16[2,152,608]{2,1,0:T(8,128)(2,1)S(1)}, u32[]{:S(2)}, u32[]{:S(2)}) %collective-permute-start.36) | collective-permute-done | bytes 369696 | tf_op jit(solution)/shard_map/ppermute | solution.py:78
  167.6 2.7 %collective-permute-done.35 = bf16[2,152,608]{2,1,0:T(8,128)(2,1)S(1)} collective-permute-done((bf16[2,152,608]{2,1,0:T(8,128)(2,1)S(1)}, bf16[2,152,608]{2,1,0:T(8,128)(2,1)S(1)}, u32[]{:S(2)}, u32[]{:S(2)}) %collective-permute-start.35) | collective-permute-done | bytes 369696 | tf_op jit(solution)/shard_map/ppermute | solution.py:78
  170.8 8.2 %collective-permute-done.40 = bf16[2,152,608]{2,1,0:T(8,128)(2,1)S(1)} collective-permute-done((bf16[2,152,608]{2,1,0:T(8,128)(2,1)S(1)}, bf16[2,152,608]{2,1,0:T(8,128)(2,1)S(1)}, u32[]{:S(2)}, u32[]{:S(2)}) %collective-permute-start.40) | collective-permute-done | bytes 369696 | tf_op jit(solution)/shard_map/ppermute | solution.py:78
  180.9 5.2 %collective-permute-done.37 = bf16[2,152,608]{2,1,0:T(8,128)(2,1)S(1)} collective-permute-done((bf16[2,152,608]{2,1,0:T(8,128)(2,1)S(1)}, bf16[2,152,608]{2,1,0:T(8,128)(2,1)S(1)}, u32[]{:S(2)}, u32[]{:S(2)}) %collective-permute-start.37) | collective-permute-done | bytes 369696 | tf_op jit(solution)/shard_map/ppermute | solution.py:78
  189.2 4.4 %shard_map.216 = bf16[608,1024]{1,0:T(8,128)(2,1)} custom-call(f32[2]{0:T(128)S(1)} %divide_bitcast_fusion.scale_ref, bf16[608,2432]{1,0:T(8,128)(2,1)S(1)} %copy-done.1, bf16[2,2,152,512]{3,2,1,0:T(8,128)(2,1)} %collective-permute-done.refs_0_, bf16[2,2,152,512]{3,2,1,0:T(8,128)(2,1)S(1)} %collective-permute-done.41.refs_1_, ...), custom_call_target="tpu_custom_call", output_to_operand_aliasing={{}: (6, {})} | custom-call | tf_op jit(solution)/shard_map/pallas_call | solution.py:56
  193.6 3.2 %shard_map.217 = bf16[608,1024]{1,0:T(8,128)(2,1)} custom-call(f32[2]{0:T(128)S(1)} %divide_bitcast_fusion.scale_ref, bf16[608,2432]{1,0:T(8,128)(2,1)S(1)} %copy-done.3, bf16[512,2432]{1,0:T(8,128)(2,1)S(1)} %collective-permute-done.43.refs_0_, bf16[608,1024]{1,0:T(8,128)(2,1)} %shard_map.211.refs_1_), custom_call_target="tpu_custom_call", output_to_operand_aliasing={{}: (3, {})} | custom-call | tf_op jit(solution)/shard_map/pallas_call | solution.py:56
  200.0 5.2 %shard_map.218 = (bf16[608,2432]{1,0:T(8,128)(2,1)}, bf16[608,2432]{1,0:T(8,128)(2,1)}) custom-call(bf16[4,2,152,608]{3,2,1,0:T(8,128)(2,1)S(1)} %pad_maximum_fusion.refs_0_, bf16[4,2,152,608]{3,2,1,0:T(8,128)(2,1)S(1)} %collective-permute-done.44.refs_1_, bf16[2,2,152,608]{3,2,1,0:T(8,128)(2,1)S(1)} %pad_maximum_fusion.1.refs_2_, ...), custom_call_target="tpu_custom_call" | custom-call | tf_op jit(solution)/shard_map/pallas_call | solution.py:56
  (162 shorter events, 54.2 us)
Async XLA Ops:
  7.9 9.7 %collective-permute-start.5 = (bf16[2,4,152,512]{3,2,1,0:T(8,128)(2,1)S(1)}, bf16[2,4,152,512]{3,2,1,0:T(8,128)(2,1)S(1)}, u32[]{:S(2)}, u32[]{:S(2)}) collective-permute-start(bf16[2,4,152,512]{3,2,1,0:T(8,128)(2,1)S(1)} %get-tuple-element.174), channel_id=1, source_target_pairs={{0,2},{2,0},{4,6},{6,4},{8,10},{10,8},{12,14},{14,12},{16,18},{18,... | collective-permute-start | bytes 3735560 | tf_op jit(solution)/shard_map/ppermute | solution.py:78
  8.4 9.1 %collective-permute-start.8 = (bf16[1,608,512]{2,1,0:T(8,128)(2,1)S(1)}, bf16[1,608,512]{2,1,0:T(8,128)(2,1)S(1)}, u32[]{:S(2)}, u32[]{:S(2)}) collective-permute-start(bf16[1,608,512]{2,1,0:T(8,128)(2,1)S(1)} %get-tuple-element.180.refs_2_), channel_id=1, source_target_pairs={{0,2},{2,0},{4,6},{6,4},{8,10},{10,8},{12,14},{14,12},{16,18},{18,... | collective-permute-start | bytes 1867784 | tf_op jit(solution)/shard_map/ppermute | solution.py:78
  8.5 18.5 %collective-permute-start.6 = (bf16[1,608,512]{2,1,0:T(8,128)(2,1)S(1)}, bf16[1,608,512]{2,1,0:T(8,128)(2,1)}, u32[]{:S(2)}, u32[]{:S(2)}) collective-permute-start(bf16[1,608,512]{2,1,0:T(8,128)(2,1)S(1)} %get-tuple-element.175), channel_id=1, source_target_pairs={{0,1},{1,0},{2,3},{3,2},{4,5},{5,4},{6,7},{7,6},{8,9},{9,8},{10,11... | collective-permute-start | bytes 1867784 | tf_op jit(solution)/shard_map/ppermute | solution.py:91
  17.0 25.9 %collective-permute-start.2 = (bf16[2,608,512]{2,1,0:T(8,128)(2,1)}, bf16[2,608,512]{2,1,0:T(8,128)(2,1)}, u32[]{:S(2)}, u32[]{:S(2)}) collective-permute-start(bf16[2,608,512]{2,1,0:T(8,128)(2,1)} %get-tuple-element.227.refs_4_), channel_id=1, source_target_pairs={{0,2},{2,0},{4,6},{6,4},{8,10},{10,8},{12,14},{14,12},{16,18},{18,... | collective-permute-start | bytes 3735560 | tf_op jit(solution)/shard_map/ppermute | solution.py:78
  25.0 9.4 %collective-permute-start.3 = (bf16[2,2,152,512]{3,2,1,0:T(8,128)(2,1)}, bf16[2,2,152,512]{3,2,1,0:T(8,128)(2,1)}, u32[]{:S(2)}, u32[]{:S(2)}) collective-permute-start(bf16[2,2,152,512]{3,2,1,0:T(8,128)(2,1)} %get-tuple-element.164), channel_id=1, source_target_pairs={{0,2},{2,0},{4,6},{6,4},{8,10},{10,8},{12,14},{14,12},{16,18},{18,... | collective-permute-start | bytes 1867784 | tf_op jit(solution)/shard_map/ppermute | solution.py:78
  27.0 14.3 %collective-permute-start.4 = (bf16[2,2,152,512]{3,2,1,0:T(8,128)(2,1)}, bf16[2,2,152,512]{3,2,1,0:T(8,128)(2,1)}, u32[]{:S(2)}, u32[]{:S(2)}) collective-permute-start(bf16[2,2,152,512]{3,2,1,0:T(8,128)(2,1)} %get-tuple-element.200), channel_id=1, source_target_pairs={{0,2},{2,0},{4,6},{6,4},{8,10},{10,8},{12,14},{14,12},{16,18},{18,... | collective-permute-start | bytes 1867784 | tf_op jit(solution)/shard_map/ppermute | solution.py:78
  32.0 34.1 %collective-permute-start = (bf16[2,2,152,512]{3,2,1,0:T(8,128)(2,1)}, bf16[2,2,152,512]{3,2,1,0:T(8,128)(2,1)}, u32[]{:S(2)}, u32[]{:S(2)}) collective-permute-start(bf16[2,2,152,512]{3,2,1,0:T(8,128)(2,1)} %get-tuple-element.209), channel_id=1, source_target_pairs={{0,1},{1,0},{2,3},{3,2},{4,5},{5,4},{6,7},{7,6},{8,9},{9,8},{10,11... | collective-permute-start | bytes 1867784 | tf_op jit(solution)/shard_map/ppermute | solution.py:91
  34.4 31.7 %collective-permute-start.1 = (bf16[2,2,152,512]{3,2,1,0:T(8,128)(2,1)}, bf16[2,2,152,512]{3,2,1,0:T(8,128)(2,1)}, u32[]{:S(2)}, u32[]{:S(2)}) collective-permute-start(bf16[2,2,152,512]{3,2,1,0:T(8,128)(2,1)} %get-tuple-element.164), channel_id=1, source_target_pairs={{0,3},{1,2},{2,1},{3,0},{4,7},{5,6},{6,5},{7,4},{8,11},{9,10},{10,... | collective-permute-start | bytes 1867784 | tf_op jit(solution)/shard_map/ppermute | solution.py:100
  34.5 26.0 %collective-permute-start.16 = (f32[8,128]{1,0:T(8,128)S(1)}, f32[8,128]{1,0:T(8,128)S(1)}, u32[]{:S(2)}, u32[]{:S(2)}) collective-permute-start(f32[8,128]{1,0:T(8,128)S(1)} %max.30), channel_id=1, source_target_pairs={{0,1},{1,0},{2,3},{3,2},{4,5},{5,4},{6,7},{7,6},{8,9},{9,8},{10,11... | collective-permute-start | bytes 12296 | tf_op jit(solution)/shard_map/ppermute | solution.py:376
  41.3 30.0 %collective-permute-start.15 = (f16[4,152,608]{2,1,0:T(8,128)(2,1)}, f16[4,152,608]{2,1,0:T(8,128)(2,1)}, u32[]{:S(2)}, u32[]{:S(2)}) collective-permute-start(f16[4,152,608]{2,1,0:T(8,128)(2,1)} %get-tuple-element.309), channel_id=1, source_target_pairs={{0,4},{2,6},{4,0},{6,2},{8,12},{10,14},{12,8},{14,10},{16,20},{18,... | collective-permute-start | bytes 2217992 | tf_op jit(solution)/shard_map/ppermute | solution.py:78
  62.4 32.3 %collective-permute-start.14 = (bf16[2,2,152,512]{3,2,1,0:T(8,128)(2,1)}, bf16[2,2,152,512]{3,2,1,0:T(8,128)(2,1)}, u32[]{:S(2)}, u32[]{:S(2)}) collective-permute-start(bf16[2,2,152,512]{3,2,1,0:T(8,128)(2,1)} %copy-done.15), channel_id=1, source_target_pairs={{0,1},{1,0},{2,3},{3,2},{4,5},{5,4},{6,7},{7,6},{8,9},{9,8},{10,11... | collective-permute-start | bytes 1867784 | tf_op jit(solution)/shard_map/ppermute | solution.py:91
  64.5 20.4 %collective-permute-start.19 = (f16[4,152,608]{2,1,0:T(8,128)(2,1)S(1)}, f16[4,152,608]{2,1,0:T(8,128)(2,1)S(1)}, u32[]{:S(2)}, u32[]{:S(2)}) collective-permute-start(f16[4,152,608]{2,1,0:T(8,128)(2,1)S(1)} %get-tuple-element.307), channel_id=1, source_target_pairs={{0,4},{2,6},{4,0},{6,2},{8,12},{10,14},{12,8},{14,10},{16,20},{18,... | collective-permute-start | bytes 2217992 | tf_op jit(solution)/shard_map/ppermute | solution.py:78
  70.8 19.2 %collective-permute-start.18 = (f16[2,152,608]{2,1,0:T(8,128)(2,1)S(1)}, f16[2,152,608]{2,1,0:T(8,128)(2,1)S(1)}, u32[]{:S(2)}, u32[]{:S(2)}) collective-permute-start(f16[2,152,608]{2,1,0:T(8,128)(2,1)S(1)} %fusion.4), channel_id=1, source_target_pairs={{0,4},{2,6},{4,0},{6,2},{8,12},{10,14},{12,8},{14,10},{16,20},{18,... | collective-permute-start | bytes 1109000 | tf_op jit(solution)/shard_map/ppermute | solution.py:78
  71.3 23.4 %collective-permute-start.13 = (bf16[2,2,152,512]{3,2,1,0:T(8,128)(2,1)}, bf16[2,2,152,512]{3,2,1,0:T(8,128)(2,1)S(1)}, u32[]{:S(2)}, u32[]{:S(2)}) collective-permute-start(bf16[2,2,152,512]{3,2,1,0:T(8,128)(2,1)} %get-tuple-element.200), channel_id=1, source_target_pairs={{0,3},{1,2},{2,1},{3,0},{4,7},{5,6},{6,5},{7,4},{8,11},{9,10},{10,... | collective-permute-start | bytes 1867784 | tf_op jit(solution)/shard_map/ppermute | solution.py:100
  73.5 18.4 %collective-permute-start.17 = (f16[2,152,608]{2,1,0:T(8,128)(2,1)S(1)}, f16[2,152,608]{2,1,0:T(8,128)(2,1)S(1)}, u32[]{:S(2)}, u32[]{:S(2)}) collective-permute-start(f16[2,152,608]{2,1,0:T(8,128)(2,1)S(1)} %get-tuple-element.316), channel_id=1, source_target_pairs={{0,8},{2,10},{4,12},{6,14},{8,0},{10,2},{12,4},{14,6},{16,24},{18,... | collective-permute-start | bytes 1109000 | tf_op jit(solution)/shard_map/ppermute | solution.py:78
  85.2 17.0 %collective-permute-start.23 = (f16[2,152,608]{2,1,0:T(8,128)(2,1)S(1)}, f16[2,152,608]{2,1,0:T(8,128)(2,1)S(1)}, u32[]{:S(2)}, u32[]{:S(2)}) collective-permute-start(f16[2,152,608]{2,1,0:T(8,128)(2,1)S(1)} %get-tuple-element.315), channel_id=1, source_target_pairs={{0,8},{2,10},{4,12},{6,14},{8,0},{10,2},{12,4},{14,6},{16,24},{18,... | collective-permute-start | bytes 1109000 | tf_op jit(solution)/shard_map/ppermute | solution.py:78
  90.2 18.7 %collective-permute-start.20 = (f16[2,152,608]{2,1,0:T(8,128)(2,1)S(1)}, f16[2,152,608]{2,1,0:T(8,128)(2,1)S(1)}, u32[]{:S(2)}, u32[]{:S(2)}) collective-permute-start(f16[2,152,608]{2,1,0:T(8,128)(2,1)S(1)} %multiply_convert_fusion.2), channel_id=1, source_target_pairs={{0,8},{2,10},{4,12},{6,14},{8,0},{10,2},{12,4},{14,6},{16,24},{18,... | collective-permute-start | bytes 1109000 | tf_op jit(solution)/shard_map/ppermute | solution.py:78
  92.0 28.6 %collective-permute-start.22 = (f16[152,608]{1,0:T(8,128)(2,1)S(1)}, f16[152,608]{1,0:T(8,128)(2,1)S(1)}, u32[]{:S(2)}, u32[]{:S(2)}) collective-permute-start(f16[152,608]{1,0:T(8,128)(2,1)S(1)} %get-tuple-element.321), channel_id=1, source_target_pairs={{0,16},{2,18},{4,20},{6,22},{8,24},{10,26},{12,28},{14,30},{16,0},... | collective-permute-start | bytes 554504 | tf_op jit(solution)/shard_map/ppermute | solution.py:78
  100.6 20.2 %collective-permute-start.21 = (f16[152,608]{1,0:T(8,128)(2,1)S(1)}, f16[152,608]{1,0:T(8,128)(2,1)S(1)}, u32[]{:S(2)}, u32[]{:S(2)}) collective-permute-start(f16[152,608]{1,0:T(8,128)(2,1)S(1)} %get-tuple-element.312), channel_id=1, source_target_pairs={{0,4},{2,6},{4,0},{6,2},{8,12},{10,14},{12,8},{14,10},{16,20},{18,... | collective-permute-start | bytes 554504 | tf_op jit(solution)/shard_map/ppermute | solution.py:78
  102.4 17.5 %collective-permute-start.24 = (f16[152,608]{1,0:T(8,128)(2,1)S(1)}, f16[152,608]{1,0:T(8,128)(2,1)S(1)}, u32[]{:S(2)}, u32[]{:S(2)}) collective-permute-start(f16[152,608]{1,0:T(8,128)(2,1)S(1)} %get-tuple-element.318), channel_id=1, source_target_pairs={{0,16},{2,18},{4,20},{6,22},{8,24},{10,26},{12,28},{14,30},{16,0},... | collective-permute-start | bytes 554504 | tf_op jit(solution)/shard_map/ppermute | solution.py:78
  109.0 19.8 %collective-permute-start.26 = (f16[152,608]{1,0:T(8,128)(2,1)S(1)}, f16[152,608]{1,0:T(8,128)(2,1)S(1)}, u32[]{:S(2)}, u32[]{:S(2)}) collective-permute-start(f16[152,608]{1,0:T(8,128)(2,1)S(1)} %fusion.12), channel_id=1, source_target_pairs={{0,16},{2,18},{4,20},{6,22},{8,24},{10,26},{12,28},{14,30},{16,0},... | collective-permute-start | bytes 554504 | tf_op jit(solution)/shard_map/ppermute | solution.py:78
  120.0 8.8 %collective-permute-start.27 = (f32[152,608]{1,0:T(8,128)S(1)}, f32[152,608]{1,0:T(8,128)S(1)}, u32[]{:S(2)}, u32[]{:S(2)}) collective-permute-start(f32[152,608]{1,0:T(8,128)S(1)} %multiply_add_fusion.6), channel_id=1, source_target_pairs={{0,1},{1,0},{2,3},{3,2},{4,5},{5,4},{6,7},{7,6},{8,9},{9,8},{10,11... | collective-permute-start | bytes 1109000 | tf_op jit(solution)/shard_map/ppermute | solution.py:91
  132.9 60.7 %collective-permute-start.43 = (bf16[512,2432]{1,0:T(8,128)(2,1)S(1)}, bf16[512,2432]{1,0:T(8,128)(2,1)S(1)}, u32[]{:S(2)}, u32[]{:S(2)}) collective-permute-start(bf16[512,2432]{1,0:T(8,128)(2,1)S(1)} %copy-done.8), channel_id=1, source_target_pairs={{0,1},{1,0},{2,3},{3,2},{4,5},{5,4},{6,7},{7,6},{8,9},{9,8},{10,11... | collective-permute-start | bytes 7471112 | tf_op jit(solution)/shard_map/ppermute | solution.py:91
  149.6 17.5 %collective-permute-start.36 = (bf16[2,152,608]{2,1,0:T(8,128)(2,1)S(1)}, bf16[2,152,608]{2,1,0:T(8,128)(2,1)S(1)}, u32[]{:S(2)}, u32[]{:S(2)}) collective-permute-start(bf16[2,152,608]{2,1,0:T(8,128)(2,1)S(1)} %get-tuple-element.270), channel_id=1, source_target_pairs={{0,8},{2,10},{4,12},{6,14},{8,0},{10,2},{12,4},{14,6},{16,24},{18,... | collective-permute-start | bytes 1109000 | tf_op jit(solution)/shard_map/ppermute | solution.py:78
  149.6 20.7 %collective-permute-start.35 = (bf16[2,152,608]{2,1,0:T(8,128)(2,1)S(1)}, bf16[2,152,608]{2,1,0:T(8,128)(2,1)S(1)}, u32[]{:S(2)}, u32[]{:S(2)}) collective-permute-start(bf16[2,152,608]{2,1,0:T(8,128)(2,1)S(1)} %get-tuple-element.270), channel_id=1, source_target_pairs={{0,16},{2,18},{4,20},{6,22},{8,24},{10,26},{12,28},{14,30},{16,0},... | collective-permute-start | bytes 1109000 | tf_op jit(solution)/shard_map/ppermute | solution.py:78
  150.5 20.3 %collective-permute-start.39 = (bf16[2,152,608]{2,1,0:T(8,128)(2,1)S(1)}, bf16[2,152,608]{2,1,0:T(8,128)(2,1)S(1)}, u32[]{:S(2)}, u32[]{:S(2)}) collective-permute-start(bf16[2,152,608]{2,1,0:T(8,128)(2,1)S(1)} %get-tuple-element.270), channel_id=1, source_target_pairs={{0,4},{2,6},{4,0},{6,2},{8,12},{10,14},{12,8},{14,10},{16,20},{18,... | collective-permute-start | bytes 1109000 | tf_op jit(solution)/shard_map/ppermute | solution.py:78
  167.1 11.9 %collective-permute-start.40 = (bf16[2,152,608]{2,1,0:T(8,128)(2,1)S(1)}, bf16[2,152,608]{2,1,0:T(8,128)(2,1)S(1)}, u32[]{:S(2)}, u32[]{:S(2)}) collective-permute-start(bf16[2,152,608]{2,1,0:T(8,128)(2,1)S(1)} %collective-permute-done.36), channel_id=1, source_target_pairs={{0,4},{2,6},{4,0},{6,2},{8,12},{10,14},{12,8},{14,10},{16,20},{18,... | collective-permute-start | bytes 1109000 | tf_op jit(solution)/shard_map/ppermute | solution.py:78
  170.3 10.6 %collective-permute-start.38 = (bf16[2,152,608]{2,1,0:T(8,128)(2,1)S(1)}, bf16[2,152,608]{2,1,0:T(8,128)(2,1)S(1)}, u32[]{:S(2)}, u32[]{:S(2)}) collective-permute-start(bf16[2,152,608]{2,1,0:T(8,128)(2,1)S(1)} %collective-permute-done.35), channel_id=1, source_target_pairs={{0,8},{2,10},{4,12},{6,14},{8,0},{10,2},{12,4},{14,6},{16,24},{18,... | collective-permute-start | bytes 1109000 | tf_op jit(solution)/shard_map/ppermute | solution.py:78
  170.3 15.8 %collective-permute-start.37 = (bf16[2,152,608]{2,1,0:T(8,128)(2,1)S(1)}, bf16[2,152,608]{2,1,0:T(8,128)(2,1)S(1)}, u32[]{:S(2)}, u32[]{:S(2)}) collective-permute-start(bf16[2,152,608]{2,1,0:T(8,128)(2,1)S(1)} %collective-permute-done.35), channel_id=1, source_target_pairs={{0,4},{2,6},{4,0},{6,2},{8,12},{10,14},{12,8},{14,10},{16,20},{18,... | collective-permute-start | bytes 1109000 | tf_op jit(solution)/shard_map/ppermute | solution.py:78
  179.3 18.9 %collective-permute-start.44 = (bf16[4,2,152,608]{3,2,1,0:T(8,128)(2,1)S(1)}, bf16[4,2,152,608]{3,2,1,0:T(8,128)(2,1)S(1)}, u32[]{:S(2)}, u32[]{:S(2)}) collective-permute-start(bf16[4,2,152,608]{3,2,1,0:T(8,128)(2,1)S(1)} %pad_maximum_fusion.refs_0_), channel_id=1, source_target_pairs={{0,2},{2,0},{4,6},{6,4},{8,10},{10,8},{12,14},{14,12},{16,18},{18,... | collective-permute-start | bytes 4435976 | tf_op jit(solution)/shard_map/ppermute | solution.py:78
  186.7 11.0 %collective-permute-start.46 = (bf16[2,152,608]{2,1,0:T(8,128)(2,1)S(1)}, bf16[2,152,608]{2,1,0:T(8,128)(2,1)S(1)}, u32[]{:S(2)}, u32[]{:S(2)}) collective-permute-start(bf16[2,152,608]{2,1,0:T(8,128)(2,1)S(1)} %collective-permute-done.38.refs_4_), channel_id=1, source_target_pairs={{0,4},{2,6},{4,0},{6,2},{8,12},{10,14},{12,8},{14,10},{16,20},{18,... | collective-permute-start | bytes 1109000 | tf_op jit(solution)/shard_map/ppermute | solution.py:78
  188.6 9.7 %collective-permute-start.45 = (bf16[2,2,152,608]{3,2,1,0:T(8,128)(2,1)S(1)}, bf16[2,2,152,608]{3,2,1,0:T(8,128)(2,1)S(1)}, u32[]{:S(2)}, u32[]{:S(2)}) collective-permute-start(bf16[2,2,152,608]{3,2,1,0:T(8,128)(2,1)S(1)} %pad_maximum_fusion.1.refs_2_), channel_id=1, source_target_pairs={{0,2},{2,0},{4,6},{6,4},{8,10},{10,8},{12,14},{14,12},{16,18},{18,... | collective-permute-start | bytes 2217992 | tf_op jit(solution)/shard_map/ppermute | solution.py:78
  (41 other events, 312.9 us)

commit v14 on v12

--- a/solution.py
+++ b/solution.py
@@ -302,7 +302,7 @@
         return call(
             kernel, array((f, count), jnp.bfloat16), *operands,
             in_specs=in_specs, out_specs=ANY, scratch_shapes=scratch,
-            input_output_aliases=aliases, mib=20,
+            input_output_aliases=aliases, mib=16,
         )
 
     def spread(blocks, *arrays):
@@ -344,7 +344,7 @@
                 pltpu.VMEM((2, TILE, D), jnp.bfloat16),
                 pltpu.SemaphoreType.DMA((2,)),
             ],
-            mib=20,
+            mib=16,
         )
 
     def per_device(

time: 205 us -> 205 us (level)
  no operation moved by 1% of the time
where the time goes in v14:
time: 205 us
  waiting for transfers between devices  101 us (49%)
  Pallas kernels  44.9 us (22%)
  starting transfers between devices  42.5 us (21%)
  other arithmetic  5.9 us (3%)
  between operations  5.42 us (3%)
  local copies, waits for them, and re-layouts  5.09 us (2%)
    ppermute x36, waiting for transfers between devices, move_dp(): return lax.ppermute(value, 'dp', perm)  72 us
    pallas_call x15, Pallas kernels, call(): pl.pallas_call(kernel, out_shape=out_shape, compiler_params=pltpu.Compile...  44.9 us
    ppermute x36, starting transfers between devices, move_dp(): return lax.ppermute(value, 'dp', perm)  28.5 us
    ppermute x5, waiting for transfers between devices, hops(): got = lax.ppermute(value, axis, perm)  17.2 us
    ppermute x6, waiting for transfers between devices, from_tensor(): return lax.ppermute(value, 'tensor', perm)  11.5 us
    ppermute x5, starting transfers between devices, hops(): got = lax.ppermute(value, axis, perm)  7.86 us
    ppermute x6, starting transfers between devices, from_tensor(): return lax.ppermute(value, 'tensor', perm)  6.06 us
  transfers between devices with their start and end apart: 49, of which 25 were waited for; matrix products, arithmetic and copies ran while one was open for 3% of the time, Pallas kernels for 18%

profile of v14, /device:TPU:0, one launch (start us, length us, event | category | flops | bytes accessed | tf_op | source)
XLA Modules:
  0.0 204.5 jit_solution(5488591315897645510)
XLA Ops:
  5.6 2.2 %shard_map.205 = (bf16[2,4,152,512]{3,2,1,0:T(8,128)(2,1)S(1)}, bf16[2,4,152,512]{3,2,1,0:T(8,128)(2,1)S(1)}, f32[8,128]{1,0:T(8,128)S(1)}) custom-call(bf16[512,2432]{1,0:T(8,128)(2,1)S(1)} %copy-done.6), custom_call_target="tpu_custom_call" | custom-call | tf_op jit(solution)/shard_map/pallas_call | solution.py:56
  8.5 2.9 %collective-permute-start.6 = (bf16[1,608,512]{2,1,0:T(8,128)(2,1)S(1)}, bf16[1,608,512]{2,1,0:T(8,128)(2,1)}, u32[]{:S(2)}, u32[]{:S(2)}) collective-permute-start(bf16[1,608,512]{2,1,0:T(8,128)(2,1)S(1)} %get-tuple-element.175), channel_id=1, source_target_pairs={{0,1},{1,0},{2,3},{3,2},{4,5},{5,4},{6,7},{7,6},{8,9},{9,8},{10,11... | collective-permute-start | bytes 1867784 | tf_op jit(solution)/shard_map/ppermute | solution.py:91
  11.4 3.4 %shard_map.206 = (bf16[2,2,152,512]{3,2,1,0:T(8,128)(2,1)}, bf16[2,2,152,512]{3,2,1,0:T(8,128)(2,1)}, bf16[2,2,152,512]{3,2,1,0:T(8,128)(2,1)S(1)}, bf16[2,2,152,512]{3,2,1,0:T(8,128)(2,1)}, f32[8,128]{1,0:T(8,128)S(1)}) custom-call(bf16[512,2432]{1,0:T(8,128)(2,1)S(1)} %copy-done.4), custom_call_target="tpu_custom_call" | custom-call | tf_op jit(solution)/shard_map/pallas_call | solution.py:56
  14.8 2.2 %shard_map.207 = (f32[8,128]{1,0:T(8,128)S(1)}, bf16[2,608,512]{2,1,0:T(8,128)(2,1)}) custom-call(f32[2]{0:T(128)S(1)} %divide_bitcast_fusion.scale_ref, bf16[608,1024]{1,0:T(8,128)(2,1)S(1)} %copy-done.14, f32[8,128]{1,0:T(8,128)S(1)} %get-tuple-element.170.top_s_ref, f32[8,128]{1,0:T(8,128)S(1)} %get-tuple-element.171.top_f_ref, ...), custom_call_target="tpu_custom_call" | custom-call | tf_op jit(solution)/shard_map/pallas_call | solution.py:56
  17.5 2.1 %shard_map.208 = f32[1216,608]{1,0:T(8,128)S(1)} custom-call(bf16[1216,512]{1,0:T(8,128)(2,1)S(1)} %bitcast.94, bf16[1216,512]{1,0:T(8,128)(2,1)S(1)} %bitcast.96, bf16[1,608,512]{2,1,0:T(8,128)(2,1)S(1)} %get-tuple-element.180.refs_2_, bf16[1,608,512]{2,1,0:T(8,128)(2,1)S(1)} %collective-permute-done.8.refs_3_), custom_call_target="tpu_custom_call" | custom-call | tf_op jit(solution)/shard_map/pallas_call | solution.py:56
  21.3 2.1 %collective-permute-done.9 = f32[8,128]{1,0:T(8,128)S(1)} collective-permute-done((f32[8,128]{1,0:T(8,128)S(1)}, f32[8,128]{1,0:T(8,128)S(1)}, u32[]{:S(2)}, u32[]{:S(2)}) %collective-permute-start.9) | collective-permute-done | bytes 4128 | tf_op jit(solution)/shard_map/ppermute | solution.py:376
  27.5 2.6 %collective-permute-start.12 = (f32[8,128]{1,0:T(8,128)S(1)}, f32[8,128]{1,0:T(8,128)S(1)}, u32[]{:S(2)}, u32[]{:S(2)}) collective-permute-start(f32[8,128]{1,0:T(8,128)S(1)} %max.29), channel_id=1, source_target_pairs={{0,16},{2,18},{4,20},{6,22},{8,24},{10,26},{12,28},{14,30},{16,0},... | collective-permute-start | bytes 12296 | tf_op jit(solution)/shard_map/ppermute | solution.py:376
  37.8 3.6 %shard_map.209 = f32[1216,608]{1,0:T(8,128)S(1)} custom-call(bf16[1216,512]{1,0:T(8,128)(2,1)S(1)} %bitcast.95, bf16[1216,512]{1,0:T(8,128)(2,1)S(1)} %bitcast.97, bf16[1,608,512]{2,1,0:T(8,128)(2,1)} %collective-permute-done.6.refs_2_, bf16[1,608,512]{2,1,0:T(8,128)(2,1)} %collective-permute-done.11.refs_3_), custom_call_target="tpu_custom_call" | custom-call | tf_op jit(solution)/shard_map/pallas_call | solution.py:56
  43.0 3.2 %shard_map.210.refs_4_ = bf16[608,1024]{1,0:T(8,128)(2,1)} custom-call(f32[2]{0:T(128)S(1)} %divide_bitcast_fusion.scale_ref, bf16[608,2432]{1,0:T(8,128)(2,1)S(1)} %copy-done, bf16[512,2432]{1,0:T(8,128)(2,1)S(1)} %copy-done.5), custom_call_target="tpu_custom_call" | custom-call | tf_op jit(solution)/shard_map/pallas_call | solution.py:56
  46.2 3.2 %shard_map.211.refs_1_ = bf16[608,1024]{1,0:T(8,128)(2,1)} custom-call(f32[2]{0:T(128)S(1)} %divide_bitcast_fusion.scale_ref, bf16[608,2432]{1,0:T(8,128)(2,1)S(1)} %copy-done.2, bf16[512,2432]{1,0:T(8,128)(2,1)S(1)} %copy-done.7), custom_call_target="tpu_custom_call" | custom-call | tf_op jit(solution)/shard_map/pallas_call | solution.py:56
  49.4 11.2 %collective-permute-done.16 = f32[8,128]{1,0:T(8,128)S(1)} collective-permute-done((f32[8,128]{1,0:T(8,128)S(1)}, f32[8,128]{1,0:T(8,128)S(1)}, u32[]{:S(2)}, u32[]{:S(2)}) %collective-permute-start.16) | collective-permute-done | bytes 4128 | tf_op jit(solution)/shard_map/ppermute | solution.py:376
  66.2 4.5 %shard_map.212 = f32[608,608]{1,0:T(8,128)S(1)} custom-call(bf16[608,512]{1,0:T(8,128)(2,1)} %bitcast.13.refs_0_, bf16[608,512]{1,0:T(8,128)(2,1)} %bitcast.14.refs_1_, bf16[608,512]{1,0:T(8,128)(2,1)} %bitcast.15.refs_2_, bf16[608,512]{1,0:T(8,128)(2,1)} %bitcast.16.refs_3_, bf16[2,608,512]{2,1,0:T(8,128)(2,1)} %get-tuple-element.227.refs_4_, ...), custom_call_target="tpu_custom_call" | custom-call | tf_op jit(solution)/shard_map/pallas_call | solution.py:56
  75.1 9.7 %collective-permute-done.19 = f16[4,152,608]{2,1,0:T(8,128)(2,1)S(1)} collective-permute-done((f16[4,152,608]{2,1,0:T(8,128)(2,1)S(1)}, f16[4,152,608]{2,1,0:T(8,128)(2,1)S(1)}, u32[]{:S(2)}, u32[]{:S(2)}) %collective-permute-start.19) | collective-permute-done | bytes 739360 | tf_op jit(solution)/shard_map/ppermute | solution.py:78
  86.8 3.2 %collective-permute-done.18 = f16[2,152,608]{2,1,0:T(8,128)(2,1)S(1)} collective-permute-done((f16[2,152,608]{2,1,0:T(8,128)(2,1)S(1)}, f16[2,152,608]{2,1,0:T(8,128)(2,1)S(1)}, u32[]{:S(2)}, u32[]{:S(2)}) %collective-permute-start.18) | collective-permute-done | bytes 369696 | tf_op jit(solution)/shard_map/ppermute | solution.py:78
  92.0 2.7 %collective-permute-start.25 = (f16[152,608]{1,0:T(8,128)(2,1)S(1)}, f16[152,608]{1,0:T(8,128)(2,1)S(1)}, u32[]{:S(2)}, u32[]{:S(2)}) collective-permute-start(f16[152,608]{1,0:T(8,128)(2,1)S(1)} %get-tuple-element.319), channel_id=1, source_target_pairs={{0,16},{2,18},{4,20},{6,22},{8,24},{10,26},{12,28},{14,30},{16,0},... | collective-permute-start | bytes 554504 | tf_op jit(solution)/shard_map/ppermute | solution.py:78
  94.7 4.2 %shard_map.213 = f32[608,608]{1,0:T(8,128)S(1)} custom-call(bf16[608,512]{1,0:T(8,128)(2,1)S(1)} %bitcast.99, bf16[608,512]{1,0:T(8,128)(2,1)} %bitcast.23.refs_1_, bf16[608,512]{1,0:T(8,128)(2,1)} %bitcast.24.refs_2_, bf16[608,512]{1,0:T(8,128)(2,1)S(1)} %bitcast.98, bf16[2,608,512]{2,1,0:T(8,128)(2,1)} %get-tuple-element.227.refs_4_, ...), custom_call_target="tpu_custom_call" | custom-call | tf_op jit(solution)/shard_map/pallas_call | solution.py:56
  102.3 2.1 %collective-permute-start.24 = (f16[152,608]{1,0:T(8,128)(2,1)S(1)}, f16[152,608]{1,0:T(8,128)(2,1)S(1)}, u32[]{:S(2)}, u32[]{:S(2)}) collective-permute-start(f16[152,608]{1,0:T(8,128)(2,1)S(1)} %get-tuple-element.320), channel_id=1, source_target_pairs={{0,16},{2,18},{4,20},{6,22},{8,24},{10,26},{12,28},{14,30},{16,0},... | collective-permute-start | bytes 554504 | tf_op jit(solution)/shard_map/ppermute | solution.py:78
  104.5 3.0 %collective-permute-done.25 = f16[152,608]{1,0:T(8,128)(2,1)S(1)} collective-permute-done((f16[152,608]{1,0:T(8,128)(2,1)S(1)}, f16[152,608]{1,0:T(8,128)(2,1)S(1)}, u32[]{:S(2)}, u32[]{:S(2)}) %collective-permute-start.25) | collective-permute-done | bytes 184864 | tf_op jit(solution)/shard_map/ppermute | solution.py:78
  107.5 10.3 %collective-permute-done.24 = f16[152,608]{1,0:T(8,128)(2,1)S(1)} collective-permute-done((f16[152,608]{1,0:T(8,128)(2,1)S(1)}, f16[152,608]{1,0:T(8,128)(2,1)S(1)}, u32[]{:S(2)}, u32[]{:S(2)}) %collective-permute-start.24) | collective-permute-done | bytes 184864 | tf_op jit(solution)/shard_map/ppermute | solution.py:78
  119.2 8.5 %collective-permute-done.27 = f32[152,608]{1,0:T(8,128)S(1)} collective-permute-done((f32[152,608]{1,0:T(8,128)S(1)}, f32[152,608]{1,0:T(8,128)S(1)}, u32[]{:S(2)}, u32[]{:S(2)}) %collective-permute-start.27) | collective-permute-done | bytes 369696 | tf_op jit(solution)/shard_map/ppermute | solution.py:91
  128.8 3.1 %collective-permute-done.28 = f32[8,128]{1,0:T(8,128)S(1)} collective-permute-done((f32[8,128]{1,0:T(8,128)S(1)}, f32[8,128]{1,0:T(8,128)S(1)}, u32[]{:S(2)}, u32[]{:S(2)}) %collective-permute-start.28) | collective-permute-done | bytes 4128 | tf_op jit(solution)/shard_map/ppermute | solution.py:91
  132.5 2.3 %collective-permute-start.30 = (f32[8,128]{1,0:T(8,128)S(1)}, f32[8,128]{1,0:T(8,128)S(1)}, u32[]{:S(2)}, u32[]{:S(2)}) collective-permute-start(f32[8,128]{1,0:T(8,128)S(1)} %add.78), channel_id=1, source_target_pairs={{0,16},{2,18},{4,20},{6,22},{8,24},{10,26},{12,28},{14,30},{16,0},... | collective-permute-start | bytes 12296 | tf_op jit(solution)/shard_map/ppermute | solution.py:78
  134.8 2.0 %collective-permute-start.31 = (f32[8,128]{1,0:T(8,128)S(1)}, f32[8,128]{1,0:T(8,128)S(1)}, u32[]{:S(2)}, u32[]{:S(2)}) collective-permute-start(f32[8,128]{1,0:T(8,128)S(1)} %add.78), channel_id=1, source_target_pairs={{0,24},{2,26},{4,28},{6,30},{8,16},{10,18},{12,20},{14,22},{16,8},... | collective-permute-start | bytes 12296 | tf_op jit(solution)/shard_map/ppermute | solution.py:78
  137.0 3.2 %collective-permute-done.31 = f32[8,128]{1,0:T(8,128)S(1)} collective-permute-done((f32[8,128]{1,0:T(8,128)S(1)}, f32[8,128]{1,0:T(8,128)S(1)}, u32[]{:S(2)}, u32[]{:S(2)}) %collective-permute-start.31) | collective-permute-done | bytes 4128 | tf_op jit(solution)/shard_map/ppermute | solution.py:78
  140.2 2.3 %collective-permute-start.33 = (f32[8,128]{1,0:T(8,128)S(1)}, f32[8,128]{1,0:T(8,128)S(1)}, u32[]{:S(2)}, u32[]{:S(2)}) collective-permute-start(f32[8,128]{1,0:T(8,128)S(1)} %add_add_fusion.1), channel_id=1, source_target_pairs={{0,4},{2,6},{4,0},{6,2},{8,12},{10,14},{12,8},{14,10},{16,20},{18,... | collective-permute-start | bytes 12296 | tf_op jit(solution)/shard_map/ppermute | solution.py:78
  145.6 2.1 %shard_map.215 = (bf16[2,152,608]{2,1,0:T(8,128)(2,1)S(1)}, f32[152,608]{1,0:T(8,128)}, f32[152,608]{1,0:T(8,128)}, f32[152,608]{1,0:T(8,128)}, f32[152,608]{1,0...) custom-call(f32[8,128]{1,0:T(8,128)S(1)} %add_add_fusion.squares_ref, ...), custom_call_target="tpu_custom_call" | custom-call | tf_op jit(solution)/shard_map/pallas_call | solution.py:56
  150.2 16.0 %collective-permute-done.36 = bf16[2,152,608]{2,1,0:T(8,128)(2,1)S(1)} collective-permute-done((bf16[2,152,608]{2,1,0:T(8,128)(2,1)S(1)}, bf16[2,152,608]{2,1,0:T(8,128)(2,1)S(1)}, u32[]{:S(2)}, u32[]{:S(2)}) %collective-permute-start.36) | collective-permute-done | bytes 369696 | tf_op jit(solution)/shard_map/ppermute | solution.py:78
  168.7 9.4 %collective-permute-done.40 = bf16[2,152,608]{2,1,0:T(8,128)(2,1)S(1)} collective-permute-done((bf16[2,152,608]{2,1,0:T(8,128)(2,1)S(1)}, bf16[2,152,608]{2,1,0:T(8,128)(2,1)S(1)}, u32[]{:S(2)}, u32[]{:S(2)}) %collective-permute-start.40) | collective-permute-done | bytes 369696 | tf_op jit(solution)/shard_map/ppermute | solution.py:78
  179.0 6.2 %collective-permute-done.37 = bf16[2,152,608]{2,1,0:T(8,128)(2,1)S(1)} collective-permute-done((bf16[2,152,608]{2,1,0:T(8,128)(2,1)S(1)}, bf16[2,152,608]{2,1,0:T(8,128)(2,1)S(1)}, u32[]{:S(2)}, u32[]{:S(2)}) %collective-permute-start.37) | collective-permute-done | bytes 369696 | tf_op jit(solution)/shard_map/ppermute | solution.py:78
  188.3 4.4 %shard_map.216 = bf16[608,1024]{1,0:T(8,128)(2,1)} custom-call(f32[2]{0:T(128)S(1)} %divide_bitcast_fusion.scale_ref, bf16[608,2432]{1,0:T(8,128)(2,1)S(1)} %copy-done.1, bf16[2,2,152,512]{3,2,1,0:T(8,128)(2,1)} %collective-permute-done.refs_0_, bf16[2,2,152,512]{3,2,1,0:T(8,128)(2,1)S(1)} %collective-permute-done.41.refs_1_, ...), custom_call_target="tpu_custom_call", output_to_operand_aliasing={{}: (6, {})} | custom-call | tf_op jit(solution)/shard_map/pallas_call | solution.py:56
  192.7 3.2 %shard_map.217 = bf16[608,1024]{1,0:T(8,128)(2,1)} custom-call(f32[2]{0:T(128)S(1)} %divide_bitcast_fusion.scale_ref, bf16[608,2432]{1,0:T(8,128)(2,1)S(1)} %copy-done.3, bf16[512,2432]{1,0:T(8,128)(2,1)S(1)} %collective-permute-done.43.refs_0_, bf16[608,1024]{1,0:T(8,128)(2,1)} %shard_map.211.refs_1_), custom_call_target="tpu_custom_call", output_to_operand_aliasing={{}: (3, {})} | custom-call | tf_op jit(solution)/shard_map/pallas_call | solution.py:56
  199.1 5.2 %shard_map.218 = (bf16[608,2432]{1,0:T(8,128)(2,1)}, bf16[608,2432]{1,0:T(8,128)(2,1)}) custom-call(bf16[4,2,152,608]{3,2,1,0:T(8,128)(2,1)S(1)} %pad_maximum_fusion.refs_0_, bf16[4,2,152,608]{3,2,1,0:T(8,128)(2,1)S(1)} %collective-permute-done.44.refs_1_, bf16[2,2,152,608]{3,2,1,0:T(8,128)(2,1)S(1)} %pad_maximum_fusion.1.refs_2_, ...), custom_call_target="tpu_custom_call" | custom-call | tf_op jit(solution)/shard_map/pallas_call | solution.py:56
  (162 shorter events, 52.9 us)
Async XLA Ops:
  7.9 9.7 %collective-permute-start.5 = (bf16[2,4,152,512]{3,2,1,0:T(8,128)(2,1)S(1)}, bf16[2,4,152,512]{3,2,1,0:T(8,128)(2,1)S(1)}, u32[]{:S(2)}, u32[]{:S(2)}) collective-permute-start(bf16[2,4,152,512]{3,2,1,0:T(8,128)(2,1)S(1)} %get-tuple-element.174), channel_id=1, source_target_pairs={{0,2},{2,0},{4,6},{6,4},{8,10},{10,8},{12,14},{14,12},{16,18},{18,... | collective-permute-start | bytes 3735560 | tf_op jit(solution)/shard_map/ppermute | solution.py:78
  8.4 9.1 %collective-permute-start.8 = (bf16[1,608,512]{2,1,0:T(8,128)(2,1)S(1)}, bf16[1,608,512]{2,1,0:T(8,128)(2,1)S(1)}, u32[]{:S(2)}, u32[]{:S(2)}) collective-permute-start(bf16[1,608,512]{2,1,0:T(8,128)(2,1)S(1)} %get-tuple-element.180.refs_2_), channel_id=1, source_target_pairs={{0,2},{2,0},{4,6},{6,4},{8,10},{10,8},{12,14},{14,12},{16,18},{18,... | collective-permute-start | bytes 1867784 | tf_op jit(solution)/shard_map/ppermute | solution.py:78
  8.5 18.5 %collective-permute-start.6 = (bf16[1,608,512]{2,1,0:T(8,128)(2,1)S(1)}, bf16[1,608,512]{2,1,0:T(8,128)(2,1)}, u32[]{:S(2)}, u32[]{:S(2)}) collective-permute-start(bf16[1,608,512]{2,1,0:T(8,128)(2,1)S(1)} %get-tuple-element.175), channel_id=1, source_target_pairs={{0,1},{1,0},{2,3},{3,2},{4,5},{5,4},{6,7},{7,6},{8,9},{9,8},{10,11... | collective-permute-start | bytes 1867784 | tf_op jit(solution)/shard_map/ppermute | solution.py:91
  17.0 25.9 %collective-permute-start.2 = (bf16[2,608,512]{2,1,0:T(8,128)(2,1)}, bf16[2,608,512]{2,1,0:T(8,128)(2,1)}, u32[]{:S(2)}, u32[]{:S(2)}) collective-permute-start(bf16[2,608,512]{2,1,0:T(8,128)(2,1)} %get-tuple-element.227.refs_4_), channel_id=1, source_target_pairs={{0,2},{2,0},{4,6},{6,4},{8,10},{10,8},{12,14},{14,12},{16,18},{18,... | collective-permute-start | bytes 3735560 | tf_op jit(solution)/shard_map/ppermute | solution.py:78
  25.0 9.4 %collective-permute-start.3 = (bf16[2,2,152,512]{3,2,1,0:T(8,128)(2,1)}, bf16[2,2,152,512]{3,2,1,0:T(8,128)(2,1)}, u32[]{:S(2)}, u32[]{:S(2)}) collective-permute-start(bf16[2,2,152,512]{3,2,1,0:T(8,128)(2,1)} %get-tuple-element.164), channel_id=1, source_target_pairs={{0,2},{2,0},{4,6},{6,4},{8,10},{10,8},{12,14},{14,12},{16,18},{18,... | collective-permute-start | bytes 1867784 | tf_op jit(solution)/shard_map/ppermute | solution.py:78
  27.0 14.3 %collective-permute-start.4 = (bf16[2,2,152,512]{3,2,1,0:T(8,128)(2,1)}, bf16[2,2,152,512]{3,2,1,0:T(8,128)(2,1)}, u32[]{:S(2)}, u32[]{:S(2)}) collective-permute-start(bf16[2,2,152,512]{3,2,1,0:T(8,128)(2,1)} %get-tuple-element.200), channel_id=1, source_target_pairs={{0,2},{2,0},{4,6},{6,4},{8,10},{10,8},{12,14},{14,12},{16,18},{18,... | collective-permute-start | bytes 1867784 | tf_op jit(solution)/shard_map/ppermute | solution.py:78
  32.0 34.1 %collective-permute-start = (bf16[2,2,152,512]{3,2,1,0:T(8,128)(2,1)}, bf16[2,2,152,512]{3,2,1,0:T(8,128)(2,1)}, u32[]{:S(2)}, u32[]{:S(2)}) collective-permute-start(bf16[2,2,152,512]{3,2,1,0:T(8,128)(2,1)} %get-tuple-element.209), channel_id=1, source_target_pairs={{0,1},{1,0},{2,3},{3,2},{4,5},{5,4},{6,7},{7,6},{8,9},{9,8},{10,11... | collective-permute-start | bytes 1867784 | tf_op jit(solution)/shard_map/ppermute | solution.py:91
  34.4 31.7 %collective-permute-start.1 = (bf16[2,2,152,512]{3,2,1,0:T(8,128)(2,1)}, bf16[2,2,152,512]{3,2,1,0:T(8,128)(2,1)}, u32[]{:S(2)}, u32[]{:S(2)}) collective-permute-start(bf16[2,2,152,512]{3,2,1,0:T(8,128)(2,1)} %get-tuple-element.164), channel_id=1, source_target_pairs={{0,3},{1,2},{2,1},{3,0},{4,7},{5,6},{6,5},{7,4},{8,11},{9,10},{10,... | collective-permute-start | bytes 1867784 | tf_op jit(solution)/shard_map/ppermute | solution.py:100
  34.5 26.0 %collective-permute-start.16 = (f32[8,128]{1,0:T(8,128)S(1)}, f32[8,128]{1,0:T(8,128)S(1)}, u32[]{:S(2)}, u32[]{:S(2)}) collective-permute-start(f32[8,128]{1,0:T(8,128)S(1)} %max.30), channel_id=1, source_target_pairs={{0,1},{1,0},{2,3},{3,2},{4,5},{5,4},{6,7},{7,6},{8,9},{9,8},{10,11... | collective-permute-start | bytes 12296 | tf_op jit(solution)/shard_map/ppermute | solution.py:376
  41.3 30.0 %collective-permute-start.15 = (f16[4,152,608]{2,1,0:T(8,128)(2,1)}, f16[4,152,608]{2,1,0:T(8,128)(2,1)}, u32[]{:S(2)}, u32[]{:S(2)}) collective-permute-start(f16[4,152,608]{2,1,0:T(8,128)(2,1)} %get-tuple-element.309), channel_id=1, source_target_pairs={{0,4},{2,6},{4,0},{6,2},{8,12},{10,14},{12,8},{14,10},{16,20},{18,... | collective-permute-start | bytes 2217992 | tf_op jit(solution)/shard_map/ppermute | solution.py:78
  62.4 32.3 %collective-permute-start.14 = (bf16[2,2,152,512]{3,2,1,0:T(8,128)(2,1)}, bf16[2,2,152,512]{3,2,1,0:T(8,128)(2,1)}, u32[]{:S(2)}, u32[]{:S(2)}) collective-permute-start(bf16[2,2,152,512]{3,2,1,0:T(8,128)(2,1)} %copy-done.15), channel_id=1, source_target_pairs={{0,1},{1,0},{2,3},{3,2},{4,5},{5,4},{6,7},{7,6},{8,9},{9,8},{10,11... | collective-permute-start | bytes 1867784 | tf_op jit(solution)/shard_map/ppermute | solution.py:91
  64.5 20.4 %collective-permute-start.19 = (f16[4,152,608]{2,1,0:T(8,128)(2,1)S(1)}, f16[4,152,608]{2,1,0:T(8,128)(2,1)S(1)}, u32[]{:S(2)}, u32[]{:S(2)}) collective-permute-start(f16[4,152,608]{2,1,0:T(8,128)(2,1)S(1)} %get-tuple-element.307), channel_id=1, source_target_pairs={{0,4},{2,6},{4,0},{6,2},{8,12},{10,14},{12,8},{14,10},{16,20},{18,... | collective-permute-start | bytes 2217992 | tf_op jit(solution)/shard_map/ppermute | solution.py:78
  70.8 19.2 %collective-permute-start.18 = (f16[2,152,608]{2,1,0:T(8,128)(2,1)S(1)}, f16[2,152,608]{2,1,0:T(8,128)(2,1)S(1)}, u32[]{:S(2)}, u32[]{:S(2)}) collective-permute-start(f16[2,152,608]{2,1,0:T(8,128)(2,1)S(1)} %fusion.4), channel_id=1, source_target_pairs={{0,4},{2,6},{4,0},{6,2},{8,12},{10,14},{12,8},{14,10},{16,20},{18,... | collective-permute-start | bytes 1109000 | tf_op jit(solution)/shard_map/ppermute | solution.py:78
  71.3 23.4 %collective-permute-start.13 = (bf16[2,2,152,512]{3,2,1,0:T(8,128)(2,1)}, bf16[2,2,152,512]{3,2,1,0:T(8,128)(2,1)S(1)}, u32[]{:S(2)}, u32[]{:S(2)}) collective-permute-start(bf16[2,2,152,512]{3,2,1,0:T(8,128)(2,1)} %get-tuple-element.200), channel_id=1, source_target_pairs={{0,3},{1,2},{2,1},{3,0},{4,7},{5,6},{6,5},{7,4},{8,11},{9,10},{10,... | collective-permute-start | bytes 1867784 | tf_op jit(solution)/shard_map/ppermute | solution.py:100
  73.5 18.4 %collective-permute-start.17 = (f16[2,152,608]{2,1,0:T(8,128)(2,1)S(1)}, f16[2,152,608]{2,1,0:T(8,128)(2,1)S(1)}, u32[]{:S(2)}, u32[]{:S(2)}) collective-permute-start(f16[2,152,608]{2,1,0:T(8,128)(2,1)S(1)} %get-tuple-element.316), channel_id=1, source_target_pairs={{0,8},{2,10},{4,12},{6,14},{8,0},{10,2},{12,4},{14,6},{16,24},{18,... | collective-permute-start | bytes 1109000 | tf_op jit(solution)/shard_map/ppermute | solution.py:78
  85.1 17.0 %collective-permute-start.23 = (f16[2,152,608]{2,1,0:T(8,128)(2,1)S(1)}, f16[2,152,608]{2,1,0:T(8,128)(2,1)S(1)}, u32[]{:S(2)}, u32[]{:S(2)}) collective-permute-start(f16[2,152,608]{2,1,0:T(8,128)(2,1)S(1)} %get-tuple-element.311), channel_id=1, source_target_pairs={{0,8},{2,10},{4,12},{6,14},{8,0},{10,2},{12,4},{14,6},{16,24},{18,... | collective-permute-start | bytes 1109000 | tf_op jit(solution)/shard_map/ppermute | solution.py:78
  90.2 28.5 %collective-permute-start.20 = (f16[2,152,608]{2,1,0:T(8,128)(2,1)S(1)}, f16[2,152,608]{2,1,0:T(8,128)(2,1)S(1)}, u32[]{:S(2)}, u32[]{:S(2)}) collective-permute-start(f16[2,152,608]{2,1,0:T(8,128)(2,1)S(1)} %multiply_convert_fusion.2), channel_id=1, source_target_pairs={{0,8},{2,10},{4,12},{6,14},{8,0},{10,2},{12,4},{14,6},{16,24},{18,... | collective-permute-start | bytes 1109000 | tf_op jit(solution)/shard_map/ppermute | solution.py:78
  92.0 15.4 %collective-permute-start.25 = (f16[152,608]{1,0:T(8,128)(2,1)S(1)}, f16[152,608]{1,0:T(8,128)(2,1)S(1)}, u32[]{:S(2)}, u32[]{:S(2)}) collective-permute-start(f16[152,608]{1,0:T(8,128)(2,1)S(1)} %get-tuple-element.319), channel_id=1, source_target_pairs={{0,16},{2,18},{4,20},{6,22},{8,24},{10,26},{12,28},{14,30},{16,0},... | collective-permute-start | bytes 554504 | tf_op jit(solution)/shard_map/ppermute | solution.py:78
  99.0 19.6 %collective-permute-start.22 = (f16[152,608]{1,0:T(8,128)(2,1)S(1)}, f16[152,608]{1,0:T(8,128)(2,1)S(1)}, u32[]{:S(2)}, u32[]{:S(2)}) collective-permute-start(f16[152,608]{1,0:T(8,128)(2,1)S(1)} %get-tuple-element.312), channel_id=1, source_target_pairs={{0,4},{2,6},{4,0},{6,2},{8,12},{10,14},{12,8},{14,10},{16,20},{18,... | collective-permute-start | bytes 554504 | tf_op jit(solution)/shard_map/ppermute | solution.py:78
  100.6 18.3 %collective-permute-start.21 = (f16[152,608]{1,0:T(8,128)(2,1)S(1)}, f16[152,608]{1,0:T(8,128)(2,1)S(1)}, u32[]{:S(2)}, u32[]{:S(2)}) collective-permute-start(f16[152,608]{1,0:T(8,128)(2,1)S(1)} %get-tuple-element.314), channel_id=1, source_target_pairs={{0,4},{2,6},{4,0},{6,2},{8,12},{10,14},{12,8},{14,10},{16,20},{18,... | collective-permute-start | bytes 554504 | tf_op jit(solution)/shard_map/ppermute | solution.py:78
  102.3 15.5 %collective-permute-start.24 = (f16[152,608]{1,0:T(8,128)(2,1)S(1)}, f16[152,608]{1,0:T(8,128)(2,1)S(1)}, u32[]{:S(2)}, u32[]{:S(2)}) collective-permute-start(f16[152,608]{1,0:T(8,128)(2,1)S(1)} %get-tuple-element.320), channel_id=1, source_target_pairs={{0,16},{2,18},{4,20},{6,22},{8,24},{10,26},{12,28},{14,30},{16,0},... | collective-permute-start | bytes 554504 | tf_op jit(solution)/shard_map/ppermute | solution.py:78
  117.9 9.8 %collective-permute-start.27 = (f32[152,608]{1,0:T(8,128)S(1)}, f32[152,608]{1,0:T(8,128)S(1)}, u32[]{:S(2)}, u32[]{:S(2)}) collective-permute-start(f32[152,608]{1,0:T(8,128)S(1)} %multiply_add_fusion.5), channel_id=1, source_target_pairs={{0,1},{1,0},{2,3},{3,2},{4,5},{5,4},{6,7},{7,6},{8,9},{9,8},{10,11... | collective-permute-start | bytes 1109000 | tf_op jit(solution)/shard_map/ppermute | solution.py:91
  131.8 60.9 %collective-permute-start.43 = (bf16[512,2432]{1,0:T(8,128)(2,1)S(1)}, bf16[512,2432]{1,0:T(8,128)(2,1)S(1)}, u32[]{:S(2)}, u32[]{:S(2)}) collective-permute-start(bf16[512,2432]{1,0:T(8,128)(2,1)S(1)} %copy-done.8), channel_id=1, source_target_pairs={{0,1},{1,0},{2,3},{3,2},{4,5},{5,4},{6,7},{7,6},{8,9},{9,8},{10,11... | collective-permute-start | bytes 7471112 | tf_op jit(solution)/shard_map/ppermute | solution.py:91
  147.7 18.5 %collective-permute-start.36 = (bf16[2,152,608]{2,1,0:T(8,128)(2,1)S(1)}, bf16[2,152,608]{2,1,0:T(8,128)(2,1)S(1)}, u32[]{:S(2)}, u32[]{:S(2)}) collective-permute-start(bf16[2,152,608]{2,1,0:T(8,128)(2,1)S(1)} %get-tuple-element.270), channel_id=1, source_target_pairs={{0,8},{2,10},{4,12},{6,14},{8,0},{10,2},{12,4},{14,6},{16,24},{18,... | collective-permute-start | bytes 1109000 | tf_op jit(solution)/shard_map/ppermute | solution.py:78
  147.7 20.7 %collective-permute-start.35 = (bf16[2,152,608]{2,1,0:T(8,128)(2,1)S(1)}, bf16[2,152,608]{2,1,0:T(8,128)(2,1)S(1)}, u32[]{:S(2)}, u32[]{:S(2)}) collective-permute-start(bf16[2,152,608]{2,1,0:T(8,128)(2,1)S(1)} %get-tuple-element.270), channel_id=1, source_target_pairs={{0,16},{2,18},{4,20},{6,22},{8,24},{10,26},{12,28},{14,30},{16,0},... | collective-permute-start | bytes 1109000 | tf_op jit(solution)/shard_map/ppermute | solution.py:78
  149.6 19.1 %collective-permute-start.39 = (bf16[2,152,608]{2,1,0:T(8,128)(2,1)S(1)}, bf16[2,152,608]{2,1,0:T(8,128)(2,1)S(1)}, u32[]{:S(2)}, u32[]{:S(2)}) collective-permute-start(bf16[2,152,608]{2,1,0:T(8,128)(2,1)S(1)} %get-tuple-element.270), channel_id=1, source_target_pairs={{0,4},{2,6},{4,0},{6,2},{8,12},{10,14},{12,8},{14,10},{16,20},{18,... | collective-permute-start | bytes 1109000 | tf_op jit(solution)/shard_map/ppermute | solution.py:78
  166.2 11.9 %collective-permute-start.40 = (bf16[2,152,608]{2,1,0:T(8,128)(2,1)S(1)}, bf16[2,152,608]{2,1,0:T(8,128)(2,1)S(1)}, u32[]{:S(2)}, u32[]{:S(2)}) collective-permute-start(bf16[2,152,608]{2,1,0:T(8,128)(2,1)S(1)} %collective-permute-done.36), channel_id=1, source_target_pairs={{0,4},{2,6},{4,0},{6,2},{8,12},{10,14},{12,8},{14,10},{16,20},{18,... | collective-permute-start | bytes 1109000 | tf_op jit(solution)/shard_map/ppermute | solution.py:78
  168.4 10.6 %collective-permute-start.38 = (bf16[2,152,608]{2,1,0:T(8,128)(2,1)S(1)}, bf16[2,152,608]{2,1,0:T(8,128)(2,1)S(1)}, u32[]{:S(2)}, u32[]{:S(2)}) collective-permute-start(bf16[2,152,608]{2,1,0:T(8,128)(2,1)S(1)} %collective-permute-done.35), channel_id=1, source_target_pairs={{0,8},{2,10},{4,12},{6,14},{8,0},{10,2},{12,4},{14,6},{16,24},{18,... | collective-permute-start | bytes 1109000 | tf_op jit(solution)/shard_map/ppermute | solution.py:78
  168.4 16.8 %collective-permute-start.37 = (bf16[2,152,608]{2,1,0:T(8,128)(2,1)S(1)}, bf16[2,152,608]{2,1,0:T(8,128)(2,1)S(1)}, u32[]{:S(2)}, u32[]{:S(2)}) collective-permute-start(bf16[2,152,608]{2,1,0:T(8,128)(2,1)S(1)} %collective-permute-done.35), channel_id=1, source_target_pairs={{0,4},{2,6},{4,0},{6,2},{8,12},{10,14},{12,8},{14,10},{16,20},{18,... | collective-permute-start | bytes 1109000 | tf_op jit(solution)/shard_map/ppermute | solution.py:78
  178.5 18.9 %collective-permute-start.44 = (bf16[4,2,152,608]{3,2,1,0:T(8,128)(2,1)S(1)}, bf16[4,2,152,608]{3,2,1,0:T(8,128)(2,1)S(1)}, u32[]{:S(2)}, u32[]{:S(2)}) collective-permute-start(bf16[4,2,152,608]{3,2,1,0:T(8,128)(2,1)S(1)} %pad_maximum_fusion.refs_0_), channel_id=1, source_target_pairs={{0,2},{2,0},{4,6},{6,4},{8,10},{10,8},{12,14},{14,12},{16,18},{18,... | collective-permute-start | bytes 4435976 | tf_op jit(solution)/shard_map/ppermute | solution.py:78
  185.8 11.0 %collective-permute-start.46 = (bf16[2,152,608]{2,1,0:T(8,128)(2,1)S(1)}, bf16[2,152,608]{2,1,0:T(8,128)(2,1)S(1)}, u32[]{:S(2)}, u32[]{:S(2)}) collective-permute-start(bf16[2,152,608]{2,1,0:T(8,128)(2,1)S(1)} %collective-permute-done.38.refs_4_), channel_id=1, source_target_pairs={{0,4},{2,6},{4,0},{6,2},{8,12},{10,14},{12,8},{14,10},{16,20},{18,... | collective-permute-start | bytes 1109000 | tf_op jit(solution)/shard_map/ppermute | solution.py:78
  187.7 9.7 %collective-permute-start.45 = (bf16[2,2,152,608]{3,2,1,0:T(8,128)(2,1)S(1)}, bf16[2,2,152,608]{3,2,1,0:T(8,128)(2,1)S(1)}, u32[]{:S(2)}, u32[]{:S(2)}) collective-permute-start(bf16[2,2,152,608]{3,2,1,0:T(8,128)(2,1)S(1)} %pad_maximum_fusion.1.refs_2_), channel_id=1, source_target_pairs={{0,2},{2,0},{4,6},{6,4},{8,10},{10,8},{12,14},{14,12},{16,18},{18,... | collective-permute-start | bytes 2217992 | tf_op jit(solution)/shard_map/ppermute | solution.py:78
  (41 other events, 317.5 us)
